TPU v7x, 32 devices: a whole 2x2x4 slice. The times are simulated.
32 devices in a mesh: groups: 2 (over x), ctx: 16 (over z, y, core).
Axes of the slice: x: 2, y: 2, z: 4, core: 2. Of those that a mesh axis runs over, the one named last changes fastest.
Arguments:
- queries: bfloat16 [4096, 8192], P(('groups', 'ctx')), parts along dimension 0, may hold values from -112 to 112
- keys: bfloat16 [4096, 1024], P(('groups', 'ctx')), parts along dimension 0, may hold values from -4.04 to 4.04
- values: bfloat16 [4096, 1024], P(('groups', 'ctx')), parts along dimension 0, may hold values from -4 to 4
- norm_gain: float32 [8192], replicated, may hold values from 0.1 to 1.9
- expert_ids: int32 [4096, 2], P(('groups', 'ctx')), parts along dimension 0, may hold values from 0 to 15, as said below
- gates: float32 [4096, 2], P(('groups', 'ctx')), parts along dimension 0, may hold values from 0.2 to 1
- w_gate: bfloat16 [8192, 12288], P(None, 'ctx'), may hold values from -0.0625 to 0.0625
- w_up: bfloat16 [8192, 12288], P(None, 'ctx'), may hold values from -0.0625 to 0.0625
- w_down: bfloat16 [12288, 8192], P('ctx'), may hold values from -0.0546875 to 0.0546875
Outputs:
- attention: bfloat16 [4096, 8192], P(('groups', 'ctx')), parts along dimension 0
- mixed: bfloat16 [4096, 8192], P(('groups', 'ctx')), parts along dimension 0
There are 2 independent parts, one for each index of `groups`. A program takes and returns all parts, laid end to end along the dimension named above; an argument that names none is the same for every part. Nothing has to cross between parts.
Inputs may be any that keep to these rules, and one draw needn't show every extreme that they name: `expert_ids`: each token names two different experts. In each aligned block of 128 rows (the rows of one device) between 8 and 16 rows name expert 0, and in some block exactly 16 do.
All inputs are finite; a program needn't handle non-finite values.
Results may differ from a plain program's by a relative error of at most 0.02.
Values may be sent and summed in bfloat16 or wider, within the bound.
No kernel may reach another device: no remote copies, remote signals or barrier semaphores. Data moves between devices by JAX's collectives and lax.ppermute only.
A program may use at most 128 MiB of HBM per device.

v0:
```python
import functools
import math

import jax
import jax.numpy as jnp
from jax import lax
from jax.experimental import pallas as pl
from jax.experimental.pallas import tpu as pltpu
from jax.sharding import PartitionSpec as P

HQ = 64
HK = 8
DH = 128
CAP = 16
GROUP = HQ // HK
WIDE = GROUP * DH
LOG_SCALE = math.log2(math.e) / math.sqrt(DH)
MASKED = -1e30
PIECES = 2
SUM_LIMIT = 2.0**100
PARTS = 3
STACK = 4
MIB = 1 << 20


def in_hbm(x):
    return pltpu.with_memory_space_constraint(x, pltpu.HBM)


def ring_order(chips):
    return list(range(0, chips, 2)) + list(range(1, chips, 2))[::-1]


def permutations(chips):
    order = ring_order(chips)
    right, left = [], []
    for place in range(chips):
        here, there = order[place], order[(place + 1) % chips]
        for core in range(2):
            right.append((2 * here + core, 2 * there + core))
            left.append((2 * there + core, 2 * here + core))
    sibling = [(i, i ^ 1) for i in range(2 * chips)]
    return right, left, sibling


def chip_at(me, step, chips):
    chip = me // 2
    place = jnp.where(chip % 2 == 0, chip // 2, chips - 1 - chip // 2)
    source = (place - step + 2 * chips) % chips
    return jnp.where(source < chips // 2, 2 * source, 2 * (chips - 1 - source) + 1)


def head_rows(queries, first):
    return jnp.concatenate(
        [queries[:, h * DH : (h + 1) * DH] for h in range(first, first + STACK)], axis=0
    )


def with_ones(values):
    return jnp.concatenate([values, jnp.ones_like(values)], axis=1)


def scores_of(queries, keys):
    return LOG_SCALE * lax.dot_general(
        queries, keys, (((1,), (1,)), ((), ())), preferred_element_type=jnp.float32
    )


def weights_of(scores, shift):
    return jnp.exp2(scores - jnp.concatenate([shift] * (scores.shape[1] // DH), axis=1))


def row_top(scores):
    return jnp.broadcast_to(jnp.max(scores, axis=1, keepdims=True), (scores.shape[0], DH))


def diagonal(tokens):
    shape = (STACK * tokens, tokens)
    token = lax.broadcasted_iota(jnp.int32, shape, 0) % tokens
    return lax.broadcasted_iota(jnp.int32, shape, 1) <= token


def head_group(q_ref, group):
    return q_ref[:, pl.ds(pl.multiple_of(group * WIDE, WIDE), WIDE)]


def for_groups(body):
    def step(group, carry):
        body(group, pl.ds(pl.multiple_of(group * DH, DH), DH))
        return carry

    lax.fori_loop(0, HK, step, 0)


def own_kernel(q_ref, own_ref, acc_ref, total_ref, shift_ref):
    tokens = q_ref.shape[0]
    allowed = diagonal(tokens)

    def one_group(group, columns):
        keys, values = own_ref[:tokens, columns], with_ones(own_ref[tokens:, columns])
        queries = head_group(q_ref, group)
        for first in range(0, GROUP, STACK):
            rows = slice(first * tokens, (first + STACK) * tokens)
            scores = jnp.where(allowed, scores_of(head_rows(queries, first), keys), MASKED)
            shift = row_top(scores)
            weights = weights_of(scores, shift).astype(jnp.bfloat16)
            update = jnp.dot(weights, values, preferred_element_type=jnp.float32)
            acc_ref[group, rows, :] = update[:, :DH]
            total_ref[group, rows, :] = update[:, DH:]
            shift_ref[group, rows, :] = shift

    for_groups(one_group)


def fold(queries, first, keys, values, shift):
    weights = weights_of(scores_of(head_rows(queries, first), keys), shift).astype(jnp.bfloat16)
    return jnp.dot(weights, values, preferred_element_type=jnp.float32)


def block_factors(earlier):
    return [jnp.where(flag, 1.0, 0.0).astype(jnp.bfloat16) for flag in earlier]


def join_blocks(blocks, factors, columns):
    pairs = [block(columns) for block in blocks]
    keys = jnp.concatenate([key for key, _ in pairs], axis=0)
    values = [with_ones(value) * factor for (_, value), factor in zip(pairs, factors)]
    return keys, jnp.concatenate(values, axis=0)


def fold_blocks(q_ref, blocks, earlier, shift_ref, acc_ref, total_ref):
    tokens = q_ref.shape[0]

    @pl.when(functools.reduce(jnp.logical_or, earlier))
    def _():
        factors = block_factors(earlier)

        def one_group(group, columns):
            keys, values = join_blocks(blocks, factors, columns)
            queries = head_group(q_ref, group)
            for first in range(0, GROUP, STACK):
                rows = slice(first * tokens, (first + STACK) * tokens)
                update = fold(queries, first, keys, values, shift_ref[group, rows, :])
                acc_ref[group, rows, :] += update[:, :DH]
                total_ref[group, rows, :] += update[:, DH:]

        for_groups(one_group)


def in_one(ref):
    tokens = ref.shape[0] // 2
    return lambda columns: (ref[:tokens, columns], ref[tokens:, columns])


def in_two(key_ref, value_ref):
    return lambda columns: (key_ref[:, columns], value_ref[:, columns])


def is_earlier(me, place, sibling, chips):
    core = 1 - me % 2 if sibling else me % 2
    return 2 * chip_at(me, place, chips) + core < me


def step_kernel(chips, places, me_ref, q_ref, *refs):
    count = len(places)
    blocks, shift_ref, state = refs[:count], refs[count], refs[count + 3 :]
    me = me_ref[0]
    earlier = [is_earlier(me, place, sibling, chips) for place, sibling in places]
    fold_blocks(q_ref, [in_one(ref) for ref in blocks], earlier, shift_ref, *state)


def allowed_in(chip, me, tokens):
    shape = (STACK * tokens, 2 * tokens)
    token = lax.broadcasted_iota(jnp.int32, shape, 0) % tokens
    column = lax.broadcasted_iota(jnp.int32, shape, 1)
    sibling = jnp.where(jnp.logical_or(me % 2 == 1, chip < me // 2), 2 * tokens, 0)
    own = jnp.where(chip < me // 2, 2 * tokens, token)
    return column <= jnp.where(column < tokens, own, sibling)


def running_attention(chips, me, sources, q_ref, out_ref, rows_ref, table_ref, scratch, sem):
    keys_ref, values_ref, acc_ref, total_ref, top_ref = scratch
    tokens = q_ref.shape[0]
    half = chips // 2
    places = [0] + [p for step in range(1, half) for p in (step, -step)] + [half]

    def fetch(source, target):
        copy = pltpu.make_async_copy(source, target, sem)
        copy.start()
        copy.wait()

    def one_head(head, carry):
        columns = pl.ds(pl.multiple_of(head * DH, DH), DH)
        queries = head_group(q_ref, head)
        for i, place in enumerate(places):
            if place != half:
                for core in range(2):
                    rows = pl.ds(core * tokens, tokens)
                    block = sources[2 * i + core]
                    fetch(block.at[pl.ds(0, tokens), columns], keys_ref.at[i, rows])
                    fetch(block.at[pl.ds(tokens, tokens), columns], values_ref.at[i, rows])
            else:
                key, value, sib_key, sib_value = sources[2 * i :]
                for core, (k, v) in enumerate(((key, value), (sib_key, sib_value))):
                    rows = pl.ds(core * tokens, tokens)
                    fetch(k.at[:, columns], keys_ref.at[i, rows])
                    fetch(v.at[:, columns], values_ref.at[i, rows])
        acc_ref[...] = jnp.zeros_like(acc_ref)
        total_ref[...] = jnp.zeros_like(total_ref)
        top_ref[...] = jnp.full_like(top_ref, 2 * MASKED)

        def one_chip(i, inner):
            forward = (i + 1) // 2
            place = jnp.where(i % 2 == 1, forward, -forward)
            chip = chip_at(me, place, chips)

            @pl.when(chip <= me // 2)
            def _():
                allowed = allowed_in(chip, me, tokens)
                keys, values = keys_ref[i], with_ones(values_ref[i])
                for first in range(0, GROUP, STACK):
                    rows = slice(first * tokens, (first + STACK) * tokens)
                    scores = jnp.where(allowed, scores_of(head_rows(queries, first), keys), MASKED)
                    old = top_ref[rows, :]
                    top = jnp.maximum(old, row_top(scores))
                    factor = jnp.exp2(old - top)
                    weights = weights_of(scores, top).astype(jnp.bfloat16)
                    update = jnp.dot(weights, values, preferred_element_type=jnp.float32)
                    acc_ref[rows, :] = acc_ref[rows, :] * factor + update[:, :DH]
                    total_ref[rows, :] = total_ref[rows, :] * factor + update[:, DH:]
                    top_ref[rows, :] = top

            return inner

        lax.fori_loop(0, chips, one_chip, 0)
        put_heads(out_ref, rows_ref, table_ref, head, divide(acc_ref[...], total_ref[...]))
        return carry

    lax.fori_loop(0, HK, one_head, 0)


def divide(acc, total):
    inverse = pl.reciprocal(total, approx=True)
    inverse = inverse * (2.0 - total * inverse)
    return (acc * inverse).astype(jnp.bfloat16)


def put_heads(out_ref, rows_ref, table_ref, group, result):
    tokens = out_ref.shape[0]
    columns = pl.ds(pl.multiple_of(group * WIDE, WIDE), WIDE)
    result = jnp.concatenate([result[h * tokens : (h + 1) * tokens] for h in range(GROUP)], axis=1)
    out_ref[:, columns] = result
    rows_ref[:, columns] = jnp.dot(table_ref[...], result, preferred_element_type=jnp.float32)


def last_kernel(chips, me_ref, q_ref, *refs):
    late_left, late_right, key, value, sib_key, sib_value, shift_ref = refs[:7]
    acc_ref, total_ref, gain_ref, table_ref = refs[7:11]
    sources = refs[11 : 13 + 2 * chips]
    keep_ref, give_ref, result_ref = refs[13 + 2 * chips : 16 + 2 * chips]
    out_ref, rows_ref, worst_ref, sem, out_sems, *scratch = refs[16 + 2 * chips :]
    tokens, width = q_ref.shape
    me = me_ref[0]
    half = chips // 2
    places = [(half - 1, True), (1 - half, True), (half, False), (half, True)]
    blocks = [in_one(late_left), in_one(late_right), in_two(key, value), in_two(sib_key, sib_value)]
    factors = block_factors([is_earlier(me, *place, chips) for place in places])
    worst_ref[...] = jnp.zeros_like(worst_ref)

    def write_out(group):
        columns = pl.ds(pl.multiple_of(group * WIDE, WIDE), WIDE)
        return pltpu.make_async_copy(
            out_ref.at[:, columns], result_ref.at[:, columns], out_sems.at[group]
        )

    def one_group(group, columns):
        keys, values = join_blocks(blocks, factors, columns)
        queries = head_group(q_ref, group)
        results = []
        for first in range(0, GROUP, STACK):
            rows = slice(first * tokens, (first + STACK) * tokens)
            update = fold(queries, first, keys, values, shift_ref[group, rows, :])
            total = total_ref[group, rows, :] + update[:, DH:]
            worst_ref[...] = jnp.maximum(worst_ref[...], total)
            results.append(divide(acc_ref[group, rows, :] + update[:, :DH], total))
        put_heads(out_ref, rows_ref, table_ref, group, jnp.concatenate(results, axis=0))
        write_out(group).start()

    for_groups(one_group)

    def norm_rows():
        core = me % 2
        squares = rows_ref[...] * rows_ref[...]
        scale = lax.rsqrt(jnp.sum(squares, axis=1, keepdims=True) / width + 1e-05)
        for side, ref in ((core, keep_ref), (1 - core, give_ref)):
            columns = pl.ds(pl.multiple_of(side * (width // 2), width // 2), width // 2)
            ref[...] = (rows_ref[:, columns] * scale * gain_ref[:, columns]).astype(jnp.bfloat16)

    norm_rows()
    fits = jnp.max(worst_ref[...]) <= SUM_LIMIT
    for group in range(HK):
        write_out(group).wait()

    @pl.when(jnp.logical_not(fits))
    def _():
        running_attention(chips, me, sources, q_ref, out_ref, rows_ref, table_ref, scratch, sem)
        for group in range(HK):
            write_out(group).start()
        for group in range(HK):
            write_out(group).wait()
        norm_rows()


class Attention:
    def __init__(self, me, queries, chips):
        self.me, self.queries, self.chips = me, queries, chips
        tokens = queries.shape[0]
        self.state_shape = pltpu.VMEM((HK, GROUP * tokens, DH), jnp.float32)

    def call(self, kernel, name, args, others, out_shape, out_others, scratch, aliases=None):
        tokens, width = self.queries.shape
        vmem, anywhere = pl.BlockSpec(memory_space=pltpu.VMEM), pl.BlockSpec(memory_space=pl.ANY)
        smem = pl.BlockSpec(memory_space=pltpu.SMEM)
        return pl.pallas_call(
            kernel,
            in_specs=[smem if x is self.me else vmem for x in args] + [anywhere] * len(others),
            out_specs=[vmem] * len(out_shape) + [anywhere] * len(out_others),
            out_shape=[*out_shape, *out_others],
            scratch_shapes=scratch,
            input_output_aliases=aliases or {},
            compiler_params=pltpu.CompilerParams(vmem_limit_bytes=12 * MIB),
            cost_estimate=pl.CostEstimate(
                flops=4 * tokens * width * tokens, bytes_accessed=4 * MIB, transcendentals=0
            ),
            name=name,
        )(*args, *others)

    def own(self, own):
        *state, shift = self.call(
            own_kernel, "attend_own", (self.queries, own), (), [self.state_shape] * 3, (), ()
        )
        return state, shift

    def step(self, blocks, places, shift, state):
        count = len(blocks)
        return self.call(
            functools.partial(step_kernel, self.chips, places),
            "attend_step",
            (self.me, self.queries, *blocks, shift, *state),
            (),
            [self.state_shape] * 2,
            (),
            (),
            {count + 3: 0, count + 4: 1},
        )

    def last(self, late, pieces, shift, state, gain, table, sources):
        tokens, width = self.queries.shape
        rows = GROUP * tokens
        out = jax.ShapeDtypeStruct((tokens, width), jnp.bfloat16)
        picked = pltpu.VMEM((CAP, width // 2), jnp.bfloat16)
        return self.call(
            functools.partial(last_kernel, self.chips),
            "attend_last",
            (self.me, self.queries, *late, *pieces, shift, *state, gain, table),
            sources,
            [picked, picked],
            [out],
            [
                pltpu.VMEM((tokens, width), jnp.bfloat16),
                pltpu.VMEM((CAP, width), jnp.float32),
                pltpu.VMEM((STACK * tokens, DH), jnp.float32),
                pltpu.SemaphoreType.DMA,
                pltpu.SemaphoreType.DMA((HK,)),
                pltpu.VMEM((self.chips, 2 * tokens, DH), jnp.bfloat16),
                pltpu.VMEM((self.chips, 2 * tokens, DH), jnp.bfloat16),
            ]
            + [pltpu.VMEM((rows, DH), jnp.float32)] * 3,
        )


def stack_kernel(upper_ref, lower_ref, out_ref, sems):
    rows = upper_ref.shape[0]
    copies = [
        pltpu.make_async_copy(ref, out_ref.at[pl.ds(i * rows, rows)], sems.at[i])
        for i, ref in enumerate((upper_ref, lower_ref))
    ]
    for copy in copies:
        copy.start()
    for copy in copies:
        copy.wait()


def stack(upper, lower):
    anywhere = pl.BlockSpec(memory_space=pl.ANY)
    return pl.pallas_call(
        stack_kernel,
        in_specs=[anywhere] * 2,
        out_specs=anywhere,
        out_shape=pltpu.VMEM((2 * upper.shape[0], upper.shape[1]), upper.dtype),
        scratch_shapes=[pltpu.SemaphoreType.DMA((2,))],
        compiler_params=pltpu.CompilerParams(vmem_limit_bytes=MIB),
        name="stack",
    )(in_hbm(upper), in_hbm(lower))


def load_kernel(start, source_ref, target_ref, sem):
    columns = pl.ds(start, target_ref.shape[1])
    copy = pltpu.make_async_copy(source_ref.at[:, columns], target_ref, sem)
    copy.start()
    copy.wait()


def load(x, piece=0, pieces=1):
    rows, width = x.shape[0], x.shape[1] // pieces
    return pl.pallas_call(
        functools.partial(load_kernel, piece * width),
        in_specs=[pl.BlockSpec(memory_space=pl.ANY)],
        out_specs=pl.BlockSpec(memory_space=pl.ANY),
        out_shape=pltpu.VMEM((rows, width), x.dtype),
        scratch_shapes=[pltpu.SemaphoreType.DMA],
        compiler_params=pltpu.CompilerParams(vmem_limit_bytes=MIB),
        cost_estimate=pl.CostEstimate(flops=0, bytes_accessed=rows * width, transcendentals=0),
        name="load",
    )(in_hbm(x))


def gather_kernel(*refs):
    blocks, out_ref = refs[:-1], refs[-1]
    middle = out_ref.shape[0] // 2
    parts = [(ref[:CAP], ref[CAP:]) for ref in blocks[:-2]] + [(blocks[-2][...], blocks[-1][...])]
    for j, (mine, other) in enumerate(parts):
        out_ref[j * CAP : (j + 1) * CAP] = mine
        out_ref[middle + j * CAP : middle + (j + 1) * CAP] = other


def gather(blocks):
    vmem = pl.BlockSpec(memory_space=pltpu.VMEM)
    width = blocks[0].shape[1]
    return pl.pallas_call(
        gather_kernel,
        in_specs=[vmem] * len(blocks),
        out_specs=vmem,
        out_shape=pltpu.VMEM((2 * CAP * (len(blocks) - 1), width), jnp.bfloat16),
        compiler_params=pltpu.CompilerParams(vmem_limit_bytes=4 * MIB),
        name="gather",
    )(*blocks)


def hidden_kernel(second, me_ref, rows_ref, gate_ref, up_ref, *refs):
    half = rows_ref.shape[1]
    middle = rows_ref.shape[0] // 2
    depth = min(1024, half)
    if second:
        gate_in, up_in, out_ref, gate_sum, up_sum = refs
        gate_sum[...] = gate_in[...]
        up_sum[...] = up_in[...]
    else:
        gate_sum, up_sum = refs
        gate_sum[...] = jnp.zeros_like(gate_sum)
        up_sum[...] = jnp.zeros_like(up_sum)
    side = 1 - me_ref[0] % 2 if second else me_ref[0] % 2

    def one_part(step, carry):
        part = rows_ref[:, pl.ds(pl.multiple_of(step * depth, depth), depth)]
        if second:
            part = jnp.concatenate([part[middle:], part[:middle]], axis=0)
        place = pl.ds(pl.multiple_of(side * half + step * depth, depth), depth)
        gate_sum[...] += jnp.dot(part, gate_ref[place, :], preferred_element_type=jnp.float32)
        up_sum[...] += jnp.dot(part, up_ref[place, :], preferred_element_type=jnp.float32)
        return carry

    lax.fori_loop(0, half // depth, one_part, 0)
    if second:
        gate = gate_sum[...]
        out_ref[...] = (gate / (1.0 + jnp.exp(-gate)) * up_sum[...]).astype(jnp.bfloat16)


def hidden_call(me, rows, w_gate, w_up, sums=None):
    count, half = rows.shape
    units = w_gate.shape[1]
    vmem = pl.BlockSpec(memory_space=pltpu.VMEM)
    sum_shape = pltpu.VMEM((count, units), jnp.float32)
    second = sums is not None
    return pl.pallas_call(
        functools.partial(hidden_kernel, second),
        in_specs=[pl.BlockSpec(memory_space=pltpu.SMEM)] + [vmem] * (5 if second else 3),
        out_specs=vmem if second else [vmem] * 2,
        out_shape=pltpu.VMEM((count, units), jnp.bfloat16) if second else [sum_shape] * 2,
        scratch_shapes=[sum_shape] * (2 if second else 0),
        compiler_params=pltpu.CompilerParams(vmem_limit_bytes=16 * MIB),
        cost_estimate=pl.CostEstimate(
            flops=4 * count * half * units,
            bytes_accessed=4 * half * units + 2 * count * half,
            transcendentals=count * units,
        ),
        name="hidden",
    )(me, rows, w_gate, w_up, *(sums or ()))


def down_kernel(hidden_ref, down_ref, own_ref, sib_ref):
    middle, width = own_ref.shape
    cols = min(1024, width)

    def one_part(step, carry):
        columns = pl.ds(pl.multiple_of(step * cols, cols), cols)
        part = jnp.dot(hidden_ref[...], down_ref[:, columns], preferred_element_type=jnp.float32)
        part = part.astype(jnp.bfloat16)
        own_ref[:, columns] = part[:middle]
        sib_ref[:, columns] = part[middle:]
        return carry

    lax.fori_loop(0, width // cols, one_part, 0)


def down_call(hidden, w_down):
    rows, units = hidden.shape
    width = w_down.shape[1]
    vmem = pl.BlockSpec(memory_space=pltpu.VMEM)
    return pl.pallas_call(
        down_kernel,
        in_specs=[vmem] * 2,
        out_specs=[vmem] * 2,
        out_shape=[pltpu.VMEM((rows // 2, width), jnp.bfloat16)] * 2,
        compiler_params=pltpu.CompilerParams(vmem_limit_bytes=16 * MIB),
        cost_estimate=pl.CostEstimate(
            flops=2 * rows * width * units,
            bytes_accessed=2 * width * units + 2 * rows * width,
            transcendentals=0,
        ),
        name="down",
    )(hidden, w_down)


def spread_kernel(a_ref, b_ref, c_ref, d_ref, table_ref, *rest):
    out_ref = rest[-1]
    total = a_ref[...].astype(jnp.float32) + b_ref[...].astype(jnp.float32)
    total += c_ref[...].astype(jnp.float32) + d_ref[...].astype(jnp.float32)
    total = total.astype(jnp.bfloat16)
    out_ref[...] = lax.dot_general(
        table_ref[...],
        jnp.concatenate([total] * PARTS, axis=0),
        (((0,), (0,)), ((), ())),
        preferred_element_type=jnp.float32,
    ).astype(jnp.bfloat16)


def spread_call(parts, table, piece, pieces, previous):
    tokens = table.shape[1]
    piece_width = parts[0].shape[1]
    cols = min(2048, piece_width)
    steps = piece_width // cols
    earlier = [] if previous is None else [previous]
    return pl.pallas_call(
        spread_kernel,
        grid=(steps,),
        in_specs=[pl.BlockSpec((CAP, cols), lambda i: (0, i))] * 4
        + [pl.BlockSpec((PARTS * CAP, tokens), lambda i: (0, 0))]
        + [pl.BlockSpec(memory_space=pl.ANY)] * len(earlier),
        out_specs=pl.BlockSpec((tokens, cols), lambda i: (0, piece * steps + i)),
        out_shape=jax.ShapeDtypeStruct((tokens, piece_width * pieces), jnp.bfloat16),
        input_output_aliases={5: 0} if earlier else {},
        compiler_params=pltpu.CompilerParams(
            dimension_semantics=("arbitrary",), vmem_limit_bytes=16 * MIB
        ),
        name="spread",
    )(*parts, table, *earlier)


def reduce_chip_rows(mine, other, half, chips, go_right, go_left):
    middle = mine.shape[1] // 2

    def block(index):
        rows = slice(index * CAP, (index + 1) * CAP)
        return mine[rows].astype(jnp.float32) + other[rows].astype(jnp.float32)

    far = block(chips - 1).astype(jnp.bfloat16)
    ahead, back = far[:, :middle], far[:, middle:]
    for distance in range(half - 1, -1, -1):
        ahead, back = lax.optimization_barrier((ahead, back))
        to_right, to_left = go_right(ahead), go_left(back)
        yield
        if distance == 0:
            break
        ahead, back = block(half - 1 + distance), block(distance)
        if distance == half - 1:
            ahead = jnp.concatenate(
                [ahead[:, :middle] + to_right.astype(jnp.float32), ahead[:, middle:]], axis=1
            )
            back = jnp.concatenate(
                [back[:, :middle], back[:, middle:] + to_left.astype(jnp.float32)], axis=1
            )
        else:
            ahead = ahead + to_right.astype(jnp.float32)
            back = back + to_left.astype(jnp.float32)
        ahead, back = ahead.astype(jnp.bfloat16), back.astype(jnp.bfloat16)
    return (mine, other, to_right, to_left)


def run_together(generators):
    results = [None] * len(generators)
    active = list(range(len(generators)))
    while active:
        for i in list(active):
            try:
                next(generators[i])
            except StopIteration as stop:
                results[i] = stop.value
                active.remove(i)
    return results


def per_device(chips, queries, keys, values, norm_gain, expert_ids, gates, w_gate, w_up, w_down):
    right, left, sibling = permutations(chips)
    half = chips // 2
    go_right = lambda x: lax.ppermute(x, "ctx", right)
    go_left = lambda x: lax.ppermute(x, "ctx", left)
    swap = lambda x: lax.ppermute(x, "ctx", sibling)

    me = lax.axis_index("ctx").astype(jnp.int32).reshape(1)
    tokens = queries.shape[0]
    hits = (expert_ids == 0).astype(jnp.float32)
    chosen = jnp.sum(hits, axis=1)
    position = jnp.arange(tokens, dtype=jnp.int32)
    before = (position[None, :] < position[:, None]).astype(jnp.float32)
    slot = jnp.sum(before * chosen[None, :], axis=1).astype(jnp.int32)
    table = jnp.logical_and(
        slot[None, :] == jnp.arange(CAP, dtype=jnp.int32)[:, None], chosen[None, :] > 0
    ).astype(jnp.float32)
    rest = jnp.sum(gates * hits, axis=1)
    weights = []
    for _ in range(PARTS):
        part = lax.reduce_precision(rest, 8, 7)
        weights.append(table * part[None, :])
        rest = rest - part
    weighted = jnp.concatenate(weights, axis=0).astype(jnp.bfloat16)
    table = table.astype(jnp.bfloat16)

    own = stack(keys, values)
    own, me = lax.optimization_barrier((own, me))
    attention = Attention(me, load(queries), chips)
    from_left, from_right = go_right(own), go_left(own)
    late, late_places = [swap(own)], [(0, True)]
    state, shift = attention.own(own)
    state, w_down = lax.optimization_barrier((state, w_down))
    downs = [load(w_down, piece, PIECES) for piece in range(PIECES)]
    mine, others = [own], []
    for step in range(1, half):
        from_left, from_right, state, late, downs = lax.optimization_barrier(
            (from_left, from_right, state, late, downs)
        )
        blocks = [from_left, from_right, *late]
        places = [(step, False), (-step, False), *late_places]
        mine += [from_left, from_right]
        others += late
        late = [swap(from_left), swap(from_right)]
        late_places = [(step, True), (-step, True)]
        if step < half - 1:
            from_left, from_right = go_right(from_left), go_left(from_right)
        else:
            far_keys, far_values = go_right(from_left[:tokens]), go_left(from_right[tokens:])
        state = attention.step(blocks, places, shift, state)
    others += late
    far_keys, far_values, state = lax.optimization_barrier((far_keys, far_values, state))
    opposite = (far_keys, far_values, swap(far_keys), swap(far_values))
    sources = [x for pair in zip(mine, others) for x in pair] + list(opposite)
    keep, give, result = attention.last(
        late, opposite, shift, state, norm_gain[None, :], table, sources
    )

    keep, give, w_gate, w_up = lax.optimization_barrier((keep, give, w_gate, w_up))
    block = jnp.concatenate([keep, swap(give)], axis=0)
    from_left, from_right = block, block
    blocks_right, blocks_left = [block], []
    for step in range(1, half):
        from_left, from_right = go_right(from_left), go_left(from_right)
        if step == 1:
            w_gate = load(w_gate)
        elif step == 2:
            w_up = load(w_up)
        from_left, from_right, w_gate, w_up = lax.optimization_barrier(
            (from_left, from_right, w_gate, w_up)
        )
        blocks_right.append(from_left)
        blocks_left.append(from_right)
    far = [go_right(from_left[:CAP]), go_left(from_right[CAP:])]
    rows = gather(blocks_right + blocks_left + far)
    other_rows = swap(rows)
    hidden = hidden_call(me, other_rows, w_gate, w_up, hidden_call(me, rows, w_gate, w_up))

    sums = []
    for piece in range(PIECES):
        mine, theirs = down_call(hidden, downs[piece])
        sums.append(reduce_chip_rows(mine, swap(theirs), half, chips, go_right, go_left))
    mixed = None
    for piece, parts in enumerate(run_together(sums)):
        mixed = spread_call(parts, weighted, piece, PIECES, mixed)
    return (result, mixed)


def solution(mesh):
    placed = (
        P(("groups", "ctx"), None),
        P(("groups", "ctx"), None),
        P(("groups", "ctx"), None),
        P(),
        P(("groups", "ctx"), None),
        P(("groups", "ctx"), None),
        P(None, "ctx"),
        P(None, "ctx"),
        P("ctx", None),
    )
    return jax.shard_map(
        functools.partial(per_device, mesh.shape["ctx"] // 2),
        mesh=mesh,
        in_specs=placed,
        out_specs=(P(("groups", "ctx"), None), P(("groups", "ctx"), None)),
        check_vma=False,
    )
```

profile of v0, /device:TPU:0, one launch (start us, length us, event | category | flops | bytes accessed | tf_op | source)
XLA Modules:
  0.0 196.4 jit_solution(13463758185424162036)
XLA Ops:
  1.7 3.1 %collective-permute-start = (bf16[256,1024]{1,0:T(8,128)(2,1)S(1)}, bf16[256,1024]{1,0:T(8,128)(2,1)S(1)}, u32[]{:S(2)}, u32[]{:S(2)}) collective-permute-start(bf16[256,1024]{1,0:T(8,128)(2,1)S(1)} %stack.1.own_ref.refs_11_), channel_id=1, source_target_pairs={{0,4},{1,5},{4,8},{5,9},{8,12},{9,13},{12,14},{13,15},{14,10},{15,... | collective-permute-start | bytes 1572872 | tf_op jit(solution)/shard_map/ppermute | solution.py:616
  4.8 1.6 load.5.q_ref
  6.4 6.1 %attend_own.1 = (f32[8,1024,128]{2,1,0:T(8,128)S(1)}, f32[8,1024,128]{2,1,0:T(8,128)S(1)}, f32[8,1024,128]{2,1,0:T(8,128)S(1)}) custom-call(bf16[128,8192]{1,0:T(8,128)(2,1)S(1)} %load.5.q_ref, bf16[256,1024]{1,0:T(8,128)(2,1)S(1)} %stack.1.own_ref.refs_11_), custom_call_target="tpu_custom_call" | custom-call | flops 536870912 | bytes 4194304 | tf_op jit(solution)/shard_map/attend_own/pallas_call | solution.py:324
  12.5 2.8 %load.6.down_ref = bf16[768,4096]{1,0:T(8,128)(2,1)S(1)} custom-call(bf16[768,8192]{1,0:T(8,128)(2,1)} %source_ref.3), custom_call_target="tpu_custom_call" | custom-call | bytes 3145728 | tf_op jit(solution)/shard_map/load/pallas_call | solution.py:416
  15.3 2.8 %load.7.down_ref = bf16[768,4096]{1,0:T(8,128)(2,1)S(1)} custom-call(bf16[768,8192]{1,0:T(8,128)(2,1)} %source_ref.3), custom_call_target="tpu_custom_call" | custom-call | bytes 3145728 | tf_op jit(solution)/shard_map/load/pallas_call | solution.py:416
  18.2 2.1 %collective-permute-start.3 = (bf16[256,1024]{1,0:T(8,128)(2,1)S(1)}, bf16[256,1024]{1,0:T(8,128)(2,1)S(1)}, u32[]{:S(2)}, u32[]{:S(2)}) collective-permute-start(bf16[256,1024]{1,0:T(8,128)(2,1)S(1)} %collective-permute-done.refs_0_.refs_13_), channel_id=1, source_target_pairs={{0,4},{1,5},{4,8},{5,9},{8,12},{9,13},{12,14},{13,15},{14,10},{15,... | collective-permute-start | bytes 1572872 | tf_op jit(solution)/shard_map/ppermute | solution.py:616
  20.8 12.0 %collective-permute-done.3.refs_0_.refs_17_ = bf16[256,1024]{1,0:T(8,128)(2,1)S(1)} collective-permute-done((bf16[256,1024]{1,0:T(8,128)(2,1)S(1)}, bf16[256,1024]{1,0:T(8,128)(2,1)S(1)}, u32[]{:S(2)}, u32[]{:S(2)}) %collective-permute-start.3) | collective-permute-done | bytes 524320 | tf_op jit(solution)/shard_map/ppermute | solution.py:616
  32.8 1.5 collective-permute-done.4.refs_1_.refs_19_
  34.3 1.6 collective-permute-start.7
  36.9 10.7 %collective-permute-done.7.refs_0_.refs_21_ = bf16[256,1024]{1,0:T(8,128)(2,1)S(1)} collective-permute-done((bf16[256,1024]{1,0:T(8,128)(2,1)S(1)}, bf16[256,1024]{1,0:T(8,128)(2,1)S(1)}, u32[]{:S(2)}, u32[]{:S(2)}) %collective-permute-start.7) | collective-permute-done | bytes 524320 | tf_op jit(solution)/shard_map/ppermute | solution.py:616
  49.5 1.6 collective-permute-start.13
  51.6 6.2 %collective-permute-done.13.refs_2_.refs_25_ = bf16[128,1024]{1,0:T(8,128)(2,1)S(1)} collective-permute-done((bf16[128,1024]{1,0:T(8,128)(2,1)S(1)}, bf16[128,1024]{1,0:T(8,128)(2,1)S(1)}, u32[]{:S(2)}, u32[]{:S(2)}) %collective-permute-start.13) | collective-permute-done | bytes 262176 | tf_op jit(solution)/shard_map/ppermute | solution.py:616
  60.9 8.1 %attend_last.1 = (bf16[16,4096]{1,0:T(8,128)(2,1)S(1)}, bf16[16,4096]{1,0:T(8,128)(2,1)S(1)}, bf16[128,8192]{1,0:T(8,128)(2,1)}) custom-call(s32[1]{0:T(128)} %bitcast.me_ref, bf16[128,8192]{1,0:T(8,128)(2,1)S(1)} %load.5.q_ref, bf16[256,1024]{1,0:T(8,128)(2,1)S(1)} %collective-permute-done.11.refs_0_.refs_22_, ...), custom_call_target="tpu_custom_call" | custom-call | flops 536870912 | bytes 4194304 | tf_op jit(solution)/shard_map/attend_last/pallas_call | solution.py:324
  70.5 1.6 collective-permute-start.18
  72.6 4.6 %load.8.gate_ref = bf16[8192,768]{1,0:T(8,128)(2,1)S(1)} custom-call(bf16[8192,768]{1,0:T(8,128)(2,1)} %source_ref.4), custom_call_target="tpu_custom_call" | custom-call | bytes 6291456 | tf_op jit(solution)/shard_map/load/pallas_call | solution.py:416
  77.2 1.7 collective-permute-done.18.refs_1_
  82.2 4.6 %load.9.up_ref = bf16[8192,768]{1,0:T(8,128)(2,1)S(1)} custom-call(bf16[8192,768]{1,0:T(8,128)(2,1)} %source_ref.5), custom_call_target="tpu_custom_call" | custom-call | bytes 6291456 | tf_op jit(solution)/shard_map/load/pallas_call | solution.py:416
  87.4 48.0 %collective-permute-done.21.refs_5_ = bf16[32,4096]{1,0:T(8,128)(2,1)S(1)} collective-permute-done((bf16[32,4096]{1,0:T(8,128)(2,1)S(1)}, bf16[32,4096]{1,0:T(8,128)(2,1)S(1)}, u32[]{:S(2)}, u32[]{:S(2)}) %collective-permute-start.21) | collective-permute-done | bytes 262176 | tf_op jit(solution)/shard_map/ppermute | solution.py:617
  135.4 1.7 collective-permute-start.22
  137.4 4.8 %collective-permute-done.22.refs_3_ = bf16[32,4096]{1,0:T(8,128)(2,1)S(1)} collective-permute-done((bf16[32,4096]{1,0:T(8,128)(2,1)S(1)}, bf16[32,4096]{1,0:T(8,128)(2,1)S(1)}, u32[]{:S(2)}, u32[]{:S(2)}) %collective-permute-start.22) | collective-permute-done | bytes 262176 | tf_op jit(solution)/shard_map/ppermute | solution.py:616
  145.7 2.9 %collective-permute-done.24.refs_7_ = bf16[16,4096]{1,0:T(8,128)(2,1)S(1)} collective-permute-done((bf16[16,4096]{1,0:T(8,128)(2,1)S(1)}, bf16[16,4096]{1,0:T(8,128)(2,1)S(1)}, u32[]{:S(2)}, u32[]{:S(2)}) %collective-permute-start.24) | collective-permute-done | bytes 131104 | tf_op jit(solution)/shard_map/ppermute | solution.py:616
  148.6 1.5 collective-permute-done.25.refs_8_
  150.3 4.1 %hidden.2 = (f32[256,768]{1,0:T(8,128)S(1)}, f32[256,768]{1,0:T(8,128)S(1)}) custom-call(s32[1]{0:T(128)} %bitcast.me_ref, bf16[256,4096]{1,0:T(8,128)(2,1)S(1)} %gather.1.rows_ref, bf16[8192,768]{1,0:T(8,128)(2,1)S(1)} %load.8.gate_ref, bf16[8192,768]{1,0:T(8,128)(2,1)S(1)} %load.9.up_ref), custom_call_target="tpu_custom_call" | custom-call | flops 3221225472 | bytes 14680064 | tf_op jit(solution)/shard_map/hidden/pallas_call | solution.py:485
  154.4 4.3 %hidden.3.hidden_ref = bf16[256,768]{1,0:T(8,128)(2,1)S(1)} custom-call(s32[1]{0:T(128)} %bitcast.me_ref, bf16[256,4096]{1,0:T(8,128)(2,1)S(1)} %collective-permute-done.26.rows_ref, bf16[8192,768]{1,0:T(8,128)(2,1)S(1)} %load.8.gate_ref, bf16[8192,768]{1,0:T(8,128)(2,1)S(1)} %load.9.up_ref, f32[256,768]{1,0:T(8,128)S(1)} %get-tuple-element.142.refs_0_, ...), custom_call_target="tpu_custom_call" | custom-call | flops 3221225472 | bytes 14680064 | tf_op jit(solution)/shard_map/hidden/pallas_call | solution.py:485
  158.8 2.3 %down.2 = (bf16[128,4096]{1,0:T(8,128)(2,1)S(1)}, bf16[128,4096]{1,0:T(8,128)(2,1)S(1)}) custom-call(bf16[256,768]{1,0:T(8,128)(2,1)S(1)} %hidden.3.hidden_ref, bf16[768,4096]{1,0:T(8,128)(2,1)S(1)} %bitcast.3), custom_call_target="tpu_custom_call" | custom-call | flops 1610612736 | bytes 8388608 | tf_op jit(solution)/shard_map/down/pallas_call | solution.py:520
  161.6 2.3 %down.3 = (bf16[128,4096]{1,0:T(8,128)(2,1)S(1)}, bf16[128,4096]{1,0:T(8,128)(2,1)S(1)}) custom-call(bf16[256,768]{1,0:T(8,128)(2,1)S(1)} %hidden.3.hidden_ref, bf16[768,4096]{1,0:T(8,128)(2,1)S(1)} %load.6.down_ref), custom_call_target="tpu_custom_call" | custom-call | flops 1610612736 | bytes 8388608 | tf_op jit(solution)/shard_map/down/pallas_call | solution.py:520
  172.4 1.6 collective-permute-start.40
  183.8 1.5 collective-permute-start.34
  186.9 1.5 collective-permute-start.43
  189.0 2.9 %collective-permute-done.43.c_ref = bf16[16,4096]{1,0:T(8,128)(2,1)S(1)} collective-permute-done((bf16[16,4096]{1,0:T(8,128)(2,1)S(1)}, bf16[16,4096]{1,0:T(8,128)(2,1)S(1)}, u32[]{:S(2)}, u32[]{:S(2)}) %collective-permute-start.43) | collective-permute-done | bytes 131104 | tf_op jit(solution)/shard_map/ppermute | solution.py:616
  193.4 1.5 spread.2.rest_0_
  194.9 1.5 spread.3
  (123 shorter events, 40.3 us)
Async XLA Ops:
  1.7 16.4 %collective-permute-start = (bf16[256,1024]{1,0:T(8,128)(2,1)S(1)}, bf16[256,1024]{1,0:T(8,128)(2,1)S(1)}, u32[]{:S(2)}, u32[]{:S(2)}) collective-permute-start(bf16[256,1024]{1,0:T(8,128)(2,1)S(1)} %stack.1.own_ref.refs_11_), channel_id=1, source_target_pairs={{0,4},{1,5},{4,8},{5,9},{8,12},{9,13},{12,14},{13,15},{14,10},{15,... | collective-permute-start | bytes 1572872 | tf_op jit(solution)/shard_map/ppermute | solution.py:616
  4.8 13.4 %collective-permute-start.1 = (bf16[256,1024]{1,0:T(8,128)(2,1)S(1)}, bf16[256,1024]{1,0:T(8,128)(2,1)S(1)}, u32[]{:S(2)}, u32[]{:S(2)}) collective-permute-start(bf16[256,1024]{1,0:T(8,128)(2,1)S(1)} %stack.1.own_ref.refs_11_), channel_id=1, source_target_pairs={{4,0},{5,1},{8,4},{9,5},{12,8},{13,9},{14,12},{15,13},{10,14},{11,... | collective-permute-start | bytes 1572872 | tf_op jit(solution)/shard_map/ppermute | solution.py:617
  4.8 13.4 %collective-permute-start.2 = (bf16[256,1024]{1,0:T(8,128)(2,1)S(1)}, bf16[256,1024]{1,0:T(8,128)(2,1)S(1)}, u32[]{:S(2)}, u32[]{:S(2)}) collective-permute-start(bf16[256,1024]{1,0:T(8,128)(2,1)S(1)} %stack.1.own_ref.refs_11_), channel_id=1, source_target_pairs={{0,1},{1,0},{2,3},{3,2},{4,5},{5,4},{6,7},{7,6},{8,9},{9,8},{10,11... | collective-permute-start | bytes 1572872 | tf_op jit(solution)/shard_map/ppermute | solution.py:618
  18.2 14.6 %collective-permute-start.3 = (bf16[256,1024]{1,0:T(8,128)(2,1)S(1)}, bf16[256,1024]{1,0:T(8,128)(2,1)S(1)}, u32[]{:S(2)}, u32[]{:S(2)}) collective-permute-start(bf16[256,1024]{1,0:T(8,128)(2,1)S(1)} %collective-permute-done.refs_0_.refs_13_), channel_id=1, source_target_pairs={{0,4},{1,5},{4,8},{5,9},{8,12},{9,13},{12,14},{13,15},{14,10},{15,... | collective-permute-start | bytes 1572872 | tf_op jit(solution)/shard_map/ppermute | solution.py:616
  20.2 14.1 %collective-permute-start.4 = (bf16[256,1024]{1,0:T(8,128)(2,1)S(1)}, bf16[256,1024]{1,0:T(8,128)(2,1)S(1)}, u32[]{:S(2)}, u32[]{:S(2)}) collective-permute-start(bf16[256,1024]{1,0:T(8,128)(2,1)S(1)} %collective-permute-done.1.refs_1_.refs_15_), channel_id=1, source_target_pairs={{4,0},{5,1},{8,4},{9,5},{12,8},{13,9},{14,12},{15,13},{10,14},{11,... | collective-permute-start | bytes 1572872 | tf_op jit(solution)/shard_map/ppermute | solution.py:617
  20.2 14.1 %collective-permute-start.5 = (bf16[256,1024]{1,0:T(8,128)(2,1)S(1)}, bf16[256,1024]{1,0:T(8,128)(2,1)S(1)}, u32[]{:S(2)}, u32[]{:S(2)}) collective-permute-start(bf16[256,1024]{1,0:T(8,128)(2,1)S(1)} %collective-permute-done.refs_0_.refs_13_), channel_id=1, source_target_pairs={{0,1},{1,0},{2,3},{3,2},{4,5},{5,4},{6,7},{7,6},{8,9},{9,8},{10,11... | collective-permute-start | bytes 1572872 | tf_op jit(solution)/shard_map/ppermute | solution.py:618
  20.5 13.8 %collective-permute-start.6 = (bf16[256,1024]{1,0:T(8,128)(2,1)S(1)}, bf16[256,1024]{1,0:T(8,128)(2,1)S(1)}, u32[]{:S(2)}, u32[]{:S(2)}) collective-permute-start(bf16[256,1024]{1,0:T(8,128)(2,1)S(1)} %collective-permute-done.1.refs_1_.refs_15_), channel_id=1, source_target_pairs={{0,1},{1,0},{2,3},{3,2},{4,5},{5,4},{6,7},{7,6},{8,9},{9,8},{10,11... | collective-permute-start | bytes 1572872 | tf_op jit(solution)/shard_map/ppermute | solution.py:618
  34.3 13.3 %collective-permute-start.7 = (bf16[256,1024]{1,0:T(8,128)(2,1)S(1)}, bf16[256,1024]{1,0:T(8,128)(2,1)S(1)}, u32[]{:S(2)}, u32[]{:S(2)}) collective-permute-start(bf16[256,1024]{1,0:T(8,128)(2,1)S(1)} %collective-permute-done.3.refs_0_.refs_17_), channel_id=1, source_target_pairs={{0,4},{1,5},{4,8},{5,9},{8,12},{9,13},{12,14},{13,15},{14,10},{15,... | collective-permute-start | bytes 1572872 | tf_op jit(solution)/shard_map/ppermute | solution.py:616
  35.9 13.0 %collective-permute-start.8 = (bf16[256,1024]{1,0:T(8,128)(2,1)S(1)}, bf16[256,1024]{1,0:T(8,128)(2,1)S(1)}, u32[]{:S(2)}, u32[]{:S(2)}) collective-permute-start(bf16[256,1024]{1,0:T(8,128)(2,1)S(1)} %collective-permute-done.4.refs_1_.refs_19_), channel_id=1, source_target_pairs={{4,0},{5,1},{8,4},{9,5},{12,8},{13,9},{14,12},{15,13},{10,14},{11,... | collective-permute-start | bytes 1572872 | tf_op jit(solution)/shard_map/ppermute | solution.py:617
  36.4 12.5 %collective-permute-start.9 = (bf16[256,1024]{1,0:T(8,128)(2,1)S(1)}, bf16[256,1024]{1,0:T(8,128)(2,1)S(1)}, u32[]{:S(2)}, u32[]{:S(2)}) collective-permute-start(bf16[256,1024]{1,0:T(8,128)(2,1)S(1)} %collective-permute-done.3.refs_0_.refs_17_), channel_id=1, source_target_pairs={{0,1},{1,0},{2,3},{3,2},{4,5},{5,4},{6,7},{7,6},{8,9},{9,8},{10,11... | collective-permute-start | bytes 1572872 | tf_op jit(solution)/shard_map/ppermute | solution.py:618
  36.4 12.5 %collective-permute-start.10 = (bf16[256,1024]{1,0:T(8,128)(2,1)S(1)}, bf16[256,1024]{1,0:T(8,128)(2,1)S(1)}, u32[]{:S(2)}, u32[]{:S(2)}) collective-permute-start(bf16[256,1024]{1,0:T(8,128)(2,1)S(1)} %collective-permute-done.4.refs_1_.refs_19_), channel_id=1, source_target_pairs={{0,1},{1,0},{2,3},{3,2},{4,5},{5,4},{6,7},{7,6},{8,9},{9,8},{10,11... | collective-permute-start | bytes 1572872 | tf_op jit(solution)/shard_map/ppermute | solution.py:618
  48.9 12.0 %collective-permute-start.11 = (bf16[256,1024]{1,0:T(8,128)(2,1)S(1)}, bf16[256,1024]{1,0:T(8,128)(2,1)S(1)}, u32[]{:S(2)}, u32[]{:S(2)}) collective-permute-start(bf16[256,1024]{1,0:T(8,128)(2,1)S(1)} %collective-permute-done.7.refs_0_.refs_21_), channel_id=1, source_target_pairs={{0,1},{1,0},{2,3},{3,2},{4,5},{5,4},{6,7},{7,6},{8,9},{9,8},{10,11... | collective-permute-start | bytes 1572872 | tf_op jit(solution)/shard_map/ppermute | solution.py:618
  48.9 12.0 %collective-permute-start.12 = (bf16[256,1024]{1,0:T(8,128)(2,1)S(1)}, bf16[256,1024]{1,0:T(8,128)(2,1)S(1)}, u32[]{:S(2)}, u32[]{:S(2)}) collective-permute-start(bf16[256,1024]{1,0:T(8,128)(2,1)S(1)} %collective-permute-done.8.refs_1_.refs_23_), channel_id=1, source_target_pairs={{0,1},{1,0},{2,3},{3,2},{4,5},{5,4},{6,7},{7,6},{8,9},{9,8},{10,11... | collective-permute-start | bytes 1572872 | tf_op jit(solution)/shard_map/ppermute | solution.py:618
  49.5 8.3 %collective-permute-start.13 = (bf16[128,1024]{1,0:T(8,128)(2,1)S(1)}, bf16[128,1024]{1,0:T(8,128)(2,1)S(1)}, u32[]{:S(2)}, u32[]{:S(2)}) collective-permute-start(bf16[128,1024]{1,0:T(8,128)(2,1)S(1)} %slice.136), channel_id=1, source_target_pairs={{0,4},{1,5},{4,8},{5,9},{8,12},{9,13},{12,14},{13,15},{14,10},{15,... | collective-permute-start | bytes 786440 | tf_op jit(solution)/shard_map/ppermute | solution.py:616
  51.1 8.0 %collective-permute-start.14 = (bf16[128,1024]{1,0:T(8,128)(2,1)S(1)}, bf16[128,1024]{1,0:T(8,128)(2,1)S(1)}, u32[]{:S(2)}, u32[]{:S(2)}) collective-permute-start(bf16[128,1024]{1,0:T(8,128)(2,1)S(1)} %slice.137), channel_id=1, source_target_pairs={{4,0},{5,1},{8,4},{9,5},{12,8},{13,9},{14,12},{15,13},{10,14},{11,... | collective-permute-start | bytes 786440 | tf_op jit(solution)/shard_map/ppermute | solution.py:617
  70.5 8.4 %collective-permute-start.18 = (bf16[32,4096]{1,0:T(8,128)(2,1)S(1)}, bf16[32,4096]{1,0:T(8,128)(2,1)S(1)}, u32[]{:S(2)}, u32[]{:S(2)}) collective-permute-start(bf16[32,4096]{1,0:T(8,128)(2,1)S(1)} %constant_dynamic-update-slice_fusion.refs_0_), channel_id=1, source_target_pairs={{0,4},{1,5},{4,8},{5,9},{8,12},{9,13},{12,14},{13,15},{14,10},{15,... | collective-permute-start | bytes 786440 | tf_op jit(solution)/shard_map/ppermute | solution.py:616
  72.1 8.1 %collective-permute-start.19 = (bf16[32,4096]{1,0:T(8,128)(2,1)S(1)}, bf16[32,4096]{1,0:T(8,128)(2,1)S(1)}, u32[]{:S(2)}, u32[]{:S(2)}) collective-permute-start(bf16[32,4096]{1,0:T(8,128)(2,1)S(1)} %constant_dynamic-update-slice_fusion.refs_0_), channel_id=1, source_target_pairs={{4,0},{5,1},{8,4},{9,5},{12,8},{13,9},{14,12},{15,13},{10,14},{11,... | collective-permute-start | bytes 786440 | tf_op jit(solution)/shard_map/ppermute | solution.py:617
  80.2 7.2 %collective-permute-start.20 = (bf16[32,4096]{1,0:T(8,128)(2,1)S(1)}, bf16[32,4096]{1,0:T(8,128)(2,1)S(1)}, u32[]{:S(2)}, u32[]{:S(2)}) collective-permute-start(bf16[32,4096]{1,0:T(8,128)(2,1)S(1)} %collective-permute-done.18.refs_1_), channel_id=1, source_target_pairs={{0,4},{1,5},{4,8},{5,9},{8,12},{9,13},{12,14},{13,15},{14,10},{15,... | collective-permute-start | bytes 786440 | tf_op jit(solution)/shard_map/ppermute | solution.py:616
  81.0 54.4 %collective-permute-start.21 = (bf16[32,4096]{1,0:T(8,128)(2,1)S(1)}, bf16[32,4096]{1,0:T(8,128)(2,1)S(1)}, u32[]{:S(2)}, u32[]{:S(2)}) collective-permute-start(bf16[32,4096]{1,0:T(8,128)(2,1)S(1)} %collective-permute-done.19.refs_4_), channel_id=1, source_target_pairs={{4,0},{5,1},{8,4},{9,5},{12,8},{13,9},{14,12},{15,13},{10,14},{11,... | collective-permute-start | bytes 786440 | tf_op jit(solution)/shard_map/ppermute | solution.py:617
  135.4 6.8 %collective-permute-start.22 = (bf16[32,4096]{1,0:T(8,128)(2,1)S(1)}, bf16[32,4096]{1,0:T(8,128)(2,1)S(1)}, u32[]{:S(2)}, u32[]{:S(2)}) collective-permute-start(bf16[32,4096]{1,0:T(8,128)(2,1)S(1)} %collective-permute-done.20.refs_2_), channel_id=1, source_target_pairs={{0,4},{1,5},{4,8},{5,9},{8,12},{9,13},{12,14},{13,15},{14,10},{15,... | collective-permute-start | bytes 786440 | tf_op jit(solution)/shard_map/ppermute | solution.py:616
  137.2 6.4 %collective-permute-start.23 = (bf16[32,4096]{1,0:T(8,128)(2,1)S(1)}, bf16[32,4096]{1,0:T(8,128)(2,1)S(1)}, u32[]{:S(2)}, u32[]{:S(2)}) collective-permute-start(bf16[32,4096]{1,0:T(8,128)(2,1)S(1)} %collective-permute-done.21.refs_5_), channel_id=1, source_target_pairs={{4,0},{5,1},{8,4},{9,5},{12,8},{13,9},{14,12},{15,13},{10,14},{11,... | collective-permute-start | bytes 786440 | tf_op jit(solution)/shard_map/ppermute | solution.py:617
  143.5 5.0 %collective-permute-start.24 = (bf16[16,4096]{1,0:T(8,128)(2,1)S(1)}, bf16[16,4096]{1,0:T(8,128)(2,1)S(1)}, u32[]{:S(2)}, u32[]{:S(2)}) collective-permute-start(bf16[16,4096]{1,0:T(8,128)(2,1)S(1)} %slice.138), channel_id=1, source_target_pairs={{0,4},{1,5},{4,8},{5,9},{8,12},{9,13},{12,14},{13,15},{14,10},{15,... | collective-permute-start | bytes 393224 | tf_op jit(solution)/shard_map/ppermute | solution.py:616
  169.2 6.5 %collective-permute-start.31 = (bf16[16,4096]{1,0:T(8,128)(2,1)S(1)}, bf16[16,4096]{1,0:T(8,128)(2,1)S(1)}, u32[]{:S(2)}, u32[]{:S(2)}) collective-permute-start(bf16[16,4096]{1,0:T(8,128)(2,1)S(1)} %pad_maximum_fusion.1), channel_id=1, source_target_pairs={{4,0},{5,1},{8,4},{9,5},{12,8},{13,9},{14,12},{15,13},{10,14},{11,... | collective-permute-start | bytes 393224 | tf_op jit(solution)/shard_map/ppermute | solution.py:617
  170.6 6.3 %collective-permute-start.30 = (bf16[16,4096]{1,0:T(8,128)(2,1)S(1)}, bf16[16,4096]{1,0:T(8,128)(2,1)S(1)}, u32[]{:S(2)}, u32[]{:S(2)}) collective-permute-start(bf16[16,4096]{1,0:T(8,128)(2,1)S(1)} %pad_maximum_fusion), channel_id=1, source_target_pairs={{0,4},{1,5},{4,8},{5,9},{8,12},{9,13},{12,14},{13,15},{14,10},{15,... | collective-permute-start | bytes 393224 | tf_op jit(solution)/shard_map/ppermute | solution.py:616
  172.4 6.7 %collective-permute-start.40 = (bf16[16,4096]{1,0:T(8,128)(2,1)S(1)}, bf16[16,4096]{1,0:T(8,128)(2,1)S(1)}, u32[]{:S(2)}, u32[]{:S(2)}) collective-permute-start(bf16[16,4096]{1,0:T(8,128)(2,1)S(1)} %pad_maximum_fusion.3), channel_id=1, source_target_pairs={{4,0},{5,1},{8,4},{9,5},{12,8},{13,9},{14,12},{15,13},{10,14},{11,... | collective-permute-start | bytes 393224 | tf_op jit(solution)/shard_map/ppermute | solution.py:617
  174.0 5.9 %collective-permute-start.39 = (bf16[16,4096]{1,0:T(8,128)(2,1)S(1)}, bf16[16,4096]{1,0:T(8,128)(2,1)S(1)}, u32[]{:S(2)}, u32[]{:S(2)}) collective-permute-start(bf16[16,4096]{1,0:T(8,128)(2,1)S(1)} %pad_maximum_fusion.2), channel_id=1, source_target_pairs={{0,4},{1,5},{4,8},{5,9},{8,12},{9,13},{12,14},{13,15},{14,10},{15,... | collective-permute-start | bytes 393224 | tf_op jit(solution)/shard_map/ppermute | solution.py:616
  177.0 5.7 %collective-permute-start.33 = (bf16[16,4096]{1,0:T(8,128)(2,1)S(1)}, bf16[16,4096]{1,0:T(8,128)(2,1)S(1)}, u32[]{:S(2)}, u32[]{:S(2)}) collective-permute-start(bf16[16,4096]{1,0:T(8,128)(2,1)S(1)} %get-tuple-element.152), channel_id=1, source_target_pairs={{4,0},{5,1},{8,4},{9,5},{12,8},{13,9},{14,12},{15,13},{10,14},{11,... | collective-permute-start | bytes 393224 | tf_op jit(solution)/shard_map/ppermute | solution.py:617
  177.6 6.1 %collective-permute-start.32 = (bf16[16,4096]{1,0:T(8,128)(2,1)S(1)}, bf16[16,4096]{1,0:T(8,128)(2,1)S(1)}, u32[]{:S(2)}, u32[]{:S(2)}) collective-permute-start(bf16[16,4096]{1,0:T(8,128)(2,1)S(1)} %get-tuple-element.151), channel_id=1, source_target_pairs={{0,4},{1,5},{4,8},{5,9},{8,12},{9,13},{12,14},{13,15},{14,10},{15,... | collective-permute-start | bytes 393224 | tf_op jit(solution)/shard_map/ppermute | solution.py:616
  179.9 6.3 %collective-permute-start.42 = (bf16[16,4096]{1,0:T(8,128)(2,1)S(1)}, bf16[16,4096]{1,0:T(8,128)(2,1)S(1)}, u32[]{:S(2)}, u32[]{:S(2)}) collective-permute-start(bf16[16,4096]{1,0:T(8,128)(2,1)S(1)} %get-tuple-element.163), channel_id=1, source_target_pairs={{4,0},{5,1},{8,4},{9,5},{12,8},{13,9},{14,12},{15,13},{10,14},{11,... | collective-permute-start | bytes 393224 | tf_op jit(solution)/shard_map/ppermute | solution.py:617
  180.6 6.2 %collective-permute-start.41 = (bf16[16,4096]{1,0:T(8,128)(2,1)S(1)}, bf16[16,4096]{1,0:T(8,128)(2,1)S(1)}, u32[]{:S(2)}, u32[]{:S(2)}) collective-permute-start(bf16[16,4096]{1,0:T(8,128)(2,1)S(1)} %get-tuple-element.162), channel_id=1, source_target_pairs={{0,4},{1,5},{4,8},{5,9},{8,12},{9,13},{12,14},{13,15},{14,10},{15,... | collective-permute-start | bytes 393224 | tf_op jit(solution)/shard_map/ppermute | solution.py:616
  183.8 11.0 %collective-permute-start.34 = (bf16[16,4096]{1,0:T(8,128)(2,1)S(1)}, bf16[16,4096]{1,0:T(8,128)(2,1)S(1)}, u32[]{:S(2)}, u32[]{:S(2)}) collective-permute-start(bf16[16,4096]{1,0:T(8,128)(2,1)S(1)} %get-tuple-element.153), channel_id=1, source_target_pairs={{0,4},{1,5},{4,8},{5,9},{8,12},{9,13},{12,14},{13,15},{14,10},{15,... | collective-permute-start | bytes 393224 | tf_op jit(solution)/shard_map/ppermute | solution.py:616
  185.4 9.5 %collective-permute-start.35 = (bf16[16,4096]{1,0:T(8,128)(2,1)S(1)}, bf16[16,4096]{1,0:T(8,128)(2,1)S(1)}, u32[]{:S(2)}, u32[]{:S(2)}) collective-permute-start(bf16[16,4096]{1,0:T(8,128)(2,1)S(1)} %get-tuple-element.154), channel_id=1, source_target_pairs={{4,0},{5,1},{8,4},{9,5},{12,8},{13,9},{14,12},{15,13},{10,14},{11,... | collective-permute-start | bytes 393224 | tf_op jit(solution)/shard_map/ppermute | solution.py:617
  (19 other events, 105.2 us)
where the time goes:
time: 197 us; the launch traced here: 196 us
  waiting for transfers between devices  109 us (55%)
  Pallas kernels  47.8 us (24%)
  starting transfers between devices  37.2 us (19%)
    ppermute x16, waiting for transfers between devices, per_device(): go_left = lambda x: lax.ppermute(x, 'ctx', left)  61 us
    ppermute x16, waiting for transfers between devices, per_device(): go_right = lambda x: lax.ppermute(x, 'ctx', right)  45.4 us
    ppermute x16, starting transfers between devices, per_device(): go_right = lambda x: lax.ppermute(x, 'ctx', right)  22.4 us
    pallas_call x5, Pallas kernels, load(): pl.pallas_call(functools.partial(load_kernel, piece * width), in_specs=[p...  16.4 us
    pallas_call x5, Pallas kernels, call(): pl.pallas_call(kernel, in_specs=[smem if x is self.me else vmem for x in...  14.3 us
    ppermute x16, starting transfers between devices, per_device(): go_left = lambda x: lax.ppermute(x, 'ctx', left)  11.8 us
    pallas_call x2, Pallas kernels, hidden_call(): pl.pallas_call(functools.partial(hidden_kernel, second), in_specs=[pl.Blo...  8.4 us
    pallas_call x2, Pallas kernels, down_call(): pl.pallas_call(down_kernel, in_specs=[vmem] * 2, out_specs=[vmem] * 2, ou...  4.61 us
  transfers between devices with their start and end apart: 45, of which 30 were waited for; matrix products, arithmetic and copies ran while one was open for 0% of the time, Pallas kernels for 15%

commit v1 on v0

v1 whole, which is shorter than its diff:
```python
import functools
import math

import jax
import jax.numpy as jnp
from jax import lax
from jax.experimental import pallas as pl
from jax.experimental.pallas import tpu as pltpu
from jax.sharding import PartitionSpec as P

HQ = 64
HK = 8
DH = 128
CAP = 16
GROUP = HQ // HK
WIDE = GROUP * DH
LOG_SCALE = math.log2(math.e) / math.sqrt(DH)
MASKED = -1e30
PIECES = 2
ATTEND_MIB = 14
SUM_LIMIT = 2.0**100
PARTS = 3
STACK = 4
MIB = 1 << 20


def in_hbm(x):
    return pltpu.with_memory_space_constraint(x, pltpu.HBM)


def ring_order(chips):
    return list(range(0, chips, 2)) + list(range(1, chips, 2))[::-1]


def permutations(chips):
    order = ring_order(chips)
    right, left = [], []
    for place in range(chips):
        here, there = order[place], order[(place + 1) % chips]
        for core in range(2):
            right.append((2 * here + core, 2 * there + core))
            left.append((2 * there + core, 2 * here + core))
    sibling = [(i, i ^ 1) for i in range(2 * chips)]
    return right, left, sibling


def chip_at(me, step, chips):
    chip = me // 2
    place = jnp.where(chip % 2 == 0, chip // 2, chips - 1 - chip // 2)
    source = (place - step + 2 * chips) % chips
    return jnp.where(source < chips // 2, 2 * source, 2 * (chips - 1 - source) + 1)


def head_rows(own, sib, first):
    pieces = []
    for h in range(first, first + STACK):
        columns = slice(h * DH, (h + 1) * DH)
        pieces += [own[:, columns], sib[:, columns]]
    return jnp.concatenate(pieces, axis=0)


def with_ones(values):
    return jnp.concatenate([values, jnp.ones_like(values)], axis=1)


def scores_of(queries, keys):
    return LOG_SCALE * lax.dot_general(
        queries, keys, (((1,), (1,)), ((), ())), preferred_element_type=jnp.float32
    )


def weights_of(scores, shift):
    return jnp.exp2(scores - jnp.concatenate([shift] * (scores.shape[1] // DH), axis=1))


def row_top(scores):
    return jnp.broadcast_to(jnp.max(scores, axis=1, keepdims=True), (scores.shape[0], DH))


def allowed_here(core, tokens):
    rows, columns = STACK * 2 * tokens, 2 * tokens

    def position(axis):
        place = lax.broadcasted_iota(jnp.int32, (rows, columns), axis) % (2 * tokens)
        return jnp.where(place < tokens, core * tokens + place, (1 - core) * tokens + place - tokens)

    return position(1) <= position(0)


def group_queries(queries, group):
    columns = pl.ds(pl.multiple_of(group * WIDE, WIDE), WIDE)
    return [ref[:, columns] for ref in queries]


def for_groups(body):
    def step(group, carry):
        body(group, pl.ds(pl.multiple_of(group * DH, DH), DH))
        return carry

    lax.fori_loop(0, HK // 2, step, 0)


def fold(queries, first, keys, values, shift):
    scores = scores_of(head_rows(*queries, first), keys)
    return jnp.dot(
        weights_of(scores, shift).astype(jnp.bfloat16), values, preferred_element_type=jnp.float32
    )


def block_of(ref, columns):
    tokens = ref.shape[0] // 2
    return ref[:tokens, columns], ref[tokens:, columns]


def join_blocks(refs, factors, columns):
    pairs = [block_of(ref, columns) for ref in refs]
    keys = jnp.concatenate([key for key, _ in pairs], axis=0)
    values = [with_ones(value) * factor for (_, value), factor in zip(pairs, factors)]
    return keys, jnp.concatenate(values, axis=0)


def factors_of(me, places, chips):
    flags = [chip_at(me, place, chips) < me // 2 for place in places]
    return flags, [jnp.where(flag, 1.0, 0.0).astype(jnp.bfloat16) for flag in flags]


def chunks(tokens):
    size = STACK * 2 * tokens
    return [(first, slice(first // STACK * size, (first // STACK + 1) * size)) for first in range(0, GROUP, STACK)]


def own_kernel(loads, me_ref, q_ref, sib_q_ref, own_ref, sib_ref, *refs):
    acc_ref, total_ref, shift_ref = refs[loads : loads + 3]
    copies = start_loads(loads, refs[:loads], refs[loads + 3 :])
    tokens = q_ref.shape[0]
    allowed = allowed_here(me_ref[0] % 2, tokens)

    def one_group(group, columns):
        keys, values = join_blocks((own_ref, sib_ref), (1, 1), columns)
        queries = group_queries((q_ref, sib_q_ref), group)
        for first, rows in chunks(tokens):
            scores = jnp.where(allowed, scores_of(head_rows(*queries, first), keys), MASKED)
            shift = row_top(scores)
            weights = weights_of(scores, shift).astype(jnp.bfloat16)
            update = jnp.dot(weights, values, preferred_element_type=jnp.float32)
            acc_ref[group, rows, :] = update[:, :DH]
            total_ref[group, rows, :] = update[:, DH:]
            shift_ref[group, rows, :] = shift

    for_groups(one_group)
    for copy in copies:
        copy.wait()


def start_loads(loads, sources, rest):
    copies = [
        pltpu.make_async_copy(source, target, sem)
        for source, target, sem in zip(sources, rest[:loads], rest[loads : 2 * loads])
    ]
    for copy in copies:
        copy.start()
    return copies


def step_kernel(chips, places, loads, me_ref, q_ref, sib_q_ref, *refs):
    count = len(places)
    blocks, shift_ref = refs[:count], refs[count]
    refs = refs[count + 3 :]
    acc_ref, total_ref = refs[loads : loads + 2]
    copies = start_loads(loads, refs[:loads], refs[loads + 2 :])
    tokens = q_ref.shape[0]
    flags, factors = factors_of(me_ref[0], places, chips)

    @pl.when(functools.reduce(jnp.logical_or, flags))
    def _():
        def one_group(group, columns):
            keys, values = join_blocks(blocks, factors, columns)
            queries = group_queries((q_ref, sib_q_ref), group)
            for first, rows in chunks(tokens):
                update = fold(queries, first, keys, values, shift_ref[group, rows, :])
                acc_ref[group, rows, :] += update[:, :DH]
                total_ref[group, rows, :] += update[:, DH:]

        for_groups(one_group)

    for copy in copies:
        copy.wait()


def divide(acc, total):
    inverse = pl.reciprocal(total, approx=True)
    inverse = inverse * (2.0 - total * inverse)
    return (acc * inverse).astype(jnp.bfloat16)


def put_heads(out_refs, rows_ref, tables, group, result):
    tokens = out_refs[0].shape[0]
    columns = pl.ds(pl.multiple_of(group * WIDE, WIDE), WIDE)
    for i, (out_ref, table) in enumerate(zip(out_refs, tables)):
        pieces = [
            result[(2 * h + i) * tokens : (2 * h + i + 1) * tokens] for h in range(GROUP)
        ]
        piece = jnp.concatenate(pieces, axis=1)
        out_ref[:, columns] = piece
        rows_ref[i * CAP : (i + 1) * CAP, columns] = jnp.dot(
            table[...], piece, preferred_element_type=jnp.float32
        )


def running_attention(chips, me, sources, q_refs, put, scratch, sem):
    keys_ref, values_ref, acc_ref, total_ref, top_ref = scratch
    tokens = q_refs[0].shape[0]

    def fetch(source, target):
        copy = pltpu.make_async_copy(source, target, sem)
        copy.start()
        copy.wait()

    def one_group(group, columns):
        queries = group_queries(q_refs, group)
        for i in range(chips):
            for j, block in enumerate(sources[2 * i : 2 * i + 2]):
                rows = pl.ds(j * tokens, tokens)
                fetch(block.at[pl.ds(0, tokens), columns], keys_ref.at[i, rows])
                fetch(block.at[pl.ds(tokens, tokens), columns], values_ref.at[i, rows])
        acc_ref[...] = jnp.zeros_like(acc_ref)
        total_ref[...] = jnp.zeros_like(total_ref)
        top_ref[...] = jnp.full_like(top_ref, 2 * MASKED)

        def one_chip(i, inner):
            place = jnp.where(i % 2 == 1, (i + 1) // 2, -(i // 2))
            chip = chip_at(me, place, chips)

            @pl.when(chip <= me // 2)
            def _():
                keys, values = keys_ref[i], with_ones(values_ref[i])
                barred = jnp.where(chip == me // 2, MASKED, 0.0)
                bias = jnp.where(allowed_here(me % 2, tokens), 0.0, barred)
                for first, rows in chunks(tokens):
                    scores = scores_of(head_rows(*queries, first), keys)
                    scores = jnp.where(bias < 0.0, MASKED, scores)
                    old = top_ref[rows, :]
                    top = jnp.maximum(old, row_top(scores))
                    factor = jnp.exp2(old - top)
                    weights = weights_of(scores, top).astype(jnp.bfloat16)
                    update = jnp.dot(weights, values, preferred_element_type=jnp.float32)
                    acc_ref[rows, :] = acc_ref[rows, :] * factor + update[:, :DH]
                    total_ref[rows, :] = total_ref[rows, :] * factor + update[:, DH:]
                    top_ref[rows, :] = top

            return inner

        lax.fori_loop(0, chips, one_chip, 0)
        put(group, divide(acc_ref[...], total_ref[...]))

    for_groups(one_group)


def last_kernel(chips, me_ref, q_ref, sib_q_ref, *refs):
    blocks, (shift_ref, acc_ref, total_ref, gain_ref) = refs[:2], refs[2:6]
    tables, sources = refs[6:8], refs[8 : 8 + 2 * chips]
    out_refs, picked_refs = refs[8 + 2 * chips : 10 + 2 * chips], refs[10 + 2 * chips : 12 + 2 * chips]
    rows_ref, worst_ref, sem, *scratch = refs[12 + 2 * chips :]
    q_refs = (q_ref, sib_q_ref)
    tokens, half_width = q_ref.shape
    me = me_ref[0]
    _, factors = factors_of(me, [chips // 2] * 2, chips)
    worst_ref[...] = jnp.zeros_like(worst_ref)

    def put(group, result):
        put_heads(out_refs, rows_ref, tables, group, result)

    def one_group(group, columns):
        keys, values = join_blocks(blocks, factors, columns)
        queries = group_queries(q_refs, group)
        results = []
        for first, rows in chunks(tokens):
            update = fold(queries, first, keys, values, shift_ref[group, rows, :])
            total = total_ref[group, rows, :] + update[:, DH:]
            worst_ref[...] = jnp.maximum(worst_ref[...], total)
            results.append(divide(acc_ref[group, rows, :] + update[:, :DH], total))
        put(group, jnp.concatenate(results, axis=0))

    for_groups(one_group)
    fits = jnp.max(worst_ref[...]) <= SUM_LIMIT

    @pl.when(jnp.logical_not(fits))
    def _():
        running_attention(chips, me, sources, q_refs, put, scratch, sem)

    columns = pl.ds(pl.multiple_of(me % 2 * half_width, half_width), half_width)
    gain = gain_ref[:, columns]
    for i, ref in enumerate(picked_refs):
        rows = rows_ref[i * CAP : (i + 1) * CAP, :]
        squares = jnp.broadcast_to(jnp.sum(rows * rows, axis=1, keepdims=True), (CAP, DH))
        upper = squares.astype(jnp.bfloat16)
        lower = (squares - upper.astype(jnp.float32)).astype(jnp.bfloat16)
        lane = lax.broadcasted_iota(jnp.int32, (CAP, DH), 1)
        both = jnp.where(lane < DH // 2, upper.astype(jnp.float32), lower.astype(jnp.float32))
        ref[:, :half_width] = (rows * gain).astype(jnp.bfloat16)
        ref[:, half_width:] = both.astype(jnp.bfloat16)


class Attention:
    def __init__(self, me, queries, chips):
        self.me, self.queries, self.chips = me, queries, chips
        self.tokens, self.width = queries[0].shape
        self.rows = 2 * GROUP * self.tokens
        self.state_shape = pltpu.VMEM((HK // 2, self.rows, DH), jnp.float32)

    def call(self, kernel, name, args, others, out_shape, out_others, scratch, aliases=None):
        vmem, anywhere = pl.BlockSpec(memory_space=pltpu.VMEM), pl.BlockSpec(memory_space=pl.ANY)
        return pl.pallas_call(
            kernel,
            in_specs=[pl.BlockSpec(memory_space=pltpu.SMEM)]
            + [vmem] * (2 + len(args))
            + [anywhere] * len(others),
            out_specs=[vmem] * len(out_shape) + [anywhere] * len(out_others),
            out_shape=[*out_shape, *out_others],
            scratch_shapes=scratch,
            input_output_aliases=aliases or {},
            compiler_params=pltpu.CompilerParams(vmem_limit_bytes=ATTEND_MIB * MIB),
            cost_estimate=pl.CostEstimate(
                flops=4 * self.tokens * self.width * self.tokens,
                bytes_accessed=4 * MIB,
                transcendentals=0,
            ),
            name=name,
        )(self.me, *self.queries, *args, *others)

    def own(self, own, sib, weights=()):
        loads = len(weights)
        results = self.call(
            functools.partial(own_kernel, loads),
            "attend_own",
            (own, sib),
            [in_hbm(x) for x in weights],
            [self.state_shape] * 3,
            [pltpu.VMEM(x.shape, x.dtype) for x in weights],
            [pltpu.SemaphoreType.DMA] * loads,
        )
        return list(results[:2]), results[2], results[3:]

    def step(self, blocks, places, shift, state, weights=()):
        count, loads = len(blocks), len(weights)
        results = self.call(
            functools.partial(step_kernel, self.chips, places, loads),
            "attend_step",
            (*blocks, shift, *state),
            [in_hbm(x) for x in weights],
            [self.state_shape] * 2,
            [pltpu.VMEM(x.shape, x.dtype) for x in weights],
            [pltpu.SemaphoreType.DMA] * loads,
            {count + 4: 0, count + 5: 1},
        )
        return list(results[:2]), results[2:]

    def last(self, blocks, shift, state, gain, tables, sources):
        out = pltpu.VMEM((self.tokens, self.width), jnp.bfloat16)
        picked = pltpu.VMEM((CAP, self.width + DH), jnp.bfloat16)
        kept = pltpu.VMEM((self.chips, 2 * self.tokens, DH), jnp.bfloat16)
        sums = pltpu.VMEM((self.rows, DH), jnp.float32)
        return self.call(
            functools.partial(last_kernel, self.chips),
            "attend_last",
            (*blocks, shift, *state, gain, *tables),
            sources,
            [out, out, picked, picked],
            [],
            [
                pltpu.VMEM((2 * CAP, self.width), jnp.float32),
                pltpu.VMEM((STACK * 2 * self.tokens, DH), jnp.float32),
                pltpu.SemaphoreType.DMA,
                kept,
                kept,
                sums,
                sums,
                sums,
            ],
        )


def halves_kernel(me_ref, *refs):
    count = len(refs) - 3
    sources, (keep_ref, give_ref, sems) = refs[:count], refs[count:]
    rows, width = sources[0].shape
    core = me_ref[0] % 2
    copies = []
    for side, target in ((core, keep_ref), (1 - core, give_ref)):
        columns = pl.ds(pl.multiple_of(side * (width // 2), width // 2), width // 2)
        for i, source in enumerate(sources):
            copies.append((source.at[:, columns], target.at[pl.ds(i * rows, rows)]))
    copies = [pltpu.make_async_copy(*ends, sems.at[i]) for i, ends in enumerate(copies)]
    for copy in copies:
        copy.start()
    for copy in copies:
        copy.wait()


def halves(me, *arrays):
    rows, width = arrays[0].shape
    anywhere = pl.BlockSpec(memory_space=pl.ANY)
    out = pltpu.VMEM((len(arrays) * rows, width // 2), arrays[0].dtype)
    return pl.pallas_call(
        halves_kernel,
        in_specs=[pl.BlockSpec(memory_space=pltpu.SMEM)] + [anywhere] * len(arrays),
        out_specs=[anywhere] * 2,
        out_shape=[out, out],
        scratch_shapes=[pltpu.SemaphoreType.DMA((2 * len(arrays),))],
        compiler_params=pltpu.CompilerParams(vmem_limit_bytes=MIB),
        name="halves",
    )(me, *(in_hbm(x) for x in arrays))


def beside_kernel(me_ref, keep_ref, other_ref, out_ref, sems):
    width = keep_ref.shape[1]
    core = me_ref[0] % 2
    copies = []
    for i, (side, source) in enumerate(((core, keep_ref), (1 - core, other_ref))):
        columns = pl.ds(pl.multiple_of(side * width, width), width)
        copies.append(pltpu.make_async_copy(source, out_ref.at[:, columns], sems.at[i]))
    for copy in copies:
        copy.start()
    for copy in copies:
        copy.wait()


def beside(me, keep, other):
    rows, width = keep.shape
    anywhere = pl.BlockSpec(memory_space=pl.ANY)
    return pl.pallas_call(
        beside_kernel,
        in_specs=[pl.BlockSpec(memory_space=pltpu.SMEM)] + [anywhere] * 2,
        out_specs=anywhere,
        out_shape=jax.ShapeDtypeStruct((rows, 2 * width), keep.dtype),
        scratch_shapes=[pltpu.SemaphoreType.DMA((2,))],
        compiler_params=pltpu.CompilerParams(vmem_limit_bytes=MIB),
        name="beside",
    )(me, keep, other)


def gather_kernel(*refs):
    for j, ref in enumerate(refs[:-1]):
        refs[-1][j * CAP : (j + 1) * CAP] = ref[...]


def gather(blocks):
    vmem = pl.BlockSpec(memory_space=pltpu.VMEM)
    return pl.pallas_call(
        gather_kernel,
        in_specs=[vmem] * len(blocks),
        out_specs=vmem,
        out_shape=pltpu.VMEM((CAP * len(blocks), blocks[0].shape[1]), jnp.bfloat16),
        compiler_params=pltpu.CompilerParams(vmem_limit_bytes=4 * MIB),
        name="gather",
    )(*blocks)


def hidden_kernel(second, me_ref, rows_ref, gate_ref, up_ref, *refs):
    half = rows_ref.shape[1] - DH
    middle = rows_ref.shape[0] // 2
    depth = min(1024, half)
    if second:
        own_ref, gate_in, up_in, source_ref, out_ref, target_ref, gate_sum, up_sum, sem = refs
        gate_sum[...] = gate_in[...]
        up_sum[...] = up_in[...]
    else:
        source_ref, gate_sum, up_sum, target_ref, sem = refs
        gate_sum[...] = jnp.zeros_like(gate_sum)
        up_sum[...] = jnp.zeros_like(up_sum)
    side = 1 - me_ref[0] % 2 if second else me_ref[0] % 2
    columns = pl.ds(target_ref.shape[1] if second else 0, target_ref.shape[1])
    load = pltpu.make_async_copy(source_ref.at[:, columns], target_ref, sem)
    load.start()

    def one_part(step, carry):
        part = rows_ref[:, pl.ds(pl.multiple_of(step * depth, depth), depth)]
        if second:
            part = jnp.concatenate([part[middle:], part[:middle]], axis=0)
        place = pl.ds(pl.multiple_of(side * half + step * depth, depth), depth)
        gate_sum[...] += jnp.dot(part, gate_ref[place, :], preferred_element_type=jnp.float32)
        up_sum[...] += jnp.dot(part, up_ref[place, :], preferred_element_type=jnp.float32)
        return carry

    lax.fori_loop(0, half // depth, one_part, 0)
    if second:
        squares = own_ref[:, half:].astype(jnp.float32)
        others = rows_ref[:, half:].astype(jnp.float32)
        squares += jnp.concatenate([others[middle:], others[:middle]], axis=0)
        squares = squares[:, :1] + squares[:, DH // 2 : DH // 2 + 1]
        factor = lax.rsqrt(squares / (2 * half) + 1e-05)
        gate = gate_sum[...] * factor
        out_ref[...] = (gate / (1.0 + jnp.exp(-gate)) * (up_sum[...] * factor)).astype(jnp.bfloat16)
    load.wait()


def hidden_call(me, rows, w_gate, w_up, w_down, own=None, sums=()):
    count, half = rows.shape[0], rows.shape[1] - DH
    units, width = w_down.shape
    vmem, anywhere = pl.BlockSpec(memory_space=pltpu.VMEM), pl.BlockSpec(memory_space=pl.ANY)
    sum_shape = pltpu.VMEM((count, units), jnp.float32)
    second = own is not None
    more = (own, *sums) if second else ()
    outs = [pltpu.VMEM((count, units), jnp.bfloat16)] if second else [sum_shape] * 2
    return pl.pallas_call(
        functools.partial(hidden_kernel, second),
        in_specs=[pl.BlockSpec(memory_space=pltpu.SMEM)] + [vmem] * (3 + len(more)) + [anywhere],
        out_specs=[vmem] * len(outs) + [anywhere],
        out_shape=outs + [pltpu.VMEM((units, width // 2), w_down.dtype)],
        scratch_shapes=[sum_shape] * (2 if second else 0) + [pltpu.SemaphoreType.DMA],
        compiler_params=pltpu.CompilerParams(vmem_limit_bytes=12 * MIB),
        cost_estimate=pl.CostEstimate(
            flops=4 * count * half * units,
            bytes_accessed=4 * half * units + 2 * count * half,
            transcendentals=count * units,
        ),
        name="hidden",
    )(me, rows, w_gate, w_up, *more, in_hbm(w_down))


def down_kernel(hidden_ref, down_ref, own_ref, sib_ref):
    middle, width = own_ref.shape
    cols = min(1024, width)

    def one_part(step, carry):
        columns = pl.ds(pl.multiple_of(step * cols, cols), cols)
        part = jnp.dot(hidden_ref[...], down_ref[:, columns], preferred_element_type=jnp.float32)
        part = part.astype(jnp.bfloat16)
        own_ref[:, columns] = part[:middle]
        sib_ref[:, columns] = part[middle:]
        return carry

    lax.fori_loop(0, width // cols, one_part, 0)


def down_call(hidden, w_down):
    rows, units = hidden.shape
    width = w_down.shape[1]
    vmem = pl.BlockSpec(memory_space=pltpu.VMEM)
    return pl.pallas_call(
        down_kernel,
        in_specs=[vmem] * 2,
        out_specs=[vmem] * 2,
        out_shape=[pltpu.VMEM((rows // 2, width), jnp.bfloat16)] * 2,
        compiler_params=pltpu.CompilerParams(vmem_limit_bytes=16 * MIB),
        cost_estimate=pl.CostEstimate(
            flops=2 * rows * width * units,
            bytes_accessed=2 * width * units + 2 * rows * width,
            transcendentals=0,
        ),
        name="down",
    )(hidden, w_down)


def spread_kernel(a_ref, b_ref, c_ref, d_ref, table_ref, *rest):
    out_ref = rest[-1]
    total = a_ref[...].astype(jnp.float32) + b_ref[...].astype(jnp.float32)
    total += c_ref[...].astype(jnp.float32) + d_ref[...].astype(jnp.float32)
    total = total.astype(jnp.bfloat16)
    out_ref[...] = lax.dot_general(
        table_ref[...],
        jnp.concatenate([total] * PARTS, axis=0),
        (((0,), (0,)), ((), ())),
        preferred_element_type=jnp.float32,
    ).astype(jnp.bfloat16)


def spread_call(parts, table, piece, pieces, previous):
    tokens = table.shape[1]
    piece_width = parts[0].shape[1]
    cols = min(2048, piece_width)
    steps = piece_width // cols
    earlier = [] if previous is None else [previous]
    return pl.pallas_call(
        spread_kernel,
        grid=(steps,),
        in_specs=[pl.BlockSpec((CAP, cols), lambda i: (0, i))] * 4
        + [pl.BlockSpec((PARTS * CAP, tokens), lambda i: (0, 0))]
        + [pl.BlockSpec(memory_space=pl.ANY)] * len(earlier),
        out_specs=pl.BlockSpec((tokens, cols), lambda i: (0, piece * steps + i)),
        out_shape=jax.ShapeDtypeStruct((tokens, piece_width * pieces), jnp.bfloat16),
        input_output_aliases={5: 0} if earlier else {},
        compiler_params=pltpu.CompilerParams(
            dimension_semantics=("arbitrary",), vmem_limit_bytes=16 * MIB
        ),
        name="spread",
    )(*parts, table, *earlier)


def reduce_chip_rows(mine, other, half, chips, go_right, go_left):
    middle = mine.shape[1] // 2

    def block(index):
        rows = slice(index * CAP, (index + 1) * CAP)
        return mine[rows].astype(jnp.float32) + other[rows].astype(jnp.float32)

    far = block(chips - 1).astype(jnp.bfloat16)
    ahead, back = far[:, :middle], far[:, middle:]
    for distance in range(half - 1, -1, -1):
        ahead, back = lax.optimization_barrier((ahead, back))
        to_right, to_left = go_right(ahead), go_left(back)
        yield
        if distance == 0:
            break
        ahead, back = block(half - 1 + distance), block(distance)
        if distance == half - 1:
            ahead = jnp.concatenate(
                [ahead[:, :middle] + to_right.astype(jnp.float32), ahead[:, middle:]], axis=1
            )
            back = jnp.concatenate(
                [back[:, :middle], back[:, middle:] + to_left.astype(jnp.float32)], axis=1
            )
        else:
            ahead = ahead + to_right.astype(jnp.float32)
            back = back + to_left.astype(jnp.float32)
        ahead, back = ahead.astype(jnp.bfloat16), back.astype(jnp.bfloat16)
    return (mine, other, to_right, to_left)


def run_together(generators):
    results = [None] * len(generators)
    active = list(range(len(generators)))
    while active:
        for i in list(active):
            try:
                next(generators[i])
            except StopIteration as stop:
                results[i] = stop.value
                active.remove(i)
    return results


def per_device(chips, queries, keys, values, norm_gain, expert_ids, gates, w_gate, w_up, w_down):
    right, left, sibling = permutations(chips)
    half = chips // 2
    go_right = lambda x: lax.ppermute(x, "ctx", right)
    go_left = lambda x: lax.ppermute(x, "ctx", left)
    swap = lambda x: lax.ppermute(x, "ctx", sibling)

    me = lax.axis_index("ctx").astype(jnp.int32).reshape(1)
    tokens = queries.shape[0]
    hits = (expert_ids == 0).astype(jnp.float32)
    chosen = jnp.sum(hits, axis=1)
    position = jnp.arange(tokens, dtype=jnp.int32)
    before = (position[None, :] < position[:, None]).astype(jnp.float32)
    slot = jnp.sum(before * chosen[None, :], axis=1).astype(jnp.int32)
    table = jnp.logical_and(
        slot[None, :] == jnp.arange(CAP, dtype=jnp.int32)[:, None], chosen[None, :] > 0
    ).astype(jnp.float32)
    rest = jnp.sum(gates * hits, axis=1)
    weights = []
    for _ in range(PARTS):
        part = lax.reduce_precision(rest, 8, 7)
        weights.append(table * part[None, :])
        rest = rest - part
    weighted = jnp.concatenate(weights, axis=0).astype(jnp.bfloat16)
    table = table.astype(jnp.bfloat16)

    own, give = halves(me, keys, values)
    sib = swap(give)
    from_left, from_right = [go_right(own)], [go_left(own)]
    q_own, q_give = halves(me, queries)
    from_left.append(go_right(sib))
    from_right.append(go_left(sib))
    q_sib = swap(q_give)
    sib_table = swap(table)
    attention = Attention(me, (q_own, q_sib), chips)
    state, shift, (w_gate,) = attention.own(own, sib, (w_gate,))
    sources = [own, sib]
    for step in range(1, half):
        from_left, from_right, state = lax.optimization_barrier((from_left, from_right, state))
        blocks, places = from_left + from_right, [step, step, -step, -step]
        sources += blocks
        if step < half - 1:
            from_left, from_right = [go_right(x) for x in from_left], [go_left(x) for x in from_right]
        else:
            opposite = [go_right(from_left[0]), go_left(from_right[1])]
        if step == 2:
            state, (w_up,) = attention.step(blocks, places, shift, state, (w_up,))
        else:
            state, _ = attention.step(blocks, places, shift, state)
    opposite, state = lax.optimization_barrier((opposite, state))
    sources += opposite
    mine, theirs, *picked = attention.last(
        opposite, shift, state, norm_gain[None, :], (table, sib_table), sources
    )

    from_left, from_right = list(picked), list(picked)
    blocks_right, blocks_left = [picked], []
    result = None
    for step in range(1, half):
        from_left, from_right = [go_right(x) for x in from_left], [go_left(x) for x in from_right]
        from_left, from_right, mine, theirs = lax.optimization_barrier(
            (from_left, from_right, mine, theirs)
        )
        if step == 1:
            theirs = swap(theirs)
        elif step == 2:
            theirs = beside(me, mine, theirs)
        blocks_right.append(from_left)
        blocks_left.append(from_right)
    result = theirs
    far = [go_right(from_left[0]), go_left(from_right[1])]
    blocks = blocks_right + blocks_left + [far]
    rows = gather([own for own, _ in blocks] + [sib for _, sib in blocks])
    *first, down_low = hidden_call(me, rows, w_gate, w_up, w_down)
    hidden, down_high = hidden_call(me, swap(rows), w_gate, w_up, w_down, rows, first)
    downs = [down_low, down_high]

    sums = []
    for piece in range(PIECES):
        mine, theirs = down_call(hidden, downs[piece])
        sums.append(reduce_chip_rows(mine, swap(theirs), half, chips, go_right, go_left))
    mixed = None
    for piece, parts in enumerate(run_together(sums)):
        mixed = spread_call(parts, weighted, piece, PIECES, mixed)
    return (result, mixed)


def solution(mesh):
    placed = (
        P(("groups", "ctx"), None),
        P(("groups", "ctx"), None),
        P(("groups", "ctx"), None),
        P(),
        P(("groups", "ctx"), None),
        P(("groups", "ctx"), None),
        P(None, "ctx"),
        P(None, "ctx"),
        P("ctx", None),
    )
    return jax.shard_map(
        functools.partial(per_device, mesh.shape["ctx"] // 2),
        mesh=mesh,
        in_specs=placed,
        out_specs=(P(("groups", "ctx"), None), P(("groups", "ctx"), None)),
        check_vma=False,
    )
```

time: 197 us -> 189 us (0.959)
  waiting for transfers between devices: 109 us -> 52.9 us
  starting transfers between devices: 37.2 us -> 85.8 us
  Pallas kernels: 47.8 us -> 34 us
  local copies, waits for them, and re-layouts: 0.17 us -> 13.8 us
    ppermute x16 -> x22, waiting for transfers between devices: 61 us -> 18.5 us  [per_device(): go_left = lambda x: lax.ppermute(x, 'ctx', left)]
    ppermute x16 -> x22, starting transfers between devices: 22.4 us -> 60.7 us  [per_device(): go_right = lambda x: lax.ppermute(x, 'ctx', right)]
    pallas_call x11 -> x8, Pallas kernels: 31.7 us -> 17.7 us  [the longest x5 13.6 us: call(): pl.pallas_call(kernel, in_specs=[pl.BlockSpec(memory_space=pltpu.SMEM)] +...]
    unnamed x13 -> x14, local copies, waits for them, and re-layouts: 0.04 us -> 13.7 us
    ppermute x16 -> x22, starting transfers between devices: 11.8 us -> 23.7 us  [per_device(): go_left = lambda x: lax.ppermute(x, 'ctx', left)]
    ppermute x16 -> x22, waiting for transfers between devices: 45.4 us -> 34 us  [per_device(): go_right = lambda x: lax.ppermute(x, 'ctx', right)]
    ppermute x13 -> x7, waiting for transfers between devices: 2.96 us -> 0.46 us  [per_device(): swap = lambda x: lax.ppermute(x, 'ctx', sibling)]
  transfers between devices with their start and end apart: 45 -> 51, of which waited for: 30 -> 34; matrix products, arithmetic and copies ran while one was open for 0% -> 0% of each run, Pallas kernels for 15% -> 10%
where the time goes in v1:
time: 189 us; the launch traced here: 188 us
  starting transfers between devices  85.8 us (45%)
  waiting for transfers between devices  52.9 us (28%)
  Pallas kernels  34 us (18%)
  local copies, waits for them, and re-layouts  13.8 us (7%)
    ppermute x22, starting transfers between devices, per_device(): go_right = lambda x: lax.ppermute(x, 'ctx', right)  60.7 us
    ppermute x22, waiting for transfers between devices, per_device(): go_right = lambda x: lax.ppermute(x, 'ctx', right)  34 us
    ppermute x22, starting transfers between devices, per_device(): go_left = lambda x: lax.ppermute(x, 'ctx', left)  23.7 us
    ppermute x22, waiting for transfers between devices, per_device(): go_left = lambda x: lax.ppermute(x, 'ctx', left)  18.5 us
    unnamed x14, local copies, waits for them, and re-layouts  13.7 us
    pallas_call x5, Pallas kernels, call(): pl.pallas_call(kernel, in_specs=[pl.BlockSpec(memory_space=pltpu.SMEM)] +...  13.6 us
    pallas_call x2, Pallas kernels, hidden_call(): pl.pallas_call(functools.partial(hidden_kernel, second), in_specs=[pl.Blo...  8.58 us
    pallas_call x2, Pallas kernels, down_call(): pl.pallas_call(down_kernel, in_specs=[vmem] * 2, out_specs=[vmem] * 2, ou...  4.61 us
  transfers between devices with their start and end apart: 51, of which 34 were waited for; matrix products, arithmetic and copies ran while one was open for 0% of the time, Pallas kernels for 10%

profile of v1, /device:TPU:0, one launch (start us, length us, event | category | flops | bytes accessed | tf_op | source)
XLA Modules:
  0.0 188.3 jit_solution(13591470697979579253)
XLA Ops:
  4.0 3.0 %collective-permute-start.1 = (bf16[256,512]{1,0:T(8,128)(2,1)S(1)}, bf16[256,512]{1,0:T(8,128)(2,1)S(1)}, u32[]{:S(2)}, u32[]{:S(2)}) collective-permute-start(bf16[256,512]{1,0:T(8,128)(2,1)S(1)} %get-tuple-element.87.own_ref.refs_8_), channel_id=1, source_target_pairs={{0,4},{1,5},{4,8},{5,9},{8,12},{9,13},{12,14},{13,15},{14,10},{15,... | collective-permute-start | bytes 786440 | tf_op jit(solution)/shard_map/ppermute | solution.py:636
  7.0 2.0 %collective-permute-start.3 = (bf16[256,512]{1,0:T(8,128)(2,1)S(1)}, bf16[256,512]{1,0:T(8,128)(2,1)S(1)}, u32[]{:S(2)}, u32[]{:S(2)}) collective-permute-start(bf16[256,512]{1,0:T(8,128)(2,1)S(1)} %collective-permute-done.2.sib_ref.refs_9_), channel_id=1, source_target_pairs={{0,4},{1,5},{4,8},{5,9},{8,12},{9,13},{12,14},{13,15},{14,10},{15,... | collective-permute-start | bytes 786440 | tf_op jit(solution)/shard_map/ppermute | solution.py:636
  9.0 4.6 %attend_own.1 = (f32[4,2048,128]{2,1,0:T(8,128)S(1)}, f32[4,2048,128]{2,1,0:T(8,128)S(1)}, f32[4,2048,128]{2,1,0:T(8,128)S(1)}, bf16[8192,768]{1,0:T(8,128)(2,1)S(1)}) custom-call(s32[1]{0:T(128)} %bitcast.me_ref, bf16[128,4096]{1,0:T(8,128)(2,1)S(1)} %get-tuple-element.85.q_ref, bf16[128,4096]{1,0:T(8,128)(2,1)S(1)} %collective-permute-done.sib_q_ref, ...), custom_call_target="tpu_custom_call" | custom-call | flops 268435456 | bytes 4194304 | tf_op jit(solution)/shard_map/attend_own/pallas_call | solution.py:313
  13.6 4.6 %copy-done = bf16[8192,768]{1,0:T(8,128)(2,1)} copy-done((bf16[8192,768]{1,0:T(8,128)(2,1)}, bf16[8192,768]{1,0:T(8,128)(2,1)S(1)}, u32[]{:S(2)}) %copy-start) | copy-done | bytes 12582936
  24.7 5.2 %collective-permute-done.6.refs_0_.refs_14_ = bf16[256,512]{1,0:T(8,128)(2,1)S(1)} collective-permute-done((bf16[256,512]{1,0:T(8,128)(2,1)S(1)}, bf16[256,512]{1,0:T(8,128)(2,1)S(1)}, u32[]{:S(2)}, u32[]{:S(2)}) %collective-permute-start.6) | collective-permute-done | bytes 262176 | tf_op jit(solution)/shard_map/ppermute | solution.py:636
  29.9 3.5 %collective-permute-done.7.refs_1_.refs_15_ = bf16[256,512]{1,0:T(8,128)(2,1)S(1)} collective-permute-done((bf16[256,512]{1,0:T(8,128)(2,1)S(1)}, bf16[256,512]{1,0:T(8,128)(2,1)S(1)}, u32[]{:S(2)}, u32[]{:S(2)}) %collective-permute-start.7) | collective-permute-done | bytes 262176 | tf_op jit(solution)/shard_map/ppermute | solution.py:636
  33.4 2.6 %collective-permute-done.9.refs_3_.refs_17_ = bf16[256,512]{1,0:T(8,128)(2,1)S(1)} collective-permute-done((bf16[256,512]{1,0:T(8,128)(2,1)S(1)}, bf16[256,512]{1,0:T(8,128)(2,1)S(1)}, u32[]{:S(2)}, u32[]{:S(2)}) %collective-permute-start.9) | collective-permute-done | bytes 262176 | tf_op jit(solution)/shard_map/ppermute | solution.py:637
  40.0 4.6 %attend_step.4 = (f32[4,2048,128]{2,1,0:T(8,128)S(1)}, f32[4,2048,128]{2,1,0:T(8,128)S(1)}, bf16[8192,768]{1,0:T(8,128)(2,1)S(1)}) custom-call(s32[1]{0:T(128)} %bitcast.me_ref, bf16[128,4096]{1,0:T(8,128)(2,1)S(1)} %get-tuple-element.85.q_ref, bf16[128,4096]{1,0:T(8,128)(2,1)S(1)} %collective-permute-done.sib_q_ref, ...), custom_call_target="tpu_custom_call", output_to_operand_aliasing={{0}: (8, {}), {1}: (9, {})} | custom-call | flops 268435456 | bytes 4194304 | tf_op jit(solution)/shard_map/attend_step/pallas_call | solution.py:313
  44.7 2.6 %collective-permute-done.11.refs_1_.refs_19_ = bf16[256,512]{1,0:T(8,128)(2,1)S(1)} collective-permute-done((bf16[256,512]{1,0:T(8,128)(2,1)S(1)}, bf16[256,512]{1,0:T(8,128)(2,1)S(1)}, u32[]{:S(2)}, u32[]{:S(2)}) %collective-permute-start.11) | collective-permute-done | bytes 262176 | tf_op jit(solution)/shard_map/ppermute | solution.py:636
  47.2 2.8 %collective-permute-done.13.refs_3_.refs_21_ = bf16[256,512]{1,0:T(8,128)(2,1)S(1)} collective-permute-done((bf16[256,512]{1,0:T(8,128)(2,1)S(1)}, bf16[256,512]{1,0:T(8,128)(2,1)S(1)}, u32[]{:S(2)}, u32[]{:S(2)}) %collective-permute-start.13) | collective-permute-done | bytes 262176 | tf_op jit(solution)/shard_map/ppermute | solution.py:637
  50.0 2.0 %collective-permute-start.15 = (bf16[256,512]{1,0:T(8,128)(2,1)S(1)}, bf16[256,512]{1,0:T(8,128)(2,1)S(1)}, u32[]{:S(2)}, u32[]{:S(2)}) collective-permute-start(bf16[256,512]{1,0:T(8,128)(2,1)S(1)} %collective-permute-done.13.refs_3_.refs_21_), channel_id=1, source_target_pairs={{4,0},{5,1},{8,4},{9,5},{12,8},{13,9},{14,12},{15,13},{10,14},{11,... | collective-permute-start | bytes 786440 | tf_op jit(solution)/shard_map/ppermute | solution.py:637
  52.3 4.1 %collective-permute-done.14.refs_0_.refs_22_ = bf16[256,512]{1,0:T(8,128)(2,1)S(1)} collective-permute-done((bf16[256,512]{1,0:T(8,128)(2,1)S(1)}, bf16[256,512]{1,0:T(8,128)(2,1)S(1)}, u32[]{:S(2)}, u32[]{:S(2)}) %collective-permute-start.14) | collective-permute-done | bytes 262176 | tf_op jit(solution)/shard_map/ppermute | solution.py:636
  56.4 4.4 %attend_last.1 = (bf16[128,4096]{1,0:T(8,128)(2,1)S(1)}, bf16[128,4096]{1,0:T(8,128)(2,1)S(1)}, bf16[16,4224]{1,0:T(8,128)(2,1)S(1)}, bf16[16,4224]{1,0:T(8,128)(2,1)S(1)}) custom-call(s32[1]{0:T(128)} %bitcast.me_ref, bf16[128,4096]{1,0:T(8,128)(2,1)S(1)} %get-tuple-element.85.q_ref, bf16[128,4096]{1,0:T(8,128)(2,1)S(1)} %collective-permute-done.sib_q_ref, ...), custom_call_target="tpu_custom_call" | custom-call | flops 268435456 | bytes 4194304 | tf_op jit(solution)/shard_map/attend_last/pallas_call | solution.py:313
  67.3 2.4 %collective-permute-done.19.refs_4_ = bf16[16,4224]{1,0:T(8,128)(2,1)S(1)} collective-permute-done((bf16[16,4224]{1,0:T(8,128)(2,1)S(1)}, bf16[16,4224]{1,0:T(8,128)(2,1)S(1)}, u32[]{:S(2)}, u32[]{:S(2)}) %collective-permute-start.19) | collective-permute-done | bytes 135200 | tf_op jit(solution)/shard_map/ppermute | solution.py:637
  69.7 1.8 collective-permute-done.20.refs_12_
  71.5 40.2 %collective-permute-start.21 = (bf16[16,4224]{1,0:T(8,128)(2,1)S(1)}, bf16[16,4224]{1,0:T(8,128)(2,1)S(1)}, u32[]{:S(2)}, u32[]{:S(2)}) collective-permute-start(bf16[16,4224]{1,0:T(8,128)(2,1)S(1)} %collective-permute-done.17.refs_1_), channel_id=1, source_target_pairs={{0,4},{1,5},{4,8},{5,9},{8,12},{9,13},{12,14},{13,15},{14,10},{15,... | collective-permute-start | bytes 405512 | tf_op jit(solution)/shard_map/ppermute | solution.py:636
  111.8 1.7 collective-permute-start.22
  113.8 1.8 collective-permute-done.21.refs_2_
  115.7 2.5 %collective-permute-done.22.refs_10_ = bf16[16,4224]{1,0:T(8,128)(2,1)S(1)} collective-permute-done((bf16[16,4224]{1,0:T(8,128)(2,1)S(1)}, bf16[16,4224]{1,0:T(8,128)(2,1)S(1)}, u32[]{:S(2)}, u32[]{:S(2)}) %collective-permute-start.22) | collective-permute-done | bytes 135200 | tf_op jit(solution)/shard_map/ppermute | solution.py:636
  118.2 1.8 collective-permute-done.23.refs_5_
  120.0 1.9 collective-permute-done.24.refs_13_
  132.1 3.0 %collective-permute-done.30.refs_7_ = bf16[16,4224]{1,0:T(8,128)(2,1)S(1)} collective-permute-done((bf16[16,4224]{1,0:T(8,128)(2,1)S(1)}, bf16[16,4224]{1,0:T(8,128)(2,1)S(1)}, u32[]{:S(2)}, u32[]{:S(2)}) %collective-permute-start.30) | collective-permute-done | bytes 135200 | tf_op jit(solution)/shard_map/ppermute | solution.py:636
  135.6 4.6 %copy-done.1 = bf16[8192,768]{1,0:T(8,128)(2,1)S(1)} copy-done((bf16[8192,768]{1,0:T(8,128)(2,1)S(1)}, bf16[8192,768]{1,0:T(8,128)(2,1)}, u32[]{:S(2)}) %copy-start.1) | copy-done | bytes 12582936
  140.2 4.6 %copy-done.3 = bf16[8192,768]{1,0:T(8,128)(2,1)S(1)} copy-done((bf16[8192,768]{1,0:T(8,128)(2,1)S(1)}, bf16[8192,768]{1,0:T(8,128)(2,1)}, u32[]{:S(2)}) %copy-start.3) | copy-done | bytes 12582936
  144.8 4.0 %hidden.2 = (f32[256,768]{1,0:T(8,128)S(1)}, f32[256,768]{1,0:T(8,128)S(1)}, bf16[768,4096]{1,0:T(8,128)(2,1)S(1)}) custom-call(s32[1]{0:T(128)} %bitcast.me_ref, bf16[256,4224]{1,0:T(8,128)(2,1)S(1)} %gather.1.rows_ref.refs_0_, bf16[8192,768]{1,0:T(8,128)(2,1)S(1)} %copy-done.1, bf16[8192,768]{1,0:T(8,128)(2,1)S(1)} %copy-done.3, bf16[768,8192]{1,0:T(8,128)(2,1)} %refs_3_.1), custom_call_target="tpu_custom_call" | custom-call | flops 3221225472 | bytes 14680064 | tf_op jit(solution)/shard_map/hidden/pallas_call | solution.py:505
  148.8 4.5 %hidden.3 = (bf16[256,768]{1,0:T(8,128)(2,1)S(1)}, bf16[768,4096]{1,0:T(8,128)(2,1)S(1)}) custom-call(s32[1]{0:T(128)} %bitcast.me_ref, bf16[256,4224]{1,0:T(8,128)(2,1)S(1)} %collective-permute-done.32.rows_ref, bf16[8192,768]{1,0:T(8,128)(2,1)S(1)} %copy-done.1, bf16[8192,768]{1,0:T(8,128)(2,1)S(1)} %copy-done.3, ...), custom_call_target="tpu_custom_call" | custom-call | flops 3221225472 | bytes 14680064 | tf_op jit(solution)/shard_map/hidden/pallas_call | solution.py:505
  153.4 2.3 %down.3 = (bf16[128,4096]{1,0:T(8,128)(2,1)S(1)}, bf16[128,4096]{1,0:T(8,128)(2,1)S(1)}) custom-call(bf16[256,768]{1,0:T(8,128)(2,1)S(1)} %get-tuple-element.145.hidden_ref, bf16[768,4096]{1,0:T(8,128)(2,1)S(1)} %get-tuple-element.157.down_ref), custom_call_target="tpu_custom_call" | custom-call | flops 1610612736 | bytes 8388608 | tf_op jit(solution)/shard_map/down/pallas_call | solution.py:540
  156.3 2.3 %down.2 = (bf16[128,4096]{1,0:T(8,128)(2,1)S(1)}, bf16[128,4096]{1,0:T(8,128)(2,1)S(1)}) custom-call(bf16[256,768]{1,0:T(8,128)(2,1)S(1)} %get-tuple-element.145.hidden_ref, bf16[768,4096]{1,0:T(8,128)(2,1)S(1)} %get-tuple-element.146.down_ref), custom_call_target="tpu_custom_call" | custom-call | flops 1610612736 | bytes 8388608 | tf_op jit(solution)/shard_map/down/pallas_call | solution.py:540
  158.8 1.7 collective-permute-start.44
  161.5 1.7 collective-permute-start.35
  171.7 1.9 %collective-permute-start.48 = (bf16[16,4096]{1,0:T(8,128)(2,1)S(1)}, bf16[16,4096]{1,0:T(8,128)(2,1)S(1)}, u32[]{:S(2)}, u32[]{:S(2)}) collective-permute-start(bf16[16,4096]{1,0:T(8,128)(2,1)S(1)} %get-tuple-element.165), channel_id=1, source_target_pairs={{4,0},{5,1},{8,4},{9,5},{12,8},{13,9},{14,12},{15,13},{10,14},{11,... | collective-permute-start | bytes 393224 | tf_op jit(solution)/shard_map/ppermute | solution.py:637
  177.5 1.8 collective-permute-start.49
  (127 shorter events, 54.8 us)
Async XLA Ops:
  2.2 6.8 %collective-permute-start = (bf16[128,4096]{1,0:T(8,128)(2,1)S(1)}, bf16[128,4096]{1,0:T(8,128)(2,1)S(1)}, u32[]{:S(2)}, u32[]{:S(2)}) collective-permute-start(bf16[128,4096]{1,0:T(8,128)(2,1)S(1)} %get-tuple-element.86), channel_id=1, source_target_pairs={{0,1},{1,0},{2,3},{3,2},{4,5},{5,4},{6,7},{7,6},{8,9},{9,8},{10,11... | collective-permute-start | bytes 3145736 | tf_op jit(solution)/shard_map/ppermute | solution.py:638
  4.0 14.2 %collective-permute-start.1 = (bf16[256,512]{1,0:T(8,128)(2,1)S(1)}, bf16[256,512]{1,0:T(8,128)(2,1)S(1)}, u32[]{:S(2)}, u32[]{:S(2)}) collective-permute-start(bf16[256,512]{1,0:T(8,128)(2,1)S(1)} %get-tuple-element.87.own_ref.refs_8_), channel_id=1, source_target_pairs={{0,4},{1,5},{4,8},{5,9},{8,12},{9,13},{12,14},{13,15},{14,10},{15,... | collective-permute-start | bytes 786440 | tf_op jit(solution)/shard_map/ppermute | solution.py:636
  7.0 11.2 %collective-permute-start.4 = (bf16[256,512]{1,0:T(8,128)(2,1)S(1)}, bf16[256,512]{1,0:T(8,128)(2,1)S(1)}, u32[]{:S(2)}, u32[]{:S(2)}) collective-permute-start(bf16[256,512]{1,0:T(8,128)(2,1)S(1)} %get-tuple-element.87.own_ref.refs_8_), channel_id=1, source_target_pairs={{4,0},{5,1},{8,4},{9,5},{12,8},{13,9},{14,12},{15,13},{10,14},{11,... | collective-permute-start | bytes 786440 | tf_op jit(solution)/shard_map/ppermute | solution.py:637
  7.0 12.1 %collective-permute-start.3 = (bf16[256,512]{1,0:T(8,128)(2,1)S(1)}, bf16[256,512]{1,0:T(8,128)(2,1)S(1)}, u32[]{:S(2)}, u32[]{:S(2)}) collective-permute-start(bf16[256,512]{1,0:T(8,128)(2,1)S(1)} %collective-permute-done.2.sib_ref.refs_9_), channel_id=1, source_target_pairs={{0,4},{1,5},{4,8},{5,9},{8,12},{9,13},{12,14},{13,15},{14,10},{15,... | collective-permute-start | bytes 786440 | tf_op jit(solution)/shard_map/ppermute | solution.py:636
  9.0 11.6 %collective-permute-start.5 = (bf16[256,512]{1,0:T(8,128)(2,1)S(1)}, bf16[256,512]{1,0:T(8,128)(2,1)S(1)}, u32[]{:S(2)}, u32[]{:S(2)}) collective-permute-start(bf16[256,512]{1,0:T(8,128)(2,1)S(1)} %collective-permute-done.2.sib_ref.refs_9_), channel_id=1, source_target_pairs={{4,0},{5,1},{8,4},{9,5},{12,8},{13,9},{14,12},{15,13},{10,14},{11,... | collective-permute-start | bytes 786440 | tf_op jit(solution)/shard_map/ppermute | solution.py:637
  20.6 9.2 %collective-permute-start.6 = (bf16[256,512]{1,0:T(8,128)(2,1)S(1)}, bf16[256,512]{1,0:T(8,128)(2,1)S(1)}, u32[]{:S(2)}, u32[]{:S(2)}) collective-permute-start(bf16[256,512]{1,0:T(8,128)(2,1)S(1)} %collective-permute-done.1.refs_0_.refs_10_), channel_id=1, source_target_pairs={{0,4},{1,5},{4,8},{5,9},{8,12},{9,13},{12,14},{13,15},{14,10},{15,... | collective-permute-start | bytes 786440 | tf_op jit(solution)/shard_map/ppermute | solution.py:636
  22.2 11.2 %collective-permute-start.7 = (bf16[256,512]{1,0:T(8,128)(2,1)S(1)}, bf16[256,512]{1,0:T(8,128)(2,1)S(1)}, u32[]{:S(2)}, u32[]{:S(2)}) collective-permute-start(bf16[256,512]{1,0:T(8,128)(2,1)S(1)} %collective-permute-done.3.refs_1_.refs_11_), channel_id=1, source_target_pairs={{0,4},{1,5},{4,8},{5,9},{8,12},{9,13},{12,14},{13,15},{14,10},{15,... | collective-permute-start | bytes 786440 | tf_op jit(solution)/shard_map/ppermute | solution.py:636
  23.8 9.6 %collective-permute-start.8 = (bf16[256,512]{1,0:T(8,128)(2,1)S(1)}, bf16[256,512]{1,0:T(8,128)(2,1)S(1)}, u32[]{:S(2)}, u32[]{:S(2)}) collective-permute-start(bf16[256,512]{1,0:T(8,128)(2,1)S(1)} %collective-permute-done.4.refs_2_.refs_12_), channel_id=1, source_target_pairs={{4,0},{5,1},{8,4},{9,5},{12,8},{13,9},{14,12},{15,13},{10,14},{11,... | collective-permute-start | bytes 786440 | tf_op jit(solution)/shard_map/ppermute | solution.py:637
  24.2 11.7 %collective-permute-start.9 = (bf16[256,512]{1,0:T(8,128)(2,1)S(1)}, bf16[256,512]{1,0:T(8,128)(2,1)S(1)}, u32[]{:S(2)}, u32[]{:S(2)}) collective-permute-start(bf16[256,512]{1,0:T(8,128)(2,1)S(1)} %collective-permute-done.5.refs_3_.refs_13_), channel_id=1, source_target_pairs={{4,0},{5,1},{8,4},{9,5},{12,8},{13,9},{14,12},{15,13},{10,14},{11,... | collective-permute-start | bytes 786440 | tf_op jit(solution)/shard_map/ppermute | solution.py:637
  36.0 8.7 %collective-permute-start.10 = (bf16[256,512]{1,0:T(8,128)(2,1)S(1)}, bf16[256,512]{1,0:T(8,128)(2,1)S(1)}, u32[]{:S(2)}, u32[]{:S(2)}) collective-permute-start(bf16[256,512]{1,0:T(8,128)(2,1)S(1)} %collective-permute-done.6.refs_0_.refs_14_), channel_id=1, source_target_pairs={{0,4},{1,5},{4,8},{5,9},{8,12},{9,13},{12,14},{13,15},{14,10},{15,... | collective-permute-start | bytes 786440 | tf_op jit(solution)/shard_map/ppermute | solution.py:636
  37.5 9.7 %collective-permute-start.11 = (bf16[256,512]{1,0:T(8,128)(2,1)S(1)}, bf16[256,512]{1,0:T(8,128)(2,1)S(1)}, u32[]{:S(2)}, u32[]{:S(2)}) collective-permute-start(bf16[256,512]{1,0:T(8,128)(2,1)S(1)} %collective-permute-done.7.refs_1_.refs_15_), channel_id=1, source_target_pairs={{0,4},{1,5},{4,8},{5,9},{8,12},{9,13},{12,14},{13,15},{14,10},{15,... | collective-permute-start | bytes 786440 | tf_op jit(solution)/shard_map/ppermute | solution.py:636
  38.1 9.1 %collective-permute-start.12 = (bf16[256,512]{1,0:T(8,128)(2,1)S(1)}, bf16[256,512]{1,0:T(8,128)(2,1)S(1)}, u32[]{:S(2)}, u32[]{:S(2)}) collective-permute-start(bf16[256,512]{1,0:T(8,128)(2,1)S(1)} %collective-permute-done.8.refs_2_.refs_16_), channel_id=1, source_target_pairs={{4,0},{5,1},{8,4},{9,5},{12,8},{13,9},{14,12},{15,13},{10,14},{11,... | collective-permute-start | bytes 786440 | tf_op jit(solution)/shard_map/ppermute | solution.py:637
  39.5 10.5 %collective-permute-start.13 = (bf16[256,512]{1,0:T(8,128)(2,1)S(1)}, bf16[256,512]{1,0:T(8,128)(2,1)S(1)}, u32[]{:S(2)}, u32[]{:S(2)}) collective-permute-start(bf16[256,512]{1,0:T(8,128)(2,1)S(1)} %collective-permute-done.9.refs_3_.refs_17_), channel_id=1, source_target_pairs={{4,0},{5,1},{8,4},{9,5},{12,8},{13,9},{14,12},{15,13},{10,14},{11,... | collective-permute-start | bytes 786440 | tf_op jit(solution)/shard_map/ppermute | solution.py:637
  50.0 6.4 %collective-permute-start.14 = (bf16[256,512]{1,0:T(8,128)(2,1)S(1)}, bf16[256,512]{1,0:T(8,128)(2,1)S(1)}, u32[]{:S(2)}, u32[]{:S(2)}) collective-permute-start(bf16[256,512]{1,0:T(8,128)(2,1)S(1)} %collective-permute-done.10.refs_0_.refs_18_), channel_id=1, source_target_pairs={{0,4},{1,5},{4,8},{5,9},{8,12},{9,13},{12,14},{13,15},{14,10},{15,... | collective-permute-start | bytes 786440 | tf_op jit(solution)/shard_map/ppermute | solution.py:636
  50.0 6.4 %collective-permute-start.15 = (bf16[256,512]{1,0:T(8,128)(2,1)S(1)}, bf16[256,512]{1,0:T(8,128)(2,1)S(1)}, u32[]{:S(2)}, u32[]{:S(2)}) collective-permute-start(bf16[256,512]{1,0:T(8,128)(2,1)S(1)} %collective-permute-done.13.refs_3_.refs_21_), channel_id=1, source_target_pairs={{4,0},{5,1},{8,4},{9,5},{12,8},{13,9},{14,12},{15,13},{10,14},{11,... | collective-permute-start | bytes 786440 | tf_op jit(solution)/shard_map/ppermute | solution.py:637
  63.3 6.5 %collective-permute-start.19 = (bf16[16,4224]{1,0:T(8,128)(2,1)S(1)}, bf16[16,4224]{1,0:T(8,128)(2,1)S(1)}, u32[]{:S(2)}, u32[]{:S(2)}) collective-permute-start(bf16[16,4224]{1,0:T(8,128)(2,1)S(1)} %get-tuple-element.120.refs_0_), channel_id=1, source_target_pairs={{4,0},{5,1},{8,4},{9,5},{12,8},{13,9},{14,12},{15,13},{10,14},{11,... | collective-permute-start | bytes 405512 | tf_op jit(solution)/shard_map/ppermute | solution.py:637
  63.8 7.7 %collective-permute-start.20 = (bf16[16,4224]{1,0:T(8,128)(2,1)S(1)}, bf16[16,4224]{1,0:T(8,128)(2,1)S(1)}, u32[]{:S(2)}, u32[]{:S(2)}) collective-permute-start(bf16[16,4224]{1,0:T(8,128)(2,1)S(1)} %get-tuple-element.121.refs_8_), channel_id=1, source_target_pairs={{4,0},{5,1},{8,4},{9,5},{12,8},{13,9},{14,12},{15,13},{10,14},{11,... | collective-permute-start | bytes 405512 | tf_op jit(solution)/shard_map/ppermute | solution.py:637
  71.5 50.3 %collective-permute-start.25 = (bf16[128,4096]{1,0:T(8,128)(2,1)S(1)}, bf16[128,4096]{1,0:T(8,128)(2,1)S(1)}, u32[]{:S(2)}, u32[]{:S(2)}) collective-permute-start(bf16[128,4096]{1,0:T(8,128)(2,1)S(1)} %get-tuple-element.129), channel_id=1, source_target_pairs={{0,1},{1,0},{2,3},{3,2},{4,5},{5,4},{6,7},{7,6},{8,9},{9,8},{10,11... | collective-permute-start | bytes 3145736 | tf_op jit(solution)/shard_map/ppermute | solution.py:638
  71.5 44.1 %collective-permute-start.21 = (bf16[16,4224]{1,0:T(8,128)(2,1)S(1)}, bf16[16,4224]{1,0:T(8,128)(2,1)S(1)}, u32[]{:S(2)}, u32[]{:S(2)}) collective-permute-start(bf16[16,4224]{1,0:T(8,128)(2,1)S(1)} %collective-permute-done.17.refs_1_), channel_id=1, source_target_pairs={{0,4},{1,5},{4,8},{5,9},{8,12},{9,13},{12,14},{13,15},{14,10},{15,... | collective-permute-start | bytes 405512 | tf_op jit(solution)/shard_map/ppermute | solution.py:636
  111.8 6.4 %collective-permute-start.22 = (bf16[16,4224]{1,0:T(8,128)(2,1)S(1)}, bf16[16,4224]{1,0:T(8,128)(2,1)S(1)}, u32[]{:S(2)}, u32[]{:S(2)}) collective-permute-start(bf16[16,4224]{1,0:T(8,128)(2,1)S(1)} %collective-permute-done.18.refs_9_), channel_id=1, source_target_pairs={{0,4},{1,5},{4,8},{5,9},{8,12},{9,13},{12,14},{13,15},{14,10},{15,... | collective-permute-start | bytes 405512 | tf_op jit(solution)/shard_map/ppermute | solution.py:636
  113.5 6.5 %collective-permute-start.23 = (bf16[16,4224]{1,0:T(8,128)(2,1)S(1)}, bf16[16,4224]{1,0:T(8,128)(2,1)S(1)}, u32[]{:S(2)}, u32[]{:S(2)}) collective-permute-start(bf16[16,4224]{1,0:T(8,128)(2,1)S(1)} %collective-permute-done.19.refs_4_), channel_id=1, source_target_pairs={{4,0},{5,1},{8,4},{9,5},{12,8},{13,9},{14,12},{15,13},{10,14},{11,... | collective-permute-start | bytes 405512 | tf_op jit(solution)/shard_map/ppermute | solution.py:637
  113.8 8.1 %collective-permute-start.24 = (bf16[16,4224]{1,0:T(8,128)(2,1)S(1)}, bf16[16,4224]{1,0:T(8,128)(2,1)S(1)}, u32[]{:S(2)}, u32[]{:S(2)}) collective-permute-start(bf16[16,4224]{1,0:T(8,128)(2,1)S(1)} %collective-permute-done.20.refs_12_), channel_id=1, source_target_pairs={{4,0},{5,1},{8,4},{9,5},{12,8},{13,9},{14,12},{15,13},{10,14},{11,... | collective-permute-start | bytes 405512 | tf_op jit(solution)/shard_map/ppermute | solution.py:637
  121.9 6.0 %collective-permute-start.26 = (bf16[16,4224]{1,0:T(8,128)(2,1)S(1)}, bf16[16,4224]{1,0:T(8,128)(2,1)S(1)}, u32[]{:S(2)}, u32[]{:S(2)}) collective-permute-start(bf16[16,4224]{1,0:T(8,128)(2,1)S(1)} %collective-permute-done.21.refs_2_), channel_id=1, source_target_pairs={{0,4},{1,5},{4,8},{5,9},{8,12},{9,13},{12,14},{13,15},{14,10},{15,... | collective-permute-start | bytes 405512 | tf_op jit(solution)/shard_map/ppermute | solution.py:636
  122.2 7.1 %collective-permute-start.27 = (bf16[16,4224]{1,0:T(8,128)(2,1)S(1)}, bf16[16,4224]{1,0:T(8,128)(2,1)S(1)}, u32[]{:S(2)}, u32[]{:S(2)}) collective-permute-start(bf16[16,4224]{1,0:T(8,128)(2,1)S(1)} %collective-permute-done.22.refs_10_), channel_id=1, source_target_pairs={{0,4},{1,5},{4,8},{5,9},{8,12},{9,13},{12,14},{13,15},{14,10},{15,... | collective-permute-start | bytes 405512 | tf_op jit(solution)/shard_map/ppermute | solution.py:636
  122.6 6.8 %collective-permute-start.28 = (bf16[16,4224]{1,0:T(8,128)(2,1)S(1)}, bf16[16,4224]{1,0:T(8,128)(2,1)S(1)}, u32[]{:S(2)}, u32[]{:S(2)}) collective-permute-start(bf16[16,4224]{1,0:T(8,128)(2,1)S(1)} %collective-permute-done.23.refs_5_), channel_id=1, source_target_pairs={{4,0},{5,1},{8,4},{9,5},{12,8},{13,9},{14,12},{15,13},{10,14},{11,... | collective-permute-start | bytes 405512 | tf_op jit(solution)/shard_map/ppermute | solution.py:637
  135.6 13.3 %collective-permute-start.32 = (bf16[256,4224]{1,0:T(8,128)(2,1)S(1)}, bf16[256,4224]{1,0:T(8,128)(2,1)S(1)}, u32[]{:S(2)}, u32[]{:S(2)}) collective-permute-start(bf16[256,4224]{1,0:T(8,128)(2,1)S(1)} %gather.1.rows_ref.refs_0_), channel_id=1, source_target_pairs={{0,1},{1,0},{2,3},{3,2},{4,5},{5,4},{6,7},{7,6},{8,9},{9,8},{10,11... | collective-permute-start | bytes 6488072 | tf_op jit(solution)/shard_map/ppermute | solution.py:638
  164.8 6.3 %collective-permute-start.45 = (bf16[16,4096]{1,0:T(8,128)(2,1)S(1)}, bf16[16,4096]{1,0:T(8,128)(2,1)S(1)}, u32[]{:S(2)}, u32[]{:S(2)}) collective-permute-start(bf16[16,4096]{1,0:T(8,128)(2,1)S(1)} %pad_maximum_fusion.2), channel_id=1, source_target_pairs={{0,4},{1,5},{4,8},{5,9},{8,12},{9,13},{12,14},{13,15},{14,10},{15,... | collective-permute-start | bytes 393224 | tf_op jit(solution)/shard_map/ppermute | solution.py:636
  165.2 6.2 %collective-permute-start.46 = (bf16[16,4096]{1,0:T(8,128)(2,1)S(1)}, bf16[16,4096]{1,0:T(8,128)(2,1)S(1)}, u32[]{:S(2)}, u32[]{:S(2)}) collective-permute-start(bf16[16,4096]{1,0:T(8,128)(2,1)S(1)} %pad_maximum_fusion.3), channel_id=1, source_target_pairs={{4,0},{5,1},{8,4},{9,5},{12,8},{13,9},{14,12},{15,13},{10,14},{11,... | collective-permute-start | bytes 393224 | tf_op jit(solution)/shard_map/ppermute | solution.py:637
  168.2 6.2 %collective-permute-start.36 = (bf16[16,4096]{1,0:T(8,128)(2,1)S(1)}, bf16[16,4096]{1,0:T(8,128)(2,1)S(1)}, u32[]{:S(2)}, u32[]{:S(2)}) collective-permute-start(bf16[16,4096]{1,0:T(8,128)(2,1)S(1)} %pad_maximum_fusion), channel_id=1, source_target_pairs={{0,4},{1,5},{4,8},{5,9},{8,12},{9,13},{12,14},{13,15},{14,10},{15,... | collective-permute-start | bytes 393224 | tf_op jit(solution)/shard_map/ppermute | solution.py:636
  168.7 5.9 %collective-permute-start.37 = (bf16[16,4096]{1,0:T(8,128)(2,1)S(1)}, bf16[16,4096]{1,0:T(8,128)(2,1)S(1)}, u32[]{:S(2)}, u32[]{:S(2)}) collective-permute-start(bf16[16,4096]{1,0:T(8,128)(2,1)S(1)} %pad_maximum_fusion.1), channel_id=1, source_target_pairs={{4,0},{5,1},{8,4},{9,5},{12,8},{13,9},{14,12},{15,13},{10,14},{11,... | collective-permute-start | bytes 393224 | tf_op jit(solution)/shard_map/ppermute | solution.py:637
  171.5 5.8 %collective-permute-start.47 = (bf16[16,4096]{1,0:T(8,128)(2,1)S(1)}, bf16[16,4096]{1,0:T(8,128)(2,1)S(1)}, u32[]{:S(2)}, u32[]{:S(2)}) collective-permute-start(bf16[16,4096]{1,0:T(8,128)(2,1)S(1)} %get-tuple-element.164), channel_id=1, source_target_pairs={{0,4},{1,5},{4,8},{5,9},{8,12},{9,13},{12,14},{13,15},{14,10},{15,... | collective-permute-start | bytes 393224 | tf_op jit(solution)/shard_map/ppermute | solution.py:636
  174.7 5.9 %collective-permute-start.38 = (bf16[16,4096]{1,0:T(8,128)(2,1)S(1)}, bf16[16,4096]{1,0:T(8,128)(2,1)S(1)}, u32[]{:S(2)}, u32[]{:S(2)}) collective-permute-start(bf16[16,4096]{1,0:T(8,128)(2,1)S(1)} %get-tuple-element.153), channel_id=1, source_target_pairs={{0,4},{1,5},{4,8},{5,9},{8,12},{9,13},{12,14},{13,15},{14,10},{15,... | collective-permute-start | bytes 393224 | tf_op jit(solution)/shard_map/ppermute | solution.py:636
  (26 other events, 147.2 us)

commit v2 on v1

--- a/solution.py
+++ b/solution.py
@@ -17,7 +17,8 @@
 LOG_SCALE = math.log2(math.e) / math.sqrt(DH)
 MASKED = -1e30
 PIECES = 2
-ATTEND_MIB = 14
+ATTEND_MIB = 11
+SMALL = pl.CostEstimate(flops=1, bytes_accessed=1, transcendentals=0)
 SUM_LIMIT = 2.0**100
 PARTS = 3
 STACK = 4
@@ -259,8 +260,9 @@
 def last_kernel(chips, me_ref, q_ref, sib_q_ref, *refs):
     blocks, (shift_ref, acc_ref, total_ref, gain_ref) = refs[:2], refs[2:6]
     tables, sources = refs[6:8], refs[8 : 8 + 2 * chips]
-    out_refs, picked_refs = refs[8 + 2 * chips : 10 + 2 * chips], refs[10 + 2 * chips : 12 + 2 * chips]
-    rows_ref, worst_ref, sem, *scratch = refs[12 + 2 * chips :]
+    refs = refs[8 + 2 * chips :]
+    out_refs, picked_ref = refs[:2], refs[2]
+    rows_ref, worst_ref, sem, *scratch = refs[3:]
     q_refs = (q_ref, sib_q_ref)
     tokens, half_width = q_ref.shape
     me = me_ref[0]
@@ -289,16 +291,13 @@
         running_attention(chips, me, sources, q_refs, put, scratch, sem)
 
     columns = pl.ds(pl.multiple_of(me % 2 * half_width, half_width), half_width)
-    gain = gain_ref[:, columns]
-    for i, ref in enumerate(picked_refs):
-        rows = rows_ref[i * CAP : (i + 1) * CAP, :]
-        squares = jnp.broadcast_to(jnp.sum(rows * rows, axis=1, keepdims=True), (CAP, DH))
-        upper = squares.astype(jnp.bfloat16)
-        lower = (squares - upper.astype(jnp.float32)).astype(jnp.bfloat16)
-        lane = lax.broadcasted_iota(jnp.int32, (CAP, DH), 1)
-        both = jnp.where(lane < DH // 2, upper.astype(jnp.float32), lower.astype(jnp.float32))
-        ref[:, :half_width] = (rows * gain).astype(jnp.bfloat16)
-        ref[:, half_width:] = both.astype(jnp.bfloat16)
+    rows = rows_ref[...]
+    squares = jnp.broadcast_to(jnp.sum(rows * rows, axis=1, keepdims=True), (2 * CAP, DH))
+    upper = squares.astype(jnp.bfloat16).astype(jnp.float32)
+    lower = (squares - upper).astype(jnp.bfloat16).astype(jnp.float32)
+    lane = lax.broadcasted_iota(jnp.int32, squares.shape, 1)
+    picked_ref[:, :half_width] = (rows * gain_ref[:, columns]).astype(jnp.bfloat16)
+    picked_ref[:, half_width:] = jnp.where(lane < DH // 2, upper, lower).astype(jnp.bfloat16)
 
 
 class Attention:
@@ -320,11 +319,7 @@
             scratch_shapes=scratch,
             input_output_aliases=aliases or {},
             compiler_params=pltpu.CompilerParams(vmem_limit_bytes=ATTEND_MIB * MIB),
-            cost_estimate=pl.CostEstimate(
-                flops=4 * self.tokens * self.width * self.tokens,
-                bytes_accessed=4 * MIB,
-                transcendentals=0,
-            ),
+            cost_estimate=SMALL,
             name=name,
         )(self.me, *self.queries, *args, *others)
 
@@ -357,7 +352,7 @@
 
     def last(self, blocks, shift, state, gain, tables, sources):
         out = pltpu.VMEM((self.tokens, self.width), jnp.bfloat16)
-        picked = pltpu.VMEM((CAP, self.width + DH), jnp.bfloat16)
+        picked = pltpu.VMEM((2 * CAP, self.width + DH), jnp.bfloat16)
         kept = pltpu.VMEM((self.chips, 2 * self.tokens, DH), jnp.bfloat16)
         sums = pltpu.VMEM((self.rows, DH), jnp.float32)
         return self.call(
@@ -365,7 +360,7 @@
             "attend_last",
             (*blocks, shift, *state, gain, *tables),
             sources,
-            [out, out, picked, picked],
+            [out, out, picked],
             [],
             [
                 pltpu.VMEM((2 * CAP, self.width), jnp.float32),
@@ -380,16 +375,18 @@
         )
 
 
-def halves_kernel(me_ref, *refs):
-    count = len(refs) - 3
-    sources, (keep_ref, give_ref, sems) = refs[:count], refs[count:]
-    rows, width = sources[0].shape
+def halves_kernel(stacks, me_ref, *refs):
+    count = sum(stacks)
+    sources, outs, sems = list(refs[:count]), refs[count:-1], refs[-1]
     core = me_ref[0] % 2
     copies = []
-    for side, target in ((core, keep_ref), (1 - core, give_ref)):
-        columns = pl.ds(pl.multiple_of(side * (width // 2), width // 2), width // 2)
-        for i, source in enumerate(sources):
-            copies.append((source.at[:, columns], target.at[pl.ds(i * rows, rows)]))
+    for size, keep_ref, give_ref in zip(stacks, outs[::2], outs[1::2]):
+        for i in range(size):
+            source = sources.pop(0)
+            rows, width = source.shape
+            for side, target in ((core, keep_ref), (1 - core, give_ref)):
+                columns = pl.ds(pl.multiple_of(side * (width // 2), width // 2), width // 2)
+                copies.append((source.at[:, columns], target.at[pl.ds(i * rows, rows)]))
     copies = [pltpu.make_async_copy(*ends, sems.at[i]) for i, ends in enumerate(copies)]
     for copy in copies:
         copy.start()
@@ -397,17 +394,21 @@
         copy.wait()
 
 
-def halves(me, *arrays):
-    rows, width = arrays[0].shape
+def halves(me, *stacks):
     anywhere = pl.BlockSpec(memory_space=pl.ANY)
-    out = pltpu.VMEM((len(arrays) * rows, width // 2), arrays[0].dtype)
+    arrays = [x for stack in stacks for x in stack]
+    outs = []
+    for stack in stacks:
+        rows, width = stack[0].shape
+        outs += [pltpu.VMEM((len(stack) * rows, width // 2), stack[0].dtype)] * 2
     return pl.pallas_call(
-        halves_kernel,
+        functools.partial(halves_kernel, [len(stack) for stack in stacks]),
         in_specs=[pl.BlockSpec(memory_space=pltpu.SMEM)] + [anywhere] * len(arrays),
-        out_specs=[anywhere] * 2,
-        out_shape=[out, out],
+        out_specs=[anywhere] * len(outs),
+        out_shape=outs,
         scratch_shapes=[pltpu.SemaphoreType.DMA((2 * len(arrays),))],
         compiler_params=pltpu.CompilerParams(vmem_limit_bytes=MIB),
+        cost_estimate=SMALL,
         name="halves",
     )(me, *(in_hbm(x) for x in arrays))
 
@@ -435,13 +436,37 @@
         out_shape=jax.ShapeDtypeStruct((rows, 2 * width), keep.dtype),
         scratch_shapes=[pltpu.SemaphoreType.DMA((2,))],
         compiler_params=pltpu.CompilerParams(vmem_limit_bytes=MIB),
+        cost_estimate=SMALL,
         name="beside",
     )(me, keep, other)
 
 
+def load_kernel(source_ref, target_ref, sem):
+    copy = pltpu.make_async_copy(source_ref, target_ref, sem)
+    copy.start()
+    copy.wait()
+
+
+def load(x):
+    return pl.pallas_call(
+        load_kernel,
+        in_specs=[pl.BlockSpec(memory_space=pl.ANY)],
+        out_specs=pl.BlockSpec(memory_space=pl.ANY),
+        out_shape=pltpu.VMEM(x.shape, x.dtype),
+        scratch_shapes=[pltpu.SemaphoreType.DMA],
+        compiler_params=pltpu.CompilerParams(vmem_limit_bytes=MIB),
+        cost_estimate=SMALL,
+        name="load",
+    )(in_hbm(x))
+
+
 def gather_kernel(*refs):
-    for j, ref in enumerate(refs[:-1]):
-        refs[-1][j * CAP : (j + 1) * CAP] = ref[...]
+    blocks, out_ref = refs[:-1], refs[-1]
+    middle = out_ref.shape[0] // 2
+    parts = [(ref[:CAP], ref[CAP:]) for ref in blocks[:-2]] + [(blocks[-2][...], blocks[-1][...])]
+    for j, (mine, other) in enumerate(parts):
+        out_ref[j * CAP : (j + 1) * CAP] = mine
+        out_ref[middle + j * CAP : middle + (j + 1) * CAP] = other
 
 
 def gather(blocks):
@@ -450,8 +475,9 @@
         gather_kernel,
         in_specs=[vmem] * len(blocks),
         out_specs=vmem,
-        out_shape=pltpu.VMEM((CAP * len(blocks), blocks[0].shape[1]), jnp.bfloat16),
+        out_shape=pltpu.VMEM((2 * CAP * (len(blocks) - 1), blocks[0].shape[1]), jnp.bfloat16),
         compiler_params=pltpu.CompilerParams(vmem_limit_bytes=4 * MIB),
+        cost_estimate=SMALL,
         name="gather",
     )(*blocks)
 
@@ -508,7 +534,7 @@
         out_specs=[vmem] * len(outs) + [anywhere],
         out_shape=outs + [pltpu.VMEM((units, width // 2), w_down.dtype)],
         scratch_shapes=[sum_shape] * (2 if second else 0) + [pltpu.SemaphoreType.DMA],
-        compiler_params=pltpu.CompilerParams(vmem_limit_bytes=12 * MIB),
+        compiler_params=pltpu.CompilerParams(vmem_limit_bytes=8 * MIB),
         cost_estimate=pl.CostEstimate(
             flops=4 * count * half * units,
             bytes_accessed=4 * half * units + 2 * count * half,
@@ -542,7 +568,7 @@
         in_specs=[vmem] * 2,
         out_specs=[vmem] * 2,
         out_shape=[pltpu.VMEM((rows // 2, width), jnp.bfloat16)] * 2,
-        compiler_params=pltpu.CompilerParams(vmem_limit_bytes=16 * MIB),
+        compiler_params=pltpu.CompilerParams(vmem_limit_bytes=8 * MIB),
         cost_estimate=pl.CostEstimate(
             flops=2 * rows * width * units,
             bytes_accessed=2 * width * units + 2 * rows * width,
@@ -656,53 +682,50 @@
     weighted = jnp.concatenate(weights, axis=0).astype(jnp.bfloat16)
     table = table.astype(jnp.bfloat16)
 
-    own, give = halves(me, keys, values)
-    sib = swap(give)
-    from_left, from_right = [go_right(own)], [go_left(own)]
-    q_own, q_give = halves(me, queries)
-    from_left.append(go_right(sib))
-    from_right.append(go_left(sib))
-    q_sib = swap(q_give)
+    own, give, q_own, q_give = halves(me, (keys, values), (queries,))
+    across_right, across_left = [
+        lax.ppermute(give, "ctx", [(i, j ^ 1) for i, j in pairs]) for pairs in (right, left)
+    ]
+    chains = [(go_right(own), go_left(own)), (across_right, across_left)]
+    sib, q_sib = swap(give), swap(q_give)
     sib_table = swap(table)
     attention = Attention(me, (q_own, q_sib), chips)
-    state, shift, (w_gate,) = attention.own(own, sib, (w_gate,))
+    state, shift, _ = attention.own(own, sib)
     sources = [own, sib]
     for step in range(1, half):
-        from_left, from_right, state = lax.optimization_barrier((from_left, from_right, state))
-        blocks, places = from_left + from_right, [step, step, -step, -step]
+        *chains[0], state = lax.optimization_barrier((*chains[0], state))
+        chains[1], _, state = lax.optimization_barrier((chains[1], chains[0], state))
+        blocks = [chain[side] for side in range(2) for chain in chains]
         sources += blocks
         if step < half - 1:
-            from_left, from_right = [go_right(x) for x in from_left], [go_left(x) for x in from_right]
+            chains = [(go_right(chain[0]), go_left(chain[1])) for chain in chains]
         else:
-            opposite = [go_right(from_left[0]), go_left(from_right[1])]
-        if step == 2:
-            state, (w_up,) = attention.step(blocks, places, shift, state, (w_up,))
-        else:
-            state, _ = attention.step(blocks, places, shift, state)
+            opposite = [go_right(chains[0][0]), go_left(chains[1][1])]
+        state, _ = attention.step(blocks, [step, step, -step, -step], shift, state)
     opposite, state = lax.optimization_barrier((opposite, state))
     sources += opposite
-    mine, theirs, *picked = attention.last(
+    mine, theirs, picked = attention.last(
         opposite, shift, state, norm_gain[None, :], (table, sib_table), sources
     )
 
-    from_left, from_right = list(picked), list(picked)
-    blocks_right, blocks_left = [picked], []
-    result = None
+    picked, w_gate = lax.optimization_barrier((picked, w_gate))
+    from_left, from_right, blocks_right, blocks_left = picked, picked, [picked], []
     for step in range(1, half):
-        from_left, from_right = [go_right(x) for x in from_left], [go_left(x) for x in from_right]
-        from_left, from_right, mine, theirs = lax.optimization_barrier(
-            (from_left, from_right, mine, theirs)
+        from_left, from_right = go_right(from_left), go_left(from_right)
+        if step == 1:
+            w_gate = load(w_gate)
+        elif step == 2:
+            w_up = load(w_up)
+            theirs = swap(theirs)
+        from_left, from_right, w_gate, w_up, theirs = lax.optimization_barrier(
+            (from_left, from_right, w_gate, w_up, theirs)
         )
-        if step == 1:
-            theirs = swap(theirs)
-        elif step == 2:
-            theirs = beside(me, mine, theirs)
         blocks_right.append(from_left)
         blocks_left.append(from_right)
-    result = theirs
-    far = [go_right(from_left[0]), go_left(from_right[1])]
-    blocks = blocks_right + blocks_left + [far]
-    rows = gather([own for own, _ in blocks] + [sib for _, sib in blocks])
+    far = [go_right(from_left[:CAP]), go_left(from_right[CAP:])]
+    result = beside(me, mine, theirs)
+    far, result = lax.optimization_barrier((far, result))
+    rows = gather(blocks_right + blocks_left + far)
     *first, down_low = hidden_call(me, rows, w_gate, w_up, w_down)
     hidden, down_high = hidden_call(me, swap(rows), w_gate, w_up, w_down, rows, first)
     downs = [down_low, down_high]

time: 189 us -> 177 us (0.937)
  starting transfers between devices: 85.8 us -> 44.1 us
  waiting for transfers between devices: 52.9 us -> 94.2 us
  local copies, waits for them, and re-layouts: 13.8 us -> 0.09 us
  Pallas kernels: 34 us -> 37 us
    ppermute x22 -> x18, waiting for transfers between devices: 18.5 us -> 63.5 us  [per_device(): go_left = lambda x: lax.ppermute(x, 'ctx', left)]
    ppermute x22 -> x18, starting transfers between devices: 60.7 us -> 30.6 us  [per_device(): go_right = lambda x: lax.ppermute(x, 'ctx', right)]
    ppermute x22 -> x18, starting transfers between devices: 23.7 us -> 9.63 us  [per_device(): go_left = lambda x: lax.ppermute(x, 'ctx', left)]
    unnamed x14 -> x6, local copies, waits for them, and re-layouts: 13.7 us -> 0.01 us
    pallas_call x2 -> x3, Pallas kernels: 2.69 us -> 11 us  [the longest x2 9.17 us: load(): pl.pallas_call(load_kernel, in_specs=[pl.BlockSpec(memory_space=pl.ANY)],...]
    pallas_call x5, Pallas kernels: 13.6 us -> 8.29 us  [call(): pl.pallas_call(kernel, in_specs=[pl.BlockSpec(memory_space=pltpu.SMEM)] +...]
    ppermute x22 -> x18, waiting for transfers between devices: 34 us -> 29 us  [per_device(): go_right = lambda x: lax.ppermute(x, 'ctx', right)]
    ppermute x0 -> x2, starting transfers between devices: none -> 2.2 us  [per_device(): lax.ppermute(give, 'ctx', [(i, j ^ 1) for i, j in pairs])]
  transfers between devices with their start and end apart: 51 -> 45, of which waited for: 34 -> 35; matrix products, arithmetic and copies ran while one was open for 0% -> 1% of each run, Pallas kernels for 10% -> 13%
where the time goes in v2:
time: 177 us
  waiting for transfers between devices  94.2 us (53%)
  starting transfers between devices  44.1 us (25%)
  Pallas kernels  37 us (21%)
    ppermute x18, waiting for transfers between devices, per_device(): go_left = lambda x: lax.ppermute(x, 'ctx', left)  63.5 us
    ppermute x18, starting transfers between devices, per_device(): go_right = lambda x: lax.ppermute(x, 'ctx', right)  30.6 us
    ppermute x18, waiting for transfers between devices, per_device(): go_right = lambda x: lax.ppermute(x, 'ctx', right)  29 us
    ppermute x18, starting transfers between devices, per_device(): go_left = lambda x: lax.ppermute(x, 'ctx', left)  9.63 us
    pallas_call x2, Pallas kernels, load(): pl.pallas_call(load_kernel, in_specs=[pl.BlockSpec(memory_space=pl.ANY)],...  9.17 us
    pallas_call x2, Pallas kernels, hidden_call(): pl.pallas_call(functools.partial(hidden_kernel, second), in_specs=[pl.Blo...  8.58 us
    pallas_call x5, Pallas kernels, call(): pl.pallas_call(kernel, in_specs=[pl.BlockSpec(memory_space=pltpu.SMEM)] +...  8.29 us
    pallas_call x2, Pallas kernels, down_call(): pl.pallas_call(down_kernel, in_specs=[vmem] * 2, out_specs=[vmem] * 2, ou...  4.6 us
  transfers between devices with their start and end apart: 45, of which 35 were waited for; matrix products, arithmetic and copies ran while one was open for 1% of the time, Pallas kernels for 13%

profile of v2, /device:TPU:0, one launch (start us, length us, event | category | flops | bytes accessed | tf_op | source)
XLA Modules:
  0.0 177.1 jit_solution(17769482816320135247)
XLA Ops:
  0.6 1.9 %halves.1 = (bf16[256,512]{1,0:T(8,128)(2,1)S(1)}, bf16[256,512]{1,0:T(8,128)(2,1)S(1)}, bf16[128,4096]{1,0:T(8,128)(2,1)S(1)}, bf16[128,4096]{1,0:T(8,128)(2,1)S(1)}) custom-call(s32[1]{0:T(128)} %bitcast.me_ref, bf16[128,1024]{1,0:T(8,128)(2,1)} %refs_0_.2, bf16[128,1024]{1,0:T(8,128)(2,1)} %refs_1_.1, bf16[128,8192]{1,0:T(8,128)(2,1)} %refs_2_.1), custom_call_target="tpu_custom_call" | custom-call | flops 1 | bytes 1 | tf_op jit(solution)/shard_map/halves/pallas_call | solution.py:404
  3.1 3.0 %collective-permute-start.1 = (bf16[256,512]{1,0:T(8,128)(2,1)S(1)}, bf16[256,512]{1,0:T(8,128)(2,1)S(1)}, u32[]{:S(2)}, u32[]{:S(2)}) collective-permute-start(bf16[256,512]{1,0:T(8,128)(2,1)S(1)} %get-tuple-element.93.own_ref.refs_8_), channel_id=1, source_target_pairs={{0,4},{1,5},{4,8},{5,9},{8,12},{9,13},{12,14},{13,15},{14,10},{15,... | collective-permute-start | bytes 786440 | tf_op jit(solution)/shard_map/ppermute | solution.py:662
  8.3 3.8 %attend_own.1 = (f32[4,2048,128]{2,1,0:T(8,128)S(1)}, f32[4,2048,128]{2,1,0:T(8,128)S(1)}, f32[4,2048,128]{2,1,0:T(8,128)S(1)}) custom-call(s32[1]{0:T(128)} %bitcast.me_ref, bf16[128,4096]{1,0:T(8,128)(2,1)S(1)} %get-tuple-element.91.q_ref, bf16[128,4096]{1,0:T(8,128)(2,1)S(1)} %collective-permute-done.sib_q_ref, ...), custom_call_target="tpu_custom_call" | custom-call | flops 1 | bytes 1 | tf_op jit(solution)/shard_map/attend_own/pallas_call | solution.py:312
  13.2 2.2 %collective-permute-done.2.refs_2_.refs_12_ = bf16[256,512]{1,0:T(8,128)(2,1)S(1)} collective-permute-done((bf16[256,512]{1,0:T(8,128)(2,1)S(1)}, bf16[256,512]{1,0:T(8,128)(2,1)S(1)}, u32[]{:S(2)}, u32[]{:S(2)}) %collective-permute-start.2) | collective-permute-done | bytes 262176 | tf_op jit(solution)/shard_map/ppermute | solution.py:663
  18.5 1.9 %collective-permute-start.10 = (bf16[256,512]{1,0:T(8,128)(2,1)S(1)}, bf16[256,512]{1,0:T(8,128)(2,1)S(1)}, u32[]{:S(2)}, u32[]{:S(2)}) collective-permute-start(bf16[256,512]{1,0:T(8,128)(2,1)S(1)} %collective-permute-done.6.refs_1_.refs_11_), channel_id=1, source_target_pairs={{0,4},{1,5},{4,8},{5,9},{8,12},{9,13},{12,14},{13,15},{14,10},{15,... | collective-permute-start | bytes 786440 | tf_op jit(solution)/shard_map/ppermute | solution.py:662
  20.6 3.4 %collective-permute-done.4.refs_0_.refs_14_ = bf16[256,512]{1,0:T(8,128)(2,1)S(1)} collective-permute-done((bf16[256,512]{1,0:T(8,128)(2,1)S(1)}, bf16[256,512]{1,0:T(8,128)(2,1)S(1)}, u32[]{:S(2)}, u32[]{:S(2)}) %collective-permute-start.4) | collective-permute-done | bytes 262176 | tf_op jit(solution)/shard_map/ppermute | solution.py:662
  24.0 1.7 collective-permute-done.5.refs_2_.refs_16_
  25.7 2.4 %collective-permute-start.8 = (bf16[256,512]{1,0:T(8,128)(2,1)S(1)}, bf16[256,512]{1,0:T(8,128)(2,1)S(1)}, u32[]{:S(2)}, u32[]{:S(2)}) collective-permute-start(bf16[256,512]{1,0:T(8,128)(2,1)S(1)} %collective-permute-done.4.refs_0_.refs_14_), channel_id=1, source_target_pairs={{0,4},{1,5},{4,8},{5,9},{8,12},{9,13},{12,14},{13,15},{14,10},{15,... | collective-permute-start | bytes 786440 | tf_op jit(solution)/shard_map/ppermute | solution.py:662
  33.1 2.1 %collective-permute-done.8.refs_0_.refs_18_ = bf16[256,512]{1,0:T(8,128)(2,1)S(1)} collective-permute-done((bf16[256,512]{1,0:T(8,128)(2,1)S(1)}, bf16[256,512]{1,0:T(8,128)(2,1)S(1)}, u32[]{:S(2)}, u32[]{:S(2)}) %collective-permute-start.8) | collective-permute-done | bytes 262176 | tf_op jit(solution)/shard_map/ppermute | solution.py:662
  36.9 3.3 %collective-permute-start.12 = (bf16[256,512]{1,0:T(8,128)(2,1)S(1)}, bf16[256,512]{1,0:T(8,128)(2,1)S(1)}, u32[]{:S(2)}, u32[]{:S(2)}) collective-permute-start(bf16[256,512]{1,0:T(8,128)(2,1)S(1)} %collective-permute-done.8.refs_0_.refs_18_), channel_id=1, source_target_pairs={{0,4},{1,5},{4,8},{5,9},{8,12},{9,13},{12,14},{13,15},{14,10},{15,... | collective-permute-start | bytes 786440 | tf_op jit(solution)/shard_map/ppermute | solution.py:662
  43.2 3.1 %collective-permute-done.12.refs_0_.refs_22_ = bf16[256,512]{1,0:T(8,128)(2,1)S(1)} collective-permute-done((bf16[256,512]{1,0:T(8,128)(2,1)S(1)}, bf16[256,512]{1,0:T(8,128)(2,1)S(1)}, u32[]{:S(2)}, u32[]{:S(2)}) %collective-permute-start.12) | collective-permute-done | bytes 262176 | tf_op jit(solution)/shard_map/ppermute | solution.py:662
  46.3 4.9 %collective-permute-done.15.refs_1_.refs_23_ = bf16[256,512]{1,0:T(8,128)(2,1)S(1)} collective-permute-done((bf16[256,512]{1,0:T(8,128)(2,1)S(1)}, bf16[256,512]{1,0:T(8,128)(2,1)S(1)}, u32[]{:S(2)}, u32[]{:S(2)}) %collective-permute-start.15) | collective-permute-done | bytes 262176 | tf_op jit(solution)/shard_map/ppermute | solution.py:663
  51.2 4.4 %attend_last.1 = (bf16[128,4096]{1,0:T(8,128)(2,1)S(1)}, bf16[128,4096]{1,0:T(8,128)(2,1)S(1)}, bf16[32,4224]{1,0:T(8,128)(2,1)S(1)}) custom-call(s32[1]{0:T(128)} %bitcast.me_ref, bf16[128,4096]{1,0:T(8,128)(2,1)S(1)} %get-tuple-element.91.q_ref, bf16[128,4096]{1,0:T(8,128)(2,1)S(1)} %collective-permute-done.sib_q_ref, ...), custom_call_target="tpu_custom_call" | custom-call | flops 1 | bytes 1 | tf_op jit(solution)/shard_map/attend_last/pallas_call | solution.py:312
  57.7 4.6 %load.2.gate_ref = bf16[8192,768]{1,0:T(8,128)(2,1)S(1)} custom-call(bf16[8192,768]{1,0:T(8,128)(2,1)} %source_ref), custom_call_target="tpu_custom_call" | custom-call | flops 1 | bytes 1 | tf_op jit(solution)/shard_map/load/pallas_call | solution.py:451
  67.1 4.6 %load.3.up_ref = bf16[8192,768]{1,0:T(8,128)(2,1)S(1)} custom-call(bf16[8192,768]{1,0:T(8,128)(2,1)} %source_ref.1), custom_call_target="tpu_custom_call" | custom-call | flops 1 | bytes 1 | tf_op jit(solution)/shard_map/load/pallas_call | solution.py:451
  71.7 2.3 %collective-permute-done.19.refs_2_ = bf16[32,4224]{1,0:T(8,128)(2,1)S(1)} collective-permute-done((bf16[32,4224]{1,0:T(8,128)(2,1)S(1)}, bf16[32,4224]{1,0:T(8,128)(2,1)S(1)}, u32[]{:S(2)}, u32[]{:S(2)}) %collective-permute-start.19) | collective-permute-done | bytes 270368 | tf_op jit(solution)/shard_map/ppermute | solution.py:662
  73.9 40.2 %collective-permute-done.20.refs_5_ = bf16[32,4224]{1,0:T(8,128)(2,1)S(1)} collective-permute-done((bf16[32,4224]{1,0:T(8,128)(2,1)S(1)}, bf16[32,4224]{1,0:T(8,128)(2,1)S(1)}, u32[]{:S(2)}, u32[]{:S(2)}) %collective-permute-start.20) | collective-permute-done | bytes 270368 | tf_op jit(solution)/shard_map/ppermute | solution.py:663
  114.1 1.7 collective-permute-start.22
  116.2 6.1 %collective-permute-done.22.refs_3_ = bf16[32,4224]{1,0:T(8,128)(2,1)S(1)} collective-permute-done((bf16[32,4224]{1,0:T(8,128)(2,1)S(1)}, bf16[32,4224]{1,0:T(8,128)(2,1)S(1)}, u32[]{:S(2)}, u32[]{:S(2)}) %collective-permute-start.22) | collective-permute-done | bytes 270368 | tf_op jit(solution)/shard_map/ppermute | solution.py:662
  123.4 1.8 %collective-permute-start.24 = (bf16[16,4224]{1,0:T(8,128)(2,1)S(1)}, bf16[16,4224]{1,0:T(8,128)(2,1)S(1)}, u32[]{:S(2)}, u32[]{:S(2)}) collective-permute-start(bf16[16,4224]{1,0:T(8,128)(2,1)S(1)} %slice.130), channel_id=1, source_target_pairs={{0,4},{1,5},{4,8},{5,9},{8,12},{9,13},{12,14},{13,15},{14,10},{15,... | collective-permute-start | bytes 405512 | tf_op jit(solution)/shard_map/ppermute | solution.py:662
  128.5 2.0 %collective-permute-done.25.refs_8_ = bf16[16,4224]{1,0:T(8,128)(2,1)S(1)} collective-permute-done((bf16[16,4224]{1,0:T(8,128)(2,1)S(1)}, bf16[16,4224]{1,0:T(8,128)(2,1)S(1)}, u32[]{:S(2)}, u32[]{:S(2)}) %collective-permute-start.25) | collective-permute-done | bytes 135200 | tf_op jit(solution)/shard_map/ppermute | solution.py:663
  130.7 4.0 %hidden.2 = (f32[256,768]{1,0:T(8,128)S(1)}, f32[256,768]{1,0:T(8,128)S(1)}, bf16[768,4096]{1,0:T(8,128)(2,1)S(1)}) custom-call(s32[1]{0:T(128)} %bitcast.me_ref, bf16[256,4224]{1,0:T(8,128)(2,1)S(1)} %gather.1.rows_ref.refs_0_, bf16[8192,768]{1,0:T(8,128)(2,1)S(1)} %load.2.gate_ref, bf16[8192,768]{1,0:T(8,128)(2,1)S(1)} %load.3.up_ref, ...), custom_call_target="tpu_custom_call" | custom-call | flops 3221225472 | bytes 14680064 | tf_op jit(solution)/shard_map/hidden/pallas_call | solution.py:531
  134.9 4.5 %hidden.3 = (bf16[256,768]{1,0:T(8,128)(2,1)S(1)}, bf16[768,4096]{1,0:T(8,128)(2,1)S(1)}) custom-call(s32[1]{0:T(128)} %bitcast.me_ref, bf16[256,4224]{1,0:T(8,128)(2,1)S(1)} %collective-permute-done.26.rows_ref, bf16[8192,768]{1,0:T(8,128)(2,1)S(1)} %load.2.gate_ref, bf16[8192,768]{1,0:T(8,128)(2,1)S(1)} %load.3.up_ref, ...), custom_call_target="tpu_custom_call" | custom-call | flops 3221225472 | bytes 14680064 | tf_op jit(solution)/shard_map/hidden/pallas_call | solution.py:531
  139.5 2.3 %down.2 = (bf16[128,4096]{1,0:T(8,128)(2,1)S(1)}, bf16[128,4096]{1,0:T(8,128)(2,1)S(1)}) custom-call(bf16[256,768]{1,0:T(8,128)(2,1)S(1)} %get-tuple-element.157.hidden_ref, bf16[768,4096]{1,0:T(8,128)(2,1)S(1)} %get-tuple-element.158.down_ref), custom_call_target="tpu_custom_call" | custom-call | flops 1610612736 | bytes 8388608 | tf_op jit(solution)/shard_map/down/pallas_call | solution.py:566
  142.2 2.3 %down.3 = (bf16[128,4096]{1,0:T(8,128)(2,1)S(1)}, bf16[128,4096]{1,0:T(8,128)(2,1)S(1)}) custom-call(bf16[256,768]{1,0:T(8,128)(2,1)S(1)} %get-tuple-element.157.hidden_ref, bf16[768,4096]{1,0:T(8,128)(2,1)S(1)} %get-tuple-element.169.down_ref), custom_call_target="tpu_custom_call" | custom-call | flops 1610612736 | bytes 8388608 | tf_op jit(solution)/shard_map/down/pallas_call | solution.py:566
  152.8 1.7 collective-permute-start.40
  158.0 1.8 %collective-permute-start.32 = (bf16[16,4096]{1,0:T(8,128)(2,1)S(1)}, bf16[16,4096]{1,0:T(8,128)(2,1)S(1)}, u32[]{:S(2)}, u32[]{:S(2)}) collective-permute-start(bf16[16,4096]{1,0:T(8,128)(2,1)S(1)} %get-tuple-element.165), channel_id=1, source_target_pairs={{0,4},{1,5},{4,8},{5,9},{8,12},{9,13},{12,14},{13,15},{14,10},{15,... | collective-permute-start | bytes 393224 | tf_op jit(solution)/shard_map/ppermute | solution.py:662
  160.9 1.7 collective-permute-start.41
  164.0 2.3 %collective-permute-start.34 = (bf16[16,4096]{1,0:T(8,128)(2,1)S(1)}, bf16[16,4096]{1,0:T(8,128)(2,1)S(1)}, u32[]{:S(2)}, u32[]{:S(2)}) collective-permute-start(bf16[16,4096]{1,0:T(8,128)(2,1)S(1)} %get-tuple-element.167), channel_id=1, source_target_pairs={{0,4},{1,5},{4,8},{5,9},{8,12},{9,13},{12,14},{13,15},{14,10},{15,... | collective-permute-start | bytes 393224 | tf_op jit(solution)/shard_map/ppermute | solution.py:662
  167.1 2.0 %collective-permute-start.43 = (bf16[16,4096]{1,0:T(8,128)(2,1)S(1)}, bf16[16,4096]{1,0:T(8,128)(2,1)S(1)}, u32[]{:S(2)}, u32[]{:S(2)}) collective-permute-start(bf16[16,4096]{1,0:T(8,128)(2,1)S(1)} %get-tuple-element.178), channel_id=1, source_target_pairs={{0,4},{1,5},{4,8},{5,9},{8,12},{9,13},{12,14},{13,15},{14,10},{15,... | collective-permute-start | bytes 393224 | tf_op jit(solution)/shard_map/ppermute | solution.py:662
  169.2 2.9 %collective-permute-done.43.c_ref = bf16[16,4096]{1,0:T(8,128)(2,1)S(1)} collective-permute-done((bf16[16,4096]{1,0:T(8,128)(2,1)S(1)}, bf16[16,4096]{1,0:T(8,128)(2,1)S(1)}, u32[]{:S(2)}, u32[]{:S(2)}) %collective-permute-start.43) | collective-permute-done | bytes 131104 | tf_op jit(solution)/shard_map/ppermute | solution.py:662
  172.1 2.0 %collective-permute-done.44.d_ref = bf16[16,4096]{1,0:T(8,128)(2,1)S(1)} collective-permute-done((bf16[16,4096]{1,0:T(8,128)(2,1)S(1)}, bf16[16,4096]{1,0:T(8,128)(2,1)S(1)}, u32[]{:S(2)}, u32[]{:S(2)}) %collective-permute-start.44) | collective-permute-done | bytes 131104 | tf_op jit(solution)/shard_map/ppermute | solution.py:663
  (110 shorter events, 47.2 us)
Async XLA Ops:
  2.5 5.8 %collective-permute-start = (bf16[128,4096]{1,0:T(8,128)(2,1)S(1)}, bf16[128,4096]{1,0:T(8,128)(2,1)S(1)}, u32[]{:S(2)}, u32[]{:S(2)}) collective-permute-start(bf16[128,4096]{1,0:T(8,128)(2,1)S(1)} %get-tuple-element.92), channel_id=1, source_target_pairs={{0,1},{1,0},{2,3},{3,2},{4,5},{5,4},{6,7},{7,6},{8,9},{9,8},{10,11... | collective-permute-start | bytes 3145736 | tf_op jit(solution)/shard_map/ppermute | solution.py:664
  3.1 10.0 %collective-permute-start.1 = (bf16[256,512]{1,0:T(8,128)(2,1)S(1)}, bf16[256,512]{1,0:T(8,128)(2,1)S(1)}, u32[]{:S(2)}, u32[]{:S(2)}) collective-permute-start(bf16[256,512]{1,0:T(8,128)(2,1)S(1)} %get-tuple-element.93.own_ref.refs_8_), channel_id=1, source_target_pairs={{0,4},{1,5},{4,8},{5,9},{8,12},{9,13},{12,14},{13,15},{14,10},{15,... | collective-permute-start | bytes 786440 | tf_op jit(solution)/shard_map/ppermute | solution.py:662
  6.1 9.2 %collective-permute-start.2 = (bf16[256,512]{1,0:T(8,128)(2,1)S(1)}, bf16[256,512]{1,0:T(8,128)(2,1)S(1)}, u32[]{:S(2)}, u32[]{:S(2)}) collective-permute-start(bf16[256,512]{1,0:T(8,128)(2,1)S(1)} %get-tuple-element.93.own_ref.refs_8_), channel_id=1, source_target_pairs={{4,0},{5,1},{8,4},{9,5},{12,8},{13,9},{14,12},{15,13},{10,14},{11,... | collective-permute-start | bytes 786440 | tf_op jit(solution)/shard_map/ppermute | solution.py:663
  6.1 12.3 %collective-permute-start.6 = (bf16[256,512]{1,0:T(8,128)(2,1)S(1)}, bf16[256,512]{1,0:T(8,128)(2,1)S(1)}, u32[]{:S(2)}, u32[]{:S(2)}) collective-permute-start(bf16[256,512]{1,0:T(8,128)(2,1)S(1)} %get-tuple-element.94), channel_id=1, source_target_pairs={{0,5},{1,4},{4,9},{5,8},{8,13},{9,12},{12,15},{13,14},{14,11},{15,... | collective-permute-start | bytes 786440 | tf_op jit(solution)/shard_map/ppermute | solution.py:687
  7.3 11.3 %collective-permute-start.7 = (bf16[256,512]{1,0:T(8,128)(2,1)S(1)}, bf16[256,512]{1,0:T(8,128)(2,1)S(1)}, u32[]{:S(2)}, u32[]{:S(2)}) collective-permute-start(bf16[256,512]{1,0:T(8,128)(2,1)S(1)} %get-tuple-element.94), channel_id=1, source_target_pairs={{4,1},{5,0},{8,5},{9,4},{12,9},{13,8},{14,13},{15,12},{10,15},{11,... | collective-permute-start | bytes 786440 | tf_op jit(solution)/shard_map/ppermute | solution.py:687
  15.3 8.7 %collective-permute-start.4 = (bf16[256,512]{1,0:T(8,128)(2,1)S(1)}, bf16[256,512]{1,0:T(8,128)(2,1)S(1)}, u32[]{:S(2)}, u32[]{:S(2)}) collective-permute-start(bf16[256,512]{1,0:T(8,128)(2,1)S(1)} %collective-permute-done.1.refs_0_.refs_10_), channel_id=1, source_target_pairs={{0,4},{1,5},{4,8},{5,9},{8,12},{9,13},{12,14},{13,15},{14,10},{15,... | collective-permute-start | bytes 786440 | tf_op jit(solution)/shard_map/ppermute | solution.py:662
  16.9 8.8 %collective-permute-start.5 = (bf16[256,512]{1,0:T(8,128)(2,1)S(1)}, bf16[256,512]{1,0:T(8,128)(2,1)S(1)}, u32[]{:S(2)}, u32[]{:S(2)}) collective-permute-start(bf16[256,512]{1,0:T(8,128)(2,1)S(1)} %collective-permute-done.2.refs_2_.refs_12_), channel_id=1, source_target_pairs={{4,0},{5,1},{8,4},{9,5},{12,8},{13,9},{14,12},{15,13},{10,14},{11,... | collective-permute-start | bytes 786440 | tf_op jit(solution)/shard_map/ppermute | solution.py:663
  18.5 11.0 %collective-permute-start.10 = (bf16[256,512]{1,0:T(8,128)(2,1)S(1)}, bf16[256,512]{1,0:T(8,128)(2,1)S(1)}, u32[]{:S(2)}, u32[]{:S(2)}) collective-permute-start(bf16[256,512]{1,0:T(8,128)(2,1)S(1)} %collective-permute-done.6.refs_1_.refs_11_), channel_id=1, source_target_pairs={{0,4},{1,5},{4,8},{5,9},{8,12},{9,13},{12,14},{13,15},{14,10},{15,... | collective-permute-start | bytes 786440 | tf_op jit(solution)/shard_map/ppermute | solution.py:662
  20.5 10.5 %collective-permute-start.11 = (bf16[256,512]{1,0:T(8,128)(2,1)S(1)}, bf16[256,512]{1,0:T(8,128)(2,1)S(1)}, u32[]{:S(2)}, u32[]{:S(2)}) collective-permute-start(bf16[256,512]{1,0:T(8,128)(2,1)S(1)} %collective-permute-done.7.refs_3_.refs_13_), channel_id=1, source_target_pairs={{4,0},{5,1},{8,4},{9,5},{12,8},{13,9},{14,12},{15,13},{10,14},{11,... | collective-permute-start | bytes 786440 | tf_op jit(solution)/shard_map/ppermute | solution.py:663
  25.7 9.5 %collective-permute-start.8 = (bf16[256,512]{1,0:T(8,128)(2,1)S(1)}, bf16[256,512]{1,0:T(8,128)(2,1)S(1)}, u32[]{:S(2)}, u32[]{:S(2)}) collective-permute-start(bf16[256,512]{1,0:T(8,128)(2,1)S(1)} %collective-permute-done.4.refs_0_.refs_14_), channel_id=1, source_target_pairs={{0,4},{1,5},{4,8},{5,9},{8,12},{9,13},{12,14},{13,15},{14,10},{15,... | collective-permute-start | bytes 786440 | tf_op jit(solution)/shard_map/ppermute | solution.py:662
  28.1 8.8 %collective-permute-start.9 = (bf16[256,512]{1,0:T(8,128)(2,1)S(1)}, bf16[256,512]{1,0:T(8,128)(2,1)S(1)}, u32[]{:S(2)}, u32[]{:S(2)}) collective-permute-start(bf16[256,512]{1,0:T(8,128)(2,1)S(1)} %collective-permute-done.5.refs_2_.refs_16_), channel_id=1, source_target_pairs={{4,0},{5,1},{8,4},{9,5},{12,8},{13,9},{14,12},{15,13},{10,14},{11,... | collective-permute-start | bytes 786440 | tf_op jit(solution)/shard_map/ppermute | solution.py:663
  31.0 9.8 %collective-permute-start.13 = (bf16[256,512]{1,0:T(8,128)(2,1)S(1)}, bf16[256,512]{1,0:T(8,128)(2,1)S(1)}, u32[]{:S(2)}, u32[]{:S(2)}) collective-permute-start(bf16[256,512]{1,0:T(8,128)(2,1)S(1)} %collective-permute-done.10.refs_1_.refs_15_), channel_id=1, source_target_pairs={{0,4},{1,5},{4,8},{5,9},{8,12},{9,13},{12,14},{13,15},{14,10},{15,... | collective-permute-start | bytes 786440 | tf_op jit(solution)/shard_map/ppermute | solution.py:662
  32.6 10.0 %collective-permute-start.14 = (bf16[256,512]{1,0:T(8,128)(2,1)S(1)}, bf16[256,512]{1,0:T(8,128)(2,1)S(1)}, u32[]{:S(2)}, u32[]{:S(2)}) collective-permute-start(bf16[256,512]{1,0:T(8,128)(2,1)S(1)} %collective-permute-done.11.refs_3_.refs_17_), channel_id=1, source_target_pairs={{4,0},{5,1},{8,4},{9,5},{12,8},{13,9},{14,12},{15,13},{10,14},{11,... | collective-permute-start | bytes 786440 | tf_op jit(solution)/shard_map/ppermute | solution.py:663
  36.9 9.4 %collective-permute-start.12 = (bf16[256,512]{1,0:T(8,128)(2,1)S(1)}, bf16[256,512]{1,0:T(8,128)(2,1)S(1)}, u32[]{:S(2)}, u32[]{:S(2)}) collective-permute-start(bf16[256,512]{1,0:T(8,128)(2,1)S(1)} %collective-permute-done.8.refs_0_.refs_18_), channel_id=1, source_target_pairs={{0,4},{1,5},{4,8},{5,9},{8,12},{9,13},{12,14},{13,15},{14,10},{15,... | collective-permute-start | bytes 786440 | tf_op jit(solution)/shard_map/ppermute | solution.py:662
  42.5 8.7 %collective-permute-start.15 = (bf16[256,512]{1,0:T(8,128)(2,1)S(1)}, bf16[256,512]{1,0:T(8,128)(2,1)S(1)}, u32[]{:S(2)}, u32[]{:S(2)}) collective-permute-start(bf16[256,512]{1,0:T(8,128)(2,1)S(1)} %collective-permute-done.14.refs_3_.refs_21_), channel_id=1, source_target_pairs={{4,0},{5,1},{8,4},{9,5},{12,8},{13,9},{14,12},{15,13},{10,14},{11,... | collective-permute-start | bytes 786440 | tf_op jit(solution)/shard_map/ppermute | solution.py:663
  42.9 8.3 %collective-permute-start.16 = (bf16[16,128]{1,0:T(8,128)(2,1)S(1)}, bf16[16,128]{1,0:T(8,128)(2,1)S(1)}, u32[]{:S(2)}, u32[]{:S(2)}) collective-permute-start(bf16[16,128]{1,0:T(8,128)(2,1)S(1)} %convert_convert_fusion.refs_6_), channel_id=1, source_target_pairs={{0,1},{1,0},{2,3},{3,2},{4,5},{5,4},{6,7},{7,6},{8,9},{9,8},{10,11... | collective-permute-start | bytes 12296 | tf_op jit(solution)/shard_map/ppermute | solution.py:664
  55.6 8.1 %collective-permute-start.17 = (bf16[32,4224]{1,0:T(8,128)(2,1)S(1)}, bf16[32,4224]{1,0:T(8,128)(2,1)S(1)}, u32[]{:S(2)}, u32[]{:S(2)}) collective-permute-start(bf16[32,4224]{1,0:T(8,128)(2,1)S(1)} %get-tuple-element.133.refs_0_), channel_id=1, source_target_pairs={{0,4},{1,5},{4,8},{5,9},{8,12},{9,13},{12,14},{13,15},{14,10},{15,... | collective-permute-start | bytes 811016 | tf_op jit(solution)/shard_map/ppermute | solution.py:662
  57.3 7.8 %collective-permute-start.18 = (bf16[32,4224]{1,0:T(8,128)(2,1)S(1)}, bf16[32,4224]{1,0:T(8,128)(2,1)S(1)}, u32[]{:S(2)}, u32[]{:S(2)}) collective-permute-start(bf16[32,4224]{1,0:T(8,128)(2,1)S(1)} %get-tuple-element.133.refs_0_), channel_id=1, source_target_pairs={{4,0},{5,1},{8,4},{9,5},{12,8},{13,9},{14,12},{15,13},{10,14},{11,... | collective-permute-start | bytes 811016 | tf_op jit(solution)/shard_map/ppermute | solution.py:663
  65.0 49.1 %collective-permute-start.21 = (bf16[128,4096]{1,0:T(8,128)(2,1)S(1)}, bf16[128,4096]{1,0:T(8,128)(2,1)S(1)}, u32[]{:S(2)}, u32[]{:S(2)}) collective-permute-start(bf16[128,4096]{1,0:T(8,128)(2,1)S(1)} %get-tuple-element.140), channel_id=1, source_target_pairs={{0,1},{1,0},{2,3},{3,2},{4,5},{5,4},{6,7},{7,6},{8,9},{9,8},{10,11... | collective-permute-start | bytes 3145736 | tf_op jit(solution)/shard_map/ppermute | solution.py:664
  65.0 8.9 %collective-permute-start.19 = (bf16[32,4224]{1,0:T(8,128)(2,1)S(1)}, bf16[32,4224]{1,0:T(8,128)(2,1)S(1)}, u32[]{:S(2)}, u32[]{:S(2)}) collective-permute-start(bf16[32,4224]{1,0:T(8,128)(2,1)S(1)} %collective-permute-done.17.refs_1_), channel_id=1, source_target_pairs={{0,4},{1,5},{4,8},{5,9},{8,12},{9,13},{12,14},{13,15},{14,10},{15,... | collective-permute-start | bytes 811016 | tf_op jit(solution)/shard_map/ppermute | solution.py:662
  66.6 47.5 %collective-permute-start.20 = (bf16[32,4224]{1,0:T(8,128)(2,1)S(1)}, bf16[32,4224]{1,0:T(8,128)(2,1)S(1)}, u32[]{:S(2)}, u32[]{:S(2)}) collective-permute-start(bf16[32,4224]{1,0:T(8,128)(2,1)S(1)} %collective-permute-done.18.refs_4_), channel_id=1, source_target_pairs={{4,0},{5,1},{8,4},{9,5},{12,8},{13,9},{14,12},{15,13},{10,14},{11,... | collective-permute-start | bytes 811016 | tf_op jit(solution)/shard_map/ppermute | solution.py:663
  114.1 8.1 %collective-permute-start.22 = (bf16[32,4224]{1,0:T(8,128)(2,1)S(1)}, bf16[32,4224]{1,0:T(8,128)(2,1)S(1)}, u32[]{:S(2)}, u32[]{:S(2)}) collective-permute-start(bf16[32,4224]{1,0:T(8,128)(2,1)S(1)} %collective-permute-done.19.refs_2_), channel_id=1, source_target_pairs={{0,4},{1,5},{4,8},{5,9},{8,12},{9,13},{12,14},{13,15},{14,10},{15,... | collective-permute-start | bytes 811016 | tf_op jit(solution)/shard_map/ppermute | solution.py:662
  115.9 7.5 %collective-permute-start.23 = (bf16[32,4224]{1,0:T(8,128)(2,1)S(1)}, bf16[32,4224]{1,0:T(8,128)(2,1)S(1)}, u32[]{:S(2)}, u32[]{:S(2)}) collective-permute-start(bf16[32,4224]{1,0:T(8,128)(2,1)S(1)} %collective-permute-done.20.refs_5_), channel_id=1, source_target_pairs={{4,0},{5,1},{8,4},{9,5},{12,8},{13,9},{14,12},{15,13},{10,14},{11,... | collective-permute-start | bytes 811016 | tf_op jit(solution)/shard_map/ppermute | solution.py:663
  149.8 6.4 %collective-permute-start.31 = (bf16[16,4096]{1,0:T(8,128)(2,1)S(1)}, bf16[16,4096]{1,0:T(8,128)(2,1)S(1)}, u32[]{:S(2)}, u32[]{:S(2)}) collective-permute-start(bf16[16,4096]{1,0:T(8,128)(2,1)S(1)} %pad_maximum_fusion.1), channel_id=1, source_target_pairs={{4,0},{5,1},{8,4},{9,5},{12,8},{13,9},{14,12},{15,13},{10,14},{11,... | collective-permute-start | bytes 393224 | tf_op jit(solution)/shard_map/ppermute | solution.py:663
  151.3 6.3 %collective-permute-start.30 = (bf16[16,4096]{1,0:T(8,128)(2,1)S(1)}, bf16[16,4096]{1,0:T(8,128)(2,1)S(1)}, u32[]{:S(2)}, u32[]{:S(2)}) collective-permute-start(bf16[16,4096]{1,0:T(8,128)(2,1)S(1)} %pad_maximum_fusion), channel_id=1, source_target_pairs={{0,4},{1,5},{4,8},{5,9},{8,12},{9,13},{12,14},{13,15},{14,10},{15,... | collective-permute-start | bytes 393224 | tf_op jit(solution)/shard_map/ppermute | solution.py:662
  152.8 7.0 %collective-permute-start.40 = (bf16[16,4096]{1,0:T(8,128)(2,1)S(1)}, bf16[16,4096]{1,0:T(8,128)(2,1)S(1)}, u32[]{:S(2)}, u32[]{:S(2)}) collective-permute-start(bf16[16,4096]{1,0:T(8,128)(2,1)S(1)} %pad_maximum_fusion.3), channel_id=1, source_target_pairs={{4,0},{5,1},{8,4},{9,5},{12,8},{13,9},{14,12},{15,13},{10,14},{11,... | collective-permute-start | bytes 393224 | tf_op jit(solution)/shard_map/ppermute | solution.py:663
  154.5 5.9 %collective-permute-start.39 = (bf16[16,4096]{1,0:T(8,128)(2,1)S(1)}, bf16[16,4096]{1,0:T(8,128)(2,1)S(1)}, u32[]{:S(2)}, u32[]{:S(2)}) collective-permute-start(bf16[16,4096]{1,0:T(8,128)(2,1)S(1)} %pad_maximum_fusion.2), channel_id=1, source_target_pairs={{0,4},{1,5},{4,8},{5,9},{8,12},{9,13},{12,14},{13,15},{14,10},{15,... | collective-permute-start | bytes 393224 | tf_op jit(solution)/shard_map/ppermute | solution.py:662
  158.0 5.9 %collective-permute-start.32 = (bf16[16,4096]{1,0:T(8,128)(2,1)S(1)}, bf16[16,4096]{1,0:T(8,128)(2,1)S(1)}, u32[]{:S(2)}, u32[]{:S(2)}) collective-permute-start(bf16[16,4096]{1,0:T(8,128)(2,1)S(1)} %get-tuple-element.165), channel_id=1, source_target_pairs={{0,4},{1,5},{4,8},{5,9},{8,12},{9,13},{12,14},{13,15},{14,10},{15,... | collective-permute-start | bytes 393224 | tf_op jit(solution)/shard_map/ppermute | solution.py:662
  160.6 6.0 %collective-permute-start.42 = (bf16[16,4096]{1,0:T(8,128)(2,1)S(1)}, bf16[16,4096]{1,0:T(8,128)(2,1)S(1)}, u32[]{:S(2)}, u32[]{:S(2)}) collective-permute-start(bf16[16,4096]{1,0:T(8,128)(2,1)S(1)} %get-tuple-element.177), channel_id=1, source_target_pairs={{4,0},{5,1},{8,4},{9,5},{12,8},{13,9},{14,12},{15,13},{10,14},{11,... | collective-permute-start | bytes 393224 | tf_op jit(solution)/shard_map/ppermute | solution.py:663
  160.9 6.1 %collective-permute-start.41 = (bf16[16,4096]{1,0:T(8,128)(2,1)S(1)}, bf16[16,4096]{1,0:T(8,128)(2,1)S(1)}, u32[]{:S(2)}, u32[]{:S(2)}) collective-permute-start(bf16[16,4096]{1,0:T(8,128)(2,1)S(1)} %get-tuple-element.176), channel_id=1, source_target_pairs={{0,4},{1,5},{4,8},{5,9},{8,12},{9,13},{12,14},{13,15},{14,10},{15,... | collective-permute-start | bytes 393224 | tf_op jit(solution)/shard_map/ppermute | solution.py:662
  164.0 11.6 %collective-permute-start.34 = (bf16[16,4096]{1,0:T(8,128)(2,1)S(1)}, bf16[16,4096]{1,0:T(8,128)(2,1)S(1)}, u32[]{:S(2)}, u32[]{:S(2)}) collective-permute-start(bf16[16,4096]{1,0:T(8,128)(2,1)S(1)} %get-tuple-element.167), channel_id=1, source_target_pairs={{0,4},{1,5},{4,8},{5,9},{8,12},{9,13},{12,14},{13,15},{14,10},{15,... | collective-permute-start | bytes 393224 | tf_op jit(solution)/shard_map/ppermute | solution.py:662
  166.3 9.3 %collective-permute-start.35 = (bf16[16,4096]{1,0:T(8,128)(2,1)S(1)}, bf16[16,4096]{1,0:T(8,128)(2,1)S(1)}, u32[]{:S(2)}, u32[]{:S(2)}) collective-permute-start(bf16[16,4096]{1,0:T(8,128)(2,1)S(1)} %get-tuple-element.168), channel_id=1, source_target_pairs={{4,0},{5,1},{8,4},{9,5},{12,8},{13,9},{14,12},{15,13},{10,14},{11,... | collective-permute-start | bytes 393224 | tf_op jit(solution)/shard_map/ppermute | solution.py:663
  (16 other events, 91.4 us)

commit v3 on v2

--- a/solution.py
+++ b/solution.py
@@ -109,6 +109,8 @@
 
 
 def block_of(ref, columns):
+    if isinstance(ref, tuple):
+        return ref[0][:, columns], ref[1][:, columns]
     tokens = ref.shape[0] // 2
     return ref[:tokens, columns], ref[tokens:, columns]
 
@@ -219,11 +221,14 @@
 
     def one_group(group, columns):
         queries = group_queries(q_refs, group)
-        for i in range(chips):
+        for i in range(chips - 1):
             for j, block in enumerate(sources[2 * i : 2 * i + 2]):
                 rows = pl.ds(j * tokens, tokens)
                 fetch(block.at[pl.ds(0, tokens), columns], keys_ref.at[i, rows])
                 fetch(block.at[pl.ds(tokens, tokens), columns], values_ref.at[i, rows])
+        for j, block in enumerate(sources[2 * chips - 2 :]):
+            target = (values_ref if j % 2 else keys_ref).at[chips - 1, pl.ds(j // 2 * tokens, tokens)]
+            fetch(block.at[:, columns], target)
         acc_ref[...] = jnp.zeros_like(acc_ref)
         total_ref[...] = jnp.zeros_like(total_ref)
         top_ref[...] = jnp.full_like(top_ref, 2 * MASKED)
@@ -258,11 +263,11 @@
 
 
 def last_kernel(chips, me_ref, q_ref, sib_q_ref, *refs):
-    blocks, (shift_ref, acc_ref, total_ref, gain_ref) = refs[:2], refs[2:6]
-    tables, sources = refs[6:8], refs[8 : 8 + 2 * chips]
-    refs = refs[8 + 2 * chips :]
-    out_refs, picked_ref = refs[:2], refs[2]
-    rows_ref, worst_ref, sem, *scratch = refs[3:]
+    blocks, (shift_ref, acc_ref, total_ref, gain_ref) = (refs[:2], refs[2:4]), refs[4:8]
+    tables, sources = refs[8:10], refs[10 : 12 + 2 * chips]
+    refs = refs[12 + 2 * chips :]
+    out_refs, picked_refs = refs[:2], refs[2:4]
+    rows_ref, worst_ref, sem, *scratch = refs[4:]
     q_refs = (q_ref, sib_q_ref)
     tokens, half_width = q_ref.shape
     me = me_ref[0]
@@ -296,8 +301,11 @@
     upper = squares.astype(jnp.bfloat16).astype(jnp.float32)
     lower = (squares - upper).astype(jnp.bfloat16).astype(jnp.float32)
     lane = lax.broadcasted_iota(jnp.int32, squares.shape, 1)
-    picked_ref[:, :half_width] = (rows * gain_ref[:, columns]).astype(jnp.bfloat16)
-    picked_ref[:, half_width:] = jnp.where(lane < DH // 2, upper, lower).astype(jnp.bfloat16)
+    rows = (rows * gain_ref[:, columns]).astype(jnp.bfloat16)
+    squares = jnp.where(lane < DH // 2, upper, lower).astype(jnp.bfloat16)
+    for i, ref in enumerate(picked_refs):
+        ref[:, :half_width] = rows[i * CAP : (i + 1) * CAP]
+        ref[:, half_width:] = squares[i * CAP : (i + 1) * CAP]
 
 
 class Attention:
@@ -352,7 +360,7 @@
 
     def last(self, blocks, shift, state, gain, tables, sources):
         out = pltpu.VMEM((self.tokens, self.width), jnp.bfloat16)
-        picked = pltpu.VMEM((2 * CAP, self.width + DH), jnp.bfloat16)
+        picked = pltpu.VMEM((CAP, self.width + DH), jnp.bfloat16)
         kept = pltpu.VMEM((self.chips, 2 * self.tokens, DH), jnp.bfloat16)
         sums = pltpu.VMEM((self.rows, DH), jnp.float32)
         return self.call(
@@ -360,7 +368,7 @@
             "attend_last",
             (*blocks, shift, *state, gain, *tables),
             sources,
-            [out, out, picked],
+            [out, out, picked, picked],
             [],
             [
                 pltpu.VMEM((2 * CAP, self.width), jnp.float32),
@@ -441,107 +449,137 @@
     )(me, keep, other)
 
 
-def load_kernel(source_ref, target_ref, sem):
-    copy = pltpu.make_async_copy(source_ref, target_ref, sem)
+def load_kernel(me_ref, source_ref, target_ref, sem):
+    copy = pltpu.make_async_copy(half_rows(me_ref, source_ref, False), target_ref, sem)
     copy.start()
     copy.wait()
 
 
-def load(x):
+def half_rows(me_ref, ref, sibling):
+    half = ref.shape[0] // 2
+    side = 1 - me_ref[0] % 2 if sibling else me_ref[0] % 2
+    return ref.at[pl.ds(pl.multiple_of(side * half, half), half), :]
+
+
+def load(me, x):
     return pl.pallas_call(
         load_kernel,
-        in_specs=[pl.BlockSpec(memory_space=pl.ANY)],
+        in_specs=[pl.BlockSpec(memory_space=pltpu.SMEM), pl.BlockSpec(memory_space=pl.ANY)],
         out_specs=pl.BlockSpec(memory_space=pl.ANY),
-        out_shape=pltpu.VMEM(x.shape, x.dtype),
+        out_shape=pltpu.VMEM((x.shape[0] // 2, x.shape[1]), x.dtype),
         scratch_shapes=[pltpu.SemaphoreType.DMA],
         compiler_params=pltpu.CompilerParams(vmem_limit_bytes=MIB),
         cost_estimate=SMALL,
         name="load",
-    )(in_hbm(x))
-
-
-def gather_kernel(*refs):
-    blocks, out_ref = refs[:-1], refs[-1]
-    middle = out_ref.shape[0] // 2
-    parts = [(ref[:CAP], ref[CAP:]) for ref in blocks[:-2]] + [(blocks[-2][...], blocks[-1][...])]
-    for j, (mine, other) in enumerate(parts):
-        out_ref[j * CAP : (j + 1) * CAP] = mine
-        out_ref[middle + j * CAP : middle + (j + 1) * CAP] = other
-
-
-def gather(blocks):
+    )(me, in_hbm(x))
+
+
+def place_kernel(spots, *refs):
+    blocks, out_ref = refs[: len(spots)], refs[-1]
+    for (row, column), ref in zip(spots, blocks):
+        out_ref[row : row + ref.shape[0], column : column + ref.shape[1]] = ref[...]
+
+
+def place(blocks, spots, shape, rows=None):
     vmem = pl.BlockSpec(memory_space=pltpu.VMEM)
+    earlier = [] if rows is None else [rows]
     return pl.pallas_call(
-        gather_kernel,
-        in_specs=[vmem] * len(blocks),
+        functools.partial(place_kernel, spots),
+        in_specs=[vmem] * (len(blocks) + len(earlier)),
         out_specs=vmem,
-        out_shape=pltpu.VMEM((2 * CAP * (len(blocks) - 1), blocks[0].shape[1]), jnp.bfloat16),
+        out_shape=pltpu.VMEM(shape, jnp.bfloat16),
+        input_output_aliases={len(blocks): 0} if earlier else {},
         compiler_params=pltpu.CompilerParams(vmem_limit_bytes=4 * MIB),
         cost_estimate=SMALL,
-        name="gather",
-    )(*blocks)
-
-
-def hidden_kernel(second, me_ref, rows_ref, gate_ref, up_ref, *refs):
-    half = rows_ref.shape[1] - DH
-    middle = rows_ref.shape[0] // 2
+        name="place",
+    )(*blocks, *earlier)
+
+
+def contract(rows_ref, gate_ref, up_ref, gate_sum, up_sum, order):
+    half = gate_ref.shape[0]
     depth = min(1024, half)
-    if second:
-        own_ref, gate_in, up_in, source_ref, out_ref, target_ref, gate_sum, up_sum, sem = refs
-        gate_sum[...] = gate_in[...]
-        up_sum[...] = up_in[...]
-    else:
-        source_ref, gate_sum, up_sum, target_ref, sem = refs
-        gate_sum[...] = jnp.zeros_like(gate_sum)
-        up_sum[...] = jnp.zeros_like(up_sum)
-    side = 1 - me_ref[0] % 2 if second else me_ref[0] % 2
-    columns = pl.ds(target_ref.shape[1] if second else 0, target_ref.shape[1])
-    load = pltpu.make_async_copy(source_ref.at[:, columns], target_ref, sem)
-    load.start()
 
     def one_part(step, carry):
-        part = rows_ref[:, pl.ds(pl.multiple_of(step * depth, depth), depth)]
-        if second:
-            part = jnp.concatenate([part[middle:], part[:middle]], axis=0)
-        place = pl.ds(pl.multiple_of(side * half + step * depth, depth), depth)
-        gate_sum[...] += jnp.dot(part, gate_ref[place, :], preferred_element_type=jnp.float32)
-        up_sum[...] += jnp.dot(part, up_ref[place, :], preferred_element_type=jnp.float32)
+        columns = pl.ds(pl.multiple_of(step * depth, depth), depth)
+        part = order(rows_ref[:, columns])
+        gate_sum[...] += jnp.dot(part, gate_ref[columns, :], preferred_element_type=jnp.float32)
+        up_sum[...] += jnp.dot(part, up_ref[columns, :], preferred_element_type=jnp.float32)
         return carry
 
     lax.fori_loop(0, half // depth, one_part, 0)
-    if second:
-        squares = own_ref[:, half:].astype(jnp.float32)
-        others = rows_ref[:, half:].astype(jnp.float32)
-        squares += jnp.concatenate([others[middle:], others[:middle]], axis=0)
-        squares = squares[:, :1] + squares[:, DH // 2 : DH // 2 + 1]
-        factor = lax.rsqrt(squares / (2 * half) + 1e-05)
-        gate = gate_sum[...] * factor
-        out_ref[...] = (gate / (1.0 + jnp.exp(-gate)) * (up_sum[...] * factor)).astype(jnp.bfloat16)
-    load.wait()
-
-
-def hidden_call(me, rows, w_gate, w_up, w_down, own=None, sums=()):
-    count, half = rows.shape[0], rows.shape[1] - DH
-    units, width = w_down.shape
+
+
+def first_kernel(me_ref, rows_ref, gate_ref, up_ref, *refs):
+    sources, (gate_sum, up_sum), targets, sems = refs[:2], refs[2:4], refs[4:6], refs[6]
+    copies = [
+        pltpu.make_async_copy(half_rows(me_ref, source, True), target, sems.at[i])
+        for i, (source, target) in enumerate(zip(sources, targets))
+    ]
+    for copy in copies:
+        copy.start()
+    gate_sum[...] = jnp.zeros_like(gate_sum)
+    up_sum[...] = jnp.zeros_like(up_sum)
+    contract(rows_ref, gate_ref, up_ref, gate_sum, up_sum, lambda part: part)
+    for copy in copies:
+        copy.wait()
+
+
+def second_kernel(rows_ref, gate_ref, up_ref, own_ref, gate_in, up_in, source_ref, out_ref, *refs):
+    targets, (gate_sum, up_sum, sems) = refs[:PIECES], refs[PIECES:]
+    piece = targets[0].shape[1]
+    copies = [
+        pltpu.make_async_copy(source_ref.at[:, pl.ds(i * piece, piece)], target, sems.at[i])
+        for i, target in enumerate(targets)
+    ]
+    for copy in copies:
+        copy.start()
+    middle, half = rows_ref.shape[0] // 2, gate_ref.shape[0]
+
+    def order(part):
+        return jnp.concatenate([part[middle:], part[:middle]], axis=0)
+
+    gate_sum[...] = gate_in[...]
+    up_sum[...] = up_in[...]
+    contract(rows_ref, gate_ref, up_ref, gate_sum, up_sum, order)
+    squares = own_ref[:, half:].astype(jnp.float32) + order(rows_ref[:, half:].astype(jnp.float32))
+    squares = squares[:, :1] + squares[:, DH // 2 : DH // 2 + 1]
+    factor = lax.rsqrt(squares / (2 * half) + 1e-05)
+    gate = gate_sum[...] * factor
+    out_ref[...] = (gate / (1.0 + jnp.exp(-gate)) * (up_sum[...] * factor)).astype(jnp.bfloat16)
+    for copy in copies:
+        copy.wait()
+
+
+def hidden_calls(me, rows, other_rows, loaded, w_gate, w_up, w_down):
+    count, units, width = rows.shape[0], w_down.shape[0], w_down.shape[1]
     vmem, anywhere = pl.BlockSpec(memory_space=pltpu.VMEM), pl.BlockSpec(memory_space=pl.ANY)
-    sum_shape = pltpu.VMEM((count, units), jnp.float32)
-    second = own is not None
-    more = (own, *sums) if second else ()
-    outs = [pltpu.VMEM((count, units), jnp.bfloat16)] if second else [sum_shape] * 2
-    return pl.pallas_call(
-        functools.partial(hidden_kernel, second),
-        in_specs=[pl.BlockSpec(memory_space=pltpu.SMEM)] + [vmem] * (3 + len(more)) + [anywhere],
-        out_specs=[vmem] * len(outs) + [anywhere],
-        out_shape=outs + [pltpu.VMEM((units, width // 2), w_down.dtype)],
-        scratch_shapes=[sum_shape] * (2 if second else 0) + [pltpu.SemaphoreType.DMA],
-        compiler_params=pltpu.CompilerParams(vmem_limit_bytes=8 * MIB),
-        cost_estimate=pl.CostEstimate(
-            flops=4 * count * half * units,
-            bytes_accessed=4 * half * units + 2 * count * half,
-            transcendentals=count * units,
-        ),
-        name="hidden",
-    )(me, rows, w_gate, w_up, *more, in_hbm(w_down))
+    sums = [pltpu.VMEM((count, units), jnp.float32)] * 2
+    params = pltpu.CompilerParams(vmem_limit_bytes=8 * MIB)
+    cost = pl.CostEstimate(
+        flops=2 * count * width * units, bytes_accessed=2 * width * units, transcendentals=count * units
+    )
+    *partial, gate, up = pl.pallas_call(
+        first_kernel,
+        in_specs=[pl.BlockSpec(memory_space=pltpu.SMEM)] + [vmem] * 3 + [anywhere] * 2,
+        out_specs=[vmem] * 2 + [anywhere] * 2,
+        out_shape=sums + [pltpu.VMEM((width // 2, units), w_gate.dtype)] * 2,
+        scratch_shapes=[pltpu.SemaphoreType.DMA((2,))],
+        compiler_params=params,
+        cost_estimate=cost,
+        name="hidden_first",
+    )(me, rows, *loaded, in_hbm(w_gate), in_hbm(w_up))
+    hidden, *downs = pl.pallas_call(
+        second_kernel,
+        in_specs=[vmem] * 6 + [anywhere],
+        out_specs=[vmem] + [anywhere] * PIECES,
+        out_shape=[pltpu.VMEM((count, units), jnp.bfloat16)]
+        + [pltpu.VMEM((units, width // PIECES), w_down.dtype)] * PIECES,
+        scratch_shapes=sums + [pltpu.SemaphoreType.DMA((PIECES,))],
+        compiler_params=params,
+        cost_estimate=cost,
+        name="hidden_second",
+    )(other_rows, gate, up, rows, *partial, in_hbm(w_down))
+    return hidden, downs
 
 
 def down_kernel(hidden_ref, down_ref, own_ref, sib_ref):
@@ -700,35 +738,48 @@
         if step < half - 1:
             chains = [(go_right(chain[0]), go_left(chain[1])) for chain in chains]
         else:
-            opposite = [go_right(chains[0][0]), go_left(chains[1][1])]
+            opposite = [
+                part for chain in chains for part in (go_right(chain[0][:tokens]), go_left(chain[1][tokens:]))
+            ]
         state, _ = attention.step(blocks, [step, step, -step, -step], shift, state)
     opposite, state = lax.optimization_barrier((opposite, state))
     sources += opposite
-    mine, theirs, picked = attention.last(
+    mine, theirs, *picked = attention.last(
         opposite, shift, state, norm_gain[None, :], (table, sib_table), sources
     )
 
     picked, w_gate = lax.optimization_barrier((picked, w_gate))
-    from_left, from_right, blocks_right, blocks_left = picked, picked, [picked], []
+    chains = [(go_right(x), go_left(x)) for x in picked]
+    width = picked[0].shape[1]
+    middle = width // DH // 2 * DH
+    shape = (2 * chips * CAP, width)
+    spots = lambda index: [(index * CAP, 0), ((chips + index) * CAP, 0)]
+    rows = place(picked, spots(0), shape)
+    loaded = [load(me, w_gate)]
     for step in range(1, half):
-        from_left, from_right = go_right(from_left), go_left(from_right)
         if step == 1:
-            w_gate = load(w_gate)
+            chains, rows, loaded = lax.optimization_barrier((chains, rows, loaded))
+        *chains[0], rows, loaded = lax.optimization_barrier((*chains[0], rows, loaded))
+        chains[1], _, rows, theirs = lax.optimization_barrier((chains[1], chains[0], rows, theirs))
+        blocks = [chain[side] for side in range(2) for chain in chains]
+        if step < half - 1:
+            chains = [(go_right(chain[0]), go_left(chain[1])) for chain in chains]
+        else:
+            far = [
+                part
+                for chain in chains
+                for part in (go_right(chain[0][:, :middle]), go_left(chain[1][:, middle:]))
+            ]
+        rows = place(blocks, spots(step) + spots(half - 1 + step), shape, rows)
+        if step == 1:
+            loaded = loaded + [load(me, w_up)]
         elif step == 2:
-            w_up = load(w_up)
             theirs = swap(theirs)
-        from_left, from_right, w_gate, w_up, theirs = lax.optimization_barrier(
-            (from_left, from_right, w_gate, w_up, theirs)
-        )
-        blocks_right.append(from_left)
-        blocks_left.append(from_right)
-    far = [go_right(from_left[:CAP]), go_left(from_right[CAP:])]
     result = beside(me, mine, theirs)
-    far, result = lax.optimization_barrier((far, result))
-    rows = gather(blocks_right + blocks_left + far)
-    *first, down_low = hidden_call(me, rows, w_gate, w_up, w_down)
-    hidden, down_high = hidden_call(me, swap(rows), w_gate, w_up, w_down, rows, first)
-    downs = [down_low, down_high]
+    far, rows, result = lax.optimization_barrier((far, rows, result))
+    places = [(row, column) for row, _ in spots(chips - 1) for column in (0, middle)]
+    rows = place(far, places, shape, rows)
+    hidden, downs = hidden_calls(me, rows, swap(rows), loaded, w_gate, w_up, w_down)
 
     sums = []
     for piece in range(PIECES):

time: 177 us -> 179 us (1.011)
  starting transfers between devices: 44.1 us -> 92.9 us
  waiting for transfers between devices: 94.2 us -> 49.9 us
  Pallas kernels: 37 us -> 34.2 us
    ppermute x18 -> x23, starting transfers between devices: 30.6 us -> 82.1 us  [per_device(): go_right = lambda x: lax.ppermute(x, 'ctx', right)]
    ppermute x18 -> x23, waiting for transfers between devices: 63.5 us -> 28.8 us  [per_device(): go_left = lambda x: lax.ppermute(x, 'ctx', left)]
    ppermute x18 -> x23, waiting for transfers between devices: 29 us -> 19.5 us  [per_device(): go_right = lambda x: lax.ppermute(x, 'ctx', right)]
    pallas_call x5 -> x9, Pallas kernels: 17.9 us -> 15 us  [the longest x2 5.6 us: load(): pl.pallas_call(load_kernel, in_specs=[pl.BlockSpec(memory_space=pltpu.SME...]
    ppermute x18 -> x23, starting transfers between devices: 9.63 us -> 7.21 us  [per_device(): go_left = lambda x: lax.ppermute(x, 'ctx', left)]
  transfers between devices with their start and end apart: 45 -> 55, of which waited for: 35 -> 36; matrix products, arithmetic and copies ran while one was open for 1% -> 1% of each run, Pallas kernels for 13% -> 11%
where the time goes in v3:
time: 179 us
  starting transfers between devices  92.9 us (52%)
  waiting for transfers between devices  49.9 us (28%)
  Pallas kernels  34.2 us (19%)
    ppermute x23, starting transfers between devices, per_device(): go_right = lambda x: lax.ppermute(x, 'ctx', right)  82.1 us
    ppermute x23, waiting for transfers between devices, per_device(): go_left = lambda x: lax.ppermute(x, 'ctx', left)  28.8 us
    ppermute x23, waiting for transfers between devices, per_device(): go_right = lambda x: lax.ppermute(x, 'ctx', right)  19.5 us
    pallas_call x5, Pallas kernels, call(): pl.pallas_call(kernel, in_specs=[pl.BlockSpec(memory_space=pltpu.SMEM)] +...  8.36 us
    ppermute x23, starting transfers between devices, per_device(): go_left = lambda x: lax.ppermute(x, 'ctx', left)  7.21 us
    pallas_call x2, Pallas kernels, load(): pl.pallas_call(load_kernel, in_specs=[pl.BlockSpec(memory_space=pltpu.SME...  5.6 us
    pallas_call x1, Pallas kernels, hidden_calls(): pl.pallas_call(first_kernel, in_specs=[pl.BlockSpec(memory_space=pltpu.SM...  4.64 us
    pallas_call x1, Pallas kernels, hidden_calls(): pl.pallas_call(second_kernel, in_specs=[vmem] * 6 + [anywhere], out_specs...  4.63 us
  transfers between devices with their start and end apart: 55, of which 36 were waited for; matrix products, arithmetic and copies ran while one was open for 1% of the time, Pallas kernels for 11%

profile of v3, /device:TPU:0, one launch (start us, length us, event | category | flops | bytes accessed | tf_op | source)
XLA Modules:
  0.0 179.1 jit_solution(9691139389403030178)
XLA Ops:
  0.7 1.9 %halves.1 = (bf16[256,512]{1,0:T(8,128)(2,1)S(1)}, bf16[256,512]{1,0:T(8,128)(2,1)S(1)}, bf16[128,4096]{1,0:T(8,128)(2,1)S(1)}, bf16[128,4096]{1,0:T(8,128)(2,1)S(1)}) custom-call(s32[1]{0:T(128)} %bitcast.me_ref, bf16[128,1024]{1,0:T(8,128)(2,1)} %refs_0_.1, bf16[128,1024]{1,0:T(8,128)(2,1)} %refs_1_.2, bf16[128,8192]{1,0:T(8,128)(2,1)} %refs_2_.1), custom_call_target="tpu_custom_call" | custom-call | flops 1 | bytes 1 | tf_op jit(solution)/shard_map/halves/pallas_call | solution.py:412
  3.1 3.0 %collective-permute-start.1 = (bf16[256,512]{1,0:T(8,128)(2,1)S(1)}, bf16[256,512]{1,0:T(8,128)(2,1)S(1)}, u32[]{:S(2)}, u32[]{:S(2)}) collective-permute-start(bf16[256,512]{1,0:T(8,128)(2,1)S(1)} %get-tuple-element.119.own_ref.refs_10_), channel_id=1, source_target_pairs={{0,4},{1,5},{4,8},{5,9},{8,12},{9,13},{12,14},{13,15},{14,10},{15,... | collective-permute-start | bytes 786440 | tf_op jit(solution)/shard_map/ppermute | solution.py:700
  8.3 3.8 %attend_own.1 = (f32[4,2048,128]{2,1,0:T(8,128)S(1)}, f32[4,2048,128]{2,1,0:T(8,128)S(1)}, f32[4,2048,128]{2,1,0:T(8,128)S(1)}) custom-call(s32[1]{0:T(128)} %bitcast.me_ref, bf16[128,4096]{1,0:T(8,128)(2,1)S(1)} %get-tuple-element.117.q_ref, bf16[128,4096]{1,0:T(8,128)(2,1)S(1)} %collective-permute-done.sib_q_ref, ...), custom_call_target="tpu_custom_call" | custom-call | flops 1 | bytes 1 | tf_op jit(solution)/shard_map/attend_own/pallas_call | solution.py:320
  13.2 2.2 %collective-permute-done.2.refs_2_.refs_14_ = bf16[256,512]{1,0:T(8,128)(2,1)S(1)} collective-permute-done((bf16[256,512]{1,0:T(8,128)(2,1)S(1)}, bf16[256,512]{1,0:T(8,128)(2,1)S(1)}, u32[]{:S(2)}, u32[]{:S(2)}) %collective-permute-start.2) | collective-permute-done | bytes 262176 | tf_op jit(solution)/shard_map/ppermute | solution.py:701
  18.6 1.9 %collective-permute-start.10 = (bf16[256,512]{1,0:T(8,128)(2,1)S(1)}, bf16[256,512]{1,0:T(8,128)(2,1)S(1)}, u32[]{:S(2)}, u32[]{:S(2)}) collective-permute-start(bf16[256,512]{1,0:T(8,128)(2,1)S(1)} %collective-permute-done.6.refs_1_.refs_13_), channel_id=1, source_target_pairs={{0,4},{1,5},{4,8},{5,9},{8,12},{9,13},{12,14},{13,15},{14,10},{15,... | collective-permute-start | bytes 786440 | tf_op jit(solution)/shard_map/ppermute | solution.py:700
  20.7 3.3 %collective-permute-done.4.refs_0_.refs_16_ = bf16[256,512]{1,0:T(8,128)(2,1)S(1)} collective-permute-done((bf16[256,512]{1,0:T(8,128)(2,1)S(1)}, bf16[256,512]{1,0:T(8,128)(2,1)S(1)}, u32[]{:S(2)}, u32[]{:S(2)}) %collective-permute-start.4) | collective-permute-done | bytes 262176 | tf_op jit(solution)/shard_map/ppermute | solution.py:700
  25.7 2.4 %collective-permute-start.8 = (bf16[256,512]{1,0:T(8,128)(2,1)S(1)}, bf16[256,512]{1,0:T(8,128)(2,1)S(1)}, u32[]{:S(2)}, u32[]{:S(2)}) collective-permute-start(bf16[256,512]{1,0:T(8,128)(2,1)S(1)} %collective-permute-done.4.refs_0_.refs_16_), channel_id=1, source_target_pairs={{0,4},{1,5},{4,8},{5,9},{8,12},{9,13},{12,14},{13,15},{14,10},{15,... | collective-permute-start | bytes 786440 | tf_op jit(solution)/shard_map/ppermute | solution.py:700
  33.2 2.1 %collective-permute-done.8.refs_0_.refs_20_ = bf16[256,512]{1,0:T(8,128)(2,1)S(1)} collective-permute-done((bf16[256,512]{1,0:T(8,128)(2,1)S(1)}, bf16[256,512]{1,0:T(8,128)(2,1)S(1)}, u32[]{:S(2)}, u32[]{:S(2)}) %collective-permute-start.8) | collective-permute-done | bytes 262176 | tf_op jit(solution)/shard_map/ppermute | solution.py:700
  37.0 3.4 %collective-permute-start.12 = (bf16[128,512]{1,0:T(8,128)(2,1)S(1)}, bf16[128,512]{1,0:T(8,128)(2,1)S(1)}, u32[]{:S(2)}, u32[]{:S(2)}) collective-permute-start(bf16[128,512]{1,0:T(8,128)(2,1)S(1)} %slice.148), channel_id=1, source_target_pairs={{0,4},{1,5},{4,8},{5,9},{8,12},{9,13},{12,14},{13,15},{14,10},{15,... | collective-permute-start | bytes 393224 | tf_op jit(solution)/shard_map/ppermute | solution.py:700
  45.7 2.8 %collective-permute-done.16.refs_2_.refs_26_ = bf16[128,512]{1,0:T(8,128)(2,1)S(1)} collective-permute-done((bf16[128,512]{1,0:T(8,128)(2,1)S(1)}, bf16[128,512]{1,0:T(8,128)(2,1)S(1)}, u32[]{:S(2)}, u32[]{:S(2)}) %collective-permute-start.16) | collective-permute-done | bytes 131104 | tf_op jit(solution)/shard_map/ppermute | solution.py:700
  49.9 4.4 %attend_last.1 = (bf16[128,4096]{1,0:T(8,128)(2,1)S(1)}, bf16[128,4096]{1,0:T(8,128)(2,1)S(1)}, bf16[16,4224]{1,0:T(8,128)(2,1)S(1)}, bf16[16,4224]{1,0:T(8,128)(2,1)S(1)}) custom-call(s32[1]{0:T(128)} %bitcast.me_ref, bf16[128,4096]{1,0:T(8,128)(2,1)S(1)} %get-tuple-element.117.q_ref, bf16[128,4096]{1,0:T(8,128)(2,1)S(1)} %collective-permute-done.sib_q_ref, ...), custom_call_target="tpu_custom_call" | custom-call | flops 1 | bytes 1 | tf_op jit(solution)/shard_map/attend_last/pallas_call | solution.py:320
  56.4 1.8 collective-permute-start.21
  58.4 2.8 %load.2.gate_ref = bf16[4096,768]{1,0:T(8,128)(2,1)S(1)} custom-call(s32[1]{0:T(128)} %bitcast.me_ref, bf16[8192,768]{1,0:T(8,128)(2,1)} %refs_0_.2), custom_call_target="tpu_custom_call" | custom-call | flops 1 | bytes 1 | tf_op jit(solution)/shard_map/load/pallas_call | solution.py:465
  62.5 2.4 %collective-permute-done.22.refs_3_ = bf16[16,4224]{1,0:T(8,128)(2,1)S(1)} collective-permute-done((bf16[16,4224]{1,0:T(8,128)(2,1)S(1)}, bf16[16,4224]{1,0:T(8,128)(2,1)S(1)}, u32[]{:S(2)}, u32[]{:S(2)}) %collective-permute-start.22) | collective-permute-done | bytes 135200 | tf_op jit(solution)/shard_map/ppermute | solution.py:701
  65.0 40.3 %collective-permute-start.23 = (bf16[16,4224]{1,0:T(8,128)(2,1)S(1)}, bf16[16,4224]{1,0:T(8,128)(2,1)S(1)}, u32[]{:S(2)}, u32[]{:S(2)}) collective-permute-start(bf16[16,4224]{1,0:T(8,128)(2,1)S(1)} %collective-permute-done.19.refs_0_), channel_id=1, source_target_pairs={{0,4},{1,5},{4,8},{5,9},{8,12},{9,13},{12,14},{13,15},{14,10},{15,... | collective-permute-start | bytes 405512 | tf_op jit(solution)/shard_map/ppermute | solution.py:700
  105.3 3.2 %collective-permute-start.27 = (bf16[16,4224]{1,0:T(8,128)(2,1)S(1)}, bf16[16,4224]{1,0:T(8,128)(2,1)S(1)}, u32[]{:S(2)}, u32[]{:S(2)}) collective-permute-start(bf16[16,4224]{1,0:T(8,128)(2,1)S(1)} %collective-permute-done.21.refs_1_), channel_id=1, source_target_pairs={{0,4},{1,5},{4,8},{5,9},{8,12},{9,13},{12,14},{13,15},{14,10},{15,... | collective-permute-start | bytes 405512 | tf_op jit(solution)/shard_map/ppermute | solution.py:700
  108.5 2.8 %load.3.up_ref = bf16[4096,768]{1,0:T(8,128)(2,1)S(1)} custom-call(s32[1]{0:T(128)} %bitcast.me_ref, bf16[8192,768]{1,0:T(8,128)(2,1)} %refs_1_.3), custom_call_target="tpu_custom_call" | custom-call | flops 1 | bytes 1 | tf_op jit(solution)/shard_map/load/pallas_call | solution.py:465
  114.5 1.8 collective-permute-start.25
  116.5 1.8 collective-permute-start.31
  118.6 2.3 %collective-permute-done.25.refs_0_ = bf16[16,4224]{1,0:T(8,128)(2,1)S(1)} collective-permute-done((bf16[16,4224]{1,0:T(8,128)(2,1)S(1)}, bf16[16,4224]{1,0:T(8,128)(2,1)S(1)}, u32[]{:S(2)}, u32[]{:S(2)}) %collective-permute-start.25) | collective-permute-done | bytes 135200 | tf_op jit(solution)/shard_map/ppermute | solution.py:700
  120.9 1.8 %collective-permute-done.26.refs_2_ = bf16[16,4224]{1,0:T(8,128)(2,1)S(1)} collective-permute-done((bf16[16,4224]{1,0:T(8,128)(2,1)S(1)}, bf16[16,4224]{1,0:T(8,128)(2,1)S(1)}, u32[]{:S(2)}, u32[]{:S(2)}) %collective-permute-start.26) | collective-permute-done | bytes 135200 | tf_op jit(solution)/shard_map/ppermute | solution.py:701
  123.4 2.2 %collective-permute-done.32.refs_3_ = bf16[16,4224]{1,0:T(8,128)(2,1)S(1)} collective-permute-done((bf16[16,4224]{1,0:T(8,128)(2,1)S(1)}, bf16[16,4224]{1,0:T(8,128)(2,1)S(1)}, u32[]{:S(2)}, u32[]{:S(2)}) %collective-permute-start.32) | collective-permute-done | bytes 135200 | tf_op jit(solution)/shard_map/ppermute | solution.py:701
  126.1 1.8 collective-permute-start.29
  132.2 4.6 %hidden_first.1 = (f32[256,768]{1,0:T(8,128)S(1)}, f32[256,768]{1,0:T(8,128)S(1)}, bf16[4096,768]{1,0:T(8,128)(2,1)S(1)}, bf16[4096,768]{1,0:T(8,128)(2,1)S(1)}) custom-call(s32[1]{0:T(128)} %bitcast.me_ref, bf16[256,4224]{1,0:T(8,128)(2,1)S(1)} %place.9.rows_ref.own_ref, bf16[4096,768]{1,0:T(8,128)(2,1)S(1)} %load.2.gate_ref, ...), custom_call_target="tpu_custom_call" | custom-call | flops 3221225472 | bytes 12582912 | tf_op jit(solution)/shard_map/hidden_first/pallas_call | solution.py:561
  136.9 4.6 %hidden_second.1 = (bf16[256,768]{1,0:T(8,128)(2,1)S(1)}, bf16[768,4096]{1,0:T(8,128)(2,1)S(1)}, bf16[768,4096]{1,0:T(8,128)(2,1)S(1)}) custom-call(bf16[256,4224]{1,0:T(8,128)(2,1)S(1)} %collective-permute-done.36.rows_ref, bf16[4096,768]{1,0:T(8,128)(2,1)S(1)} %get-tuple-element.205.gate_ref, bf16[4096,768]{1,0:T(8,128)(2,1)S(1)} %get-tuple-element.206.up_ref, ...), custom_call_target="tpu_custom_call" | custom-call | flops 3221225472 | bytes 12582912 | tf_op jit(solution)/shard_map/hidden_second/pallas_call | solution.py:571
  141.5 2.3 %down.2 = (bf16[128,4096]{1,0:T(8,128)(2,1)S(1)}, bf16[128,4096]{1,0:T(8,128)(2,1)S(1)}) custom-call(bf16[256,768]{1,0:T(8,128)(2,1)S(1)} %get-tuple-element.209.hidden_ref, bf16[768,4096]{1,0:T(8,128)(2,1)S(1)} %get-tuple-element.210.down_ref), custom_call_target="tpu_custom_call" | custom-call | flops 1610612736 | bytes 8388608 | tf_op jit(solution)/shard_map/down/pallas_call | solution.py:604
  144.4 2.3 %down.3 = (bf16[128,4096]{1,0:T(8,128)(2,1)S(1)}, bf16[128,4096]{1,0:T(8,128)(2,1)S(1)}) custom-call(bf16[256,768]{1,0:T(8,128)(2,1)S(1)} %get-tuple-element.209.hidden_ref, bf16[768,4096]{1,0:T(8,128)(2,1)S(1)} %get-tuple-element.221.down_ref), custom_call_target="tpu_custom_call" | custom-call | flops 1610612736 | bytes 8388608 | tf_op jit(solution)/shard_map/down/pallas_call | solution.py:604
  159.9 1.8 %collective-permute-start.42 = (bf16[16,4096]{1,0:T(8,128)(2,1)S(1)}, bf16[16,4096]{1,0:T(8,128)(2,1)S(1)}, u32[]{:S(2)}, u32[]{:S(2)}) collective-permute-start(bf16[16,4096]{1,0:T(8,128)(2,1)S(1)} %get-tuple-element.217), channel_id=1, source_target_pairs={{0,4},{1,5},{4,8},{5,9},{8,12},{9,13},{12,14},{13,15},{14,10},{15,... | collective-permute-start | bytes 393224 | tf_op jit(solution)/shard_map/ppermute | solution.py:700
  165.9 2.0 %collective-permute-start.44 = (bf16[16,4096]{1,0:T(8,128)(2,1)S(1)}, bf16[16,4096]{1,0:T(8,128)(2,1)S(1)}, u32[]{:S(2)}, u32[]{:S(2)}) collective-permute-start(bf16[16,4096]{1,0:T(8,128)(2,1)S(1)} %get-tuple-element.219), channel_id=1, source_target_pairs={{0,4},{1,5},{4,8},{5,9},{8,12},{9,13},{12,14},{13,15},{14,10},{15,... | collective-permute-start | bytes 393224 | tf_op jit(solution)/shard_map/ppermute | solution.py:700
  169.2 1.8 %collective-permute-start.53 = (bf16[16,4096]{1,0:T(8,128)(2,1)S(1)}, bf16[16,4096]{1,0:T(8,128)(2,1)S(1)}, u32[]{:S(2)}, u32[]{:S(2)}) collective-permute-start(bf16[16,4096]{1,0:T(8,128)(2,1)S(1)} %get-tuple-element.230), channel_id=1, source_target_pairs={{0,4},{1,5},{4,8},{5,9},{8,12},{9,13},{12,14},{13,15},{14,10},{15,... | collective-permute-start | bytes 393224 | tf_op jit(solution)/shard_map/ppermute | solution.py:700
  171.3 2.9 %collective-permute-done.53.c_ref = bf16[16,4096]{1,0:T(8,128)(2,1)S(1)} collective-permute-done((bf16[16,4096]{1,0:T(8,128)(2,1)S(1)}, bf16[16,4096]{1,0:T(8,128)(2,1)S(1)}, u32[]{:S(2)}, u32[]{:S(2)}) %collective-permute-start.53) | collective-permute-done | bytes 131104 | tf_op jit(solution)/shard_map/ppermute | solution.py:700
  174.3 1.8 collective-permute-done.54.d_ref
  (140 shorter events, 57.8 us)
Async XLA Ops:
  3.1 10.0 %collective-permute-start.1 = (bf16[256,512]{1,0:T(8,128)(2,1)S(1)}, bf16[256,512]{1,0:T(8,128)(2,1)S(1)}, u32[]{:S(2)}, u32[]{:S(2)}) collective-permute-start(bf16[256,512]{1,0:T(8,128)(2,1)S(1)} %get-tuple-element.119.own_ref.refs_10_), channel_id=1, source_target_pairs={{0,4},{1,5},{4,8},{5,9},{8,12},{9,13},{12,14},{13,15},{14,10},{15,... | collective-permute-start | bytes 786440 | tf_op jit(solution)/shard_map/ppermute | solution.py:700
  6.1 9.2 %collective-permute-start.2 = (bf16[256,512]{1,0:T(8,128)(2,1)S(1)}, bf16[256,512]{1,0:T(8,128)(2,1)S(1)}, u32[]{:S(2)}, u32[]{:S(2)}) collective-permute-start(bf16[256,512]{1,0:T(8,128)(2,1)S(1)} %get-tuple-element.119.own_ref.refs_10_), channel_id=1, source_target_pairs={{4,0},{5,1},{8,4},{9,5},{12,8},{13,9},{14,12},{15,13},{10,14},{11,... | collective-permute-start | bytes 786440 | tf_op jit(solution)/shard_map/ppermute | solution.py:701
  6.1 12.3 %collective-permute-start.6 = (bf16[256,512]{1,0:T(8,128)(2,1)S(1)}, bf16[256,512]{1,0:T(8,128)(2,1)S(1)}, u32[]{:S(2)}, u32[]{:S(2)}) collective-permute-start(bf16[256,512]{1,0:T(8,128)(2,1)S(1)} %get-tuple-element.120), channel_id=1, source_target_pairs={{0,5},{1,4},{4,9},{5,8},{8,13},{9,12},{12,15},{13,14},{14,11},{15,... | collective-permute-start | bytes 786440 | tf_op jit(solution)/shard_map/ppermute | solution.py:725
  7.3 11.3 %collective-permute-start.7 = (bf16[256,512]{1,0:T(8,128)(2,1)S(1)}, bf16[256,512]{1,0:T(8,128)(2,1)S(1)}, u32[]{:S(2)}, u32[]{:S(2)}) collective-permute-start(bf16[256,512]{1,0:T(8,128)(2,1)S(1)} %get-tuple-element.120), channel_id=1, source_target_pairs={{4,1},{5,0},{8,5},{9,4},{12,9},{13,8},{14,13},{15,12},{10,15},{11,... | collective-permute-start | bytes 786440 | tf_op jit(solution)/shard_map/ppermute | solution.py:725
  15.3 8.7 %collective-permute-start.4 = (bf16[256,512]{1,0:T(8,128)(2,1)S(1)}, bf16[256,512]{1,0:T(8,128)(2,1)S(1)}, u32[]{:S(2)}, u32[]{:S(2)}) collective-permute-start(bf16[256,512]{1,0:T(8,128)(2,1)S(1)} %collective-permute-done.1.refs_0_.refs_12_), channel_id=1, source_target_pairs={{0,4},{1,5},{4,8},{5,9},{8,12},{9,13},{12,14},{13,15},{14,10},{15,... | collective-permute-start | bytes 786440 | tf_op jit(solution)/shard_map/ppermute | solution.py:700
  16.9 8.8 %collective-permute-start.5 = (bf16[256,512]{1,0:T(8,128)(2,1)S(1)}, bf16[256,512]{1,0:T(8,128)(2,1)S(1)}, u32[]{:S(2)}, u32[]{:S(2)}) collective-permute-start(bf16[256,512]{1,0:T(8,128)(2,1)S(1)} %collective-permute-done.2.refs_2_.refs_14_), channel_id=1, source_target_pairs={{4,0},{5,1},{8,4},{9,5},{12,8},{13,9},{14,12},{15,13},{10,14},{11,... | collective-permute-start | bytes 786440 | tf_op jit(solution)/shard_map/ppermute | solution.py:701
  18.6 11.0 %collective-permute-start.10 = (bf16[256,512]{1,0:T(8,128)(2,1)S(1)}, bf16[256,512]{1,0:T(8,128)(2,1)S(1)}, u32[]{:S(2)}, u32[]{:S(2)}) collective-permute-start(bf16[256,512]{1,0:T(8,128)(2,1)S(1)} %collective-permute-done.6.refs_1_.refs_13_), channel_id=1, source_target_pairs={{0,4},{1,5},{4,8},{5,9},{8,12},{9,13},{12,14},{13,15},{14,10},{15,... | collective-permute-start | bytes 786440 | tf_op jit(solution)/shard_map/ppermute | solution.py:700
  20.5 10.5 %collective-permute-start.11 = (bf16[256,512]{1,0:T(8,128)(2,1)S(1)}, bf16[256,512]{1,0:T(8,128)(2,1)S(1)}, u32[]{:S(2)}, u32[]{:S(2)}) collective-permute-start(bf16[256,512]{1,0:T(8,128)(2,1)S(1)} %collective-permute-done.7.refs_3_.refs_15_), channel_id=1, source_target_pairs={{4,0},{5,1},{8,4},{9,5},{12,8},{13,9},{14,12},{15,13},{10,14},{11,... | collective-permute-start | bytes 786440 | tf_op jit(solution)/shard_map/ppermute | solution.py:701
  25.7 9.6 %collective-permute-start.8 = (bf16[256,512]{1,0:T(8,128)(2,1)S(1)}, bf16[256,512]{1,0:T(8,128)(2,1)S(1)}, u32[]{:S(2)}, u32[]{:S(2)}) collective-permute-start(bf16[256,512]{1,0:T(8,128)(2,1)S(1)} %collective-permute-done.4.refs_0_.refs_16_), channel_id=1, source_target_pairs={{0,4},{1,5},{4,8},{5,9},{8,12},{9,13},{12,14},{13,15},{14,10},{15,... | collective-permute-start | bytes 786440 | tf_op jit(solution)/shard_map/ppermute | solution.py:700
  28.1 8.8 %collective-permute-start.9 = (bf16[256,512]{1,0:T(8,128)(2,1)S(1)}, bf16[256,512]{1,0:T(8,128)(2,1)S(1)}, u32[]{:S(2)}, u32[]{:S(2)}) collective-permute-start(bf16[256,512]{1,0:T(8,128)(2,1)S(1)} %collective-permute-done.5.refs_2_.refs_18_), channel_id=1, source_target_pairs={{4,0},{5,1},{8,4},{9,5},{12,8},{13,9},{14,12},{15,13},{10,14},{11,... | collective-permute-start | bytes 786440 | tf_op jit(solution)/shard_map/ppermute | solution.py:701
  31.0 9.9 %collective-permute-start.14 = (bf16[256,512]{1,0:T(8,128)(2,1)S(1)}, bf16[256,512]{1,0:T(8,128)(2,1)S(1)}, u32[]{:S(2)}, u32[]{:S(2)}) collective-permute-start(bf16[256,512]{1,0:T(8,128)(2,1)S(1)} %collective-permute-done.10.refs_1_.refs_17_), channel_id=1, source_target_pairs={{0,4},{1,5},{4,8},{5,9},{8,12},{9,13},{12,14},{13,15},{14,10},{15,... | collective-permute-start | bytes 786440 | tf_op jit(solution)/shard_map/ppermute | solution.py:700
  32.6 10.0 %collective-permute-start.15 = (bf16[256,512]{1,0:T(8,128)(2,1)S(1)}, bf16[256,512]{1,0:T(8,128)(2,1)S(1)}, u32[]{:S(2)}, u32[]{:S(2)}) collective-permute-start(bf16[256,512]{1,0:T(8,128)(2,1)S(1)} %collective-permute-done.11.refs_3_.refs_19_), channel_id=1, source_target_pairs={{4,0},{5,1},{8,4},{9,5},{12,8},{13,9},{14,12},{15,13},{10,14},{11,... | collective-permute-start | bytes 786440 | tf_op jit(solution)/shard_map/ppermute | solution.py:701
  37.0 7.9 %collective-permute-start.12 = (bf16[128,512]{1,0:T(8,128)(2,1)S(1)}, bf16[128,512]{1,0:T(8,128)(2,1)S(1)}, u32[]{:S(2)}, u32[]{:S(2)}) collective-permute-start(bf16[128,512]{1,0:T(8,128)(2,1)S(1)} %slice.148), channel_id=1, source_target_pairs={{0,4},{1,5},{4,8},{5,9},{8,12},{9,13},{12,14},{13,15},{14,10},{15,... | collective-permute-start | bytes 393224 | tf_op jit(solution)/shard_map/ppermute | solution.py:700
  54.3 6.9 %collective-permute-start.19 = (bf16[16,4224]{1,0:T(8,128)(2,1)S(1)}, bf16[16,4224]{1,0:T(8,128)(2,1)S(1)}, u32[]{:S(2)}, u32[]{:S(2)}) collective-permute-start(bf16[16,4224]{1,0:T(8,128)(2,1)S(1)} %get-tuple-element.162.refs_0_), channel_id=1, source_target_pairs={{0,4},{1,5},{4,8},{5,9},{8,12},{9,13},{12,14},{13,15},{14,10},{15,... | collective-permute-start | bytes 405512 | tf_op jit(solution)/shard_map/ppermute | solution.py:700
  56.0 6.5 %collective-permute-start.20 = (bf16[16,4224]{1,0:T(8,128)(2,1)S(1)}, bf16[16,4224]{1,0:T(8,128)(2,1)S(1)}, u32[]{:S(2)}, u32[]{:S(2)}) collective-permute-start(bf16[16,4224]{1,0:T(8,128)(2,1)S(1)} %get-tuple-element.162.refs_0_), channel_id=1, source_target_pairs={{4,0},{5,1},{8,4},{9,5},{12,8},{13,9},{14,12},{15,13},{10,14},{11,... | collective-permute-start | bytes 405512 | tf_op jit(solution)/shard_map/ppermute | solution.py:701
  58.2 6.8 %collective-permute-start.22 = (bf16[16,4224]{1,0:T(8,128)(2,1)S(1)}, bf16[16,4224]{1,0:T(8,128)(2,1)S(1)}, u32[]{:S(2)}, u32[]{:S(2)}) collective-permute-start(bf16[16,4224]{1,0:T(8,128)(2,1)S(1)} %get-tuple-element.163.refs_1_), channel_id=1, source_target_pairs={{4,0},{5,1},{8,4},{9,5},{12,8},{13,9},{14,12},{15,13},{10,14},{11,... | collective-permute-start | bytes 405512 | tf_op jit(solution)/shard_map/ppermute | solution.py:701
  65.0 46.3 %collective-permute-start.23 = (bf16[16,4224]{1,0:T(8,128)(2,1)S(1)}, bf16[16,4224]{1,0:T(8,128)(2,1)S(1)}, u32[]{:S(2)}, u32[]{:S(2)}) collective-permute-start(bf16[16,4224]{1,0:T(8,128)(2,1)S(1)} %collective-permute-done.19.refs_0_), channel_id=1, source_target_pairs={{0,4},{1,5},{4,8},{5,9},{8,12},{9,13},{12,14},{13,15},{14,10},{15,... | collective-permute-start | bytes 405512 | tf_op jit(solution)/shard_map/ppermute | solution.py:700
  105.3 7.6 %collective-permute-start.24 = (bf16[16,4224]{1,0:T(8,128)(2,1)S(1)}, bf16[16,4224]{1,0:T(8,128)(2,1)S(1)}, u32[]{:S(2)}, u32[]{:S(2)}) collective-permute-start(bf16[16,4224]{1,0:T(8,128)(2,1)S(1)} %collective-permute-done.20.refs_2_), channel_id=1, source_target_pairs={{4,0},{5,1},{8,4},{9,5},{12,8},{13,9},{14,12},{15,13},{10,14},{11,... | collective-permute-start | bytes 405512 | tf_op jit(solution)/shard_map/ppermute | solution.py:701
  105.3 7.6 %collective-permute-start.27 = (bf16[16,4224]{1,0:T(8,128)(2,1)S(1)}, bf16[16,4224]{1,0:T(8,128)(2,1)S(1)}, u32[]{:S(2)}, u32[]{:S(2)}) collective-permute-start(bf16[16,4224]{1,0:T(8,128)(2,1)S(1)} %collective-permute-done.21.refs_1_), channel_id=1, source_target_pairs={{0,4},{1,5},{4,8},{5,9},{8,12},{9,13},{12,14},{13,15},{14,10},{15,... | collective-permute-start | bytes 405512 | tf_op jit(solution)/shard_map/ppermute | solution.py:700
  114.5 11.1 %collective-permute-start.33 = (bf16[128,4096]{1,0:T(8,128)(2,1)S(1)}, bf16[128,4096]{1,0:T(8,128)(2,1)S(1)}, u32[]{:S(2)}, u32[]{:S(2)}) collective-permute-start(bf16[128,4096]{1,0:T(8,128)(2,1)S(1)} %get-tuple-element.191), channel_id=1, source_target_pairs={{0,1},{1,0},{2,3},{3,2},{4,5},{5,4},{6,7},{7,6},{8,9},{9,8},{10,11... | collective-permute-start | bytes 3145736 | tf_op jit(solution)/shard_map/ppermute | solution.py:702
  114.5 6.4 %collective-permute-start.25 = (bf16[16,4224]{1,0:T(8,128)(2,1)S(1)}, bf16[16,4224]{1,0:T(8,128)(2,1)S(1)}, u32[]{:S(2)}, u32[]{:S(2)}) collective-permute-start(bf16[16,4224]{1,0:T(8,128)(2,1)S(1)} %collective-permute-done.23.refs_0_), channel_id=1, source_target_pairs={{0,4},{1,5},{4,8},{5,9},{8,12},{9,13},{12,14},{13,15},{14,10},{15,... | collective-permute-start | bytes 405512 | tf_op jit(solution)/shard_map/ppermute | solution.py:700
  116.3 6.4 %collective-permute-start.26 = (bf16[16,4224]{1,0:T(8,128)(2,1)S(1)}, bf16[16,4224]{1,0:T(8,128)(2,1)S(1)}, u32[]{:S(2)}, u32[]{:S(2)}) collective-permute-start(bf16[16,4224]{1,0:T(8,128)(2,1)S(1)} %collective-permute-done.24.refs_2_), channel_id=1, source_target_pairs={{4,0},{5,1},{8,4},{9,5},{12,8},{13,9},{14,12},{15,13},{10,14},{11,... | collective-permute-start | bytes 405512 | tf_op jit(solution)/shard_map/ppermute | solution.py:701
  116.5 6.9 %collective-permute-start.31 = (bf16[16,4224]{1,0:T(8,128)(2,1)S(1)}, bf16[16,4224]{1,0:T(8,128)(2,1)S(1)}, u32[]{:S(2)}, u32[]{:S(2)}) collective-permute-start(bf16[16,4224]{1,0:T(8,128)(2,1)S(1)} %collective-permute-done.27.refs_1_), channel_id=1, source_target_pairs={{0,4},{1,5},{4,8},{5,9},{8,12},{9,13},{12,14},{13,15},{14,10},{15,... | collective-permute-start | bytes 405512 | tf_op jit(solution)/shard_map/ppermute | solution.py:700
  118.3 7.3 %collective-permute-start.32 = (bf16[16,4224]{1,0:T(8,128)(2,1)S(1)}, bf16[16,4224]{1,0:T(8,128)(2,1)S(1)}, u32[]{:S(2)}, u32[]{:S(2)}) collective-permute-start(bf16[16,4224]{1,0:T(8,128)(2,1)S(1)} %collective-permute-done.28.refs_3_), channel_id=1, source_target_pairs={{4,0},{5,1},{8,4},{9,5},{12,8},{13,9},{14,12},{15,13},{10,14},{11,... | collective-permute-start | bytes 405512 | tf_op jit(solution)/shard_map/ppermute | solution.py:701
  122.7 8.0 %collective-permute-start.30 = (bf16[16,2176]{1,0:T(8,128)(2,1)S(1)}, bf16[16,2176]{1,0:T(8,128)(2,1)S(1)}, u32[]{:S(2)}, u32[]{:S(2)}) collective-permute-start(bf16[16,2176]{1,0:T(8,128)(2,1)S(1)} %slice.153), channel_id=1, source_target_pairs={{4,0},{5,1},{8,4},{9,5},{12,8},{13,9},{14,12},{15,13},{10,14},{11,... | collective-permute-start | bytes 208904 | tf_op jit(solution)/shard_map/ppermute | solution.py:701
  125.6 6.5 %collective-permute-start.35 = (bf16[16,2176]{1,0:T(8,128)(2,1)S(1)}, bf16[16,2176]{1,0:T(8,128)(2,1)S(1)}, u32[]{:S(2)}, u32[]{:S(2)}) collective-permute-start(bf16[16,2176]{1,0:T(8,128)(2,1)S(1)} %slice.155), channel_id=1, source_target_pairs={{4,0},{5,1},{8,4},{9,5},{12,8},{13,9},{14,12},{15,13},{10,14},{11,... | collective-permute-start | bytes 208904 | tf_op jit(solution)/shard_map/ppermute | solution.py:701
  152.7 6.4 %collective-permute-start.41 = (bf16[16,4096]{1,0:T(8,128)(2,1)S(1)}, bf16[16,4096]{1,0:T(8,128)(2,1)S(1)}, u32[]{:S(2)}, u32[]{:S(2)}) collective-permute-start(bf16[16,4096]{1,0:T(8,128)(2,1)S(1)} %pad_maximum_fusion.1), channel_id=1, source_target_pairs={{4,0},{5,1},{8,4},{9,5},{12,8},{13,9},{14,12},{15,13},{10,14},{11,... | collective-permute-start | bytes 393224 | tf_op jit(solution)/shard_map/ppermute | solution.py:701
  153.3 6.2 %collective-permute-start.40 = (bf16[16,4096]{1,0:T(8,128)(2,1)S(1)}, bf16[16,4096]{1,0:T(8,128)(2,1)S(1)}, u32[]{:S(2)}, u32[]{:S(2)}) collective-permute-start(bf16[16,4096]{1,0:T(8,128)(2,1)S(1)} %pad_maximum_fusion), channel_id=1, source_target_pairs={{0,4},{1,5},{4,8},{5,9},{8,12},{9,13},{12,14},{13,15},{14,10},{15,... | collective-permute-start | bytes 393224 | tf_op jit(solution)/shard_map/ppermute | solution.py:700
  156.1 6.2 %collective-permute-start.50 = (bf16[16,4096]{1,0:T(8,128)(2,1)S(1)}, bf16[16,4096]{1,0:T(8,128)(2,1)S(1)}, u32[]{:S(2)}, u32[]{:S(2)}) collective-permute-start(bf16[16,4096]{1,0:T(8,128)(2,1)S(1)} %pad_maximum_fusion.3), channel_id=1, source_target_pairs={{4,0},{5,1},{8,4},{9,5},{12,8},{13,9},{14,12},{15,13},{10,14},{11,... | collective-permute-start | bytes 393224 | tf_op jit(solution)/shard_map/ppermute | solution.py:701
  162.7 6.4 %collective-permute-start.52 = (bf16[16,4096]{1,0:T(8,128)(2,1)S(1)}, bf16[16,4096]{1,0:T(8,128)(2,1)S(1)}, u32[]{:S(2)}, u32[]{:S(2)}) collective-permute-start(bf16[16,4096]{1,0:T(8,128)(2,1)S(1)} %get-tuple-element.229), channel_id=1, source_target_pairs={{4,0},{5,1},{8,4},{9,5},{12,8},{13,9},{14,12},{15,13},{10,14},{11,... | collective-permute-start | bytes 393224 | tf_op jit(solution)/shard_map/ppermute | solution.py:701
  165.9 11.7 %collective-permute-start.44 = (bf16[16,4096]{1,0:T(8,128)(2,1)S(1)}, bf16[16,4096]{1,0:T(8,128)(2,1)S(1)}, u32[]{:S(2)}, u32[]{:S(2)}) collective-permute-start(bf16[16,4096]{1,0:T(8,128)(2,1)S(1)} %get-tuple-element.219), channel_id=1, source_target_pairs={{0,4},{1,5},{4,8},{5,9},{8,12},{9,13},{12,14},{13,15},{14,10},{15,... | collective-permute-start | bytes 393224 | tf_op jit(solution)/shard_map/ppermute | solution.py:700
  167.9 9.6 %collective-permute-start.45 = (bf16[16,4096]{1,0:T(8,128)(2,1)S(1)}, bf16[16,4096]{1,0:T(8,128)(2,1)S(1)}, u32[]{:S(2)}, u32[]{:S(2)}) collective-permute-start(bf16[16,4096]{1,0:T(8,128)(2,1)S(1)} %get-tuple-element.220), channel_id=1, source_target_pairs={{4,0},{5,1},{8,4},{9,5},{12,8},{13,9},{14,12},{15,13},{10,14},{11,... | collective-permute-start | bytes 393224 | tf_op jit(solution)/shard_map/ppermute | solution.py:701
  (26 other events, 161.0 us)

commit v4 on v3

--- a/solution.py
+++ b/solution.py
@@ -266,8 +266,8 @@
     blocks, (shift_ref, acc_ref, total_ref, gain_ref) = (refs[:2], refs[2:4]), refs[4:8]
     tables, sources = refs[8:10], refs[10 : 12 + 2 * chips]
     refs = refs[12 + 2 * chips :]
-    out_refs, picked_refs = refs[:2], refs[2:4]
-    rows_ref, worst_ref, sem, *scratch = refs[4:]
+    out_refs, picked_ref = refs[:2], refs[2]
+    rows_ref, worst_ref, sem, *scratch = refs[3:]
     q_refs = (q_ref, sib_q_ref)
     tokens, half_width = q_ref.shape
     me = me_ref[0]
@@ -301,11 +301,8 @@
     upper = squares.astype(jnp.bfloat16).astype(jnp.float32)
     lower = (squares - upper).astype(jnp.bfloat16).astype(jnp.float32)
     lane = lax.broadcasted_iota(jnp.int32, squares.shape, 1)
-    rows = (rows * gain_ref[:, columns]).astype(jnp.bfloat16)
-    squares = jnp.where(lane < DH // 2, upper, lower).astype(jnp.bfloat16)
-    for i, ref in enumerate(picked_refs):
-        ref[:, :half_width] = rows[i * CAP : (i + 1) * CAP]
-        ref[:, half_width:] = squares[i * CAP : (i + 1) * CAP]
+    picked_ref[:, :half_width] = (rows * gain_ref[:, columns]).astype(jnp.bfloat16)
+    picked_ref[:, half_width:] = jnp.where(lane < DH // 2, upper, lower).astype(jnp.bfloat16)
 
 
 class Attention:
@@ -360,7 +357,7 @@
 
     def last(self, blocks, shift, state, gain, tables, sources):
         out = pltpu.VMEM((self.tokens, self.width), jnp.bfloat16)
-        picked = pltpu.VMEM((CAP, self.width + DH), jnp.bfloat16)
+        picked = pltpu.VMEM((2 * CAP, self.width + DH), jnp.bfloat16)
         kept = pltpu.VMEM((self.chips, 2 * self.tokens, DH), jnp.bfloat16)
         sums = pltpu.VMEM((self.rows, DH), jnp.float32)
         return self.call(
@@ -368,7 +365,7 @@
             "attend_last",
             (*blocks, shift, *state, gain, *tables),
             sources,
-            [out, out, picked, picked],
+            [out, out, picked],
             [],
             [
                 pltpu.VMEM((2 * CAP, self.width), jnp.float32),
@@ -421,34 +418,6 @@
     )(me, *(in_hbm(x) for x in arrays))
 
 
-def beside_kernel(me_ref, keep_ref, other_ref, out_ref, sems):
-    width = keep_ref.shape[1]
-    core = me_ref[0] % 2
-    copies = []
-    for i, (side, source) in enumerate(((core, keep_ref), (1 - core, other_ref))):
-        columns = pl.ds(pl.multiple_of(side * width, width), width)
-        copies.append(pltpu.make_async_copy(source, out_ref.at[:, columns], sems.at[i]))
-    for copy in copies:
-        copy.start()
-    for copy in copies:
-        copy.wait()
-
-
-def beside(me, keep, other):
-    rows, width = keep.shape
-    anywhere = pl.BlockSpec(memory_space=pl.ANY)
-    return pl.pallas_call(
-        beside_kernel,
-        in_specs=[pl.BlockSpec(memory_space=pltpu.SMEM)] + [anywhere] * 2,
-        out_specs=anywhere,
-        out_shape=jax.ShapeDtypeStruct((rows, 2 * width), keep.dtype),
-        scratch_shapes=[pltpu.SemaphoreType.DMA((2,))],
-        compiler_params=pltpu.CompilerParams(vmem_limit_bytes=MIB),
-        cost_estimate=SMALL,
-        name="beside",
-    )(me, keep, other)
-
-
 def load_kernel(me_ref, source_ref, target_ref, sem):
     copy = pltpu.make_async_copy(half_rows(me_ref, source_ref, False), target_ref, sem)
     copy.start()
@@ -476,13 +445,17 @@
 
 def place_kernel(spots, *refs):
     blocks, out_ref = refs[: len(spots)], refs[-1]
-    for (row, column), ref in zip(spots, blocks):
-        out_ref[row : row + ref.shape[0], column : column + ref.shape[1]] = ref[...]
-
-
-def place(blocks, spots, shape, rows=None):
+    middle = out_ref.shape[0] // 2
+    for index, ref in zip(spots, blocks):
+        for core in range(2):
+            row = core * middle + index * CAP
+            out_ref[row : row + CAP] = ref[core * CAP : (core + 1) * CAP]
+
+
+def place(blocks, spots, rows):
     vmem = pl.BlockSpec(memory_space=pltpu.VMEM)
-    earlier = [] if rows is None else [rows]
+    earlier = [] if isinstance(rows, tuple) else [rows]
+    shape = rows.shape if earlier else rows
     return pl.pallas_call(
         functools.partial(place_kernel, spots),
         in_specs=[vmem] * (len(blocks) + len(earlier)),
@@ -493,6 +466,26 @@
         cost_estimate=SMALL,
         name="place",
     )(*blocks, *earlier)
+
+
+def place_far_kernel(low_ref, high_ref, _, out_ref):
+    middle, row = out_ref.shape[0] // 2, out_ref.shape[0] // 2 - CAP
+    out_ref[row : row + CAP] = low_ref[...]
+    out_ref[middle + row : middle + row + CAP] = high_ref[...]
+
+
+def place_far(low, high, rows):
+    vmem = pl.BlockSpec(memory_space=pltpu.VMEM)
+    return pl.pallas_call(
+        place_far_kernel,
+        in_specs=[vmem] * 3,
+        out_specs=vmem,
+        out_shape=pltpu.VMEM(rows.shape, jnp.bfloat16),
+        input_output_aliases={2: 0},
+        compiler_params=pltpu.CompilerParams(vmem_limit_bytes=4 * MIB),
+        cost_estimate=SMALL,
+        name="place",
+    )(low, high, rows)
 
 
 def contract(rows_ref, gate_ref, up_ref, gate_sum, up_sum, order):
@@ -582,7 +575,19 @@
     return hidden, downs
 
 
-def down_kernel(hidden_ref, down_ref, own_ref, sib_ref):
+def down_kernel(hidden_ref, down_ref, *refs):
+    copies = []
+    if len(refs) == 2:
+        own_ref, sib_ref = refs
+    else:
+        me_ref, *parts, own_ref, sib_ref, result_ref, sems = refs
+        width = parts[0].shape[1]
+        core = me_ref[0] % 2
+        for i, (side, source) in enumerate(zip((core, 1 - core), parts)):
+            columns = pl.ds(pl.multiple_of(side * width, width), width)
+            copies.append(pltpu.make_async_copy(source, result_ref.at[:, columns], sems.at[i]))
+    for copy in copies:
+        copy.start()
     middle, width = own_ref.shape
     cols = min(1024, width)
 
@@ -595,17 +600,25 @@
         return carry
 
     lax.fori_loop(0, width // cols, one_part, 0)
-
-
-def down_call(hidden, w_down):
+    for copy in copies:
+        copy.wait()
+
+
+def down_call(hidden, w_down, halves=()):
     rows, units = hidden.shape
     width = w_down.shape[1]
-    vmem = pl.BlockSpec(memory_space=pltpu.VMEM)
+    vmem, anywhere = pl.BlockSpec(memory_space=pltpu.VMEM), pl.BlockSpec(memory_space=pl.ANY)
+    more = [pl.BlockSpec(memory_space=pltpu.SMEM), anywhere, anywhere] if halves else []
+    outs = [pltpu.VMEM((rows // 2, width), jnp.bfloat16)] * 2
+    if halves:
+        tokens, part = halves[1].shape
+        outs.append(jax.ShapeDtypeStruct((tokens, 2 * part), jnp.bfloat16))
     return pl.pallas_call(
         down_kernel,
-        in_specs=[vmem] * 2,
-        out_specs=[vmem] * 2,
-        out_shape=[pltpu.VMEM((rows // 2, width), jnp.bfloat16)] * 2,
+        in_specs=[vmem] * 2 + more,
+        out_specs=[vmem] * 2 + [anywhere] * (len(outs) - 2),
+        out_shape=outs,
+        scratch_shapes=[pltpu.SemaphoreType.DMA((2,))] if halves else [],
         compiler_params=pltpu.CompilerParams(vmem_limit_bytes=8 * MIB),
         cost_estimate=pl.CostEstimate(
             flops=2 * rows * width * units,
@@ -613,7 +626,7 @@
             transcendentals=0,
         ),
         name="down",
-    )(hidden, w_down)
+    )(hidden, w_down, *halves)
 
 
 def spread_kernel(a_ref, b_ref, c_ref, d_ref, table_ref, *rest):
@@ -744,47 +757,37 @@
         state, _ = attention.step(blocks, [step, step, -step, -step], shift, state)
     opposite, state = lax.optimization_barrier((opposite, state))
     sources += opposite
-    mine, theirs, *picked = attention.last(
+    mine, theirs, picked = attention.last(
         opposite, shift, state, norm_gain[None, :], (table, sib_table), sources
     )
 
     picked, w_gate = lax.optimization_barrier((picked, w_gate))
-    chains = [(go_right(x), go_left(x)) for x in picked]
-    width = picked[0].shape[1]
-    middle = width // DH // 2 * DH
-    shape = (2 * chips * CAP, width)
-    spots = lambda index: [(index * CAP, 0), ((chips + index) * CAP, 0)]
-    rows = place(picked, spots(0), shape)
-    loaded = [load(me, w_gate)]
+    from_left, from_right = go_right(picked), go_left(picked)
+    rows = place([picked], [0], (2 * chips * CAP, picked.shape[1]))
+    loaded, theirs = [load(me, w_gate)], swap(theirs)
     for step in range(1, half):
+        from_left, rows, loaded = lax.optimization_barrier((from_left, rows, loaded))
+        from_right, _, rows = lax.optimization_barrier((from_right, from_left, rows))
+        blocks = [from_left, from_right]
+        if step < half - 1:
+            from_left, from_right = go_right(from_left), go_left(from_right)
+        else:
+            far = go_right(from_left[:CAP]), go_left(from_right[CAP:])
+        rows = place(blocks, [step, half - 1 + step], rows)
         if step == 1:
-            chains, rows, loaded = lax.optimization_barrier((chains, rows, loaded))
-        *chains[0], rows, loaded = lax.optimization_barrier((*chains[0], rows, loaded))
-        chains[1], _, rows, theirs = lax.optimization_barrier((chains[1], chains[0], rows, theirs))
-        blocks = [chain[side] for side in range(2) for chain in chains]
-        if step < half - 1:
-            chains = [(go_right(chain[0]), go_left(chain[1])) for chain in chains]
-        else:
-            far = [
-                part
-                for chain in chains
-                for part in (go_right(chain[0][:, :middle]), go_left(chain[1][:, middle:]))
-            ]
-        rows = place(blocks, spots(step) + spots(half - 1 + step), shape, rows)
-        if step == 1:
+            rows, w_up = lax.optimization_barrier((rows, w_up))
             loaded = loaded + [load(me, w_up)]
-        elif step == 2:
-            theirs = swap(theirs)
-    result = beside(me, mine, theirs)
-    far, rows, result = lax.optimization_barrier((far, rows, result))
-    places = [(row, column) for row, _ in spots(chips - 1) for column in (0, middle)]
-    rows = place(far, places, shape, rows)
+    far, rows = lax.optimization_barrier((far, rows))
+    rows = place_far(*far, rows)
     hidden, downs = hidden_calls(me, rows, swap(rows), loaded, w_gate, w_up, w_down)
 
     sums = []
     for piece in range(PIECES):
-        mine, theirs = down_call(hidden, downs[piece])
-        sums.append(reduce_chip_rows(mine, swap(theirs), half, chips, go_right, go_left))
+        if piece == 0:
+            own, sib, result = down_call(hidden, downs[piece], (me, mine, theirs))
+        else:
+            own, sib = down_call(hidden, downs[piece])
+        sums.append(reduce_chip_rows(own, swap(sib), half, chips, go_right, go_left))
     mixed = None
     for piece, parts in enumerate(run_together(sums)):
         mixed = spread_call(parts, weighted, piece, PIECES, mixed)

time: 179 us -> 174 us (0.972)
  starting transfers between devices: 92.9 us -> 45.4 us
  waiting for transfers between devices: 49.9 us -> 93.3 us
    ppermute x23 -> x19, starting transfers between devices: 82.1 us -> 26.9 us  [per_device(): go_right = lambda x: lax.ppermute(x, 'ctx', right)]
    ppermute x23 -> x19, waiting for transfers between devices: 28.8 us -> 63 us  [per_device(): go_left = lambda x: lax.ppermute(x, 'ctx', left)]
    ppermute x23 -> x19, waiting for transfers between devices: 19.5 us -> 29.1 us  [per_device(): go_right = lambda x: lax.ppermute(x, 'ctx', right)]
    ppermute x23 -> x19, starting transfers between devices: 7.21 us -> 14.4 us  [per_device(): go_left = lambda x: lax.ppermute(x, 'ctx', left)]
  transfers between devices with their start and end apart: 55 -> 47, of which waited for: 36 -> 36; matrix products, arithmetic and copies ran while one was open for 1% -> 1% of each run, Pallas kernels for 11% -> 13%
where the time goes in v4:
time: 174 us
  waiting for transfers between devices  93.3 us (54%)
  starting transfers between devices  45.4 us (26%)
  Pallas kernels  32.9 us (19%)
    ppermute x19, waiting for transfers between devices, per_device(): go_left = lambda x: lax.ppermute(x, 'ctx', left)  63 us
    ppermute x19, waiting for transfers between devices, per_device(): go_right = lambda x: lax.ppermute(x, 'ctx', right)  29.1 us
    ppermute x19, starting transfers between devices, per_device(): go_right = lambda x: lax.ppermute(x, 'ctx', right)  26.9 us
    ppermute x19, starting transfers between devices, per_device(): go_left = lambda x: lax.ppermute(x, 'ctx', left)  14.4 us
    pallas_call x5, Pallas kernels, call(): pl.pallas_call(kernel, in_specs=[pl.BlockSpec(memory_space=pltpu.SMEM)] +...  8.36 us
    pallas_call x2, Pallas kernels, load(): pl.pallas_call(load_kernel, in_specs=[pl.BlockSpec(memory_space=pltpu.SME...  5.61 us
    pallas_call x2, Pallas kernels, down_call(): pl.pallas_call(down_kernel, in_specs=[vmem] * 2 + more, out_specs=[vmem]...  4.64 us
    pallas_call x1, Pallas kernels, hidden_calls(): pl.pallas_call(first_kernel, in_specs=[pl.BlockSpec(memory_space=pltpu.SM...  4.63 us
  transfers between devices with their start and end apart: 47, of which 36 were waited for; matrix products, arithmetic and copies ran while one was open for 1% of the time, Pallas kernels for 13%

profile of v4, /device:TPU:0, one launch (start us, length us, event | category | flops | bytes accessed | tf_op | source)
XLA Modules:
  0.0 173.6 jit_solution(1845772940186637563)
XLA Ops:
  0.7 1.9 %halves.1 = (bf16[256,512]{1,0:T(8,128)(2,1)S(1)}, bf16[256,512]{1,0:T(8,128)(2,1)S(1)}, bf16[128,4096]{1,0:T(8,128)(2,1)S(1)}, bf16[128,4096]{1,0:T(8,128)(2,1)S(1)}) custom-call(s32[1]{0:T(128)} %bitcast.me_ref.refs_0_, bf16[128,1024]{1,0:T(8,128)(2,1)} %refs_0_.1, bf16[128,1024]{1,0:T(8,128)(2,1)} %refs_1_.1, bf16[128,8192]{1,0:T(8,128)(2,1)} %refs_2_.1), custom_call_target="tpu_custom_call" | custom-call | flops 1 | bytes 1 | tf_op jit(solution)/shard_map/halves/pallas_call | solution.py:409
  3.1 3.0 %collective-permute-start.1 = (bf16[256,512]{1,0:T(8,128)(2,1)S(1)}, bf16[256,512]{1,0:T(8,128)(2,1)S(1)}, u32[]{:S(2)}, u32[]{:S(2)}) collective-permute-start(bf16[256,512]{1,0:T(8,128)(2,1)S(1)} %get-tuple-element.102.own_ref.refs_10_), channel_id=1, source_target_pairs={{0,4},{1,5},{4,8},{5,9},{8,12},{9,13},{12,14},{13,15},{14,10},{15,... | collective-permute-start | bytes 786440 | tf_op jit(solution)/shard_map/ppermute | solution.py:713
  8.3 3.8 %attend_own.1 = (f32[4,2048,128]{2,1,0:T(8,128)S(1)}, f32[4,2048,128]{2,1,0:T(8,128)S(1)}, f32[4,2048,128]{2,1,0:T(8,128)S(1)}) custom-call(s32[1]{0:T(128)} %bitcast.me_ref.refs_0_, bf16[128,4096]{1,0:T(8,128)(2,1)S(1)} %get-tuple-element.100.q_ref, bf16[128,4096]{1,0:T(8,128)(2,1)S(1)} %collective-permute-done.sib_q_ref, ...), custom_call_target="tpu_custom_call" | custom-call | flops 1 | bytes 1 | tf_op jit(solution)/shard_map/attend_own/pallas_call | solution.py:317
  13.2 2.2 %collective-permute-done.2.refs_2_.refs_14_ = bf16[256,512]{1,0:T(8,128)(2,1)S(1)} collective-permute-done((bf16[256,512]{1,0:T(8,128)(2,1)S(1)}, bf16[256,512]{1,0:T(8,128)(2,1)S(1)}, u32[]{:S(2)}, u32[]{:S(2)}) %collective-permute-start.2) | collective-permute-done | bytes 262176 | tf_op jit(solution)/shard_map/ppermute | solution.py:714
  18.6 1.9 %collective-permute-start.10 = (bf16[256,512]{1,0:T(8,128)(2,1)S(1)}, bf16[256,512]{1,0:T(8,128)(2,1)S(1)}, u32[]{:S(2)}, u32[]{:S(2)}) collective-permute-start(bf16[256,512]{1,0:T(8,128)(2,1)S(1)} %collective-permute-done.6.refs_1_.refs_13_), channel_id=1, source_target_pairs={{0,4},{1,5},{4,8},{5,9},{8,12},{9,13},{12,14},{13,15},{14,10},{15,... | collective-permute-start | bytes 786440 | tf_op jit(solution)/shard_map/ppermute | solution.py:713
  20.7 3.3 %collective-permute-done.4.refs_0_.refs_16_ = bf16[256,512]{1,0:T(8,128)(2,1)S(1)} collective-permute-done((bf16[256,512]{1,0:T(8,128)(2,1)S(1)}, bf16[256,512]{1,0:T(8,128)(2,1)S(1)}, u32[]{:S(2)}, u32[]{:S(2)}) %collective-permute-start.4) | collective-permute-done | bytes 262176 | tf_op jit(solution)/shard_map/ppermute | solution.py:713
  24.0 1.7 %collective-permute-done.5.refs_2_.refs_18_ = bf16[256,512]{1,0:T(8,128)(2,1)S(1)} collective-permute-done((bf16[256,512]{1,0:T(8,128)(2,1)S(1)}, bf16[256,512]{1,0:T(8,128)(2,1)S(1)}, u32[]{:S(2)}, u32[]{:S(2)}) %collective-permute-start.5) | collective-permute-done | bytes 262176 | tf_op jit(solution)/shard_map/ppermute | solution.py:714
  25.7 2.4 %collective-permute-start.8 = (bf16[256,512]{1,0:T(8,128)(2,1)S(1)}, bf16[256,512]{1,0:T(8,128)(2,1)S(1)}, u32[]{:S(2)}, u32[]{:S(2)}) collective-permute-start(bf16[256,512]{1,0:T(8,128)(2,1)S(1)} %collective-permute-done.4.refs_0_.refs_16_), channel_id=1, source_target_pairs={{0,4},{1,5},{4,8},{5,9},{8,12},{9,13},{12,14},{13,15},{14,10},{15,... | collective-permute-start | bytes 786440 | tf_op jit(solution)/shard_map/ppermute | solution.py:713
  33.2 2.1 %collective-permute-done.8.refs_0_.refs_20_ = bf16[256,512]{1,0:T(8,128)(2,1)S(1)} collective-permute-done((bf16[256,512]{1,0:T(8,128)(2,1)S(1)}, bf16[256,512]{1,0:T(8,128)(2,1)S(1)}, u32[]{:S(2)}, u32[]{:S(2)}) %collective-permute-start.8) | collective-permute-done | bytes 262176 | tf_op jit(solution)/shard_map/ppermute | solution.py:713
  37.0 3.7 %collective-permute-done.14.refs_1_.refs_21_ = bf16[256,512]{1,0:T(8,128)(2,1)S(1)} collective-permute-done((bf16[256,512]{1,0:T(8,128)(2,1)S(1)}, bf16[256,512]{1,0:T(8,128)(2,1)S(1)}, u32[]{:S(2)}, u32[]{:S(2)}) %collective-permute-start.14) | collective-permute-done | bytes 262176 | tf_op jit(solution)/shard_map/ppermute | solution.py:713
  40.7 1.9 %collective-permute-done.15.refs_3_.refs_23_ = bf16[256,512]{1,0:T(8,128)(2,1)S(1)} collective-permute-done((bf16[256,512]{1,0:T(8,128)(2,1)S(1)}, bf16[256,512]{1,0:T(8,128)(2,1)S(1)}, u32[]{:S(2)}, u32[]{:S(2)}) %collective-permute-start.15) | collective-permute-done | bytes 262176 | tf_op jit(solution)/shard_map/ppermute | solution.py:714
  46.9 2.1 %collective-permute-done.16.refs_2_.refs_26_ = bf16[128,512]{1,0:T(8,128)(2,1)S(1)} collective-permute-done((bf16[128,512]{1,0:T(8,128)(2,1)S(1)}, bf16[128,512]{1,0:T(8,128)(2,1)S(1)}, u32[]{:S(2)}, u32[]{:S(2)}) %collective-permute-start.16) | collective-permute-done | bytes 131104 | tf_op jit(solution)/shard_map/ppermute | solution.py:713
  49.0 1.7 collective-permute-done.17.refs_3_.refs_27_
  52.4 4.4 %attend_last.1 = (bf16[128,4096]{1,0:T(8,128)(2,1)S(1)}, bf16[128,4096]{1,0:T(8,128)(2,1)S(1)}, bf16[32,4224]{1,0:T(8,128)(2,1)S(1)}) custom-call(s32[1]{0:T(128)} %bitcast.me_ref.refs_0_, bf16[128,4096]{1,0:T(8,128)(2,1)S(1)} %get-tuple-element.100.q_ref, bf16[128,4096]{1,0:T(8,128)(2,1)S(1)} %collective-permute-done.sib_q_ref, ...), custom_call_target="tpu_custom_call" | custom-call | flops 1 | bytes 1 | tf_op jit(solution)/shard_map/attend_last/pallas_call | solution.py:317
  58.9 2.8 %load.2.gate_ref = bf16[4096,768]{1,0:T(8,128)(2,1)S(1)} custom-call(s32[1]{0:T(128)} %bitcast.me_ref.refs_0_, bf16[8192,768]{1,0:T(8,128)(2,1)} %refs_0_.2), custom_call_target="tpu_custom_call" | custom-call | flops 1 | bytes 1 | tf_op jit(solution)/shard_map/load/pallas_call | solution.py:434
  61.7 2.5 %collective-permute-done.19.refs_0_ = bf16[32,4224]{1,0:T(8,128)(2,1)S(1)} collective-permute-done((bf16[32,4224]{1,0:T(8,128)(2,1)S(1)}, bf16[32,4224]{1,0:T(8,128)(2,1)S(1)}, u32[]{:S(2)}, u32[]{:S(2)}) %collective-permute-start.19) | collective-permute-done | bytes 270368 | tf_op jit(solution)/shard_map/ppermute | solution.py:713
  64.3 2.3 %collective-permute-start.20 = (bf16[32,4224]{1,0:T(8,128)(2,1)S(1)}, bf16[32,4224]{1,0:T(8,128)(2,1)S(1)}, u32[]{:S(2)}, u32[]{:S(2)}) collective-permute-start(bf16[32,4224]{1,0:T(8,128)(2,1)S(1)} %collective-permute-done.19.refs_0_), channel_id=1, source_target_pairs={{0,4},{1,5},{4,8},{5,9},{8,12},{9,13},{12,14},{13,15},{14,10},{15,... | collective-permute-start | bytes 811016 | tf_op jit(solution)/shard_map/ppermute | solution.py:713
  67.0 2.8 %load.3.up_ref = bf16[4096,768]{1,0:T(8,128)(2,1)S(1)} custom-call(s32[1]{0:T(128)} %bitcast.me_ref.refs_0_, bf16[8192,768]{1,0:T(8,128)(2,1)} %refs_1_.2), custom_call_target="tpu_custom_call" | custom-call | flops 1 | bytes 1 | tf_op jit(solution)/shard_map/load/pallas_call | solution.py:434
  69.9 2.3 %collective-permute-done.20.refs_0_ = bf16[32,4224]{1,0:T(8,128)(2,1)S(1)} collective-permute-done((bf16[32,4224]{1,0:T(8,128)(2,1)S(1)}, bf16[32,4224]{1,0:T(8,128)(2,1)S(1)}, u32[]{:S(2)}, u32[]{:S(2)}) %collective-permute-start.20) | collective-permute-done | bytes 270368 | tf_op jit(solution)/shard_map/ppermute | solution.py:713
  72.1 2.5 %collective-permute-start.22 = (bf16[32,4224]{1,0:T(8,128)(2,1)S(1)}, bf16[32,4224]{1,0:T(8,128)(2,1)S(1)}, u32[]{:S(2)}, u32[]{:S(2)}) collective-permute-start(bf16[32,4224]{1,0:T(8,128)(2,1)S(1)} %collective-permute-done.20.refs_0_), channel_id=1, source_target_pairs={{0,4},{1,5},{4,8},{5,9},{8,12},{9,13},{12,14},{13,15},{14,10},{15,... | collective-permute-start | bytes 811016 | tf_op jit(solution)/shard_map/ppermute | solution.py:713
  75.1 4.2 %collective-permute-done.22.refs_0_ = bf16[32,4224]{1,0:T(8,128)(2,1)S(1)} collective-permute-done((bf16[32,4224]{1,0:T(8,128)(2,1)S(1)}, bf16[32,4224]{1,0:T(8,128)(2,1)S(1)}, u32[]{:S(2)}, u32[]{:S(2)}) %collective-permute-start.22) | collective-permute-done | bytes 270368 | tf_op jit(solution)/shard_map/ppermute | solution.py:713
  79.3 42.5 %collective-permute-done.25.refs_1_ = bf16[32,4224]{1,0:T(8,128)(2,1)S(1)} collective-permute-done((bf16[32,4224]{1,0:T(8,128)(2,1)S(1)}, bf16[32,4224]{1,0:T(8,128)(2,1)S(1)}, u32[]{:S(2)}, u32[]{:S(2)}) %collective-permute-start.25) | collective-permute-done | bytes 270368 | tf_op jit(solution)/shard_map/ppermute | solution.py:714
  124.0 2.9 %collective-permute-done.26.high_ref = bf16[16,4224]{1,0:T(8,128)(2,1)S(1)} collective-permute-done((bf16[16,4224]{1,0:T(8,128)(2,1)S(1)}, bf16[16,4224]{1,0:T(8,128)(2,1)S(1)}, u32[]{:S(2)}, u32[]{:S(2)}) %collective-permute-start.26) | collective-permute-done | bytes 135200 | tf_op jit(solution)/shard_map/ppermute | solution.py:714
  128.3 4.6 %hidden_first.1 = (f32[256,768]{1,0:T(8,128)S(1)}, f32[256,768]{1,0:T(8,128)S(1)}, bf16[4096,768]{1,0:T(8,128)(2,1)S(1)}, bf16[4096,768]{1,0:T(8,128)(2,1)S(1)}) custom-call(s32[1]{0:T(128)} %bitcast.me_ref.refs_0_, bf16[256,4224]{1,0:T(8,128)(2,1)S(1)} %place.9.rows_ref.own_ref, bf16[4096,768]{1,0:T(8,128)(2,1)S(1)} %load.2.gate_ref, ...), custom_call_target="tpu_custom_call" | custom-call | flops 3221225472 | bytes 12582912 | tf_op jit(solution)/shard_map/hidden_first/pallas_call | solution.py:554
  132.9 4.6 %hidden_second.1 = (bf16[256,768]{1,0:T(8,128)(2,1)S(1)}, bf16[768,4096]{1,0:T(8,128)(2,1)S(1)}, bf16[768,4096]{1,0:T(8,128)(2,1)S(1)}) custom-call(bf16[256,4224]{1,0:T(8,128)(2,1)S(1)} %collective-permute-done.27.rows_ref, bf16[4096,768]{1,0:T(8,128)(2,1)S(1)} %get-tuple-element.168.gate_ref, bf16[4096,768]{1,0:T(8,128)(2,1)S(1)} %get-tuple-element.169.up_ref, ...), custom_call_target="tpu_custom_call" | custom-call | flops 3221225472 | bytes 12582912 | tf_op jit(solution)/shard_map/hidden_second/pallas_call | solution.py:564
  137.6 2.3 %down.2 = (bf16[128,4096]{1,0:T(8,128)(2,1)S(1)}, bf16[128,4096]{1,0:T(8,128)(2,1)S(1)}, bf16[128,8192]{1,0:T(8,128)(2,1)}) custom-call(bf16[256,768]{1,0:T(8,128)(2,1)S(1)} %get-tuple-element.172.hidden_ref, bf16[768,4096]{1,0:T(8,128)(2,1)S(1)} %get-tuple-element.173.down_ref, s32[1]{0:T(128)} %bitcast.me_ref.refs_0_, ...), custom_call_target="tpu_custom_call" | custom-call | flops 1610612736 | bytes 8388608 | tf_op jit(solution)/shard_map/down/pallas_call | solution.py:616
  140.1 2.3 %down.3 = (bf16[128,4096]{1,0:T(8,128)(2,1)S(1)}, bf16[128,4096]{1,0:T(8,128)(2,1)S(1)}) custom-call(bf16[256,768]{1,0:T(8,128)(2,1)S(1)} %get-tuple-element.172.hidden_ref, bf16[768,4096]{1,0:T(8,128)(2,1)S(1)} %get-tuple-element.177.down_ref), custom_call_target="tpu_custom_call" | custom-call | flops 1610612736 | bytes 8388608 | tf_op jit(solution)/shard_map/down/pallas_call | solution.py:616
  143.0 1.8 %collective-permute-start.40 = (bf16[16,2048]{1,0:T(8,128)(2,1)S(1)}, bf16[16,2048]{1,0:T(8,128)(2,1)S(1)}, u32[]{:S(2)}, u32[]{:S(2)}) collective-permute-start(bf16[16,2048]{1,0:T(8,128)(2,1)S(1)} %get-tuple-element.191), channel_id=1, source_target_pairs={{4,0},{5,1},{8,4},{9,5},{12,8},{13,9},{14,12},{15,13},{10,14},{11,... | collective-permute-start | bytes 196616 | tf_op jit(solution)/shard_map/ppermute | solution.py:714
  145.3 1.8 %collective-permute-start.31 = (bf16[16,2048]{1,0:T(8,128)(2,1)S(1)}, bf16[16,2048]{1,0:T(8,128)(2,1)S(1)}, u32[]{:S(2)}, u32[]{:S(2)}) collective-permute-start(bf16[16,2048]{1,0:T(8,128)(2,1)S(1)} %get-tuple-element.181), channel_id=1, source_target_pairs={{4,0},{5,1},{8,4},{9,5},{12,8},{13,9},{14,12},{15,13},{10,14},{11,... | collective-permute-start | bytes 196616 | tf_op jit(solution)/shard_map/ppermute | solution.py:714
  149.4 1.7 %collective-permute-start.42 = (bf16[16,4096]{1,0:T(8,128)(2,1)S(1)}, bf16[16,4096]{1,0:T(8,128)(2,1)S(1)}, u32[]{:S(2)}, u32[]{:S(2)}) collective-permute-start(bf16[16,4096]{1,0:T(8,128)(2,1)S(1)} %pad_maximum_fusion.3), channel_id=1, source_target_pairs={{4,0},{5,1},{8,4},{9,5},{12,8},{13,9},{14,12},{15,13},{10,14},{11,... | collective-permute-start | bytes 393224 | tf_op jit(solution)/shard_map/ppermute | solution.py:714
  152.2 2.0 %collective-permute-start.33 = (bf16[16,4096]{1,0:T(8,128)(2,1)S(1)}, bf16[16,4096]{1,0:T(8,128)(2,1)S(1)}, u32[]{:S(2)}, u32[]{:S(2)}) collective-permute-start(bf16[16,4096]{1,0:T(8,128)(2,1)S(1)} %pad_maximum_fusion.1), channel_id=1, source_target_pairs={{4,0},{5,1},{8,4},{9,5},{12,8},{13,9},{14,12},{15,13},{10,14},{11,... | collective-permute-start | bytes 393224 | tf_op jit(solution)/shard_map/ppermute | solution.py:714
  161.4 1.7 collective-permute-done.44
  (121 shorter events, 48.7 us)
Async XLA Ops:
  2.5 5.8 %collective-permute-start = (bf16[128,4096]{1,0:T(8,128)(2,1)S(1)}, bf16[128,4096]{1,0:T(8,128)(2,1)S(1)}, u32[]{:S(2)}, u32[]{:S(2)}) collective-permute-start(bf16[128,4096]{1,0:T(8,128)(2,1)S(1)} %get-tuple-element.101), channel_id=1, source_target_pairs={{0,1},{1,0},{2,3},{3,2},{4,5},{5,4},{6,7},{7,6},{8,9},{9,8},{10,11... | collective-permute-start | bytes 3145736 | tf_op jit(solution)/shard_map/ppermute | solution.py:715
  3.1 10.0 %collective-permute-start.1 = (bf16[256,512]{1,0:T(8,128)(2,1)S(1)}, bf16[256,512]{1,0:T(8,128)(2,1)S(1)}, u32[]{:S(2)}, u32[]{:S(2)}) collective-permute-start(bf16[256,512]{1,0:T(8,128)(2,1)S(1)} %get-tuple-element.102.own_ref.refs_10_), channel_id=1, source_target_pairs={{0,4},{1,5},{4,8},{5,9},{8,12},{9,13},{12,14},{13,15},{14,10},{15,... | collective-permute-start | bytes 786440 | tf_op jit(solution)/shard_map/ppermute | solution.py:713
  6.1 9.2 %collective-permute-start.2 = (bf16[256,512]{1,0:T(8,128)(2,1)S(1)}, bf16[256,512]{1,0:T(8,128)(2,1)S(1)}, u32[]{:S(2)}, u32[]{:S(2)}) collective-permute-start(bf16[256,512]{1,0:T(8,128)(2,1)S(1)} %get-tuple-element.102.own_ref.refs_10_), channel_id=1, source_target_pairs={{4,0},{5,1},{8,4},{9,5},{12,8},{13,9},{14,12},{15,13},{10,14},{11,... | collective-permute-start | bytes 786440 | tf_op jit(solution)/shard_map/ppermute | solution.py:714
  6.1 12.3 %collective-permute-start.6 = (bf16[256,512]{1,0:T(8,128)(2,1)S(1)}, bf16[256,512]{1,0:T(8,128)(2,1)S(1)}, u32[]{:S(2)}, u32[]{:S(2)}) collective-permute-start(bf16[256,512]{1,0:T(8,128)(2,1)S(1)} %get-tuple-element.103), channel_id=1, source_target_pairs={{0,5},{1,4},{4,9},{5,8},{8,13},{9,12},{12,15},{13,14},{14,11},{15,... | collective-permute-start | bytes 786440 | tf_op jit(solution)/shard_map/ppermute | solution.py:738
  7.3 11.3 %collective-permute-start.7 = (bf16[256,512]{1,0:T(8,128)(2,1)S(1)}, bf16[256,512]{1,0:T(8,128)(2,1)S(1)}, u32[]{:S(2)}, u32[]{:S(2)}) collective-permute-start(bf16[256,512]{1,0:T(8,128)(2,1)S(1)} %get-tuple-element.103), channel_id=1, source_target_pairs={{4,1},{5,0},{8,5},{9,4},{12,9},{13,8},{14,13},{15,12},{10,15},{11,... | collective-permute-start | bytes 786440 | tf_op jit(solution)/shard_map/ppermute | solution.py:738
  15.3 8.7 %collective-permute-start.4 = (bf16[256,512]{1,0:T(8,128)(2,1)S(1)}, bf16[256,512]{1,0:T(8,128)(2,1)S(1)}, u32[]{:S(2)}, u32[]{:S(2)}) collective-permute-start(bf16[256,512]{1,0:T(8,128)(2,1)S(1)} %collective-permute-done.1.refs_0_.refs_12_), channel_id=1, source_target_pairs={{0,4},{1,5},{4,8},{5,9},{8,12},{9,13},{12,14},{13,15},{14,10},{15,... | collective-permute-start | bytes 786440 | tf_op jit(solution)/shard_map/ppermute | solution.py:713
  16.9 8.8 %collective-permute-start.5 = (bf16[256,512]{1,0:T(8,128)(2,1)S(1)}, bf16[256,512]{1,0:T(8,128)(2,1)S(1)}, u32[]{:S(2)}, u32[]{:S(2)}) collective-permute-start(bf16[256,512]{1,0:T(8,128)(2,1)S(1)} %collective-permute-done.2.refs_2_.refs_14_), channel_id=1, source_target_pairs={{4,0},{5,1},{8,4},{9,5},{12,8},{13,9},{14,12},{15,13},{10,14},{11,... | collective-permute-start | bytes 786440 | tf_op jit(solution)/shard_map/ppermute | solution.py:714
  18.6 11.0 %collective-permute-start.10 = (bf16[256,512]{1,0:T(8,128)(2,1)S(1)}, bf16[256,512]{1,0:T(8,128)(2,1)S(1)}, u32[]{:S(2)}, u32[]{:S(2)}) collective-permute-start(bf16[256,512]{1,0:T(8,128)(2,1)S(1)} %collective-permute-done.6.refs_1_.refs_13_), channel_id=1, source_target_pairs={{0,4},{1,5},{4,8},{5,9},{8,12},{9,13},{12,14},{13,15},{14,10},{15,... | collective-permute-start | bytes 786440 | tf_op jit(solution)/shard_map/ppermute | solution.py:713
  20.5 10.5 %collective-permute-start.11 = (bf16[256,512]{1,0:T(8,128)(2,1)S(1)}, bf16[256,512]{1,0:T(8,128)(2,1)S(1)}, u32[]{:S(2)}, u32[]{:S(2)}) collective-permute-start(bf16[256,512]{1,0:T(8,128)(2,1)S(1)} %collective-permute-done.7.refs_3_.refs_15_), channel_id=1, source_target_pairs={{4,0},{5,1},{8,4},{9,5},{12,8},{13,9},{14,12},{15,13},{10,14},{11,... | collective-permute-start | bytes 786440 | tf_op jit(solution)/shard_map/ppermute | solution.py:714
  25.7 9.6 %collective-permute-start.8 = (bf16[256,512]{1,0:T(8,128)(2,1)S(1)}, bf16[256,512]{1,0:T(8,128)(2,1)S(1)}, u32[]{:S(2)}, u32[]{:S(2)}) collective-permute-start(bf16[256,512]{1,0:T(8,128)(2,1)S(1)} %collective-permute-done.4.refs_0_.refs_16_), channel_id=1, source_target_pairs={{0,4},{1,5},{4,8},{5,9},{8,12},{9,13},{12,14},{13,15},{14,10},{15,... | collective-permute-start | bytes 786440 | tf_op jit(solution)/shard_map/ppermute | solution.py:713
  28.1 8.8 %collective-permute-start.9 = (bf16[256,512]{1,0:T(8,128)(2,1)S(1)}, bf16[256,512]{1,0:T(8,128)(2,1)S(1)}, u32[]{:S(2)}, u32[]{:S(2)}) collective-permute-start(bf16[256,512]{1,0:T(8,128)(2,1)S(1)} %collective-permute-done.5.refs_2_.refs_18_), channel_id=1, source_target_pairs={{4,0},{5,1},{8,4},{9,5},{12,8},{13,9},{14,12},{15,13},{10,14},{11,... | collective-permute-start | bytes 786440 | tf_op jit(solution)/shard_map/ppermute | solution.py:714
  31.0 9.7 %collective-permute-start.14 = (bf16[256,512]{1,0:T(8,128)(2,1)S(1)}, bf16[256,512]{1,0:T(8,128)(2,1)S(1)}, u32[]{:S(2)}, u32[]{:S(2)}) collective-permute-start(bf16[256,512]{1,0:T(8,128)(2,1)S(1)} %collective-permute-done.10.refs_1_.refs_17_), channel_id=1, source_target_pairs={{0,4},{1,5},{4,8},{5,9},{8,12},{9,13},{12,14},{13,15},{14,10},{15,... | collective-permute-start | bytes 786440 | tf_op jit(solution)/shard_map/ppermute | solution.py:713
  32.6 10.0 %collective-permute-start.15 = (bf16[256,512]{1,0:T(8,128)(2,1)S(1)}, bf16[256,512]{1,0:T(8,128)(2,1)S(1)}, u32[]{:S(2)}, u32[]{:S(2)}) collective-permute-start(bf16[256,512]{1,0:T(8,128)(2,1)S(1)} %collective-permute-done.11.refs_3_.refs_19_), channel_id=1, source_target_pairs={{4,0},{5,1},{8,4},{9,5},{12,8},{13,9},{14,12},{15,13},{10,14},{11,... | collective-permute-start | bytes 786440 | tf_op jit(solution)/shard_map/ppermute | solution.py:714
  42.6 6.4 %collective-permute-start.16 = (bf16[128,512]{1,0:T(8,128)(2,1)S(1)}, bf16[128,512]{1,0:T(8,128)(2,1)S(1)}, u32[]{:S(2)}, u32[]{:S(2)}) collective-permute-start(bf16[128,512]{1,0:T(8,128)(2,1)S(1)} %slice.144), channel_id=1, source_target_pairs={{0,4},{1,5},{4,8},{5,9},{8,12},{9,13},{12,14},{13,15},{14,10},{15,... | collective-permute-start | bytes 393224 | tf_op jit(solution)/shard_map/ppermute | solution.py:713
  44.3 6.4 %collective-permute-start.17 = (bf16[128,512]{1,0:T(8,128)(2,1)S(1)}, bf16[128,512]{1,0:T(8,128)(2,1)S(1)}, u32[]{:S(2)}, u32[]{:S(2)}) collective-permute-start(bf16[128,512]{1,0:T(8,128)(2,1)S(1)} %slice.145), channel_id=1, source_target_pairs={{4,0},{5,1},{8,4},{9,5},{12,8},{13,9},{14,12},{15,13},{10,14},{11,... | collective-permute-start | bytes 393224 | tf_op jit(solution)/shard_map/ppermute | solution.py:714
  44.8 6.3 %collective-permute-start.12 = (bf16[128,512]{1,0:T(8,128)(2,1)S(1)}, bf16[128,512]{1,0:T(8,128)(2,1)S(1)}, u32[]{:S(2)}, u32[]{:S(2)}) collective-permute-start(bf16[128,512]{1,0:T(8,128)(2,1)S(1)} %slice.142), channel_id=1, source_target_pairs={{0,4},{1,5},{4,8},{5,9},{8,12},{9,13},{12,14},{13,15},{14,10},{15,... | collective-permute-start | bytes 393224 | tf_op jit(solution)/shard_map/ppermute | solution.py:713
  46.3 6.1 %collective-permute-start.13 = (bf16[128,512]{1,0:T(8,128)(2,1)S(1)}, bf16[128,512]{1,0:T(8,128)(2,1)S(1)}, u32[]{:S(2)}, u32[]{:S(2)}) collective-permute-start(bf16[128,512]{1,0:T(8,128)(2,1)S(1)} %slice.143), channel_id=1, source_target_pairs={{4,0},{5,1},{8,4},{9,5},{12,8},{13,9},{14,12},{15,13},{10,14},{11,... | collective-permute-start | bytes 393224 | tf_op jit(solution)/shard_map/ppermute | solution.py:714
  56.8 7.5 %collective-permute-start.19 = (bf16[32,4224]{1,0:T(8,128)(2,1)S(1)}, bf16[32,4224]{1,0:T(8,128)(2,1)S(1)}, u32[]{:S(2)}, u32[]{:S(2)}) collective-permute-start(bf16[32,4224]{1,0:T(8,128)(2,1)S(1)} %get-tuple-element.144.refs_0_), channel_id=1, source_target_pairs={{0,4},{1,5},{4,8},{5,9},{8,12},{9,13},{12,14},{13,15},{14,10},{15,... | collective-permute-start | bytes 811016 | tf_op jit(solution)/shard_map/ppermute | solution.py:713
  58.5 8.5 %collective-permute-start.21 = (bf16[32,4224]{1,0:T(8,128)(2,1)S(1)}, bf16[32,4224]{1,0:T(8,128)(2,1)S(1)}, u32[]{:S(2)}, u32[]{:S(2)}) collective-permute-start(bf16[32,4224]{1,0:T(8,128)(2,1)S(1)} %get-tuple-element.144.refs_0_), channel_id=1, source_target_pairs={{4,0},{5,1},{8,4},{9,5},{12,8},{13,9},{14,12},{15,13},{10,14},{11,... | collective-permute-start | bytes 811016 | tf_op jit(solution)/shard_map/ppermute | solution.py:714
  64.3 7.8 %collective-permute-start.20 = (bf16[32,4224]{1,0:T(8,128)(2,1)S(1)}, bf16[32,4224]{1,0:T(8,128)(2,1)S(1)}, u32[]{:S(2)}, u32[]{:S(2)}) collective-permute-start(bf16[32,4224]{1,0:T(8,128)(2,1)S(1)} %collective-permute-done.19.refs_0_), channel_id=1, source_target_pairs={{0,4},{1,5},{4,8},{5,9},{8,12},{9,13},{12,14},{13,15},{14,10},{15,... | collective-permute-start | bytes 811016 | tf_op jit(solution)/shard_map/ppermute | solution.py:713
  67.0 8.1 %collective-permute-start.23 = (bf16[32,4224]{1,0:T(8,128)(2,1)S(1)}, bf16[32,4224]{1,0:T(8,128)(2,1)S(1)}, u32[]{:S(2)}, u32[]{:S(2)}) collective-permute-start(bf16[32,4224]{1,0:T(8,128)(2,1)S(1)} %collective-permute-done.21.refs_1_), channel_id=1, source_target_pairs={{4,0},{5,1},{8,4},{9,5},{12,8},{13,9},{14,12},{15,13},{10,14},{11,... | collective-permute-start | bytes 811016 | tf_op jit(solution)/shard_map/ppermute | solution.py:714
  72.1 7.2 %collective-permute-start.22 = (bf16[32,4224]{1,0:T(8,128)(2,1)S(1)}, bf16[32,4224]{1,0:T(8,128)(2,1)S(1)}, u32[]{:S(2)}, u32[]{:S(2)}) collective-permute-start(bf16[32,4224]{1,0:T(8,128)(2,1)S(1)} %collective-permute-done.20.refs_0_), channel_id=1, source_target_pairs={{0,4},{1,5},{4,8},{5,9},{8,12},{9,13},{12,14},{13,15},{14,10},{15,... | collective-permute-start | bytes 811016 | tf_op jit(solution)/shard_map/ppermute | solution.py:713
  75.1 46.8 %collective-permute-start.25 = (bf16[32,4224]{1,0:T(8,128)(2,1)S(1)}, bf16[32,4224]{1,0:T(8,128)(2,1)S(1)}, u32[]{:S(2)}, u32[]{:S(2)}) collective-permute-start(bf16[32,4224]{1,0:T(8,128)(2,1)S(1)} %collective-permute-done.23.refs_1_), channel_id=1, source_target_pairs={{4,0},{5,1},{8,4},{9,5},{12,8},{13,9},{14,12},{15,13},{10,14},{11,... | collective-permute-start | bytes 811016 | tf_op jit(solution)/shard_map/ppermute | solution.py:714
  127.8 9.8 %collective-permute-start.28 = (bf16[128,4096]{1,0:T(8,128)(2,1)S(1)}, bf16[128,4096]{1,0:T(8,128)(2,1)S(1)}, u32[]{:S(2)}, u32[]{:S(2)}) collective-permute-start(bf16[128,4096]{1,0:T(8,128)(2,1)S(1)} %get-tuple-element.175), channel_id=1, source_target_pairs={{0,1},{1,0},{2,3},{3,2},{4,5},{5,4},{6,7},{7,6},{8,9},{9,8},{10,11... | collective-permute-start | bytes 3145736 | tf_op jit(solution)/shard_map/ppermute | solution.py:715
  145.3 5.9 %collective-permute-start.31 = (bf16[16,2048]{1,0:T(8,128)(2,1)S(1)}, bf16[16,2048]{1,0:T(8,128)(2,1)S(1)}, u32[]{:S(2)}, u32[]{:S(2)}) collective-permute-start(bf16[16,2048]{1,0:T(8,128)(2,1)S(1)} %get-tuple-element.181), channel_id=1, source_target_pairs={{4,0},{5,1},{8,4},{9,5},{12,8},{13,9},{14,12},{15,13},{10,14},{11,... | collective-permute-start | bytes 196616 | tf_op jit(solution)/shard_map/ppermute | solution.py:714
  149.1 6.2 %collective-permute-start.41 = (bf16[16,4096]{1,0:T(8,128)(2,1)S(1)}, bf16[16,4096]{1,0:T(8,128)(2,1)S(1)}, u32[]{:S(2)}, u32[]{:S(2)}) collective-permute-start(bf16[16,4096]{1,0:T(8,128)(2,1)S(1)} %pad_maximum_fusion.2), channel_id=1, source_target_pairs={{0,4},{1,5},{4,8},{5,9},{8,12},{9,13},{12,14},{13,15},{14,10},{15,... | collective-permute-start | bytes 393224 | tf_op jit(solution)/shard_map/ppermute | solution.py:713
  149.4 6.1 %collective-permute-start.42 = (bf16[16,4096]{1,0:T(8,128)(2,1)S(1)}, bf16[16,4096]{1,0:T(8,128)(2,1)S(1)}, u32[]{:S(2)}, u32[]{:S(2)}) collective-permute-start(bf16[16,4096]{1,0:T(8,128)(2,1)S(1)} %pad_maximum_fusion.3), channel_id=1, source_target_pairs={{4,0},{5,1},{8,4},{9,5},{12,8},{13,9},{14,12},{15,13},{10,14},{11,... | collective-permute-start | bytes 393224 | tf_op jit(solution)/shard_map/ppermute | solution.py:714
  152.2 6.1 %collective-permute-start.32 = (bf16[16,4096]{1,0:T(8,128)(2,1)S(1)}, bf16[16,4096]{1,0:T(8,128)(2,1)S(1)}, u32[]{:S(2)}, u32[]{:S(2)}) collective-permute-start(bf16[16,4096]{1,0:T(8,128)(2,1)S(1)} %pad_maximum_fusion), channel_id=1, source_target_pairs={{0,4},{1,5},{4,8},{5,9},{8,12},{9,13},{12,14},{13,15},{14,10},{15,... | collective-permute-start | bytes 393224 | tf_op jit(solution)/shard_map/ppermute | solution.py:713
  152.2 6.1 %collective-permute-start.33 = (bf16[16,4096]{1,0:T(8,128)(2,1)S(1)}, bf16[16,4096]{1,0:T(8,128)(2,1)S(1)}, u32[]{:S(2)}, u32[]{:S(2)}) collective-permute-start(bf16[16,4096]{1,0:T(8,128)(2,1)S(1)} %pad_maximum_fusion.1), channel_id=1, source_target_pairs={{4,0},{5,1},{8,4},{9,5},{12,8},{13,9},{14,12},{15,13},{10,14},{11,... | collective-permute-start | bytes 393224 | tf_op jit(solution)/shard_map/ppermute | solution.py:714
  156.8 6.3 %collective-permute-start.44 = (bf16[16,4096]{1,0:T(8,128)(2,1)S(1)}, bf16[16,4096]{1,0:T(8,128)(2,1)S(1)}, u32[]{:S(2)}, u32[]{:S(2)}) collective-permute-start(bf16[16,4096]{1,0:T(8,128)(2,1)S(1)} %get-tuple-element.195), channel_id=1, source_target_pairs={{4,0},{5,1},{8,4},{9,5},{12,8},{13,9},{14,12},{15,13},{10,14},{11,... | collective-permute-start | bytes 393224 | tf_op jit(solution)/shard_map/ppermute | solution.py:714
  158.4 6.8 %collective-permute-start.34 = (bf16[16,4096]{1,0:T(8,128)(2,1)S(1)}, bf16[16,4096]{1,0:T(8,128)(2,1)S(1)}, u32[]{:S(2)}, u32[]{:S(2)}) collective-permute-start(bf16[16,4096]{1,0:T(8,128)(2,1)S(1)} %get-tuple-element.184), channel_id=1, source_target_pairs={{0,4},{1,5},{4,8},{5,9},{8,12},{9,13},{12,14},{13,15},{14,10},{15,... | collective-permute-start | bytes 393224 | tf_op jit(solution)/shard_map/ppermute | solution.py:713
  159.0 6.6 %collective-permute-start.35 = (bf16[16,4096]{1,0:T(8,128)(2,1)S(1)}, bf16[16,4096]{1,0:T(8,128)(2,1)S(1)}, u32[]{:S(2)}, u32[]{:S(2)}) collective-permute-start(bf16[16,4096]{1,0:T(8,128)(2,1)S(1)} %get-tuple-element.185), channel_id=1, source_target_pairs={{4,0},{5,1},{8,4},{9,5},{12,8},{13,9},{14,12},{15,13},{10,14},{11,... | collective-permute-start | bytes 393224 | tf_op jit(solution)/shard_map/ppermute | solution.py:714
  (18 other events, 116.3 us)

commit v5 on v4

--- a/solution.py
+++ b/solution.py
@@ -226,9 +226,12 @@
                 rows = pl.ds(j * tokens, tokens)
                 fetch(block.at[pl.ds(0, tokens), columns], keys_ref.at[i, rows])
                 fetch(block.at[pl.ds(tokens, tokens), columns], values_ref.at[i, rows])
-        for j, block in enumerate(sources[2 * chips - 2 :]):
-            target = (values_ref if j % 2 else keys_ref).at[chips - 1, pl.ds(j // 2 * tokens, tokens)]
-            fetch(block.at[:, columns], target)
+        whole, key, value = sources[2 * chips - 2 :]
+        own, sib = pl.ds(0, tokens), pl.ds(tokens, tokens)
+        fetch(whole.at[own, columns], keys_ref.at[chips - 1, own])
+        fetch(whole.at[sib, columns], values_ref.at[chips - 1, own])
+        fetch(key.at[:, columns], keys_ref.at[chips - 1, sib])
+        fetch(value.at[:, columns], values_ref.at[chips - 1, sib])
         acc_ref[...] = jnp.zeros_like(acc_ref)
         total_ref[...] = jnp.zeros_like(total_ref)
         top_ref[...] = jnp.full_like(top_ref, 2 * MASKED)
@@ -263,9 +266,9 @@
 
 
 def last_kernel(chips, me_ref, q_ref, sib_q_ref, *refs):
-    blocks, (shift_ref, acc_ref, total_ref, gain_ref) = (refs[:2], refs[2:4]), refs[4:8]
-    tables, sources = refs[8:10], refs[10 : 12 + 2 * chips]
-    refs = refs[12 + 2 * chips :]
+    blocks, (shift_ref, acc_ref, total_ref, gain_ref) = (refs[0], refs[1:3]), refs[3:7]
+    tables, sources = refs[7:9], refs[9 : 10 + 2 * chips]
+    refs = refs[10 + 2 * chips :]
     out_refs, picked_ref = refs[:2], refs[2]
     rows_ref, worst_ref, sem, *scratch = refs[3:]
     q_refs = (q_ref, sib_q_ref)
@@ -664,47 +667,53 @@
     )(*parts, table, *earlier)
 
 
-def reduce_chip_rows(mine, other, half, chips, go_right, go_left):
-    middle = mine.shape[1] // 2
-
-    def block(index):
-        rows = slice(index * CAP, (index + 1) * CAP)
-        return mine[rows].astype(jnp.float32) + other[rows].astype(jnp.float32)
-
-    far = block(chips - 1).astype(jnp.bfloat16)
-    ahead, back = far[:, :middle], far[:, middle:]
-    for distance in range(half - 1, -1, -1):
-        ahead, back = lax.optimization_barrier((ahead, back))
-        to_right, to_left = go_right(ahead), go_left(back)
-        yield
-        if distance == 0:
-            break
-        ahead, back = block(half - 1 + distance), block(distance)
-        if distance == half - 1:
-            ahead = jnp.concatenate(
-                [ahead[:, :middle] + to_right.astype(jnp.float32), ahead[:, middle:]], axis=1
-            )
-            back = jnp.concatenate(
-                [back[:, :middle], back[:, middle:] + to_left.astype(jnp.float32)], axis=1
-            )
-        else:
-            ahead = ahead + to_right.astype(jnp.float32)
-            back = back + to_left.astype(jnp.float32)
-        ahead, back = ahead.astype(jnp.bfloat16), back.astype(jnp.bfloat16)
-    return (mine, other, to_right, to_left)
-
-
-def run_together(generators):
-    results = [None] * len(generators)
-    active = list(range(len(generators)))
-    while active:
-        for i in list(active):
-            try:
-                next(generators[i])
-            except StopIteration as stop:
-                results[i] = stop.value
-                active.remove(i)
-    return results
+def add_kernel(row, columns, place, mine_ref, other_ref, *refs):
+    received_ref, out_ref = (refs[0] if len(refs) > 1 else None), refs[-1]
+    rows = slice(row, row + CAP)
+    total = mine_ref[rows, columns].astype(jnp.float32) + other_ref[rows, columns].astype(jnp.float32)
+    if received_ref is None:
+        out_ref[...] = total.astype(jnp.bfloat16)
+        return
+    start, width = place, received_ref.shape[1]
+    part = total[:, start : start + width] + received_ref[...].astype(jnp.float32)
+    out_ref[:, start : start + width] = part.astype(jnp.bfloat16)
+    if width < out_ref.shape[1]:
+        rest = slice(width, None) if start == 0 else slice(0, start)
+        out_ref[:, rest] = total[:, rest].astype(jnp.bfloat16)
+
+
+def add_call(mine, other, index, columns, received=None, place=0):
+    vmem = pl.BlockSpec(memory_space=pltpu.VMEM)
+    more = () if received is None else (received,)
+    return pl.pallas_call(
+        functools.partial(add_kernel, index * CAP, columns, place),
+        in_specs=[vmem] * (2 + len(more)),
+        out_specs=vmem,
+        out_shape=pltpu.VMEM((CAP, columns.stop - columns.start), jnp.bfloat16),
+        compiler_params=pltpu.CompilerParams(vmem_limit_bytes=4 * MIB),
+        cost_estimate=SMALL,
+        name="add",
+    )(mine, other, *more)
+
+
+def reduce_chip_rows(pieces, half, chips, moves, token):
+    width = pieces[0][0].shape[1]
+    middle = width // 2
+    chains = [(piece, side) for piece in range(len(pieces)) for side in range(2)]
+    received = [None] * len(chains)
+    for distance in range(half, 0, -1):
+        for i, (piece, side) in enumerate(chains):
+            mine, other = pieces[piece]
+            if distance == half:
+                columns = slice(side * middle, (side + 1) * middle)
+                total = add_call(mine, other, chips - 1, columns)
+            else:
+                received[i], token = lax.optimization_barrier((received[i], token))
+                index = distance if side else half - 1 + distance
+                place = side * middle if distance == half - 1 else 0
+                total = add_call(mine, other, index, slice(0, width), received[i], place)
+            received[i] = moves[side](total)
+    return [(*pieces[p], *received[2 * p : 2 * p + 2]) for p in range(len(pieces))]
 
 
 def per_device(chips, queries, keys, values, norm_gain, expert_ids, gates, w_gate, w_up, w_down):
@@ -751,9 +760,8 @@
         if step < half - 1:
             chains = [(go_right(chain[0]), go_left(chain[1])) for chain in chains]
         else:
-            opposite = [
-                part for chain in chains for part in (go_right(chain[0][:tokens]), go_left(chain[1][tokens:]))
-            ]
+            far_sib = go_right(chains[1][0][:tokens]), go_left(chains[1][1][tokens:])
+            opposite = [go_right(chains[0][0]), *far_sib]
         state, _ = attention.step(blocks, [step, step, -step, -step], shift, state)
     opposite, state = lax.optimization_barrier((opposite, state))
     sources += opposite
@@ -781,15 +789,15 @@
     rows = place_far(*far, rows)
     hidden, downs = hidden_calls(me, rows, swap(rows), loaded, w_gate, w_up, w_down)
 
-    sums = []
+    partial = []
     for piece in range(PIECES):
         if piece == 0:
             own, sib, result = down_call(hidden, downs[piece], (me, mine, theirs))
         else:
             own, sib = down_call(hidden, downs[piece])
-        sums.append(reduce_chip_rows(own, swap(sib), half, chips, go_right, go_left))
+        partial.append((own, swap(sib)))
     mixed = None
-    for piece, parts in enumerate(run_together(sums)):
+    for piece, parts in enumerate(reduce_chip_rows(partial, half, chips, (go_right, go_left), weighted)):
         mixed = spread_call(parts, weighted, piece, PIECES, mixed)
     return (result, mixed)
 

time: 174 us -> 171 us (0.983)
  waiting for transfers between devices: 93.3 us -> 89.2 us
    ppermute x19 -> x18, waiting for transfers between devices: 63 us -> 58.1 us  [per_device(): go_left = lambda x: lax.ppermute(x, 'ctx', left)]
    ppermute x19 -> x18, starting transfers between devices: 14.4 us -> 16.6 us  [per_device(): go_left = lambda x: lax.ppermute(x, 'ctx', left)]
  transfers between devices with their start and end apart: 47 -> 46, of which waited for: 36 -> 32; matrix products, arithmetic and copies ran while one was open for 1% -> 0% of each run, Pallas kernels for 13% -> 14%
where the time goes in v5:
time: 171 us
  waiting for transfers between devices  89.2 us (52%)
  starting transfers between devices  47 us (27%)
  Pallas kernels  33.6 us (20%)
    ppermute x18, waiting for transfers between devices, per_device(): go_left = lambda x: lax.ppermute(x, 'ctx', left)  58.1 us
    ppermute x19, waiting for transfers between devices, per_device(): go_right = lambda x: lax.ppermute(x, 'ctx', right)  29.8 us
    ppermute x19, starting transfers between devices, per_device(): go_right = lambda x: lax.ppermute(x, 'ctx', right)  26.3 us
    ppermute x18, starting transfers between devices, per_device(): go_left = lambda x: lax.ppermute(x, 'ctx', left)  16.6 us
    pallas_call x5, Pallas kernels, call(): pl.pallas_call(kernel, in_specs=[pl.BlockSpec(memory_space=pltpu.SMEM)] +...  8.31 us
    pallas_call x2, Pallas kernels, load(): pl.pallas_call(load_kernel, in_specs=[pl.BlockSpec(memory_space=pltpu.SME...  5.61 us
    pallas_call x2, Pallas kernels, down_call(): pl.pallas_call(down_kernel, in_specs=[vmem] * 2 + more, out_specs=[vmem]...  4.7 us
    pallas_call x1, Pallas kernels, hidden_calls(): pl.pallas_call(first_kernel, in_specs=[pl.BlockSpec(memory_space=pltpu.SM...  4.63 us
  transfers between devices with their start and end apart: 46, of which 32 were waited for; matrix products, arithmetic and copies ran while one was open for 0% of the time, Pallas kernels for 14%

profile of v5, /device:TPU:0, one launch (start us, length us, event | category | flops | bytes accessed | tf_op | source)
XLA Modules:
  0.0 170.8 jit_solution(17439286545932342591)
XLA Ops:
  0.6 1.9 %halves.1 = (bf16[256,512]{1,0:T(8,128)(2,1)S(1)}, bf16[256,512]{1,0:T(8,128)(2,1)S(1)}, bf16[128,4096]{1,0:T(8,128)(2,1)S(1)}, bf16[128,4096]{1,0:T(8,128)(2,1)S(1)}) custom-call(s32[1]{0:T(128)} %bitcast.me_ref.refs_0_, bf16[128,1024]{1,0:T(8,128)(2,1)} %refs_0_.1, bf16[128,1024]{1,0:T(8,128)(2,1)} %refs_1_.1, bf16[128,8192]{1,0:T(8,128)(2,1)} %refs_2_.1), custom_call_target="tpu_custom_call" | custom-call | flops 1 | bytes 1 | tf_op jit(solution)/shard_map/halves/pallas_call | solution.py:412
  3.1 3.0 %collective-permute-start.1 = (bf16[256,512]{1,0:T(8,128)(2,1)S(1)}, bf16[256,512]{1,0:T(8,128)(2,1)S(1)}, u32[]{:S(2)}, u32[]{:S(2)}) collective-permute-start(bf16[256,512]{1,0:T(8,128)(2,1)S(1)} %get-tuple-element.86.own_ref.refs_9_), channel_id=1, source_target_pairs={{0,4},{1,5},{4,8},{5,9},{8,12},{9,13},{12,14},{13,15},{14,10},{15,... | collective-permute-start | bytes 786440 | tf_op jit(solution)/shard_map/ppermute | solution.py:722
  8.3 3.8 %attend_own.1 = (f32[4,2048,128]{2,1,0:T(8,128)S(1)}, f32[4,2048,128]{2,1,0:T(8,128)S(1)}, f32[4,2048,128]{2,1,0:T(8,128)S(1)}) custom-call(s32[1]{0:T(128)} %bitcast.me_ref.refs_0_, bf16[128,4096]{1,0:T(8,128)(2,1)S(1)} %get-tuple-element.84.q_ref, bf16[128,4096]{1,0:T(8,128)(2,1)S(1)} %collective-permute-done.sib_q_ref, ...), custom_call_target="tpu_custom_call" | custom-call | flops 1 | bytes 1 | tf_op jit(solution)/shard_map/attend_own/pallas_call | solution.py:320
  13.2 2.2 %collective-permute-done.2.refs_2_.refs_13_ = bf16[256,512]{1,0:T(8,128)(2,1)S(1)} collective-permute-done((bf16[256,512]{1,0:T(8,128)(2,1)S(1)}, bf16[256,512]{1,0:T(8,128)(2,1)S(1)}, u32[]{:S(2)}, u32[]{:S(2)}) %collective-permute-start.2) | collective-permute-done | bytes 262176 | tf_op jit(solution)/shard_map/ppermute | solution.py:723
  18.5 1.9 %collective-permute-start.10 = (bf16[256,512]{1,0:T(8,128)(2,1)S(1)}, bf16[256,512]{1,0:T(8,128)(2,1)S(1)}, u32[]{:S(2)}, u32[]{:S(2)}) collective-permute-start(bf16[256,512]{1,0:T(8,128)(2,1)S(1)} %collective-permute-done.6.refs_1_.refs_12_), channel_id=1, source_target_pairs={{0,4},{1,5},{4,8},{5,9},{8,12},{9,13},{12,14},{13,15},{14,10},{15,... | collective-permute-start | bytes 786440 | tf_op jit(solution)/shard_map/ppermute | solution.py:722
  20.6 3.4 %collective-permute-done.4.refs_0_.refs_15_ = bf16[256,512]{1,0:T(8,128)(2,1)S(1)} collective-permute-done((bf16[256,512]{1,0:T(8,128)(2,1)S(1)}, bf16[256,512]{1,0:T(8,128)(2,1)S(1)}, u32[]{:S(2)}, u32[]{:S(2)}) %collective-permute-start.4) | collective-permute-done | bytes 262176 | tf_op jit(solution)/shard_map/ppermute | solution.py:722
  24.0 1.7 %collective-permute-done.5.refs_2_.refs_17_ = bf16[256,512]{1,0:T(8,128)(2,1)S(1)} collective-permute-done((bf16[256,512]{1,0:T(8,128)(2,1)S(1)}, bf16[256,512]{1,0:T(8,128)(2,1)S(1)}, u32[]{:S(2)}, u32[]{:S(2)}) %collective-permute-start.5) | collective-permute-done | bytes 262176 | tf_op jit(solution)/shard_map/ppermute | solution.py:723
  25.7 2.4 %collective-permute-start.8 = (bf16[256,512]{1,0:T(8,128)(2,1)S(1)}, bf16[256,512]{1,0:T(8,128)(2,1)S(1)}, u32[]{:S(2)}, u32[]{:S(2)}) collective-permute-start(bf16[256,512]{1,0:T(8,128)(2,1)S(1)} %collective-permute-done.4.refs_0_.refs_15_), channel_id=1, source_target_pairs={{0,4},{1,5},{4,8},{5,9},{8,12},{9,13},{12,14},{13,15},{14,10},{15,... | collective-permute-start | bytes 786440 | tf_op jit(solution)/shard_map/ppermute | solution.py:722
  33.0 2.2 %collective-permute-done.8.refs_0_.refs_19_ = bf16[256,512]{1,0:T(8,128)(2,1)S(1)} collective-permute-done((bf16[256,512]{1,0:T(8,128)(2,1)S(1)}, bf16[256,512]{1,0:T(8,128)(2,1)S(1)}, u32[]{:S(2)}, u32[]{:S(2)}) %collective-permute-start.8) | collective-permute-done | bytes 262176 | tf_op jit(solution)/shard_map/ppermute | solution.py:722
  36.9 3.2 %collective-permute-start.12 = (bf16[256,512]{1,0:T(8,128)(2,1)S(1)}, bf16[256,512]{1,0:T(8,128)(2,1)S(1)}, u32[]{:S(2)}, u32[]{:S(2)}) collective-permute-start(bf16[256,512]{1,0:T(8,128)(2,1)S(1)} %collective-permute-done.8.refs_0_.refs_19_), channel_id=1, source_target_pairs={{0,4},{1,5},{4,8},{5,9},{8,12},{9,13},{12,14},{13,15},{14,10},{15,... | collective-permute-start | bytes 786440 | tf_op jit(solution)/shard_map/ppermute | solution.py:722
  44.8 4.3 %collective-permute-done.15.refs_1_.refs_24_ = bf16[128,512]{1,0:T(8,128)(2,1)S(1)} collective-permute-done((bf16[128,512]{1,0:T(8,128)(2,1)S(1)}, bf16[128,512]{1,0:T(8,128)(2,1)S(1)}, u32[]{:S(2)}, u32[]{:S(2)}) %collective-permute-start.15) | collective-permute-done | bytes 131104 | tf_op jit(solution)/shard_map/ppermute | solution.py:722
  49.8 4.4 %attend_last.1 = (bf16[128,4096]{1,0:T(8,128)(2,1)S(1)}, bf16[128,4096]{1,0:T(8,128)(2,1)S(1)}, bf16[32,4224]{1,0:T(8,128)(2,1)S(1)}) custom-call(s32[1]{0:T(128)} %bitcast.me_ref.refs_0_, bf16[128,4096]{1,0:T(8,128)(2,1)S(1)} %get-tuple-element.84.q_ref, bf16[128,4096]{1,0:T(8,128)(2,1)S(1)} %collective-permute-done.sib_q_ref, ...), custom_call_target="tpu_custom_call" | custom-call | flops 1 | bytes 1 | tf_op jit(solution)/shard_map/attend_last/pallas_call | solution.py:320
  56.4 2.8 %load.2.gate_ref = bf16[4096,768]{1,0:T(8,128)(2,1)S(1)} custom-call(s32[1]{0:T(128)} %bitcast.me_ref.refs_0_, bf16[8192,768]{1,0:T(8,128)(2,1)} %refs_0_.2), custom_call_target="tpu_custom_call" | custom-call | flops 1 | bytes 1 | tf_op jit(solution)/shard_map/load/pallas_call | solution.py:437
  59.2 2.9 %collective-permute-done.18.refs_0_ = bf16[32,4224]{1,0:T(8,128)(2,1)S(1)} collective-permute-done((bf16[32,4224]{1,0:T(8,128)(2,1)S(1)}, bf16[32,4224]{1,0:T(8,128)(2,1)S(1)}, u32[]{:S(2)}, u32[]{:S(2)}) %collective-permute-start.18) | collective-permute-done | bytes 270368 | tf_op jit(solution)/shard_map/ppermute | solution.py:722
  62.1 2.4 %collective-permute-start.19 = (bf16[32,4224]{1,0:T(8,128)(2,1)S(1)}, bf16[32,4224]{1,0:T(8,128)(2,1)S(1)}, u32[]{:S(2)}, u32[]{:S(2)}) collective-permute-start(bf16[32,4224]{1,0:T(8,128)(2,1)S(1)} %collective-permute-done.18.refs_0_), channel_id=1, source_target_pairs={{0,4},{1,5},{4,8},{5,9},{8,12},{9,13},{12,14},{13,15},{14,10},{15,... | collective-permute-start | bytes 811016 | tf_op jit(solution)/shard_map/ppermute | solution.py:722
  64.9 2.8 %load.3.up_ref = bf16[4096,768]{1,0:T(8,128)(2,1)S(1)} custom-call(s32[1]{0:T(128)} %bitcast.me_ref.refs_0_, bf16[8192,768]{1,0:T(8,128)(2,1)} %refs_1_.2), custom_call_target="tpu_custom_call" | custom-call | flops 1 | bytes 1 | tf_op jit(solution)/shard_map/load/pallas_call | solution.py:437
  67.7 2.3 %collective-permute-done.19.refs_0_ = bf16[32,4224]{1,0:T(8,128)(2,1)S(1)} collective-permute-done((bf16[32,4224]{1,0:T(8,128)(2,1)S(1)}, bf16[32,4224]{1,0:T(8,128)(2,1)S(1)}, u32[]{:S(2)}, u32[]{:S(2)}) %collective-permute-start.19) | collective-permute-done | bytes 270368 | tf_op jit(solution)/shard_map/ppermute | solution.py:722
  70.0 2.5 %collective-permute-start.21 = (bf16[32,4224]{1,0:T(8,128)(2,1)S(1)}, bf16[32,4224]{1,0:T(8,128)(2,1)S(1)}, u32[]{:S(2)}, u32[]{:S(2)}) collective-permute-start(bf16[32,4224]{1,0:T(8,128)(2,1)S(1)} %collective-permute-done.19.refs_0_), channel_id=1, source_target_pairs={{0,4},{1,5},{4,8},{5,9},{8,12},{9,13},{12,14},{13,15},{14,10},{15,... | collective-permute-start | bytes 811016 | tf_op jit(solution)/shard_map/ppermute | solution.py:722
  73.3 3.9 %collective-permute-done.21.refs_0_ = bf16[32,4224]{1,0:T(8,128)(2,1)S(1)} collective-permute-done((bf16[32,4224]{1,0:T(8,128)(2,1)S(1)}, bf16[32,4224]{1,0:T(8,128)(2,1)S(1)}, u32[]{:S(2)}, u32[]{:S(2)}) %collective-permute-start.21) | collective-permute-done | bytes 270368 | tf_op jit(solution)/shard_map/ppermute | solution.py:722
  77.2 42.0 %collective-permute-done.24.refs_1_ = bf16[32,4224]{1,0:T(8,128)(2,1)S(1)} collective-permute-done((bf16[32,4224]{1,0:T(8,128)(2,1)S(1)}, bf16[32,4224]{1,0:T(8,128)(2,1)S(1)}, u32[]{:S(2)}, u32[]{:S(2)}) %collective-permute-start.24) | collective-permute-done | bytes 270368 | tf_op jit(solution)/shard_map/ppermute | solution.py:723
  121.3 2.9 %collective-permute-done.25.high_ref = bf16[16,4224]{1,0:T(8,128)(2,1)S(1)} collective-permute-done((bf16[16,4224]{1,0:T(8,128)(2,1)S(1)}, bf16[16,4224]{1,0:T(8,128)(2,1)S(1)}, u32[]{:S(2)}, u32[]{:S(2)}) %collective-permute-start.25) | collective-permute-done | bytes 135200 | tf_op jit(solution)/shard_map/ppermute | solution.py:723
  125.8 4.6 %hidden_first.1 = (f32[256,768]{1,0:T(8,128)S(1)}, f32[256,768]{1,0:T(8,128)S(1)}, bf16[4096,768]{1,0:T(8,128)(2,1)S(1)}, bf16[4096,768]{1,0:T(8,128)(2,1)S(1)}) custom-call(s32[1]{0:T(128)} %bitcast.me_ref.refs_0_, bf16[256,4224]{1,0:T(8,128)(2,1)S(1)} %place.9.rows_ref.own_ref, bf16[4096,768]{1,0:T(8,128)(2,1)S(1)} %load.2.gate_ref, ...), custom_call_target="tpu_custom_call" | custom-call | flops 3221225472 | bytes 12582912 | tf_op jit(solution)/shard_map/hidden_first/pallas_call | solution.py:557
  130.4 4.6 %hidden_second.1 = (bf16[256,768]{1,0:T(8,128)(2,1)S(1)}, bf16[768,4096]{1,0:T(8,128)(2,1)S(1)}, bf16[768,4096]{1,0:T(8,128)(2,1)S(1)}) custom-call(bf16[256,4224]{1,0:T(8,128)(2,1)S(1)} %collective-permute-done.26.rows_ref, bf16[4096,768]{1,0:T(8,128)(2,1)S(1)} %get-tuple-element.151.gate_ref, bf16[4096,768]{1,0:T(8,128)(2,1)S(1)} %get-tuple-element.152.up_ref, ...), custom_call_target="tpu_custom_call" | custom-call | flops 3221225472 | bytes 12582912 | tf_op jit(solution)/shard_map/hidden_second/pallas_call | solution.py:567
  135.1 2.4 %down.2 = (bf16[128,4096]{1,0:T(8,128)(2,1)S(1)}, bf16[128,4096]{1,0:T(8,128)(2,1)S(1)}, bf16[128,8192]{1,0:T(8,128)(2,1)}) custom-call(bf16[256,768]{1,0:T(8,128)(2,1)S(1)} %get-tuple-element.155.hidden_ref, bf16[768,4096]{1,0:T(8,128)(2,1)S(1)} %get-tuple-element.156.down_ref, s32[1]{0:T(128)} %bitcast.me_ref.refs_0_, ...), custom_call_target="tpu_custom_call" | custom-call | flops 1610612736 | bytes 8388608 | tf_op jit(solution)/shard_map/down/pallas_call | solution.py:619
  137.6 2.3 %down.3 = (bf16[128,4096]{1,0:T(8,128)(2,1)S(1)}, bf16[128,4096]{1,0:T(8,128)(2,1)S(1)}) custom-call(bf16[256,768]{1,0:T(8,128)(2,1)S(1)} %get-tuple-element.155.hidden_ref, bf16[768,4096]{1,0:T(8,128)(2,1)S(1)} %get-tuple-element.160.down_ref), custom_call_target="tpu_custom_call" | custom-call | flops 1610612736 | bytes 8388608 | tf_op jit(solution)/shard_map/down/pallas_call | solution.py:619
  140.5 1.8 %collective-permute-start.42 = (bf16[16,2048]{1,0:T(8,128)(2,1)S(1)}, bf16[16,2048]{1,0:T(8,128)(2,1)S(1)}, u32[]{:S(2)}, u32[]{:S(2)}) collective-permute-start(bf16[16,2048]{1,0:T(8,128)(2,1)S(1)} %add.28), channel_id=1, source_target_pairs={{4,0},{5,1},{8,4},{9,5},{12,8},{13,9},{14,12},{15,13},{10,14},{11,... | collective-permute-start | bytes 196616 | tf_op jit(solution)/shard_map/ppermute | solution.py:723
  142.8 1.8 %collective-permute-start.33 = (bf16[16,2048]{1,0:T(8,128)(2,1)S(1)}, bf16[16,2048]{1,0:T(8,128)(2,1)S(1)}, u32[]{:S(2)}, u32[]{:S(2)}) collective-permute-start(bf16[16,2048]{1,0:T(8,128)(2,1)S(1)} %add.20), channel_id=1, source_target_pairs={{4,0},{5,1},{8,4},{9,5},{12,8},{13,9},{14,12},{15,13},{10,14},{11,... | collective-permute-start | bytes 196616 | tf_op jit(solution)/shard_map/ppermute | solution.py:723
  145.0 1.8 %collective-permute-start.43 = (bf16[16,4096]{1,0:T(8,128)(2,1)S(1)}, bf16[16,4096]{1,0:T(8,128)(2,1)S(1)}, u32[]{:S(2)}, u32[]{:S(2)}) collective-permute-start(bf16[16,4096]{1,0:T(8,128)(2,1)S(1)} %add.29), channel_id=1, source_target_pairs={{4,0},{5,1},{8,4},{9,5},{12,8},{13,9},{14,12},{15,13},{10,14},{11,... | collective-permute-start | bytes 393224 | tf_op jit(solution)/shard_map/ppermute | solution.py:723
  147.2 1.8 %collective-permute-start.34 = (bf16[16,4096]{1,0:T(8,128)(2,1)S(1)}, bf16[16,4096]{1,0:T(8,128)(2,1)S(1)}, u32[]{:S(2)}, u32[]{:S(2)}) collective-permute-start(bf16[16,4096]{1,0:T(8,128)(2,1)S(1)} %add.21), channel_id=1, source_target_pairs={{4,0},{5,1},{8,4},{9,5},{12,8},{13,9},{14,12},{15,13},{10,14},{11,... | collective-permute-start | bytes 393224 | tf_op jit(solution)/shard_map/ppermute | solution.py:723
  149.4 1.7 %collective-permute-done.43.refs_0_ = bf16[16,4096]{1,0:T(8,128)(2,1)S(1)} collective-permute-done((bf16[16,4096]{1,0:T(8,128)(2,1)S(1)}, bf16[16,4096]{1,0:T(8,128)(2,1)S(1)}, u32[]{:S(2)}, u32[]{:S(2)}) %collective-permute-start.43) | collective-permute-done | bytes 131104 | tf_op jit(solution)/shard_map/ppermute | solution.py:723
  152.8 1.7 %collective-permute-start.44 = (bf16[16,4096]{1,0:T(8,128)(2,1)S(1)}, bf16[16,4096]{1,0:T(8,128)(2,1)S(1)}, u32[]{:S(2)}, u32[]{:S(2)}) collective-permute-start(bf16[16,4096]{1,0:T(8,128)(2,1)S(1)} %add.30), channel_id=1, source_target_pairs={{4,0},{5,1},{8,4},{9,5},{12,8},{13,9},{14,12},{15,13},{10,14},{11,... | collective-permute-start | bytes 393224 | tf_op jit(solution)/shard_map/ppermute | solution.py:723
  154.9 1.8 %collective-permute-start.35 = (bf16[16,4096]{1,0:T(8,128)(2,1)S(1)}, bf16[16,4096]{1,0:T(8,128)(2,1)S(1)}, u32[]{:S(2)}, u32[]{:S(2)}) collective-permute-start(bf16[16,4096]{1,0:T(8,128)(2,1)S(1)} %add.22), channel_id=1, source_target_pairs={{4,0},{5,1},{8,4},{9,5},{12,8},{13,9},{14,12},{15,13},{10,14},{11,... | collective-permute-start | bytes 393224 | tf_op jit(solution)/shard_map/ppermute | solution.py:723
  (113 shorter events, 44.8 us)
Async XLA Ops:
  2.5 5.8 %collective-permute-start = (bf16[128,4096]{1,0:T(8,128)(2,1)S(1)}, bf16[128,4096]{1,0:T(8,128)(2,1)S(1)}, u32[]{:S(2)}, u32[]{:S(2)}) collective-permute-start(bf16[128,4096]{1,0:T(8,128)(2,1)S(1)} %get-tuple-element.85), channel_id=1, source_target_pairs={{0,1},{1,0},{2,3},{3,2},{4,5},{5,4},{6,7},{7,6},{8,9},{9,8},{10,11... | collective-permute-start | bytes 3145736 | tf_op jit(solution)/shard_map/ppermute | solution.py:724
  3.1 10.0 %collective-permute-start.1 = (bf16[256,512]{1,0:T(8,128)(2,1)S(1)}, bf16[256,512]{1,0:T(8,128)(2,1)S(1)}, u32[]{:S(2)}, u32[]{:S(2)}) collective-permute-start(bf16[256,512]{1,0:T(8,128)(2,1)S(1)} %get-tuple-element.86.own_ref.refs_9_), channel_id=1, source_target_pairs={{0,4},{1,5},{4,8},{5,9},{8,12},{9,13},{12,14},{13,15},{14,10},{15,... | collective-permute-start | bytes 786440 | tf_op jit(solution)/shard_map/ppermute | solution.py:722
  6.1 9.2 %collective-permute-start.2 = (bf16[256,512]{1,0:T(8,128)(2,1)S(1)}, bf16[256,512]{1,0:T(8,128)(2,1)S(1)}, u32[]{:S(2)}, u32[]{:S(2)}) collective-permute-start(bf16[256,512]{1,0:T(8,128)(2,1)S(1)} %get-tuple-element.86.own_ref.refs_9_), channel_id=1, source_target_pairs={{4,0},{5,1},{8,4},{9,5},{12,8},{13,9},{14,12},{15,13},{10,14},{11,... | collective-permute-start | bytes 786440 | tf_op jit(solution)/shard_map/ppermute | solution.py:723
  6.1 12.3 %collective-permute-start.6 = (bf16[256,512]{1,0:T(8,128)(2,1)S(1)}, bf16[256,512]{1,0:T(8,128)(2,1)S(1)}, u32[]{:S(2)}, u32[]{:S(2)}) collective-permute-start(bf16[256,512]{1,0:T(8,128)(2,1)S(1)} %get-tuple-element.87), channel_id=1, source_target_pairs={{0,5},{1,4},{4,9},{5,8},{8,13},{9,12},{12,15},{13,14},{14,11},{15,... | collective-permute-start | bytes 786440 | tf_op jit(solution)/shard_map/ppermute | solution.py:747
  7.3 11.3 %collective-permute-start.7 = (bf16[256,512]{1,0:T(8,128)(2,1)S(1)}, bf16[256,512]{1,0:T(8,128)(2,1)S(1)}, u32[]{:S(2)}, u32[]{:S(2)}) collective-permute-start(bf16[256,512]{1,0:T(8,128)(2,1)S(1)} %get-tuple-element.87), channel_id=1, source_target_pairs={{4,1},{5,0},{8,5},{9,4},{12,9},{13,8},{14,13},{15,12},{10,15},{11,... | collective-permute-start | bytes 786440 | tf_op jit(solution)/shard_map/ppermute | solution.py:747
  15.3 8.7 %collective-permute-start.4 = (bf16[256,512]{1,0:T(8,128)(2,1)S(1)}, bf16[256,512]{1,0:T(8,128)(2,1)S(1)}, u32[]{:S(2)}, u32[]{:S(2)}) collective-permute-start(bf16[256,512]{1,0:T(8,128)(2,1)S(1)} %collective-permute-done.1.refs_0_.refs_11_), channel_id=1, source_target_pairs={{0,4},{1,5},{4,8},{5,9},{8,12},{9,13},{12,14},{13,15},{14,10},{15,... | collective-permute-start | bytes 786440 | tf_op jit(solution)/shard_map/ppermute | solution.py:722
  16.9 8.8 %collective-permute-start.5 = (bf16[256,512]{1,0:T(8,128)(2,1)S(1)}, bf16[256,512]{1,0:T(8,128)(2,1)S(1)}, u32[]{:S(2)}, u32[]{:S(2)}) collective-permute-start(bf16[256,512]{1,0:T(8,128)(2,1)S(1)} %collective-permute-done.2.refs_2_.refs_13_), channel_id=1, source_target_pairs={{4,0},{5,1},{8,4},{9,5},{12,8},{13,9},{14,12},{15,13},{10,14},{11,... | collective-permute-start | bytes 786440 | tf_op jit(solution)/shard_map/ppermute | solution.py:723
  18.5 11.0 %collective-permute-start.10 = (bf16[256,512]{1,0:T(8,128)(2,1)S(1)}, bf16[256,512]{1,0:T(8,128)(2,1)S(1)}, u32[]{:S(2)}, u32[]{:S(2)}) collective-permute-start(bf16[256,512]{1,0:T(8,128)(2,1)S(1)} %collective-permute-done.6.refs_1_.refs_12_), channel_id=1, source_target_pairs={{0,4},{1,5},{4,8},{5,9},{8,12},{9,13},{12,14},{13,15},{14,10},{15,... | collective-permute-start | bytes 786440 | tf_op jit(solution)/shard_map/ppermute | solution.py:722
  20.5 10.5 %collective-permute-start.11 = (bf16[256,512]{1,0:T(8,128)(2,1)S(1)}, bf16[256,512]{1,0:T(8,128)(2,1)S(1)}, u32[]{:S(2)}, u32[]{:S(2)}) collective-permute-start(bf16[256,512]{1,0:T(8,128)(2,1)S(1)} %collective-permute-done.7.refs_3_.refs_14_), channel_id=1, source_target_pairs={{4,0},{5,1},{8,4},{9,5},{12,8},{13,9},{14,12},{15,13},{10,14},{11,... | collective-permute-start | bytes 786440 | tf_op jit(solution)/shard_map/ppermute | solution.py:723
  25.7 9.5 %collective-permute-start.8 = (bf16[256,512]{1,0:T(8,128)(2,1)S(1)}, bf16[256,512]{1,0:T(8,128)(2,1)S(1)}, u32[]{:S(2)}, u32[]{:S(2)}) collective-permute-start(bf16[256,512]{1,0:T(8,128)(2,1)S(1)} %collective-permute-done.4.refs_0_.refs_15_), channel_id=1, source_target_pairs={{0,4},{1,5},{4,8},{5,9},{8,12},{9,13},{12,14},{13,15},{14,10},{15,... | collective-permute-start | bytes 786440 | tf_op jit(solution)/shard_map/ppermute | solution.py:722
  28.1 8.8 %collective-permute-start.9 = (bf16[256,512]{1,0:T(8,128)(2,1)S(1)}, bf16[256,512]{1,0:T(8,128)(2,1)S(1)}, u32[]{:S(2)}, u32[]{:S(2)}) collective-permute-start(bf16[256,512]{1,0:T(8,128)(2,1)S(1)} %collective-permute-done.5.refs_2_.refs_17_), channel_id=1, source_target_pairs={{4,0},{5,1},{8,4},{9,5},{12,8},{13,9},{14,12},{15,13},{10,14},{11,... | collective-permute-start | bytes 786440 | tf_op jit(solution)/shard_map/ppermute | solution.py:723
  31.0 9.8 %collective-permute-start.13 = (bf16[256,512]{1,0:T(8,128)(2,1)S(1)}, bf16[256,512]{1,0:T(8,128)(2,1)S(1)}, u32[]{:S(2)}, u32[]{:S(2)}) collective-permute-start(bf16[256,512]{1,0:T(8,128)(2,1)S(1)} %collective-permute-done.10.refs_1_.refs_16_), channel_id=1, source_target_pairs={{0,4},{1,5},{4,8},{5,9},{8,12},{9,13},{12,14},{13,15},{14,10},{15,... | collective-permute-start | bytes 786440 | tf_op jit(solution)/shard_map/ppermute | solution.py:722
  32.6 10.0 %collective-permute-start.14 = (bf16[256,512]{1,0:T(8,128)(2,1)S(1)}, bf16[256,512]{1,0:T(8,128)(2,1)S(1)}, u32[]{:S(2)}, u32[]{:S(2)}) collective-permute-start(bf16[256,512]{1,0:T(8,128)(2,1)S(1)} %collective-permute-done.11.refs_3_.refs_18_), channel_id=1, source_target_pairs={{4,0},{5,1},{8,4},{9,5},{12,8},{13,9},{14,12},{15,13},{10,14},{11,... | collective-permute-start | bytes 786440 | tf_op jit(solution)/shard_map/ppermute | solution.py:723
  36.9 12.9 %collective-permute-start.12 = (bf16[256,512]{1,0:T(8,128)(2,1)S(1)}, bf16[256,512]{1,0:T(8,128)(2,1)S(1)}, u32[]{:S(2)}, u32[]{:S(2)}) collective-permute-start(bf16[256,512]{1,0:T(8,128)(2,1)S(1)} %collective-permute-done.8.refs_0_.refs_19_), channel_id=1, source_target_pairs={{0,4},{1,5},{4,8},{5,9},{8,12},{9,13},{12,14},{13,15},{14,10},{15,... | collective-permute-start | bytes 786440 | tf_op jit(solution)/shard_map/ppermute | solution.py:722
  42.5 6.6 %collective-permute-start.15 = (bf16[128,512]{1,0:T(8,128)(2,1)S(1)}, bf16[128,512]{1,0:T(8,128)(2,1)S(1)}, u32[]{:S(2)}, u32[]{:S(2)}) collective-permute-start(bf16[128,512]{1,0:T(8,128)(2,1)S(1)} %slice.12), channel_id=1, source_target_pairs={{0,4},{1,5},{4,8},{5,9},{8,12},{9,13},{12,14},{13,15},{14,10},{15,... | collective-permute-start | bytes 393224 | tf_op jit(solution)/shard_map/ppermute | solution.py:722
  44.2 5.6 %collective-permute-start.16 = (bf16[128,512]{1,0:T(8,128)(2,1)S(1)}, bf16[128,512]{1,0:T(8,128)(2,1)S(1)}, u32[]{:S(2)}, u32[]{:S(2)}) collective-permute-start(bf16[128,512]{1,0:T(8,128)(2,1)S(1)} %slice.13), channel_id=1, source_target_pairs={{4,0},{5,1},{8,4},{9,5},{12,8},{13,9},{14,12},{15,13},{10,14},{11,... | collective-permute-start | bytes 393224 | tf_op jit(solution)/shard_map/ppermute | solution.py:723
  44.7 5.1 %collective-permute-start.17 = (bf16[16,128]{1,0:T(8,128)(2,1)S(1)}, bf16[16,128]{1,0:T(8,128)(2,1)S(1)}, u32[]{:S(2)}, u32[]{:S(2)}) collective-permute-start(bf16[16,128]{1,0:T(8,128)(2,1)S(1)} %convert_convert_fusion.refs_7_), channel_id=1, source_target_pairs={{0,1},{1,0},{2,3},{3,2},{4,5},{5,4},{6,7},{7,6},{8,9},{9,8},{10,11... | collective-permute-start | bytes 12296 | tf_op jit(solution)/shard_map/ppermute | solution.py:724
  54.3 7.8 %collective-permute-start.18 = (bf16[32,4224]{1,0:T(8,128)(2,1)S(1)}, bf16[32,4224]{1,0:T(8,128)(2,1)S(1)}, u32[]{:S(2)}, u32[]{:S(2)}) collective-permute-start(bf16[32,4224]{1,0:T(8,128)(2,1)S(1)} %get-tuple-element.127.refs_0_), channel_id=1, source_target_pairs={{0,4},{1,5},{4,8},{5,9},{8,12},{9,13},{12,14},{13,15},{14,10},{15,... | collective-permute-start | bytes 811016 | tf_op jit(solution)/shard_map/ppermute | solution.py:722
  55.9 9.0 %collective-permute-start.20 = (bf16[32,4224]{1,0:T(8,128)(2,1)S(1)}, bf16[32,4224]{1,0:T(8,128)(2,1)S(1)}, u32[]{:S(2)}, u32[]{:S(2)}) collective-permute-start(bf16[32,4224]{1,0:T(8,128)(2,1)S(1)} %get-tuple-element.127.refs_0_), channel_id=1, source_target_pairs={{4,0},{5,1},{8,4},{9,5},{12,8},{13,9},{14,12},{15,13},{10,14},{11,... | collective-permute-start | bytes 811016 | tf_op jit(solution)/shard_map/ppermute | solution.py:723
  62.1 7.9 %collective-permute-start.19 = (bf16[32,4224]{1,0:T(8,128)(2,1)S(1)}, bf16[32,4224]{1,0:T(8,128)(2,1)S(1)}, u32[]{:S(2)}, u32[]{:S(2)}) collective-permute-start(bf16[32,4224]{1,0:T(8,128)(2,1)S(1)} %collective-permute-done.18.refs_0_), channel_id=1, source_target_pairs={{0,4},{1,5},{4,8},{5,9},{8,12},{9,13},{12,14},{13,15},{14,10},{15,... | collective-permute-start | bytes 811016 | tf_op jit(solution)/shard_map/ppermute | solution.py:722
  64.9 8.1 %collective-permute-start.22 = (bf16[32,4224]{1,0:T(8,128)(2,1)S(1)}, bf16[32,4224]{1,0:T(8,128)(2,1)S(1)}, u32[]{:S(2)}, u32[]{:S(2)}) collective-permute-start(bf16[32,4224]{1,0:T(8,128)(2,1)S(1)} %collective-permute-done.20.refs_1_), channel_id=1, source_target_pairs={{4,0},{5,1},{8,4},{9,5},{12,8},{13,9},{14,12},{15,13},{10,14},{11,... | collective-permute-start | bytes 811016 | tf_op jit(solution)/shard_map/ppermute | solution.py:723
  70.0 7.2 %collective-permute-start.21 = (bf16[32,4224]{1,0:T(8,128)(2,1)S(1)}, bf16[32,4224]{1,0:T(8,128)(2,1)S(1)}, u32[]{:S(2)}, u32[]{:S(2)}) collective-permute-start(bf16[32,4224]{1,0:T(8,128)(2,1)S(1)} %collective-permute-done.19.refs_0_), channel_id=1, source_target_pairs={{0,4},{1,5},{4,8},{5,9},{8,12},{9,13},{12,14},{13,15},{14,10},{15,... | collective-permute-start | bytes 811016 | tf_op jit(solution)/shard_map/ppermute | solution.py:722
  72.9 46.2 %collective-permute-start.24 = (bf16[32,4224]{1,0:T(8,128)(2,1)S(1)}, bf16[32,4224]{1,0:T(8,128)(2,1)S(1)}, u32[]{:S(2)}, u32[]{:S(2)}) collective-permute-start(bf16[32,4224]{1,0:T(8,128)(2,1)S(1)} %collective-permute-done.22.refs_1_), channel_id=1, source_target_pairs={{4,0},{5,1},{8,4},{9,5},{12,8},{13,9},{14,12},{15,13},{10,14},{11,... | collective-permute-start | bytes 811016 | tf_op jit(solution)/shard_map/ppermute | solution.py:723
  125.2 5.2 %collective-permute-start.26 = (bf16[256,4224]{1,0:T(8,128)(2,1)S(1)}, bf16[256,4224]{1,0:T(8,128)(2,1)S(1)}, u32[]{:S(2)}, u32[]{:S(2)}) collective-permute-start(bf16[256,4224]{1,0:T(8,128)(2,1)S(1)} %place.9.rows_ref.own_ref), channel_id=1, source_target_pairs={{0,1},{1,0},{2,3},{3,2},{4,5},{5,4},{6,7},{7,6},{8,9},{9,8},{10,11... | collective-permute-start | bytes 6488072 | tf_op jit(solution)/shard_map/ppermute | solution.py:724
  125.3 9.8 %collective-permute-start.27 = (bf16[128,4096]{1,0:T(8,128)(2,1)S(1)}, bf16[128,4096]{1,0:T(8,128)(2,1)S(1)}, u32[]{:S(2)}, u32[]{:S(2)}) collective-permute-start(bf16[128,4096]{1,0:T(8,128)(2,1)S(1)} %get-tuple-element.158), channel_id=1, source_target_pairs={{0,1},{1,0},{2,3},{3,2},{4,5},{5,4},{6,7},{7,6},{8,9},{9,8},{10,11... | collective-permute-start | bytes 3145736 | tf_op jit(solution)/shard_map/ppermute | solution.py:724
  145.0 6.1 %collective-permute-start.43 = (bf16[16,4096]{1,0:T(8,128)(2,1)S(1)}, bf16[16,4096]{1,0:T(8,128)(2,1)S(1)}, u32[]{:S(2)}, u32[]{:S(2)}) collective-permute-start(bf16[16,4096]{1,0:T(8,128)(2,1)S(1)} %add.29), channel_id=1, source_target_pairs={{4,0},{5,1},{8,4},{9,5},{12,8},{13,9},{14,12},{15,13},{10,14},{11,... | collective-permute-start | bytes 393224 | tf_op jit(solution)/shard_map/ppermute | solution.py:723
  146.8 5.9 %collective-permute-start.39 = (bf16[16,4096]{1,0:T(8,128)(2,1)S(1)}, bf16[16,4096]{1,0:T(8,128)(2,1)S(1)}, u32[]{:S(2)}, u32[]{:S(2)}) collective-permute-start(bf16[16,4096]{1,0:T(8,128)(2,1)S(1)} %add.25), channel_id=1, source_target_pairs={{0,4},{1,5},{4,8},{5,9},{8,12},{9,13},{12,14},{13,15},{14,10},{15,... | collective-permute-start | bytes 393224 | tf_op jit(solution)/shard_map/ppermute | solution.py:722
  147.2 7.7 %collective-permute-start.34 = (bf16[16,4096]{1,0:T(8,128)(2,1)S(1)}, bf16[16,4096]{1,0:T(8,128)(2,1)S(1)}, u32[]{:S(2)}, u32[]{:S(2)}) collective-permute-start(bf16[16,4096]{1,0:T(8,128)(2,1)S(1)} %add.21), channel_id=1, source_target_pairs={{4,0},{5,1},{8,4},{9,5},{12,8},{13,9},{14,12},{15,13},{10,14},{11,... | collective-permute-start | bytes 393224 | tf_op jit(solution)/shard_map/ppermute | solution.py:723
  149.1 7.6 %collective-permute-start.30 = (bf16[16,4096]{1,0:T(8,128)(2,1)S(1)}, bf16[16,4096]{1,0:T(8,128)(2,1)S(1)}, u32[]{:S(2)}, u32[]{:S(2)}) collective-permute-start(bf16[16,4096]{1,0:T(8,128)(2,1)S(1)} %add.17), channel_id=1, source_target_pairs={{0,4},{1,5},{4,8},{5,9},{8,12},{9,13},{12,14},{13,15},{14,10},{15,... | collective-permute-start | bytes 393224 | tf_op jit(solution)/shard_map/ppermute | solution.py:722
  154.9 6.3 %collective-permute-start.35 = (bf16[16,4096]{1,0:T(8,128)(2,1)S(1)}, bf16[16,4096]{1,0:T(8,128)(2,1)S(1)}, u32[]{:S(2)}, u32[]{:S(2)}) collective-permute-start(bf16[16,4096]{1,0:T(8,128)(2,1)S(1)} %add.22), channel_id=1, source_target_pairs={{4,0},{5,1},{8,4},{9,5},{12,8},{13,9},{14,12},{15,13},{10,14},{11,... | collective-permute-start | bytes 393224 | tf_op jit(solution)/shard_map/ppermute | solution.py:723
  156.8 6.3 %collective-permute-start.31 = (bf16[16,4096]{1,0:T(8,128)(2,1)S(1)}, bf16[16,4096]{1,0:T(8,128)(2,1)S(1)}, u32[]{:S(2)}, u32[]{:S(2)}) collective-permute-start(bf16[16,4096]{1,0:T(8,128)(2,1)S(1)} %add.18), channel_id=1, source_target_pairs={{0,4},{1,5},{4,8},{5,9},{8,12},{9,13},{12,14},{13,15},{14,10},{15,... | collective-permute-start | bytes 393224 | tf_op jit(solution)/shard_map/ppermute | solution.py:722
  159.5 5.7 %collective-permute-start.45 = (bf16[16,4096]{1,0:T(8,128)(2,1)S(1)}, bf16[16,4096]{1,0:T(8,128)(2,1)S(1)}, u32[]{:S(2)}, u32[]{:S(2)}) collective-permute-start(bf16[16,4096]{1,0:T(8,128)(2,1)S(1)} %add.31), channel_id=1, source_target_pairs={{4,0},{5,1},{8,4},{9,5},{12,8},{13,9},{14,12},{15,13},{10,14},{11,... | collective-permute-start | bytes 393224 | tf_op jit(solution)/shard_map/ppermute | solution.py:723
  (17 other events, 83.0 us)

commit v6 on v5

--- a/solution.py
+++ b/solution.py
@@ -269,8 +269,15 @@
     blocks, (shift_ref, acc_ref, total_ref, gain_ref) = (refs[0], refs[1:3]), refs[3:7]
     tables, sources = refs[7:9], refs[9 : 10 + 2 * chips]
     refs = refs[10 + 2 * chips :]
-    out_refs, picked_ref = refs[:2], refs[2]
-    rows_ref, worst_ref, sem, *scratch = refs[3:]
+    weights, refs = refs[:2], refs[2:]
+    out_refs, picked_refs, loaded = refs[:2], refs[2:4], refs[4:6]
+    rows_ref, worst_ref, sem, load_sems, *scratch = refs[6:]
+    loads = [
+        pltpu.make_async_copy(half_rows(me_ref, weight, False), target, load_sems.at[i])
+        for i, (weight, target) in enumerate(zip(weights, loaded))
+    ]
+    for load in loads:
+        load.start()
     q_refs = (q_ref, sib_q_ref)
     tokens, half_width = q_ref.shape
     me = me_ref[0]
@@ -304,8 +311,13 @@
     upper = squares.astype(jnp.bfloat16).astype(jnp.float32)
     lower = (squares - upper).astype(jnp.bfloat16).astype(jnp.float32)
     lane = lax.broadcasted_iota(jnp.int32, squares.shape, 1)
-    picked_ref[:, :half_width] = (rows * gain_ref[:, columns]).astype(jnp.bfloat16)
-    picked_ref[:, half_width:] = jnp.where(lane < DH // 2, upper, lower).astype(jnp.bfloat16)
+    rows = (rows * gain_ref[:, columns]).astype(jnp.bfloat16)
+    squares = jnp.where(lane < DH // 2, upper, lower).astype(jnp.bfloat16)
+    for i, ref in enumerate(picked_refs):
+        ref[:, :half_width] = rows[i * CAP : (i + 1) * CAP]
+        ref[:, half_width:] = squares[i * CAP : (i + 1) * CAP]
+    for load in loads:
+        load.wait()
 
 
 class Attention:
@@ -358,22 +370,24 @@
         )
         return list(results[:2]), results[2:]
 
-    def last(self, blocks, shift, state, gain, tables, sources):
+    def last(self, blocks, shift, state, gain, tables, sources, weights):
         out = pltpu.VMEM((self.tokens, self.width), jnp.bfloat16)
-        picked = pltpu.VMEM((2 * CAP, self.width + DH), jnp.bfloat16)
+        picked = pltpu.VMEM((CAP, self.width + DH), jnp.bfloat16)
+        loaded = [pltpu.VMEM((x.shape[0] // 2, x.shape[1]), x.dtype) for x in weights]
         kept = pltpu.VMEM((self.chips, 2 * self.tokens, DH), jnp.bfloat16)
         sums = pltpu.VMEM((self.rows, DH), jnp.float32)
         return self.call(
             functools.partial(last_kernel, self.chips),
             "attend_last",
             (*blocks, shift, *state, gain, *tables),
-            sources,
-            [out, out, picked],
-            [],
+            (*sources, *(in_hbm(x) for x in weights)),
+            [out, out, picked, picked],
+            loaded,
             [
                 pltpu.VMEM((2 * CAP, self.width), jnp.float32),
                 pltpu.VMEM((STACK * 2 * self.tokens, DH), jnp.float32),
                 pltpu.SemaphoreType.DMA,
+                pltpu.SemaphoreType.DMA((len(weights),)),
                 kept,
                 kept,
                 sums,
@@ -421,38 +435,16 @@
     )(me, *(in_hbm(x) for x in arrays))
 
 
-def load_kernel(me_ref, source_ref, target_ref, sem):
-    copy = pltpu.make_async_copy(half_rows(me_ref, source_ref, False), target_ref, sem)
-    copy.start()
-    copy.wait()
-
-
 def half_rows(me_ref, ref, sibling):
     half = ref.shape[0] // 2
     side = 1 - me_ref[0] % 2 if sibling else me_ref[0] % 2
     return ref.at[pl.ds(pl.multiple_of(side * half, half), half), :]
 
 
-def load(me, x):
-    return pl.pallas_call(
-        load_kernel,
-        in_specs=[pl.BlockSpec(memory_space=pltpu.SMEM), pl.BlockSpec(memory_space=pl.ANY)],
-        out_specs=pl.BlockSpec(memory_space=pl.ANY),
-        out_shape=pltpu.VMEM((x.shape[0] // 2, x.shape[1]), x.dtype),
-        scratch_shapes=[pltpu.SemaphoreType.DMA],
-        compiler_params=pltpu.CompilerParams(vmem_limit_bytes=MIB),
-        cost_estimate=SMALL,
-        name="load",
-    )(me, in_hbm(x))
-
-
 def place_kernel(spots, *refs):
     blocks, out_ref = refs[: len(spots)], refs[-1]
-    middle = out_ref.shape[0] // 2
     for index, ref in zip(spots, blocks):
-        for core in range(2):
-            row = core * middle + index * CAP
-            out_ref[row : row + CAP] = ref[core * CAP : (core + 1) * CAP]
+        out_ref[index * CAP : (index + 1) * CAP] = ref[...]
 
 
 def place(blocks, spots, rows):
@@ -469,26 +461,6 @@
         cost_estimate=SMALL,
         name="place",
     )(*blocks, *earlier)
-
-
-def place_far_kernel(low_ref, high_ref, _, out_ref):
-    middle, row = out_ref.shape[0] // 2, out_ref.shape[0] // 2 - CAP
-    out_ref[row : row + CAP] = low_ref[...]
-    out_ref[middle + row : middle + row + CAP] = high_ref[...]
-
-
-def place_far(low, high, rows):
-    vmem = pl.BlockSpec(memory_space=pltpu.VMEM)
-    return pl.pallas_call(
-        place_far_kernel,
-        in_specs=[vmem] * 3,
-        out_specs=vmem,
-        out_shape=pltpu.VMEM(rows.shape, jnp.bfloat16),
-        input_output_aliases={2: 0},
-        compiler_params=pltpu.CompilerParams(vmem_limit_bytes=4 * MIB),
-        cost_estimate=SMALL,
-        name="place",
-    )(low, high, rows)
 
 
 def contract(rows_ref, gate_ref, up_ref, gate_sum, up_sum, order):
@@ -667,29 +639,22 @@
     )(*parts, table, *earlier)
 
 
-def add_kernel(row, columns, place, mine_ref, other_ref, *refs):
-    received_ref, out_ref = (refs[0] if len(refs) > 1 else None), refs[-1]
+def add_kernel(row, mine_ref, other_ref, *refs):
     rows = slice(row, row + CAP)
-    total = mine_ref[rows, columns].astype(jnp.float32) + other_ref[rows, columns].astype(jnp.float32)
-    if received_ref is None:
-        out_ref[...] = total.astype(jnp.bfloat16)
-        return
-    start, width = place, received_ref.shape[1]
-    part = total[:, start : start + width] + received_ref[...].astype(jnp.float32)
-    out_ref[:, start : start + width] = part.astype(jnp.bfloat16)
-    if width < out_ref.shape[1]:
-        rest = slice(width, None) if start == 0 else slice(0, start)
-        out_ref[:, rest] = total[:, rest].astype(jnp.bfloat16)
-
-
-def add_call(mine, other, index, columns, received=None, place=0):
+    total = mine_ref[rows].astype(jnp.float32) + other_ref[rows].astype(jnp.float32)
+    for ref in refs[:-1]:
+        total += ref[...].astype(jnp.float32)
+    refs[-1][...] = total.astype(jnp.bfloat16)
+
+
+def add_call(mine, other, index, received=None):
     vmem = pl.BlockSpec(memory_space=pltpu.VMEM)
     more = () if received is None else (received,)
     return pl.pallas_call(
-        functools.partial(add_kernel, index * CAP, columns, place),
+        functools.partial(add_kernel, index * CAP),
         in_specs=[vmem] * (2 + len(more)),
         out_specs=vmem,
-        out_shape=pltpu.VMEM((CAP, columns.stop - columns.start), jnp.bfloat16),
+        out_shape=pltpu.VMEM((CAP, mine.shape[1]), jnp.bfloat16),
         compiler_params=pltpu.CompilerParams(vmem_limit_bytes=4 * MIB),
         cost_estimate=SMALL,
         name="add",
@@ -697,22 +662,16 @@
 
 
 def reduce_chip_rows(pieces, half, chips, moves, token):
-    width = pieces[0][0].shape[1]
-    middle = width // 2
     chains = [(piece, side) for piece in range(len(pieces)) for side in range(2)]
     received = [None] * len(chains)
     for distance in range(half, 0, -1):
         for i, (piece, side) in enumerate(chains):
-            mine, other = pieces[piece]
-            if distance == half:
-                columns = slice(side * middle, (side + 1) * middle)
-                total = add_call(mine, other, chips - 1, columns)
-            else:
+            if distance == half and piece % 2 != side:
+                continue
+            if received[i] is not None:
                 received[i], token = lax.optimization_barrier((received[i], token))
-                index = distance if side else half - 1 + distance
-                place = side * middle if distance == half - 1 else 0
-                total = add_call(mine, other, index, slice(0, width), received[i], place)
-            received[i] = moves[side](total)
+            index = chips - 1 if distance == half else distance if side else half - 1 + distance
+            received[i] = moves[side](add_call(*pieces[piece], index, received[i]))
     return [(*pieces[p], *received[2 * p : 2 * p + 2]) for p in range(len(pieces))]
 
 
@@ -765,29 +724,28 @@
         state, _ = attention.step(blocks, [step, step, -step, -step], shift, state)
     opposite, state = lax.optimization_barrier((opposite, state))
     sources += opposite
-    mine, theirs, picked = attention.last(
-        opposite, shift, state, norm_gain[None, :], (table, sib_table), sources
+    mine, theirs, *picked, gate, up = attention.last(
+        opposite, shift, state, norm_gain[None, :], (table, sib_table), sources, (w_gate, w_up)
     )
 
-    picked, w_gate = lax.optimization_barrier((picked, w_gate))
-    from_left, from_right = go_right(picked), go_left(picked)
-    rows = place([picked], [0], (2 * chips * CAP, picked.shape[1]))
-    loaded, theirs = [load(me, w_gate)], swap(theirs)
+    moves = (go_right, go_left, go_right, go_left)
+    received = [move(picked[i // 2]) for i, move in enumerate(moves)]
+    rows = place(picked, [0, chips], (2 * chips * CAP, picked[0].shape[1]))
+    theirs = swap(theirs)
     for step in range(1, half):
-        from_left, rows, loaded = lax.optimization_barrier((from_left, rows, loaded))
-        from_right, _, rows = lax.optimization_barrier((from_right, from_left, rows))
-        blocks = [from_left, from_right]
-        if step < half - 1:
-            from_left, from_right = go_right(from_left), go_left(from_right)
-        else:
-            far = go_right(from_left[:CAP]), go_left(from_right[CAP:])
-        rows = place(blocks, [step, half - 1 + step], rows)
-        if step == 1:
-            rows, w_up = lax.optimization_barrier((rows, w_up))
-            loaded = loaded + [load(me, w_up)]
+        blocks, far = [], []
+        for i, move in enumerate(moves):
+            block, rows = lax.optimization_barrier((received[i], rows))
+            blocks.append(block)
+            if step < half - 1:
+                received[i] = move(block)
+            elif i in (0, 3):
+                far.append(move(block))
+        spots = [core * chips + side * (half - 1) + step for core in range(2) for side in range(2)]
+        rows = place(blocks, spots, rows)
     far, rows = lax.optimization_barrier((far, rows))
-    rows = place_far(*far, rows)
-    hidden, downs = hidden_calls(me, rows, swap(rows), loaded, w_gate, w_up, w_down)
+    rows = place(far, [chips - 1, 2 * chips - 1], rows)
+    hidden, downs = hidden_calls(me, rows, swap(rows), (gate, up), w_gate, w_up, w_down)
 
     partial = []
     for piece in range(PIECES):

time: 171 us -> 171 us (level)
  starting transfers between devices: 47 us -> 91.8 us
  waiting for transfers between devices: 89.2 us -> 49.6 us
  Pallas kernels: 33.6 us -> 28.2 us
    ppermute x19 -> x21, starting transfers between devices: 26.3 us -> 70.6 us  [per_device(): go_right = lambda x: lax.ppermute(x, 'ctx', right)]
    ppermute x18 -> x20, waiting for transfers between devices: 58.1 us -> 25 us  [per_device(): go_left = lambda x: lax.ppermute(x, 'ctx', left)]
    ppermute x19 -> x21, waiting for transfers between devices: 29.8 us -> 22.5 us  [per_device(): go_right = lambda x: lax.ppermute(x, 'ctx', right)]
    pallas_call x19 -> x14, Pallas kernels: 6.27 us -> 0.64 us  [add_call(): pl.pallas_call(functools.partial(add_kernel, index * CAP), in_specs=[vmem...]
    ppermute x18 -> x20, starting transfers between devices: 16.6 us -> 17.1 us  [per_device(): go_left = lambda x: lax.ppermute(x, 'ctx', left)]
  transfers between devices with their start and end apart: 46 -> 50, of which waited for: 32 -> 32; matrix products, arithmetic and copies ran while one was open for 0% -> 0% of each run, Pallas kernels for 14% -> 10%
where the time goes in v6:
time: 171 us
  starting transfers between devices  91.8 us (54%)
  waiting for transfers between devices  49.6 us (29%)
  Pallas kernels  28.2 us (16%)
    ppermute x21, starting transfers between devices, per_device(): go_right = lambda x: lax.ppermute(x, 'ctx', right)  70.6 us
    ppermute x20, waiting for transfers between devices, per_device(): go_left = lambda x: lax.ppermute(x, 'ctx', left)  25 us
    ppermute x21, waiting for transfers between devices, per_device(): go_right = lambda x: lax.ppermute(x, 'ctx', right)  22.5 us
    ppermute x20, starting transfers between devices, per_device(): go_left = lambda x: lax.ppermute(x, 'ctx', left)  17.1 us
    pallas_call x5, Pallas kernels, call(): pl.pallas_call(kernel, in_specs=[pl.BlockSpec(memory_space=pltpu.SMEM)] +...  8.57 us
    pallas_call x2, Pallas kernels, down_call(): pl.pallas_call(down_kernel, in_specs=[vmem] * 2 + more, out_specs=[vmem]...  4.7 us
    pallas_call x1, Pallas kernels, hidden_calls(): pl.pallas_call(first_kernel, in_specs=[pl.BlockSpec(memory_space=pltpu.SM...  4.63 us
    pallas_call x1, Pallas kernels, hidden_calls(): pl.pallas_call(second_kernel, in_specs=[vmem] * 6 + [anywhere], out_specs...  4.63 us
  transfers between devices with their start and end apart: 50, of which 32 were waited for; matrix products, arithmetic and copies ran while one was open for 0% of the time, Pallas kernels for 10%

profile of v6, /device:TPU:0, one launch (start us, length us, event | category | flops | bytes accessed | tf_op | source)
XLA Modules:
  0.0 170.8 jit_solution(16666628103953379618)
XLA Ops:
  0.6 1.9 %halves.1 = (bf16[256,512]{1,0:T(8,128)(2,1)S(1)}, bf16[256,512]{1,0:T(8,128)(2,1)S(1)}, bf16[128,4096]{1,0:T(8,128)(2,1)S(1)}, bf16[128,4096]{1,0:T(8,128)(2,1)S(1)}) custom-call(s32[1]{0:T(128)} %bitcast.me_ref.refs_0_, bf16[128,1024]{1,0:T(8,128)(2,1)} %refs_0_.2, bf16[128,1024]{1,0:T(8,128)(2,1)} %refs_1_.2, bf16[128,8192]{1,0:T(8,128)(2,1)} %refs_2_.1), custom_call_target="tpu_custom_call" | custom-call | flops 1 | bytes 1 | tf_op jit(solution)/shard_map/halves/pallas_call | solution.py:426
  3.1 3.0 %collective-permute-start.1 = (bf16[256,512]{1,0:T(8,128)(2,1)S(1)}, bf16[256,512]{1,0:T(8,128)(2,1)S(1)}, u32[]{:S(2)}, u32[]{:S(2)}) collective-permute-start(bf16[256,512]{1,0:T(8,128)(2,1)S(1)} %get-tuple-element.92.own_ref.refs_9_), channel_id=1, source_target_pairs={{0,4},{1,5},{4,8},{5,9},{8,12},{9,13},{12,14},{13,15},{14,10},{15,... | collective-permute-start | bytes 786440 | tf_op jit(solution)/shard_map/ppermute | solution.py:681
  8.3 3.8 %attend_own.1 = (f32[4,2048,128]{2,1,0:T(8,128)S(1)}, f32[4,2048,128]{2,1,0:T(8,128)S(1)}, f32[4,2048,128]{2,1,0:T(8,128)S(1)}) custom-call(s32[1]{0:T(128)} %bitcast.me_ref.refs_0_, bf16[128,4096]{1,0:T(8,128)(2,1)S(1)} %get-tuple-element.90.q_ref, bf16[128,4096]{1,0:T(8,128)(2,1)S(1)} %collective-permute-done.sib_q_ref, ...), custom_call_target="tpu_custom_call" | custom-call | flops 1 | bytes 1 | tf_op jit(solution)/shard_map/attend_own/pallas_call | solution.py:332
  13.2 2.2 %collective-permute-done.2.refs_2_.refs_13_ = bf16[256,512]{1,0:T(8,128)(2,1)S(1)} collective-permute-done((bf16[256,512]{1,0:T(8,128)(2,1)S(1)}, bf16[256,512]{1,0:T(8,128)(2,1)S(1)}, u32[]{:S(2)}, u32[]{:S(2)}) %collective-permute-start.2) | collective-permute-done | bytes 262176 | tf_op jit(solution)/shard_map/ppermute | solution.py:682
  18.5 1.9 %collective-permute-start.10 = (bf16[256,512]{1,0:T(8,128)(2,1)S(1)}, bf16[256,512]{1,0:T(8,128)(2,1)S(1)}, u32[]{:S(2)}, u32[]{:S(2)}) collective-permute-start(bf16[256,512]{1,0:T(8,128)(2,1)S(1)} %collective-permute-done.6.refs_1_.refs_12_), channel_id=1, source_target_pairs={{0,4},{1,5},{4,8},{5,9},{8,12},{9,13},{12,14},{13,15},{14,10},{15,... | collective-permute-start | bytes 786440 | tf_op jit(solution)/shard_map/ppermute | solution.py:681
  20.6 3.4 %collective-permute-done.4.refs_0_.refs_15_ = bf16[256,512]{1,0:T(8,128)(2,1)S(1)} collective-permute-done((bf16[256,512]{1,0:T(8,128)(2,1)S(1)}, bf16[256,512]{1,0:T(8,128)(2,1)S(1)}, u32[]{:S(2)}, u32[]{:S(2)}) %collective-permute-start.4) | collective-permute-done | bytes 262176 | tf_op jit(solution)/shard_map/ppermute | solution.py:681
  24.0 1.7 %collective-permute-done.5.refs_2_.refs_17_ = bf16[256,512]{1,0:T(8,128)(2,1)S(1)} collective-permute-done((bf16[256,512]{1,0:T(8,128)(2,1)S(1)}, bf16[256,512]{1,0:T(8,128)(2,1)S(1)}, u32[]{:S(2)}, u32[]{:S(2)}) %collective-permute-start.5) | collective-permute-done | bytes 262176 | tf_op jit(solution)/shard_map/ppermute | solution.py:682
  25.7 2.4 %collective-permute-start.8 = (bf16[256,512]{1,0:T(8,128)(2,1)S(1)}, bf16[256,512]{1,0:T(8,128)(2,1)S(1)}, u32[]{:S(2)}, u32[]{:S(2)}) collective-permute-start(bf16[256,512]{1,0:T(8,128)(2,1)S(1)} %collective-permute-done.4.refs_0_.refs_15_), channel_id=1, source_target_pairs={{0,4},{1,5},{4,8},{5,9},{8,12},{9,13},{12,14},{13,15},{14,10},{15,... | collective-permute-start | bytes 786440 | tf_op jit(solution)/shard_map/ppermute | solution.py:681
  33.0 2.2 %collective-permute-done.8.refs_0_.refs_19_ = bf16[256,512]{1,0:T(8,128)(2,1)S(1)} collective-permute-done((bf16[256,512]{1,0:T(8,128)(2,1)S(1)}, bf16[256,512]{1,0:T(8,128)(2,1)S(1)}, u32[]{:S(2)}, u32[]{:S(2)}) %collective-permute-start.8) | collective-permute-done | bytes 262176 | tf_op jit(solution)/shard_map/ppermute | solution.py:681
  36.9 3.2 %collective-permute-start.12 = (bf16[256,512]{1,0:T(8,128)(2,1)S(1)}, bf16[256,512]{1,0:T(8,128)(2,1)S(1)}, u32[]{:S(2)}, u32[]{:S(2)}) collective-permute-start(bf16[256,512]{1,0:T(8,128)(2,1)S(1)} %collective-permute-done.8.refs_0_.refs_19_), channel_id=1, source_target_pairs={{0,4},{1,5},{4,8},{5,9},{8,12},{9,13},{12,14},{13,15},{14,10},{15,... | collective-permute-start | bytes 786440 | tf_op jit(solution)/shard_map/ppermute | solution.py:681
  44.8 4.3 %collective-permute-done.15.refs_1_.refs_24_ = bf16[128,512]{1,0:T(8,128)(2,1)S(1)} collective-permute-done((bf16[128,512]{1,0:T(8,128)(2,1)S(1)}, bf16[128,512]{1,0:T(8,128)(2,1)S(1)}, u32[]{:S(2)}, u32[]{:S(2)}) %collective-permute-start.15) | collective-permute-done | bytes 131104 | tf_op jit(solution)/shard_map/ppermute | solution.py:681
  49.8 4.7 %attend_last.1 = (bf16[128,4096]{1,0:T(8,128)(2,1)S(1)}, bf16[128,4096]{1,0:T(8,128)(2,1)S(1)}, bf16[16,4224]{1,0:T(8,128)(2,1)S(1)}, bf16[16,4224]{1,0:T(8,128)...) custom-call(s32[1]{0:T(128)} %bitcast.me_ref.refs_0_, ...), custom_call_target="tpu_custom_call" | custom-call | flops 1 | bytes 1 | tf_op jit(solution)/shard_map/attend_last/pallas_call | solution.py:332
  58.6 2.2 %collective-permute-done.18.refs_0_ = bf16[16,4224]{1,0:T(8,128)(2,1)S(1)} collective-permute-done((bf16[16,4224]{1,0:T(8,128)(2,1)S(1)}, bf16[16,4224]{1,0:T(8,128)(2,1)S(1)}, u32[]{:S(2)}, u32[]{:S(2)}) %collective-permute-start.18) | collective-permute-done | bytes 135200 | tf_op jit(solution)/shard_map/ppermute | solution.py:681
  63.5 38.0 %collective-permute-start.25 = (bf16[16,4224]{1,0:T(8,128)(2,1)S(1)}, bf16[16,4224]{1,0:T(8,128)(2,1)S(1)}, u32[]{:S(2)}, u32[]{:S(2)}) collective-permute-start(bf16[16,4224]{1,0:T(8,128)(2,1)S(1)} %collective-permute-done.21.refs_2_), channel_id=1, source_target_pairs={{0,4},{1,5},{4,8},{5,9},{8,12},{9,13},{12,14},{13,15},{14,10},{15,... | collective-permute-start | bytes 405512 | tf_op jit(solution)/shard_map/ppermute | solution.py:681
  101.8 2.8 %collective-permute-done.24.refs_1_ = bf16[16,4224]{1,0:T(8,128)(2,1)S(1)} collective-permute-done((bf16[16,4224]{1,0:T(8,128)(2,1)S(1)}, bf16[16,4224]{1,0:T(8,128)(2,1)S(1)}, u32[]{:S(2)}, u32[]{:S(2)}) %collective-permute-start.24) | collective-permute-done | bytes 135200 | tf_op jit(solution)/shard_map/ppermute | solution.py:682
  104.5 5.0 %collective-permute-start.23 = (bf16[16,4224]{1,0:T(8,128)(2,1)S(1)}, bf16[16,4224]{1,0:T(8,128)(2,1)S(1)}, u32[]{:S(2)}, u32[]{:S(2)}) collective-permute-start(bf16[16,4224]{1,0:T(8,128)(2,1)S(1)} %collective-permute-done.19.refs_0_), channel_id=1, source_target_pairs={{0,4},{1,5},{4,8},{5,9},{8,12},{9,13},{12,14},{13,15},{14,10},{15,... | collective-permute-start | bytes 405512 | tf_op jit(solution)/shard_map/ppermute | solution.py:681
  109.6 2.4 %collective-permute-start.29 = (bf16[16,4224]{1,0:T(8,128)(2,1)S(1)}, bf16[16,4224]{1,0:T(8,128)(2,1)S(1)}, u32[]{:S(2)}, u32[]{:S(2)}) collective-permute-start(bf16[16,4224]{1,0:T(8,128)(2,1)S(1)} %collective-permute-done.25.refs_2_), channel_id=1, source_target_pairs={{0,4},{1,5},{4,8},{5,9},{8,12},{9,13},{12,14},{13,15},{14,10},{15,... | collective-permute-start | bytes 405512 | tf_op jit(solution)/shard_map/ppermute | solution.py:681
  112.7 2.4 %collective-permute-done.30.refs_1_ = bf16[16,4224]{1,0:T(8,128)(2,1)S(1)} collective-permute-done((bf16[16,4224]{1,0:T(8,128)(2,1)S(1)}, bf16[16,4224]{1,0:T(8,128)(2,1)S(1)}, u32[]{:S(2)}, u32[]{:S(2)}) %collective-permute-start.30) | collective-permute-done | bytes 135200 | tf_op jit(solution)/shard_map/ppermute | solution.py:682
  115.6 2.9 %collective-permute-done.28.refs_3_ = bf16[16,4224]{1,0:T(8,128)(2,1)S(1)} collective-permute-done((bf16[16,4224]{1,0:T(8,128)(2,1)S(1)}, bf16[16,4224]{1,0:T(8,128)(2,1)S(1)}, u32[]{:S(2)}, u32[]{:S(2)}) %collective-permute-start.28) | collective-permute-done | bytes 135200 | tf_op jit(solution)/shard_map/ppermute | solution.py:682
  118.5 2.1 %collective-permute-start.27 = (bf16[16,4224]{1,0:T(8,128)(2,1)S(1)}, bf16[16,4224]{1,0:T(8,128)(2,1)S(1)}, u32[]{:S(2)}, u32[]{:S(2)}) collective-permute-start(bf16[16,4224]{1,0:T(8,128)(2,1)S(1)} %collective-permute-done.23.refs_0_), channel_id=1, source_target_pairs={{0,4},{1,5},{4,8},{5,9},{8,12},{9,13},{12,14},{13,15},{14,10},{15,... | collective-permute-start | bytes 405512 | tf_op jit(solution)/shard_map/ppermute | solution.py:681
  120.6 2.9 %collective-permute-done.31.refs_1_ = bf16[16,4224]{1,0:T(8,128)(2,1)S(1)} collective-permute-done((bf16[16,4224]{1,0:T(8,128)(2,1)S(1)}, bf16[16,4224]{1,0:T(8,128)(2,1)S(1)}, u32[]{:S(2)}, u32[]{:S(2)}) %collective-permute-start.31) | collective-permute-done | bytes 135200 | tf_op jit(solution)/shard_map/ppermute | solution.py:682
  124.8 4.6 %hidden_first.1 = (f32[256,768]{1,0:T(8,128)S(1)}, f32[256,768]{1,0:T(8,128)S(1)}, bf16[4096,768]{1,0:T(8,128)(2,1)S(1)}, bf16[4096,768]{1,0:T(8,128)(2,1)S(1)}) custom-call(s32[1]{0:T(128)} %bitcast.me_ref.refs_0_, bf16[256,4224]{1,0:T(8,128)(2,1)S(1)} %place.9.rows_ref.own_ref, bf16[4096,768]{1,0:T(8,128)(2,1)S(1)} %get-tuple-element.161.gate_ref, ...), custom_call_target="tpu_custom_call" | custom-call | flops 3221225472 | bytes 12582912 | tf_op jit(solution)/shard_map/hidden_first/pallas_call | solution.py:529
  129.5 4.6 %hidden_second.1 = (bf16[256,768]{1,0:T(8,128)(2,1)S(1)}, bf16[768,4096]{1,0:T(8,128)(2,1)S(1)}, bf16[768,4096]{1,0:T(8,128)(2,1)S(1)}) custom-call(bf16[256,4224]{1,0:T(8,128)(2,1)S(1)} %collective-permute-done.32.rows_ref, bf16[4096,768]{1,0:T(8,128)(2,1)S(1)} %get-tuple-element.163.gate_ref, bf16[4096,768]{1,0:T(8,128)(2,1)S(1)} %get-tuple-element.164.up_ref, ...), custom_call_target="tpu_custom_call" | custom-call | flops 3221225472 | bytes 12582912 | tf_op jit(solution)/shard_map/hidden_second/pallas_call | solution.py:539
  134.1 2.4 %down.2 = (bf16[128,4096]{1,0:T(8,128)(2,1)S(1)}, bf16[128,4096]{1,0:T(8,128)(2,1)S(1)}, bf16[128,8192]{1,0:T(8,128)(2,1)}) custom-call(bf16[256,768]{1,0:T(8,128)(2,1)S(1)} %get-tuple-element.167.hidden_ref, bf16[768,4096]{1,0:T(8,128)(2,1)S(1)} %get-tuple-element.168.down_ref, s32[1]{0:T(128)} %bitcast.me_ref.refs_0_, ...), custom_call_target="tpu_custom_call" | custom-call | flops 1610612736 | bytes 8388608 | tf_op jit(solution)/shard_map/down/pallas_call | solution.py:591
  136.7 2.3 %down.3 = (bf16[128,4096]{1,0:T(8,128)(2,1)S(1)}, bf16[128,4096]{1,0:T(8,128)(2,1)S(1)}) custom-call(bf16[256,768]{1,0:T(8,128)(2,1)S(1)} %get-tuple-element.167.hidden_ref, bf16[768,4096]{1,0:T(8,128)(2,1)S(1)} %get-tuple-element.172.down_ref), custom_call_target="tpu_custom_call" | custom-call | flops 1610612736 | bytes 8388608 | tf_op jit(solution)/shard_map/down/pallas_call | solution.py:591
  141.8 2.5 %collective-permute-start.38 = (bf16[16,4096]{1,0:T(8,128)(2,1)S(1)}, bf16[16,4096]{1,0:T(8,128)(2,1)S(1)}, u32[]{:S(2)}, u32[]{:S(2)}) collective-permute-start(bf16[16,4096]{1,0:T(8,128)(2,1)S(1)} %add.17), channel_id=1, source_target_pairs={{4,0},{5,1},{8,4},{9,5},{12,8},{13,9},{14,12},{15,13},{10,14},{11,... | collective-permute-start | bytes 393224 | tf_op jit(solution)/shard_map/ppermute | solution.py:682
  144.4 2.1 %collective-permute-start.47 = (bf16[16,4096]{1,0:T(8,128)(2,1)S(1)}, bf16[16,4096]{1,0:T(8,128)(2,1)S(1)}, u32[]{:S(2)}, u32[]{:S(2)}) collective-permute-start(bf16[16,4096]{1,0:T(8,128)(2,1)S(1)} %add.25), channel_id=1, source_target_pairs={{4,0},{5,1},{8,4},{9,5},{12,8},{13,9},{14,12},{15,13},{10,14},{11,... | collective-permute-start | bytes 393224 | tf_op jit(solution)/shard_map/ppermute | solution.py:682
  148.2 2.5 %collective-permute-start.39 = (bf16[16,4096]{1,0:T(8,128)(2,1)S(1)}, bf16[16,4096]{1,0:T(8,128)(2,1)S(1)}, u32[]{:S(2)}, u32[]{:S(2)}) collective-permute-start(bf16[16,4096]{1,0:T(8,128)(2,1)S(1)} %add.18), channel_id=1, source_target_pairs={{4,0},{5,1},{8,4},{9,5},{12,8},{13,9},{14,12},{15,13},{10,14},{11,... | collective-permute-start | bytes 393224 | tf_op jit(solution)/shard_map/ppermute | solution.py:682
  151.0 2.0 %collective-permute-done.35.refs_0_ = bf16[16,4096]{1,0:T(8,128)(2,1)S(1)} collective-permute-done((bf16[16,4096]{1,0:T(8,128)(2,1)S(1)}, bf16[16,4096]{1,0:T(8,128)(2,1)S(1)}, u32[]{:S(2)}, u32[]{:S(2)}) %collective-permute-start.35) | collective-permute-done | bytes 131104 | tf_op jit(solution)/shard_map/ppermute | solution.py:681
  155.3 2.1 %collective-permute-start.40 = (bf16[16,4096]{1,0:T(8,128)(2,1)S(1)}, bf16[16,4096]{1,0:T(8,128)(2,1)S(1)}, u32[]{:S(2)}, u32[]{:S(2)}) collective-permute-start(bf16[16,4096]{1,0:T(8,128)(2,1)S(1)} %add.19), channel_id=1, source_target_pairs={{4,0},{5,1},{8,4},{9,5},{12,8},{13,9},{14,12},{15,13},{10,14},{11,... | collective-permute-start | bytes 393224 | tf_op jit(solution)/shard_map/ppermute | solution.py:682
  157.3 1.9 %collective-permute-done.48.refs_0_ = bf16[16,4096]{1,0:T(8,128)(2,1)S(1)} collective-permute-done((bf16[16,4096]{1,0:T(8,128)(2,1)S(1)}, bf16[16,4096]{1,0:T(8,128)(2,1)S(1)}, u32[]{:S(2)}, u32[]{:S(2)}) %collective-permute-start.48) | collective-permute-done | bytes 131104 | tf_op jit(solution)/shard_map/ppermute | solution.py:682
  166.0 1.8 %collective-permute-done.46.c_ref = bf16[16,4096]{1,0:T(8,128)(2,1)S(1)} collective-permute-done((bf16[16,4096]{1,0:T(8,128)(2,1)S(1)}, bf16[16,4096]{1,0:T(8,128)(2,1)S(1)}, u32[]{:S(2)}, u32[]{:S(2)}) %collective-permute-start.46) | collective-permute-done | bytes 131104 | tf_op jit(solution)/shard_map/ppermute | solution.py:681
  (115 shorter events, 45.6 us)
Async XLA Ops:
  3.1 10.0 %collective-permute-start.1 = (bf16[256,512]{1,0:T(8,128)(2,1)S(1)}, bf16[256,512]{1,0:T(8,128)(2,1)S(1)}, u32[]{:S(2)}, u32[]{:S(2)}) collective-permute-start(bf16[256,512]{1,0:T(8,128)(2,1)S(1)} %get-tuple-element.92.own_ref.refs_9_), channel_id=1, source_target_pairs={{0,4},{1,5},{4,8},{5,9},{8,12},{9,13},{12,14},{13,15},{14,10},{15,... | collective-permute-start | bytes 786440 | tf_op jit(solution)/shard_map/ppermute | solution.py:681
  6.1 9.2 %collective-permute-start.2 = (bf16[256,512]{1,0:T(8,128)(2,1)S(1)}, bf16[256,512]{1,0:T(8,128)(2,1)S(1)}, u32[]{:S(2)}, u32[]{:S(2)}) collective-permute-start(bf16[256,512]{1,0:T(8,128)(2,1)S(1)} %get-tuple-element.92.own_ref.refs_9_), channel_id=1, source_target_pairs={{4,0},{5,1},{8,4},{9,5},{12,8},{13,9},{14,12},{15,13},{10,14},{11,... | collective-permute-start | bytes 786440 | tf_op jit(solution)/shard_map/ppermute | solution.py:682
  6.1 12.3 %collective-permute-start.6 = (bf16[256,512]{1,0:T(8,128)(2,1)S(1)}, bf16[256,512]{1,0:T(8,128)(2,1)S(1)}, u32[]{:S(2)}, u32[]{:S(2)}) collective-permute-start(bf16[256,512]{1,0:T(8,128)(2,1)S(1)} %get-tuple-element.93), channel_id=1, source_target_pairs={{0,5},{1,4},{4,9},{5,8},{8,13},{9,12},{12,15},{13,14},{14,11},{15,... | collective-permute-start | bytes 786440 | tf_op jit(solution)/shard_map/ppermute | solution.py:706
  7.3 11.3 %collective-permute-start.7 = (bf16[256,512]{1,0:T(8,128)(2,1)S(1)}, bf16[256,512]{1,0:T(8,128)(2,1)S(1)}, u32[]{:S(2)}, u32[]{:S(2)}) collective-permute-start(bf16[256,512]{1,0:T(8,128)(2,1)S(1)} %get-tuple-element.93), channel_id=1, source_target_pairs={{4,1},{5,0},{8,5},{9,4},{12,9},{13,8},{14,13},{15,12},{10,15},{11,... | collective-permute-start | bytes 786440 | tf_op jit(solution)/shard_map/ppermute | solution.py:706
  15.3 8.7 %collective-permute-start.4 = (bf16[256,512]{1,0:T(8,128)(2,1)S(1)}, bf16[256,512]{1,0:T(8,128)(2,1)S(1)}, u32[]{:S(2)}, u32[]{:S(2)}) collective-permute-start(bf16[256,512]{1,0:T(8,128)(2,1)S(1)} %collective-permute-done.1.refs_0_.refs_11_), channel_id=1, source_target_pairs={{0,4},{1,5},{4,8},{5,9},{8,12},{9,13},{12,14},{13,15},{14,10},{15,... | collective-permute-start | bytes 786440 | tf_op jit(solution)/shard_map/ppermute | solution.py:681
  16.9 8.8 %collective-permute-start.5 = (bf16[256,512]{1,0:T(8,128)(2,1)S(1)}, bf16[256,512]{1,0:T(8,128)(2,1)S(1)}, u32[]{:S(2)}, u32[]{:S(2)}) collective-permute-start(bf16[256,512]{1,0:T(8,128)(2,1)S(1)} %collective-permute-done.2.refs_2_.refs_13_), channel_id=1, source_target_pairs={{4,0},{5,1},{8,4},{9,5},{12,8},{13,9},{14,12},{15,13},{10,14},{11,... | collective-permute-start | bytes 786440 | tf_op jit(solution)/shard_map/ppermute | solution.py:682
  18.5 11.0 %collective-permute-start.10 = (bf16[256,512]{1,0:T(8,128)(2,1)S(1)}, bf16[256,512]{1,0:T(8,128)(2,1)S(1)}, u32[]{:S(2)}, u32[]{:S(2)}) collective-permute-start(bf16[256,512]{1,0:T(8,128)(2,1)S(1)} %collective-permute-done.6.refs_1_.refs_12_), channel_id=1, source_target_pairs={{0,4},{1,5},{4,8},{5,9},{8,12},{9,13},{12,14},{13,15},{14,10},{15,... | collective-permute-start | bytes 786440 | tf_op jit(solution)/shard_map/ppermute | solution.py:681
  20.5 10.5 %collective-permute-start.11 = (bf16[256,512]{1,0:T(8,128)(2,1)S(1)}, bf16[256,512]{1,0:T(8,128)(2,1)S(1)}, u32[]{:S(2)}, u32[]{:S(2)}) collective-permute-start(bf16[256,512]{1,0:T(8,128)(2,1)S(1)} %collective-permute-done.7.refs_3_.refs_14_), channel_id=1, source_target_pairs={{4,0},{5,1},{8,4},{9,5},{12,8},{13,9},{14,12},{15,13},{10,14},{11,... | collective-permute-start | bytes 786440 | tf_op jit(solution)/shard_map/ppermute | solution.py:682
  25.7 9.5 %collective-permute-start.8 = (bf16[256,512]{1,0:T(8,128)(2,1)S(1)}, bf16[256,512]{1,0:T(8,128)(2,1)S(1)}, u32[]{:S(2)}, u32[]{:S(2)}) collective-permute-start(bf16[256,512]{1,0:T(8,128)(2,1)S(1)} %collective-permute-done.4.refs_0_.refs_15_), channel_id=1, source_target_pairs={{0,4},{1,5},{4,8},{5,9},{8,12},{9,13},{12,14},{13,15},{14,10},{15,... | collective-permute-start | bytes 786440 | tf_op jit(solution)/shard_map/ppermute | solution.py:681
  28.1 8.8 %collective-permute-start.9 = (bf16[256,512]{1,0:T(8,128)(2,1)S(1)}, bf16[256,512]{1,0:T(8,128)(2,1)S(1)}, u32[]{:S(2)}, u32[]{:S(2)}) collective-permute-start(bf16[256,512]{1,0:T(8,128)(2,1)S(1)} %collective-permute-done.5.refs_2_.refs_17_), channel_id=1, source_target_pairs={{4,0},{5,1},{8,4},{9,5},{12,8},{13,9},{14,12},{15,13},{10,14},{11,... | collective-permute-start | bytes 786440 | tf_op jit(solution)/shard_map/ppermute | solution.py:682
  31.0 9.8 %collective-permute-start.13 = (bf16[256,512]{1,0:T(8,128)(2,1)S(1)}, bf16[256,512]{1,0:T(8,128)(2,1)S(1)}, u32[]{:S(2)}, u32[]{:S(2)}) collective-permute-start(bf16[256,512]{1,0:T(8,128)(2,1)S(1)} %collective-permute-done.10.refs_1_.refs_16_), channel_id=1, source_target_pairs={{0,4},{1,5},{4,8},{5,9},{8,12},{9,13},{12,14},{13,15},{14,10},{15,... | collective-permute-start | bytes 786440 | tf_op jit(solution)/shard_map/ppermute | solution.py:681
  32.6 10.0 %collective-permute-start.14 = (bf16[256,512]{1,0:T(8,128)(2,1)S(1)}, bf16[256,512]{1,0:T(8,128)(2,1)S(1)}, u32[]{:S(2)}, u32[]{:S(2)}) collective-permute-start(bf16[256,512]{1,0:T(8,128)(2,1)S(1)} %collective-permute-done.11.refs_3_.refs_18_), channel_id=1, source_target_pairs={{4,0},{5,1},{8,4},{9,5},{12,8},{13,9},{14,12},{15,13},{10,14},{11,... | collective-permute-start | bytes 786440 | tf_op jit(solution)/shard_map/ppermute | solution.py:682
  36.9 12.9 %collective-permute-start.12 = (bf16[256,512]{1,0:T(8,128)(2,1)S(1)}, bf16[256,512]{1,0:T(8,128)(2,1)S(1)}, u32[]{:S(2)}, u32[]{:S(2)}) collective-permute-start(bf16[256,512]{1,0:T(8,128)(2,1)S(1)} %collective-permute-done.8.refs_0_.refs_19_), channel_id=1, source_target_pairs={{0,4},{1,5},{4,8},{5,9},{8,12},{9,13},{12,14},{13,15},{14,10},{15,... | collective-permute-start | bytes 786440 | tf_op jit(solution)/shard_map/ppermute | solution.py:681
  42.5 6.6 %collective-permute-start.15 = (bf16[128,512]{1,0:T(8,128)(2,1)S(1)}, bf16[128,512]{1,0:T(8,128)(2,1)S(1)}, u32[]{:S(2)}, u32[]{:S(2)}) collective-permute-start(bf16[128,512]{1,0:T(8,128)(2,1)S(1)} %slice.6), channel_id=1, source_target_pairs={{0,4},{1,5},{4,8},{5,9},{8,12},{9,13},{12,14},{13,15},{14,10},{15,... | collective-permute-start | bytes 393224 | tf_op jit(solution)/shard_map/ppermute | solution.py:681
  54.5 6.4 %collective-permute-start.18 = (bf16[16,4224]{1,0:T(8,128)(2,1)S(1)}, bf16[16,4224]{1,0:T(8,128)(2,1)S(1)}, u32[]{:S(2)}, u32[]{:S(2)}) collective-permute-start(bf16[16,4224]{1,0:T(8,128)(2,1)S(1)} %get-tuple-element.132.refs_0_), channel_id=1, source_target_pairs={{0,4},{1,5},{4,8},{5,9},{8,12},{9,13},{12,14},{13,15},{14,10},{15,... | collective-permute-start | bytes 405512 | tf_op jit(solution)/shard_map/ppermute | solution.py:681
  56.2 6.5 %collective-permute-start.20 = (bf16[16,4224]{1,0:T(8,128)(2,1)S(1)}, bf16[16,4224]{1,0:T(8,128)(2,1)S(1)}, u32[]{:S(2)}, u32[]{:S(2)}) collective-permute-start(bf16[16,4224]{1,0:T(8,128)(2,1)S(1)} %get-tuple-element.132.refs_0_), channel_id=1, source_target_pairs={{4,0},{5,1},{8,4},{9,5},{12,8},{13,9},{14,12},{15,13},{10,14},{11,... | collective-permute-start | bytes 405512 | tf_op jit(solution)/shard_map/ppermute | solution.py:682
  56.6 6.9 %collective-permute-start.21 = (bf16[16,4224]{1,0:T(8,128)(2,1)S(1)}, bf16[16,4224]{1,0:T(8,128)(2,1)S(1)}, u32[]{:S(2)}, u32[]{:S(2)}) collective-permute-start(bf16[16,4224]{1,0:T(8,128)(2,1)S(1)} %get-tuple-element.133.refs_1_), channel_id=1, source_target_pairs={{0,4},{1,5},{4,8},{5,9},{8,12},{9,13},{12,14},{13,15},{14,10},{15,... | collective-permute-start | bytes 405512 | tf_op jit(solution)/shard_map/ppermute | solution.py:681
  58.3 43.2 %collective-permute-start.22 = (bf16[16,4224]{1,0:T(8,128)(2,1)S(1)}, bf16[16,4224]{1,0:T(8,128)(2,1)S(1)}, u32[]{:S(2)}, u32[]{:S(2)}) collective-permute-start(bf16[16,4224]{1,0:T(8,128)(2,1)S(1)} %get-tuple-element.133.refs_1_), channel_id=1, source_target_pairs={{4,0},{5,1},{8,4},{9,5},{12,8},{13,9},{14,12},{15,13},{10,14},{11,... | collective-permute-start | bytes 405512 | tf_op jit(solution)/shard_map/ppermute | solution.py:682
  60.9 40.9 %collective-permute-start.19 = (bf16[16,4224]{1,0:T(8,128)(2,1)S(1)}, bf16[16,4224]{1,0:T(8,128)(2,1)S(1)}, u32[]{:S(2)}, u32[]{:S(2)}) collective-permute-start(bf16[16,4224]{1,0:T(8,128)(2,1)S(1)} %collective-permute-done.18.refs_0_), channel_id=1, source_target_pairs={{0,4},{1,5},{4,8},{5,9},{8,12},{9,13},{12,14},{13,15},{14,10},{15,... | collective-permute-start | bytes 405512 | tf_op jit(solution)/shard_map/ppermute | solution.py:681
  62.7 41.9 %collective-permute-start.24 = (bf16[16,4224]{1,0:T(8,128)(2,1)S(1)}, bf16[16,4224]{1,0:T(8,128)(2,1)S(1)}, u32[]{:S(2)}, u32[]{:S(2)}) collective-permute-start(bf16[16,4224]{1,0:T(8,128)(2,1)S(1)} %collective-permute-done.20.refs_1_), channel_id=1, source_target_pairs={{4,0},{5,1},{8,4},{9,5},{12,8},{13,9},{14,12},{15,13},{10,14},{11,... | collective-permute-start | bytes 405512 | tf_op jit(solution)/shard_map/ppermute | solution.py:682
  63.5 46.1 %collective-permute-start.25 = (bf16[16,4224]{1,0:T(8,128)(2,1)S(1)}, bf16[16,4224]{1,0:T(8,128)(2,1)S(1)}, u32[]{:S(2)}, u32[]{:S(2)}) collective-permute-start(bf16[16,4224]{1,0:T(8,128)(2,1)S(1)} %collective-permute-done.21.refs_2_), channel_id=1, source_target_pairs={{0,4},{1,5},{4,8},{5,9},{8,12},{9,13},{12,14},{13,15},{14,10},{15,... | collective-permute-start | bytes 405512 | tf_op jit(solution)/shard_map/ppermute | solution.py:681
  101.6 10.5 %collective-permute-start.26 = (bf16[16,4224]{1,0:T(8,128)(2,1)S(1)}, bf16[16,4224]{1,0:T(8,128)(2,1)S(1)}, u32[]{:S(2)}, u32[]{:S(2)}) collective-permute-start(bf16[16,4224]{1,0:T(8,128)(2,1)S(1)} %collective-permute-done.22.refs_3_), channel_id=1, source_target_pairs={{4,0},{5,1},{8,4},{9,5},{12,8},{13,9},{14,12},{15,13},{10,14},{11,... | collective-permute-start | bytes 405512 | tf_op jit(solution)/shard_map/ppermute | solution.py:682
  104.5 8.1 %collective-permute-start.23 = (bf16[16,4224]{1,0:T(8,128)(2,1)S(1)}, bf16[16,4224]{1,0:T(8,128)(2,1)S(1)}, u32[]{:S(2)}, u32[]{:S(2)}) collective-permute-start(bf16[16,4224]{1,0:T(8,128)(2,1)S(1)} %collective-permute-done.19.refs_0_), channel_id=1, source_target_pairs={{0,4},{1,5},{4,8},{5,9},{8,12},{9,13},{12,14},{13,15},{14,10},{15,... | collective-permute-start | bytes 405512 | tf_op jit(solution)/shard_map/ppermute | solution.py:681
  112.0 6.4 %collective-permute-start.28 = (bf16[16,4224]{1,0:T(8,128)(2,1)S(1)}, bf16[16,4224]{1,0:T(8,128)(2,1)S(1)}, u32[]{:S(2)}, u32[]{:S(2)}) collective-permute-start(bf16[16,4224]{1,0:T(8,128)(2,1)S(1)} %collective-permute-done.26.refs_3_), channel_id=1, source_target_pairs={{4,0},{5,1},{8,4},{9,5},{12,8},{13,9},{14,12},{15,13},{10,14},{11,... | collective-permute-start | bytes 405512 | tf_op jit(solution)/shard_map/ppermute | solution.py:682
  124.3 9.8 %collective-permute-start.33 = (bf16[128,4096]{1,0:T(8,128)(2,1)S(1)}, bf16[128,4096]{1,0:T(8,128)(2,1)S(1)}, u32[]{:S(2)}, u32[]{:S(2)}) collective-permute-start(bf16[128,4096]{1,0:T(8,128)(2,1)S(1)} %get-tuple-element.170), channel_id=1, source_target_pairs={{0,1},{1,0},{2,3},{3,2},{4,5},{5,4},{6,7},{7,6},{8,9},{9,8},{10,11... | collective-permute-start | bytes 3145736 | tf_op jit(solution)/shard_map/ppermute | solution.py:683
  139.5 7.0 %collective-permute-start.43 = (bf16[16,4096]{1,0:T(8,128)(2,1)S(1)}, bf16[16,4096]{1,0:T(8,128)(2,1)S(1)}, u32[]{:S(2)}, u32[]{:S(2)}) collective-permute-start(bf16[16,4096]{1,0:T(8,128)(2,1)S(1)} %add.21), channel_id=1, source_target_pairs={{0,4},{1,5},{4,8},{5,9},{8,12},{9,13},{12,14},{13,15},{14,10},{15,... | collective-permute-start | bytes 393224 | tf_op jit(solution)/shard_map/ppermute | solution.py:681
  141.8 6.4 %collective-permute-start.38 = (bf16[16,4096]{1,0:T(8,128)(2,1)S(1)}, bf16[16,4096]{1,0:T(8,128)(2,1)S(1)}, u32[]{:S(2)}, u32[]{:S(2)}) collective-permute-start(bf16[16,4096]{1,0:T(8,128)(2,1)S(1)} %add.17), channel_id=1, source_target_pairs={{4,0},{5,1},{8,4},{9,5},{12,8},{13,9},{14,12},{15,13},{10,14},{11,... | collective-permute-start | bytes 393224 | tf_op jit(solution)/shard_map/ppermute | solution.py:682
  144.4 6.5 %collective-permute-start.47 = (bf16[16,4096]{1,0:T(8,128)(2,1)S(1)}, bf16[16,4096]{1,0:T(8,128)(2,1)S(1)}, u32[]{:S(2)}, u32[]{:S(2)}) collective-permute-start(bf16[16,4096]{1,0:T(8,128)(2,1)S(1)} %add.25), channel_id=1, source_target_pairs={{4,0},{5,1},{8,4},{9,5},{12,8},{13,9},{14,12},{15,13},{10,14},{11,... | collective-permute-start | bytes 393224 | tf_op jit(solution)/shard_map/ppermute | solution.py:682
  146.5 6.4 %collective-permute-start.35 = (bf16[16,4096]{1,0:T(8,128)(2,1)S(1)}, bf16[16,4096]{1,0:T(8,128)(2,1)S(1)}, u32[]{:S(2)}, u32[]{:S(2)}) collective-permute-start(bf16[16,4096]{1,0:T(8,128)(2,1)S(1)} %add.14), channel_id=1, source_target_pairs={{0,4},{1,5},{4,8},{5,9},{8,12},{9,13},{12,14},{13,15},{14,10},{15,... | collective-permute-start | bytes 393224 | tf_op jit(solution)/shard_map/ppermute | solution.py:681
  146.6 8.4 %collective-permute-start.44 = (bf16[16,4096]{1,0:T(8,128)(2,1)S(1)}, bf16[16,4096]{1,0:T(8,128)(2,1)S(1)}, u32[]{:S(2)}, u32[]{:S(2)}) collective-permute-start(bf16[16,4096]{1,0:T(8,128)(2,1)S(1)} %add.22), channel_id=1, source_target_pairs={{0,4},{1,5},{4,8},{5,9},{8,12},{9,13},{12,14},{13,15},{14,10},{15,... | collective-permute-start | bytes 393224 | tf_op jit(solution)/shard_map/ppermute | solution.py:681
  148.2 7.0 %collective-permute-start.39 = (bf16[16,4096]{1,0:T(8,128)(2,1)S(1)}, bf16[16,4096]{1,0:T(8,128)(2,1)S(1)}, u32[]{:S(2)}, u32[]{:S(2)}) collective-permute-start(bf16[16,4096]{1,0:T(8,128)(2,1)S(1)} %add.18), channel_id=1, source_target_pairs={{4,0},{5,1},{8,4},{9,5},{12,8},{13,9},{14,12},{15,13},{10,14},{11,... | collective-permute-start | bytes 393224 | tf_op jit(solution)/shard_map/ppermute | solution.py:682
  155.3 7.9 %collective-permute-start.40 = (bf16[16,4096]{1,0:T(8,128)(2,1)S(1)}, bf16[16,4096]{1,0:T(8,128)(2,1)S(1)}, u32[]{:S(2)}, u32[]{:S(2)}) collective-permute-start(bf16[16,4096]{1,0:T(8,128)(2,1)S(1)} %add.19), channel_id=1, source_target_pairs={{4,0},{5,1},{8,4},{9,5},{12,8},{13,9},{14,12},{15,13},{10,14},{11,... | collective-permute-start | bytes 393224 | tf_op jit(solution)/shard_map/ppermute | solution.py:682
  (21 other events, 113.0 us)

commit v7 on v6

--- a/solution.py
+++ b/solution.py
@@ -639,22 +639,29 @@
     )(*parts, table, *earlier)
 
 
-def add_kernel(row, mine_ref, other_ref, *refs):
+def add_kernel(row, columns, place, mine_ref, other_ref, *refs):
+    received_ref, out_ref = (refs[0] if len(refs) > 1 else None), refs[-1]
     rows = slice(row, row + CAP)
-    total = mine_ref[rows].astype(jnp.float32) + other_ref[rows].astype(jnp.float32)
-    for ref in refs[:-1]:
-        total += ref[...].astype(jnp.float32)
-    refs[-1][...] = total.astype(jnp.bfloat16)
-
-
-def add_call(mine, other, index, received=None):
+    total = mine_ref[rows, columns].astype(jnp.float32) + other_ref[rows, columns].astype(jnp.float32)
+    if received_ref is None:
+        out_ref[...] = total.astype(jnp.bfloat16)
+        return
+    start, width = place, received_ref.shape[1]
+    part = total[:, start : start + width] + received_ref[...].astype(jnp.float32)
+    out_ref[:, start : start + width] = part.astype(jnp.bfloat16)
+    if width < out_ref.shape[1]:
+        rest = slice(width, None) if start == 0 else slice(0, start)
+        out_ref[:, rest] = total[:, rest].astype(jnp.bfloat16)
+
+
+def add_call(mine, other, index, columns, received=None, place=0):
     vmem = pl.BlockSpec(memory_space=pltpu.VMEM)
     more = () if received is None else (received,)
     return pl.pallas_call(
-        functools.partial(add_kernel, index * CAP),
+        functools.partial(add_kernel, index * CAP, columns, place),
         in_specs=[vmem] * (2 + len(more)),
         out_specs=vmem,
-        out_shape=pltpu.VMEM((CAP, mine.shape[1]), jnp.bfloat16),
+        out_shape=pltpu.VMEM((CAP, columns.stop - columns.start), jnp.bfloat16),
         compiler_params=pltpu.CompilerParams(vmem_limit_bytes=4 * MIB),
         cost_estimate=SMALL,
         name="add",
@@ -662,16 +669,22 @@
 
 
 def reduce_chip_rows(pieces, half, chips, moves, token):
+    width = pieces[0][0].shape[1]
+    middle = width // 2
     chains = [(piece, side) for piece in range(len(pieces)) for side in range(2)]
     received = [None] * len(chains)
     for distance in range(half, 0, -1):
         for i, (piece, side) in enumerate(chains):
-            if distance == half and piece % 2 != side:
-                continue
-            if received[i] is not None:
+            mine, other = pieces[piece]
+            if distance == half:
+                columns = slice(side * middle, (side + 1) * middle)
+                total = add_call(mine, other, chips - 1, columns)
+            else:
                 received[i], token = lax.optimization_barrier((received[i], token))
-            index = chips - 1 if distance == half else distance if side else half - 1 + distance
-            received[i] = moves[side](add_call(*pieces[piece], index, received[i]))
+                index = distance if side else half - 1 + distance
+                place = side * middle if distance == half - 1 else 0
+                total = add_call(mine, other, index, slice(0, width), received[i], place)
+            received[i] = moves[side](total)
     return [(*pieces[p], *received[2 * p : 2 * p + 2]) for p in range(len(pieces))]
 
 
@@ -728,23 +741,21 @@
         opposite, shift, state, norm_gain[None, :], (table, sib_table), sources, (w_gate, w_up)
     )
 
-    moves = (go_right, go_left, go_right, go_left)
-    received = [move(picked[i // 2]) for i, move in enumerate(moves)]
+    chains = [(0, 1), (1, 0), (0, 0), (1, 1)]
+    moves = [(go_right, go_left)[side] for _, side in chains]
+    received = [move(picked[core]) for move, (core, _) in zip(moves, chains)]
     rows = place(picked, [0, chips], (2 * chips * CAP, picked[0].shape[1]))
     theirs = swap(theirs)
     for step in range(1, half):
-        blocks, far = [], []
+        spots = [core * chips + side * (half - 1) + step for core, side in chains]
+        blocks = list(received)
         for i, move in enumerate(moves):
-            block, rows = lax.optimization_barrier((received[i], rows))
-            blocks.append(block)
-            if step < half - 1:
-                received[i] = move(block)
-            elif i in (0, 3):
-                far.append(move(block))
-        spots = [core * chips + side * (half - 1) + step for core in range(2) for side in range(2)]
-        rows = place(blocks, spots, rows)
-    far, rows = lax.optimization_barrier((far, rows))
-    rows = place(far, [chips - 1, 2 * chips - 1], rows)
+            if step < half - 1 or i < 2:
+                blocks[i], rows = lax.optimization_barrier((received[i], rows))
+                received[i] = move(blocks[i])
+        if step < half - 1:
+            rows = place(blocks, spots, rows)
+    rows = place(blocks + received[:2], spots + [chips - 1, 2 * chips - 1], rows)
     hidden, downs = hidden_calls(me, rows, swap(rows), (gate, up), w_gate, w_up, w_down)
 
     partial = []

time: 171 us -> 167 us (0.977)
  waiting for transfers between devices: 49.6 us -> 44.2 us
    ppermute x20 -> x21, starting transfers between devices: 17.1 us -> 29.3 us  [per_device(): go_left = lambda x: lax.ppermute(x, 'ctx', left)]
    ppermute x21 -> x22, starting transfers between devices: 70.6 us -> 60.1 us  [per_device(): go_right = lambda x: lax.ppermute(x, 'ctx', right)]
    ppermute x20 -> x21, waiting for transfers between devices: 25 us -> 15.6 us  [per_device(): go_left = lambda x: lax.ppermute(x, 'ctx', left)]
    ppermute x21 -> x22, waiting for transfers between devices: 22.5 us -> 27.3 us  [per_device(): go_right = lambda x: lax.ppermute(x, 'ctx', right)]
  transfers between devices with their start and end apart: 50 -> 52, of which waited for: 32 -> 31; matrix products, arithmetic and copies ran while one was open for 0% -> 0% of each run, Pallas kernels for 10% -> 11%
where the time goes in v7:
time: 167 us
  starting transfers between devices  93.5 us (56%)
  waiting for transfers between devices  44.2 us (26%)
  Pallas kernels  28.2 us (17%)
    ppermute x22, starting transfers between devices, per_device(): go_right = lambda x: lax.ppermute(x, 'ctx', right)  60.1 us
    ppermute x21, starting transfers between devices, per_device(): go_left = lambda x: lax.ppermute(x, 'ctx', left)  29.3 us
    ppermute x22, waiting for transfers between devices, per_device(): go_right = lambda x: lax.ppermute(x, 'ctx', right)  27.3 us
    ppermute x21, waiting for transfers between devices, per_device(): go_left = lambda x: lax.ppermute(x, 'ctx', left)  15.6 us
    pallas_call x5, Pallas kernels, call(): pl.pallas_call(kernel, in_specs=[pl.BlockSpec(memory_space=pltpu.SMEM)] +...  8.57 us
    pallas_call x2, Pallas kernels, down_call(): pl.pallas_call(down_kernel, in_specs=[vmem] * 2 + more, out_specs=[vmem]...  4.69 us
    pallas_call x1, Pallas kernels, hidden_calls(): pl.pallas_call(first_kernel, in_specs=[pl.BlockSpec(memory_space=pltpu.SM...  4.63 us
    pallas_call x1, Pallas kernels, hidden_calls(): pl.pallas_call(second_kernel, in_specs=[vmem] * 6 + [anywhere], out_specs...  4.63 us
  transfers between devices with their start and end apart: 52, of which 31 were waited for; matrix products, arithmetic and copies ran while one was open for 0% of the time, Pallas kernels for 11%

profile of v7, /device:TPU:0, one launch (start us, length us, event | category | flops | bytes accessed | tf_op | source)
XLA Modules:
  0.0 167.0 jit_solution(14190319050193151882)
XLA Ops:
  0.6 1.9 %halves.1 = (bf16[256,512]{1,0:T(8,128)(2,1)S(1)}, bf16[256,512]{1,0:T(8,128)(2,1)S(1)}, bf16[128,4096]{1,0:T(8,128)(2,1)S(1)}, bf16[128,4096]{1,0:T(8,128)(2,1)S(1)}) custom-call(s32[1]{0:T(128)} %bitcast.me_ref.refs_0_, bf16[128,1024]{1,0:T(8,128)(2,1)} %refs_0_.2, bf16[128,1024]{1,0:T(8,128)(2,1)} %refs_1_.2, bf16[128,8192]{1,0:T(8,128)(2,1)} %refs_2_.1), custom_call_target="tpu_custom_call" | custom-call | flops 1 | bytes 1 | tf_op jit(solution)/shard_map/halves/pallas_call | solution.py:426
  3.1 3.0 %collective-permute-start.1 = (bf16[256,512]{1,0:T(8,128)(2,1)S(1)}, bf16[256,512]{1,0:T(8,128)(2,1)S(1)}, u32[]{:S(2)}, u32[]{:S(2)}) collective-permute-start(bf16[256,512]{1,0:T(8,128)(2,1)S(1)} %get-tuple-element.85.own_ref.refs_9_), channel_id=1, source_target_pairs={{0,4},{1,5},{4,8},{5,9},{8,12},{9,13},{12,14},{13,15},{14,10},{15,... | collective-permute-start | bytes 786440 | tf_op jit(solution)/shard_map/ppermute | solution.py:694
  8.3 3.8 %attend_own.1 = (f32[4,2048,128]{2,1,0:T(8,128)S(1)}, f32[4,2048,128]{2,1,0:T(8,128)S(1)}, f32[4,2048,128]{2,1,0:T(8,128)S(1)}) custom-call(s32[1]{0:T(128)} %bitcast.me_ref.refs_0_, bf16[128,4096]{1,0:T(8,128)(2,1)S(1)} %get-tuple-element.83.q_ref, bf16[128,4096]{1,0:T(8,128)(2,1)S(1)} %collective-permute-done.sib_q_ref, ...), custom_call_target="tpu_custom_call" | custom-call | flops 1 | bytes 1 | tf_op jit(solution)/shard_map/attend_own/pallas_call | solution.py:332
  13.2 2.2 %collective-permute-done.2.refs_2_.refs_13_ = bf16[256,512]{1,0:T(8,128)(2,1)S(1)} collective-permute-done((bf16[256,512]{1,0:T(8,128)(2,1)S(1)}, bf16[256,512]{1,0:T(8,128)(2,1)S(1)}, u32[]{:S(2)}, u32[]{:S(2)}) %collective-permute-start.2) | collective-permute-done | bytes 262176 | tf_op jit(solution)/shard_map/ppermute | solution.py:695
  18.5 1.9 %collective-permute-start.10 = (bf16[256,512]{1,0:T(8,128)(2,1)S(1)}, bf16[256,512]{1,0:T(8,128)(2,1)S(1)}, u32[]{:S(2)}, u32[]{:S(2)}) collective-permute-start(bf16[256,512]{1,0:T(8,128)(2,1)S(1)} %collective-permute-done.6.refs_1_.refs_12_), channel_id=1, source_target_pairs={{0,4},{1,5},{4,8},{5,9},{8,12},{9,13},{12,14},{13,15},{14,10},{15,... | collective-permute-start | bytes 786440 | tf_op jit(solution)/shard_map/ppermute | solution.py:694
  20.6 3.4 %collective-permute-done.4.refs_0_.refs_15_ = bf16[256,512]{1,0:T(8,128)(2,1)S(1)} collective-permute-done((bf16[256,512]{1,0:T(8,128)(2,1)S(1)}, bf16[256,512]{1,0:T(8,128)(2,1)S(1)}, u32[]{:S(2)}, u32[]{:S(2)}) %collective-permute-start.4) | collective-permute-done | bytes 262176 | tf_op jit(solution)/shard_map/ppermute | solution.py:694
  24.0 1.7 %collective-permute-done.5.refs_2_.refs_17_ = bf16[256,512]{1,0:T(8,128)(2,1)S(1)} collective-permute-done((bf16[256,512]{1,0:T(8,128)(2,1)S(1)}, bf16[256,512]{1,0:T(8,128)(2,1)S(1)}, u32[]{:S(2)}, u32[]{:S(2)}) %collective-permute-start.5) | collective-permute-done | bytes 262176 | tf_op jit(solution)/shard_map/ppermute | solution.py:695
  25.7 2.4 %collective-permute-start.8 = (bf16[256,512]{1,0:T(8,128)(2,1)S(1)}, bf16[256,512]{1,0:T(8,128)(2,1)S(1)}, u32[]{:S(2)}, u32[]{:S(2)}) collective-permute-start(bf16[256,512]{1,0:T(8,128)(2,1)S(1)} %collective-permute-done.4.refs_0_.refs_15_), channel_id=1, source_target_pairs={{0,4},{1,5},{4,8},{5,9},{8,12},{9,13},{12,14},{13,15},{14,10},{15,... | collective-permute-start | bytes 786440 | tf_op jit(solution)/shard_map/ppermute | solution.py:694
  33.0 2.2 %collective-permute-done.8.refs_0_.refs_19_ = bf16[256,512]{1,0:T(8,128)(2,1)S(1)} collective-permute-done((bf16[256,512]{1,0:T(8,128)(2,1)S(1)}, bf16[256,512]{1,0:T(8,128)(2,1)S(1)}, u32[]{:S(2)}, u32[]{:S(2)}) %collective-permute-start.8) | collective-permute-done | bytes 262176 | tf_op jit(solution)/shard_map/ppermute | solution.py:694
  35.2 1.7 %collective-permute-done.9.refs_2_.refs_21_ = bf16[256,512]{1,0:T(8,128)(2,1)S(1)} collective-permute-done((bf16[256,512]{1,0:T(8,128)(2,1)S(1)}, bf16[256,512]{1,0:T(8,128)(2,1)S(1)}, u32[]{:S(2)}, u32[]{:S(2)}) %collective-permute-start.9) | collective-permute-done | bytes 262176 | tf_op jit(solution)/shard_map/ppermute | solution.py:695
  36.9 3.2 %collective-permute-start.12 = (bf16[256,512]{1,0:T(8,128)(2,1)S(1)}, bf16[256,512]{1,0:T(8,128)(2,1)S(1)}, u32[]{:S(2)}, u32[]{:S(2)}) collective-permute-start(bf16[256,512]{1,0:T(8,128)(2,1)S(1)} %collective-permute-done.8.refs_0_.refs_19_), channel_id=1, source_target_pairs={{0,4},{1,5},{4,8},{5,9},{8,12},{9,13},{12,14},{13,15},{14,10},{15,... | collective-permute-start | bytes 786440 | tf_op jit(solution)/shard_map/ppermute | solution.py:694
  40.8 1.7 %collective-permute-done.14.refs_3_.refs_22_ = bf16[256,512]{1,0:T(8,128)(2,1)S(1)} collective-permute-done((bf16[256,512]{1,0:T(8,128)(2,1)S(1)}, bf16[256,512]{1,0:T(8,128)(2,1)S(1)}, u32[]{:S(2)}, u32[]{:S(2)}) %collective-permute-start.14) | collective-permute-done | bytes 262176 | tf_op jit(solution)/shard_map/ppermute | solution.py:695
  44.8 4.3 %collective-permute-done.15.refs_1_.refs_24_ = bf16[128,512]{1,0:T(8,128)(2,1)S(1)} collective-permute-done((bf16[128,512]{1,0:T(8,128)(2,1)S(1)}, bf16[128,512]{1,0:T(8,128)(2,1)S(1)}, u32[]{:S(2)}, u32[]{:S(2)}) %collective-permute-start.15) | collective-permute-done | bytes 131104 | tf_op jit(solution)/shard_map/ppermute | solution.py:694
  49.8 4.7 %attend_last.1 = (bf16[128,4096]{1,0:T(8,128)(2,1)S(1)}, bf16[128,4096]{1,0:T(8,128)(2,1)S(1)}, bf16[16,4224]{1,0:T(8,128)(2,1)S(1)}, bf16[16,4224]{1,0:T(8,128)...) custom-call(s32[1]{0:T(128)} %bitcast.me_ref.refs_0_, ...), custom_call_target="tpu_custom_call" | custom-call | flops 1 | bytes 1 | tf_op jit(solution)/shard_map/attend_last/pallas_call | solution.py:332
  56.6 1.8 %collective-permute-start.21 = (bf16[16,4224]{1,0:T(8,128)(2,1)S(1)}, bf16[16,4224]{1,0:T(8,128)(2,1)S(1)}, u32[]{:S(2)}, u32[]{:S(2)}) collective-permute-start(bf16[16,4224]{1,0:T(8,128)(2,1)S(1)} %get-tuple-element.125.refs_0_), channel_id=1, source_target_pairs={{0,4},{1,5},{4,8},{5,9},{8,12},{9,13},{12,14},{13,15},{14,10},{15,... | collective-permute-start | bytes 405512 | tf_op jit(solution)/shard_map/ppermute | solution.py:694
  63.7 37.9 %collective-permute-start.25 = (bf16[16,4224]{1,0:T(8,128)(2,1)S(1)}, bf16[16,4224]{1,0:T(8,128)(2,1)S(1)}, u32[]{:S(2)}, u32[]{:S(2)}) collective-permute-start(bf16[16,4224]{1,0:T(8,128)(2,1)S(1)} %collective-permute-done.21.refs_2_), channel_id=1, source_target_pairs={{0,4},{1,5},{4,8},{5,9},{8,12},{9,13},{12,14},{13,15},{14,10},{15,... | collective-permute-start | bytes 405512 | tf_op jit(solution)/shard_map/ppermute | solution.py:694
  101.7 7.1 %collective-permute-start.23 = (bf16[16,4224]{1,0:T(8,128)(2,1)S(1)}, bf16[16,4224]{1,0:T(8,128)(2,1)S(1)}, u32[]{:S(2)}, u32[]{:S(2)}) collective-permute-start(bf16[16,4224]{1,0:T(8,128)(2,1)S(1)} %collective-permute-done.19.refs_0_), channel_id=1, source_target_pairs={{4,0},{5,1},{8,4},{9,5},{12,8},{13,9},{14,12},{15,13},{10,14},{11,... | collective-permute-start | bytes 405512 | tf_op jit(solution)/shard_map/ppermute | solution.py:695
  110.3 2.0 %collective-permute-start.29 = (bf16[16,4224]{1,0:T(8,128)(2,1)S(1)}, bf16[16,4224]{1,0:T(8,128)(2,1)S(1)}, u32[]{:S(2)}, u32[]{:S(2)}) collective-permute-start(bf16[16,4224]{1,0:T(8,128)(2,1)S(1)} %collective-permute-done.26.refs_3_), channel_id=1, source_target_pairs={{4,0},{5,1},{8,4},{9,5},{12,8},{13,9},{14,12},{15,13},{10,14},{11,... | collective-permute-start | bytes 405512 | tf_op jit(solution)/shard_map/ppermute | solution.py:695
  118.2 1.8 %collective-permute-done.31.refs_5_ = bf16[16,4224]{1,0:T(8,128)(2,1)S(1)} collective-permute-done((bf16[16,4224]{1,0:T(8,128)(2,1)S(1)}, bf16[16,4224]{1,0:T(8,128)(2,1)S(1)}, u32[]{:S(2)}, u32[]{:S(2)}) %collective-permute-start.31) | collective-permute-done | bytes 135200 | tf_op jit(solution)/shard_map/ppermute | solution.py:694
  121.0 4.6 %hidden_first.1 = (f32[256,768]{1,0:T(8,128)S(1)}, f32[256,768]{1,0:T(8,128)S(1)}, bf16[4096,768]{1,0:T(8,128)(2,1)S(1)}, bf16[4096,768]{1,0:T(8,128)(2,1)S(1)}) custom-call(s32[1]{0:T(128)} %bitcast.me_ref.refs_0_, bf16[256,4224]{1,0:T(8,128)(2,1)S(1)} %place.7.rows_ref.own_ref, bf16[4096,768]{1,0:T(8,128)(2,1)S(1)} %get-tuple-element.147.gate_ref, ...), custom_call_target="tpu_custom_call" | custom-call | flops 3221225472 | bytes 12582912 | tf_op jit(solution)/shard_map/hidden_first/pallas_call | solution.py:529
  125.7 4.6 %hidden_second.1 = (bf16[256,768]{1,0:T(8,128)(2,1)S(1)}, bf16[768,4096]{1,0:T(8,128)(2,1)S(1)}, bf16[768,4096]{1,0:T(8,128)(2,1)S(1)}) custom-call(bf16[256,4224]{1,0:T(8,128)(2,1)S(1)} %collective-permute-done.32.rows_ref, bf16[4096,768]{1,0:T(8,128)(2,1)S(1)} %get-tuple-element.149.gate_ref, bf16[4096,768]{1,0:T(8,128)(2,1)S(1)} %get-tuple-element.150.up_ref, ...), custom_call_target="tpu_custom_call" | custom-call | flops 3221225472 | bytes 12582912 | tf_op jit(solution)/shard_map/hidden_second/pallas_call | solution.py:539
  130.3 2.4 %down.2 = (bf16[128,4096]{1,0:T(8,128)(2,1)S(1)}, bf16[128,4096]{1,0:T(8,128)(2,1)S(1)}, bf16[128,8192]{1,0:T(8,128)(2,1)}) custom-call(bf16[256,768]{1,0:T(8,128)(2,1)S(1)} %get-tuple-element.153.hidden_ref, bf16[768,4096]{1,0:T(8,128)(2,1)S(1)} %get-tuple-element.154.down_ref, s32[1]{0:T(128)} %bitcast.me_ref.refs_0_, ...), custom_call_target="tpu_custom_call" | custom-call | flops 1610612736 | bytes 8388608 | tf_op jit(solution)/shard_map/down/pallas_call | solution.py:591
  132.8 2.3 %down.3 = (bf16[128,4096]{1,0:T(8,128)(2,1)S(1)}, bf16[128,4096]{1,0:T(8,128)(2,1)S(1)}) custom-call(bf16[256,768]{1,0:T(8,128)(2,1)S(1)} %get-tuple-element.153.hidden_ref, bf16[768,4096]{1,0:T(8,128)(2,1)S(1)} %get-tuple-element.158.down_ref), custom_call_target="tpu_custom_call" | custom-call | flops 1610612736 | bytes 8388608 | tf_op jit(solution)/shard_map/down/pallas_call | solution.py:591
  135.7 1.8 %collective-permute-start.48 = (bf16[16,2048]{1,0:T(8,128)(2,1)S(1)}, bf16[16,2048]{1,0:T(8,128)(2,1)S(1)}, u32[]{:S(2)}, u32[]{:S(2)}) collective-permute-start(bf16[16,2048]{1,0:T(8,128)(2,1)S(1)} %add.28), channel_id=1, source_target_pairs={{4,0},{5,1},{8,4},{9,5},{12,8},{13,9},{14,12},{15,13},{10,14},{11,... | collective-permute-start | bytes 196616 | tf_op jit(solution)/shard_map/ppermute | solution.py:695
  138.0 1.8 %collective-permute-start.39 = (bf16[16,2048]{1,0:T(8,128)(2,1)S(1)}, bf16[16,2048]{1,0:T(8,128)(2,1)S(1)}, u32[]{:S(2)}, u32[]{:S(2)}) collective-permute-start(bf16[16,2048]{1,0:T(8,128)(2,1)S(1)} %add.20), channel_id=1, source_target_pairs={{4,0},{5,1},{8,4},{9,5},{12,8},{13,9},{14,12},{15,13},{10,14},{11,... | collective-permute-start | bytes 196616 | tf_op jit(solution)/shard_map/ppermute | solution.py:695
  140.2 1.8 %collective-permute-start.49 = (bf16[16,4096]{1,0:T(8,128)(2,1)S(1)}, bf16[16,4096]{1,0:T(8,128)(2,1)S(1)}, u32[]{:S(2)}, u32[]{:S(2)}) collective-permute-start(bf16[16,4096]{1,0:T(8,128)(2,1)S(1)} %add.29), channel_id=1, source_target_pairs={{4,0},{5,1},{8,4},{9,5},{12,8},{13,9},{14,12},{15,13},{10,14},{11,... | collective-permute-start | bytes 393224 | tf_op jit(solution)/shard_map/ppermute | solution.py:695
  142.5 1.8 %collective-permute-start.40 = (bf16[16,4096]{1,0:T(8,128)(2,1)S(1)}, bf16[16,4096]{1,0:T(8,128)(2,1)S(1)}, u32[]{:S(2)}, u32[]{:S(2)}) collective-permute-start(bf16[16,4096]{1,0:T(8,128)(2,1)S(1)} %add.21), channel_id=1, source_target_pairs={{4,0},{5,1},{8,4},{9,5},{12,8},{13,9},{14,12},{15,13},{10,14},{11,... | collective-permute-start | bytes 393224 | tf_op jit(solution)/shard_map/ppermute | solution.py:695
  146.4 2.1 %collective-permute-done.45.refs_0_ = bf16[16,4096]{1,0:T(8,128)(2,1)S(1)} collective-permute-done((bf16[16,4096]{1,0:T(8,128)(2,1)S(1)}, bf16[16,4096]{1,0:T(8,128)(2,1)S(1)}, u32[]{:S(2)}, u32[]{:S(2)}) %collective-permute-start.45) | collective-permute-done | bytes 131104 | tf_op jit(solution)/shard_map/ppermute | solution.py:694
  148.5 1.7 %collective-permute-start.50 = (bf16[16,4096]{1,0:T(8,128)(2,1)S(1)}, bf16[16,4096]{1,0:T(8,128)(2,1)S(1)}, u32[]{:S(2)}, u32[]{:S(2)}) collective-permute-start(bf16[16,4096]{1,0:T(8,128)(2,1)S(1)} %add.30), channel_id=1, source_target_pairs={{4,0},{5,1},{8,4},{9,5},{12,8},{13,9},{14,12},{15,13},{10,14},{11,... | collective-permute-start | bytes 393224 | tf_op jit(solution)/shard_map/ppermute | solution.py:695
  150.6 1.8 %collective-permute-start.41 = (bf16[16,4096]{1,0:T(8,128)(2,1)S(1)}, bf16[16,4096]{1,0:T(8,128)(2,1)S(1)}, u32[]{:S(2)}, u32[]{:S(2)}) collective-permute-start(bf16[16,4096]{1,0:T(8,128)(2,1)S(1)} %add.22), channel_id=1, source_target_pairs={{4,0},{5,1},{8,4},{9,5},{12,8},{13,9},{14,12},{15,13},{10,14},{11,... | collective-permute-start | bytes 393224 | tf_op jit(solution)/shard_map/ppermute | solution.py:695
  155.3 1.8 %collective-permute-start.51 = (bf16[16,4096]{1,0:T(8,128)(2,1)S(1)}, bf16[16,4096]{1,0:T(8,128)(2,1)S(1)}, u32[]{:S(2)}, u32[]{:S(2)}) collective-permute-start(bf16[16,4096]{1,0:T(8,128)(2,1)S(1)} %add.31), channel_id=1, source_target_pairs={{4,0},{5,1},{8,4},{9,5},{12,8},{13,9},{14,12},{15,13},{10,14},{11,... | collective-permute-start | bytes 393224 | tf_op jit(solution)/shard_map/ppermute | solution.py:695
  163.7 1.8 %collective-permute-done.38.c_ref = bf16[16,4096]{1,0:T(8,128)(2,1)S(1)} collective-permute-done((bf16[16,4096]{1,0:T(8,128)(2,1)S(1)}, bf16[16,4096]{1,0:T(8,128)(2,1)S(1)}, u32[]{:S(2)}, u32[]{:S(2)}) %collective-permute-start.38) | collective-permute-done | bytes 131104 | tf_op jit(solution)/shard_map/ppermute | solution.py:694
  (120 shorter events, 47.0 us)
Async XLA Ops:
  3.1 10.0 %collective-permute-start.1 = (bf16[256,512]{1,0:T(8,128)(2,1)S(1)}, bf16[256,512]{1,0:T(8,128)(2,1)S(1)}, u32[]{:S(2)}, u32[]{:S(2)}) collective-permute-start(bf16[256,512]{1,0:T(8,128)(2,1)S(1)} %get-tuple-element.85.own_ref.refs_9_), channel_id=1, source_target_pairs={{0,4},{1,5},{4,8},{5,9},{8,12},{9,13},{12,14},{13,15},{14,10},{15,... | collective-permute-start | bytes 786440 | tf_op jit(solution)/shard_map/ppermute | solution.py:694
  6.1 9.2 %collective-permute-start.2 = (bf16[256,512]{1,0:T(8,128)(2,1)S(1)}, bf16[256,512]{1,0:T(8,128)(2,1)S(1)}, u32[]{:S(2)}, u32[]{:S(2)}) collective-permute-start(bf16[256,512]{1,0:T(8,128)(2,1)S(1)} %get-tuple-element.85.own_ref.refs_9_), channel_id=1, source_target_pairs={{4,0},{5,1},{8,4},{9,5},{12,8},{13,9},{14,12},{15,13},{10,14},{11,... | collective-permute-start | bytes 786440 | tf_op jit(solution)/shard_map/ppermute | solution.py:695
  6.1 12.3 %collective-permute-start.6 = (bf16[256,512]{1,0:T(8,128)(2,1)S(1)}, bf16[256,512]{1,0:T(8,128)(2,1)S(1)}, u32[]{:S(2)}, u32[]{:S(2)}) collective-permute-start(bf16[256,512]{1,0:T(8,128)(2,1)S(1)} %get-tuple-element.86), channel_id=1, source_target_pairs={{0,5},{1,4},{4,9},{5,8},{8,13},{9,12},{12,15},{13,14},{14,11},{15,... | collective-permute-start | bytes 786440 | tf_op jit(solution)/shard_map/ppermute | solution.py:719
  7.3 11.3 %collective-permute-start.7 = (bf16[256,512]{1,0:T(8,128)(2,1)S(1)}, bf16[256,512]{1,0:T(8,128)(2,1)S(1)}, u32[]{:S(2)}, u32[]{:S(2)}) collective-permute-start(bf16[256,512]{1,0:T(8,128)(2,1)S(1)} %get-tuple-element.86), channel_id=1, source_target_pairs={{4,1},{5,0},{8,5},{9,4},{12,9},{13,8},{14,13},{15,12},{10,15},{11,... | collective-permute-start | bytes 786440 | tf_op jit(solution)/shard_map/ppermute | solution.py:719
  15.3 8.7 %collective-permute-start.4 = (bf16[256,512]{1,0:T(8,128)(2,1)S(1)}, bf16[256,512]{1,0:T(8,128)(2,1)S(1)}, u32[]{:S(2)}, u32[]{:S(2)}) collective-permute-start(bf16[256,512]{1,0:T(8,128)(2,1)S(1)} %collective-permute-done.1.refs_0_.refs_11_), channel_id=1, source_target_pairs={{0,4},{1,5},{4,8},{5,9},{8,12},{9,13},{12,14},{13,15},{14,10},{15,... | collective-permute-start | bytes 786440 | tf_op jit(solution)/shard_map/ppermute | solution.py:694
  16.9 8.8 %collective-permute-start.5 = (bf16[256,512]{1,0:T(8,128)(2,1)S(1)}, bf16[256,512]{1,0:T(8,128)(2,1)S(1)}, u32[]{:S(2)}, u32[]{:S(2)}) collective-permute-start(bf16[256,512]{1,0:T(8,128)(2,1)S(1)} %collective-permute-done.2.refs_2_.refs_13_), channel_id=1, source_target_pairs={{4,0},{5,1},{8,4},{9,5},{12,8},{13,9},{14,12},{15,13},{10,14},{11,... | collective-permute-start | bytes 786440 | tf_op jit(solution)/shard_map/ppermute | solution.py:695
  18.5 11.0 %collective-permute-start.10 = (bf16[256,512]{1,0:T(8,128)(2,1)S(1)}, bf16[256,512]{1,0:T(8,128)(2,1)S(1)}, u32[]{:S(2)}, u32[]{:S(2)}) collective-permute-start(bf16[256,512]{1,0:T(8,128)(2,1)S(1)} %collective-permute-done.6.refs_1_.refs_12_), channel_id=1, source_target_pairs={{0,4},{1,5},{4,8},{5,9},{8,12},{9,13},{12,14},{13,15},{14,10},{15,... | collective-permute-start | bytes 786440 | tf_op jit(solution)/shard_map/ppermute | solution.py:694
  20.5 10.5 %collective-permute-start.11 = (bf16[256,512]{1,0:T(8,128)(2,1)S(1)}, bf16[256,512]{1,0:T(8,128)(2,1)S(1)}, u32[]{:S(2)}, u32[]{:S(2)}) collective-permute-start(bf16[256,512]{1,0:T(8,128)(2,1)S(1)} %collective-permute-done.7.refs_3_.refs_14_), channel_id=1, source_target_pairs={{4,0},{5,1},{8,4},{9,5},{12,8},{13,9},{14,12},{15,13},{10,14},{11,... | collective-permute-start | bytes 786440 | tf_op jit(solution)/shard_map/ppermute | solution.py:695
  25.7 9.5 %collective-permute-start.8 = (bf16[256,512]{1,0:T(8,128)(2,1)S(1)}, bf16[256,512]{1,0:T(8,128)(2,1)S(1)}, u32[]{:S(2)}, u32[]{:S(2)}) collective-permute-start(bf16[256,512]{1,0:T(8,128)(2,1)S(1)} %collective-permute-done.4.refs_0_.refs_15_), channel_id=1, source_target_pairs={{0,4},{1,5},{4,8},{5,9},{8,12},{9,13},{12,14},{13,15},{14,10},{15,... | collective-permute-start | bytes 786440 | tf_op jit(solution)/shard_map/ppermute | solution.py:694
  28.1 8.8 %collective-permute-start.9 = (bf16[256,512]{1,0:T(8,128)(2,1)S(1)}, bf16[256,512]{1,0:T(8,128)(2,1)S(1)}, u32[]{:S(2)}, u32[]{:S(2)}) collective-permute-start(bf16[256,512]{1,0:T(8,128)(2,1)S(1)} %collective-permute-done.5.refs_2_.refs_17_), channel_id=1, source_target_pairs={{4,0},{5,1},{8,4},{9,5},{12,8},{13,9},{14,12},{15,13},{10,14},{11,... | collective-permute-start | bytes 786440 | tf_op jit(solution)/shard_map/ppermute | solution.py:695
  31.0 9.8 %collective-permute-start.13 = (bf16[256,512]{1,0:T(8,128)(2,1)S(1)}, bf16[256,512]{1,0:T(8,128)(2,1)S(1)}, u32[]{:S(2)}, u32[]{:S(2)}) collective-permute-start(bf16[256,512]{1,0:T(8,128)(2,1)S(1)} %collective-permute-done.10.refs_1_.refs_16_), channel_id=1, source_target_pairs={{0,4},{1,5},{4,8},{5,9},{8,12},{9,13},{12,14},{13,15},{14,10},{15,... | collective-permute-start | bytes 786440 | tf_op jit(solution)/shard_map/ppermute | solution.py:694
  32.6 10.0 %collective-permute-start.14 = (bf16[256,512]{1,0:T(8,128)(2,1)S(1)}, bf16[256,512]{1,0:T(8,128)(2,1)S(1)}, u32[]{:S(2)}, u32[]{:S(2)}) collective-permute-start(bf16[256,512]{1,0:T(8,128)(2,1)S(1)} %collective-permute-done.11.refs_3_.refs_18_), channel_id=1, source_target_pairs={{4,0},{5,1},{8,4},{9,5},{12,8},{13,9},{14,12},{15,13},{10,14},{11,... | collective-permute-start | bytes 786440 | tf_op jit(solution)/shard_map/ppermute | solution.py:695
  36.9 12.9 %collective-permute-start.12 = (bf16[256,512]{1,0:T(8,128)(2,1)S(1)}, bf16[256,512]{1,0:T(8,128)(2,1)S(1)}, u32[]{:S(2)}, u32[]{:S(2)}) collective-permute-start(bf16[256,512]{1,0:T(8,128)(2,1)S(1)} %collective-permute-done.8.refs_0_.refs_19_), channel_id=1, source_target_pairs={{0,4},{1,5},{4,8},{5,9},{8,12},{9,13},{12,14},{13,15},{14,10},{15,... | collective-permute-start | bytes 786440 | tf_op jit(solution)/shard_map/ppermute | solution.py:694
  42.5 6.6 %collective-permute-start.15 = (bf16[128,512]{1,0:T(8,128)(2,1)S(1)}, bf16[128,512]{1,0:T(8,128)(2,1)S(1)}, u32[]{:S(2)}, u32[]{:S(2)}) collective-permute-start(bf16[128,512]{1,0:T(8,128)(2,1)S(1)} %slice.6), channel_id=1, source_target_pairs={{0,4},{1,5},{4,8},{5,9},{8,12},{9,13},{12,14},{13,15},{14,10},{15,... | collective-permute-start | bytes 393224 | tf_op jit(solution)/shard_map/ppermute | solution.py:694
  55.6 6.5 %collective-permute-start.20 = (bf16[16,4224]{1,0:T(8,128)(2,1)S(1)}, bf16[16,4224]{1,0:T(8,128)(2,1)S(1)}, u32[]{:S(2)}, u32[]{:S(2)}) collective-permute-start(bf16[16,4224]{1,0:T(8,128)(2,1)S(1)} %get-tuple-element.126.refs_1_), channel_id=1, source_target_pairs={{0,4},{1,5},{4,8},{5,9},{8,12},{9,13},{12,14},{13,15},{14,10},{15,... | collective-permute-start | bytes 405512 | tf_op jit(solution)/shard_map/ppermute | solution.py:694
  56.6 7.1 %collective-permute-start.21 = (bf16[16,4224]{1,0:T(8,128)(2,1)S(1)}, bf16[16,4224]{1,0:T(8,128)(2,1)S(1)}, u32[]{:S(2)}, u32[]{:S(2)}) collective-permute-start(bf16[16,4224]{1,0:T(8,128)(2,1)S(1)} %get-tuple-element.125.refs_0_), channel_id=1, source_target_pairs={{0,4},{1,5},{4,8},{5,9},{8,12},{9,13},{12,14},{13,15},{14,10},{15,... | collective-permute-start | bytes 405512 | tf_op jit(solution)/shard_map/ppermute | solution.py:694
  58.4 43.3 %collective-permute-start.22 = (bf16[16,4224]{1,0:T(8,128)(2,1)S(1)}, bf16[16,4224]{1,0:T(8,128)(2,1)S(1)}, u32[]{:S(2)}, u32[]{:S(2)}) collective-permute-start(bf16[16,4224]{1,0:T(8,128)(2,1)S(1)} %get-tuple-element.126.refs_1_), channel_id=1, source_target_pairs={{4,0},{5,1},{8,4},{9,5},{12,8},{13,9},{14,12},{15,13},{10,14},{11,... | collective-permute-start | bytes 405512 | tf_op jit(solution)/shard_map/ppermute | solution.py:695
  59.6 42.1 %collective-permute-start.19 = (bf16[16,4224]{1,0:T(8,128)(2,1)S(1)}, bf16[16,4224]{1,0:T(8,128)(2,1)S(1)}, u32[]{:S(2)}, u32[]{:S(2)}) collective-permute-start(bf16[16,4224]{1,0:T(8,128)(2,1)S(1)} %collective-permute-done.18.refs_0_), channel_id=1, source_target_pairs={{4,0},{5,1},{8,4},{9,5},{12,8},{13,9},{14,12},{15,13},{10,14},{11,... | collective-permute-start | bytes 405512 | tf_op jit(solution)/shard_map/ppermute | solution.py:695
  62.1 46.7 %collective-permute-start.24 = (bf16[16,4224]{1,0:T(8,128)(2,1)S(1)}, bf16[16,4224]{1,0:T(8,128)(2,1)S(1)}, u32[]{:S(2)}, u32[]{:S(2)}) collective-permute-start(bf16[16,4224]{1,0:T(8,128)(2,1)S(1)} %collective-permute-done.20.refs_1_), channel_id=1, source_target_pairs={{0,4},{1,5},{4,8},{5,9},{8,12},{9,13},{12,14},{13,15},{14,10},{15,... | collective-permute-start | bytes 405512 | tf_op jit(solution)/shard_map/ppermute | solution.py:694
  63.7 45.1 %collective-permute-start.25 = (bf16[16,4224]{1,0:T(8,128)(2,1)S(1)}, bf16[16,4224]{1,0:T(8,128)(2,1)S(1)}, u32[]{:S(2)}, u32[]{:S(2)}) collective-permute-start(bf16[16,4224]{1,0:T(8,128)(2,1)S(1)} %collective-permute-done.21.refs_2_), channel_id=1, source_target_pairs={{0,4},{1,5},{4,8},{5,9},{8,12},{9,13},{12,14},{13,15},{14,10},{15,... | collective-permute-start | bytes 405512 | tf_op jit(solution)/shard_map/ppermute | solution.py:694
  101.6 8.7 %collective-permute-start.26 = (bf16[16,4224]{1,0:T(8,128)(2,1)S(1)}, bf16[16,4224]{1,0:T(8,128)(2,1)S(1)}, u32[]{:S(2)}, u32[]{:S(2)}) collective-permute-start(bf16[16,4224]{1,0:T(8,128)(2,1)S(1)} %collective-permute-done.22.refs_3_), channel_id=1, source_target_pairs={{4,0},{5,1},{8,4},{9,5},{12,8},{13,9},{14,12},{15,13},{10,14},{11,... | collective-permute-start | bytes 405512 | tf_op jit(solution)/shard_map/ppermute | solution.py:695
  101.7 11.5 %collective-permute-start.23 = (bf16[16,4224]{1,0:T(8,128)(2,1)S(1)}, bf16[16,4224]{1,0:T(8,128)(2,1)S(1)}, u32[]{:S(2)}, u32[]{:S(2)}) collective-permute-start(bf16[16,4224]{1,0:T(8,128)(2,1)S(1)} %collective-permute-done.19.refs_0_), channel_id=1, source_target_pairs={{4,0},{5,1},{8,4},{9,5},{12,8},{13,9},{14,12},{15,13},{10,14},{11,... | collective-permute-start | bytes 405512 | tf_op jit(solution)/shard_map/ppermute | solution.py:695
  108.8 5.9 %collective-permute-start.27 = (bf16[16,4224]{1,0:T(8,128)(2,1)S(1)}, bf16[16,4224]{1,0:T(8,128)(2,1)S(1)}, u32[]{:S(2)}, u32[]{:S(2)}) collective-permute-start(bf16[16,4224]{1,0:T(8,128)(2,1)S(1)} %collective-permute-done.24.refs_1_), channel_id=1, source_target_pairs={{0,4},{1,5},{4,8},{5,9},{8,12},{9,13},{12,14},{13,15},{14,10},{15,... | collective-permute-start | bytes 405512 | tf_op jit(solution)/shard_map/ppermute | solution.py:694
  110.3 6.7 %collective-permute-start.29 = (bf16[16,4224]{1,0:T(8,128)(2,1)S(1)}, bf16[16,4224]{1,0:T(8,128)(2,1)S(1)}, u32[]{:S(2)}, u32[]{:S(2)}) collective-permute-start(bf16[16,4224]{1,0:T(8,128)(2,1)S(1)} %collective-permute-done.26.refs_3_), channel_id=1, source_target_pairs={{4,0},{5,1},{8,4},{9,5},{12,8},{13,9},{14,12},{15,13},{10,14},{11,... | collective-permute-start | bytes 405512 | tf_op jit(solution)/shard_map/ppermute | solution.py:695
  112.3 5.9 %collective-permute-start.28 = (bf16[16,4224]{1,0:T(8,128)(2,1)S(1)}, bf16[16,4224]{1,0:T(8,128)(2,1)S(1)}, u32[]{:S(2)}, u32[]{:S(2)}) collective-permute-start(bf16[16,4224]{1,0:T(8,128)(2,1)S(1)} %collective-permute-done.25.refs_2_), channel_id=1, source_target_pairs={{0,4},{1,5},{4,8},{5,9},{8,12},{9,13},{12,14},{13,15},{14,10},{15,... | collective-permute-start | bytes 405512 | tf_op jit(solution)/shard_map/ppermute | solution.py:694
  120.5 9.8 %collective-permute-start.33 = (bf16[128,4096]{1,0:T(8,128)(2,1)S(1)}, bf16[128,4096]{1,0:T(8,128)(2,1)S(1)}, u32[]{:S(2)}, u32[]{:S(2)}) collective-permute-start(bf16[128,4096]{1,0:T(8,128)(2,1)S(1)} %get-tuple-element.156), channel_id=1, source_target_pairs={{0,1},{1,0},{2,3},{3,2},{4,5},{5,4},{6,7},{7,6},{8,9},{9,8},{10,11... | collective-permute-start | bytes 3145736 | tf_op jit(solution)/shard_map/ppermute | solution.py:696
  140.2 6.1 %collective-permute-start.49 = (bf16[16,4096]{1,0:T(8,128)(2,1)S(1)}, bf16[16,4096]{1,0:T(8,128)(2,1)S(1)}, u32[]{:S(2)}, u32[]{:S(2)}) collective-permute-start(bf16[16,4096]{1,0:T(8,128)(2,1)S(1)} %add.29), channel_id=1, source_target_pairs={{4,0},{5,1},{8,4},{9,5},{12,8},{13,9},{14,12},{15,13},{10,14},{11,... | collective-permute-start | bytes 393224 | tf_op jit(solution)/shard_map/ppermute | solution.py:695
  142.1 6.4 %collective-permute-start.45 = (bf16[16,4096]{1,0:T(8,128)(2,1)S(1)}, bf16[16,4096]{1,0:T(8,128)(2,1)S(1)}, u32[]{:S(2)}, u32[]{:S(2)}) collective-permute-start(bf16[16,4096]{1,0:T(8,128)(2,1)S(1)} %add.25), channel_id=1, source_target_pairs={{0,4},{1,5},{4,8},{5,9},{8,12},{9,13},{12,14},{13,15},{14,10},{15,... | collective-permute-start | bytes 393224 | tf_op jit(solution)/shard_map/ppermute | solution.py:694
  142.5 8.1 %collective-permute-start.40 = (bf16[16,4096]{1,0:T(8,128)(2,1)S(1)}, bf16[16,4096]{1,0:T(8,128)(2,1)S(1)}, u32[]{:S(2)}, u32[]{:S(2)}) collective-permute-start(bf16[16,4096]{1,0:T(8,128)(2,1)S(1)} %add.21), channel_id=1, source_target_pairs={{4,0},{5,1},{8,4},{9,5},{12,8},{13,9},{14,12},{15,13},{10,14},{11,... | collective-permute-start | bytes 393224 | tf_op jit(solution)/shard_map/ppermute | solution.py:695
  144.3 8.1 %collective-permute-start.36 = (bf16[16,4096]{1,0:T(8,128)(2,1)S(1)}, bf16[16,4096]{1,0:T(8,128)(2,1)S(1)}, u32[]{:S(2)}, u32[]{:S(2)}) collective-permute-start(bf16[16,4096]{1,0:T(8,128)(2,1)S(1)} %add.17), channel_id=1, source_target_pairs={{0,4},{1,5},{4,8},{5,9},{8,12},{9,13},{12,14},{13,15},{14,10},{15,... | collective-permute-start | bytes 393224 | tf_op jit(solution)/shard_map/ppermute | solution.py:694
  150.6 6.5 %collective-permute-start.41 = (bf16[16,4096]{1,0:T(8,128)(2,1)S(1)}, bf16[16,4096]{1,0:T(8,128)(2,1)S(1)}, u32[]{:S(2)}, u32[]{:S(2)}) collective-permute-start(bf16[16,4096]{1,0:T(8,128)(2,1)S(1)} %add.22), channel_id=1, source_target_pairs={{4,0},{5,1},{8,4},{9,5},{12,8},{13,9},{14,12},{15,13},{10,14},{11,... | collective-permute-start | bytes 393224 | tf_op jit(solution)/shard_map/ppermute | solution.py:695
  152.5 6.2 %collective-permute-start.37 = (bf16[16,4096]{1,0:T(8,128)(2,1)S(1)}, bf16[16,4096]{1,0:T(8,128)(2,1)S(1)}, u32[]{:S(2)}, u32[]{:S(2)}) collective-permute-start(bf16[16,4096]{1,0:T(8,128)(2,1)S(1)} %add.18), channel_id=1, source_target_pairs={{0,4},{1,5},{4,8},{5,9},{8,12},{9,13},{12,14},{13,15},{14,10},{15,... | collective-permute-start | bytes 393224 | tf_op jit(solution)/shard_map/ppermute | solution.py:694
  (23 other events, 116.1 us)

commit v8 on v6

--- a/solution.py
+++ b/solution.py
@@ -33,11 +33,11 @@
     return list(range(0, chips, 2)) + list(range(1, chips, 2))[::-1]
 
 
-def permutations(chips):
+def permutations(chips, step=1):
     order = ring_order(chips)
     right, left = [], []
     for place in range(chips):
-        here, there = order[place], order[(place + 1) % chips]
+        here, there = order[place], order[(place + step) % chips]
         for core in range(2):
             right.append((2 * here + core, 2 * there + core))
             left.append((2 * there + core, 2 * here + core))
@@ -604,37 +604,45 @@
     )(hidden, w_down, *halves)
 
 
-def spread_kernel(a_ref, b_ref, c_ref, d_ref, table_ref, *rest):
-    out_ref = rest[-1]
-    total = a_ref[...].astype(jnp.float32) + b_ref[...].astype(jnp.float32)
-    total += c_ref[...].astype(jnp.float32) + d_ref[...].astype(jnp.float32)
-    total = total.astype(jnp.bfloat16)
-    out_ref[...] = lax.dot_general(
-        table_ref[...],
-        jnp.concatenate([total] * PARTS, axis=0),
-        (((0,), (0,)), ((), ())),
-        preferred_element_type=jnp.float32,
-    ).astype(jnp.bfloat16)
+def spread_kernel(start, *refs):
+    parts, table_ref, out_ref, kept_ref, sems = refs[:4], refs[4], *refs[-3:]
+    table = table_ref[...]
+    width = kept_ref.shape[1]
+    cols = min(1024, width)
+    copies = []
+    for i in range(width // cols):
+        columns = slice(i * cols, (i + 1) * cols)
+        total = sum(ref[:CAP, columns].astype(jnp.float32) for ref in parts).astype(jnp.bfloat16)
+        kept_ref[:, columns] = lax.dot_general(
+            table,
+            jnp.concatenate([total] * PARTS, axis=0),
+            (((0,), (0,)), ((), ())),
+            preferred_element_type=jnp.float32,
+        ).astype(jnp.bfloat16)
+        target = out_ref.at[:, pl.ds(start + i * cols, cols)]
+        copies.append(pltpu.make_async_copy(kept_ref.at[:, pl.ds(i * cols, cols)], target, sems.at[i]))
+        copies[-1].start()
+    for copy in copies:
+        copy.wait()
 
 
 def spread_call(parts, table, piece, pieces, previous):
     tokens = table.shape[1]
-    piece_width = parts[0].shape[1]
-    cols = min(2048, piece_width)
-    steps = piece_width // cols
+    width = parts[0].shape[1]
     earlier = [] if previous is None else [previous]
+    vmem, anywhere = pl.BlockSpec(memory_space=pltpu.VMEM), pl.BlockSpec(memory_space=pl.ANY)
     return pl.pallas_call(
-        spread_kernel,
-        grid=(steps,),
-        in_specs=[pl.BlockSpec((CAP, cols), lambda i: (0, i))] * 4
-        + [pl.BlockSpec((PARTS * CAP, tokens), lambda i: (0, 0))]
-        + [pl.BlockSpec(memory_space=pl.ANY)] * len(earlier),
-        out_specs=pl.BlockSpec((tokens, cols), lambda i: (0, piece * steps + i)),
-        out_shape=jax.ShapeDtypeStruct((tokens, piece_width * pieces), jnp.bfloat16),
+        functools.partial(spread_kernel, piece * width),
+        in_specs=[vmem] * 5 + [anywhere] * len(earlier),
+        out_specs=anywhere,
+        out_shape=jax.ShapeDtypeStruct((tokens, width * pieces), jnp.bfloat16),
         input_output_aliases={5: 0} if earlier else {},
-        compiler_params=pltpu.CompilerParams(
-            dimension_semantics=("arbitrary",), vmem_limit_bytes=16 * MIB
-        ),
+        scratch_shapes=[
+            pltpu.VMEM((tokens, width), jnp.bfloat16),
+            pltpu.SemaphoreType.DMA((max(1, width // 1024),)),
+        ],
+        compiler_params=pltpu.CompilerParams(vmem_limit_bytes=8 * MIB),
+        cost_estimate=SMALL,
         name="spread",
     )(*parts, table, *earlier)
 
@@ -647,40 +655,44 @@
     refs[-1][...] = total.astype(jnp.bfloat16)
 
 
-def add_call(mine, other, index, received=None):
+def add_call(mine, other, index, received=()):
     vmem = pl.BlockSpec(memory_space=pltpu.VMEM)
-    more = () if received is None else (received,)
     return pl.pallas_call(
         functools.partial(add_kernel, index * CAP),
-        in_specs=[vmem] * (2 + len(more)),
+        in_specs=[vmem] * (2 + len(received)),
         out_specs=vmem,
         out_shape=pltpu.VMEM((CAP, mine.shape[1]), jnp.bfloat16),
         compiler_params=pltpu.CompilerParams(vmem_limit_bytes=4 * MIB),
         cost_estimate=SMALL,
         name="add",
-    )(mine, other, *more)
-
-
-def reduce_chip_rows(pieces, half, chips, moves, token):
+    )(mine, other, *received)
+
+
+def reduce_chip_rows(pieces, half, chips, moves, skips, token):
     chains = [(piece, side) for piece in range(len(pieces)) for side in range(2)]
-    received = [None] * len(chains)
-    for distance in range(half, 0, -1):
+    received, far = [()] * len(chains), {}
+    for distance in range(half - 1, 0, -1):
         for i, (piece, side) in enumerate(chains):
-            if distance == half and piece % 2 != side:
-                continue
-            if received[i] is not None:
+            if received[i]:
                 received[i], token = lax.optimization_barrier((received[i], token))
-            index = chips - 1 if distance == half else distance if side else half - 1 + distance
-            received[i] = moves[side](add_call(*pieces[piece], index, received[i]))
-    return [(*pieces[p], *received[2 * p : 2 * p + 2]) for p in range(len(pieces))]
+            more = received[i]
+            if distance == half - 2 and piece % 2 == side:
+                more = (*more, far[piece])
+            index = distance if side else half - 1 + distance
+            received[i] = (moves[side](add_call(*pieces[piece], index, more)),)
+        if distance == half - 1:
+            far = {p: skips[p % 2](add_call(*piece, chips - 1)) for p, piece in enumerate(pieces)}
+    return [(*pieces[p], *received[2 * p], *received[2 * p + 1]) for p in range(len(pieces))]
 
 
 def per_device(chips, queries, keys, values, norm_gain, expert_ids, gates, w_gate, w_up, w_down):
     right, left, sibling = permutations(chips)
+    two_right, two_left, _ = permutations(chips, 2)
     half = chips // 2
     go_right = lambda x: lax.ppermute(x, "ctx", right)
     go_left = lambda x: lax.ppermute(x, "ctx", left)
     swap = lambda x: lax.ppermute(x, "ctx", sibling)
+    skips = [lambda x, pairs=pairs: lax.ppermute(x, "ctx", pairs) for pairs in (two_right, two_left)]
 
     me = lax.axis_index("ctx").astype(jnp.int32).reshape(1)
     tokens = queries.shape[0]
@@ -728,23 +740,26 @@
         opposite, shift, state, norm_gain[None, :], (table, sib_table), sources, (w_gate, w_up)
     )
 
-    moves = (go_right, go_left, go_right, go_left)
-    received = [move(picked[i // 2]) for i, move in enumerate(moves)]
+    chains = [(0, 1), (1, 0), (0, 0), (1, 1)]
+    moves = [(go_right, go_left)[side] for _, side in chains]
+    received = [move(picked[core]) for move, (core, _) in zip(moves, chains)]
     rows = place(picked, [0, chips], (2 * chips * CAP, picked[0].shape[1]))
     theirs = swap(theirs)
+    far = []
     for step in range(1, half):
-        blocks, far = [], []
+        spots = [core * chips + side * (half - 1) + step for core, side in chains]
+        blocks = list(received)
         for i, move in enumerate(moves):
-            block, rows = lax.optimization_barrier((received[i], rows))
-            blocks.append(block)
+            if step == half - 1 and i == 1:
+                far, rows = lax.optimization_barrier((far, rows))
+            blocks[i], rows = lax.optimization_barrier((received[i], rows))
             if step < half - 1:
-                received[i] = move(block)
-            elif i in (0, 3):
-                far.append(move(block))
-        spots = [core * chips + side * (half - 1) + step for core in range(2) for side in range(2)]
-        rows = place(blocks, spots, rows)
-    far, rows = lax.optimization_barrier((far, rows))
-    rows = place(far, [chips - 1, 2 * chips - 1], rows)
+                received[i] = move(blocks[i])
+            if step == half - 2 and i < 2:
+                far.append(skips[chains[i][1]](blocks[i]))
+        if step < half - 1:
+            rows = place(blocks, spots, rows)
+    rows = place(blocks + far, spots + [chips - 1, 2 * chips - 1], rows)
     hidden, downs = hidden_calls(me, rows, swap(rows), (gate, up), w_gate, w_up, w_down)
 
     partial = []
@@ -755,7 +770,7 @@
             own, sib = down_call(hidden, downs[piece])
         partial.append((own, swap(sib)))
     mixed = None
-    for piece, parts in enumerate(reduce_chip_rows(partial, half, chips, (go_right, go_left), weighted)):
+    for piece, parts in enumerate(reduce_chip_rows(partial, half, chips, (go_right, go_left), skips, weighted)):
         mixed = spread_call(parts, weighted, piece, PIECES, mixed)
     return (result, mixed)
 

time: 171 us -> 170 us (level)
  waiting for transfers between devices: 49.6 us -> 40.9 us
  starting transfers between devices: 91.8 us -> 99.5 us
    ppermute x20 -> x18, waiting for transfers between devices: 25 us -> 12.6 us  [per_device(): go_left = lambda x: lax.ppermute(x, 'ctx', left)]
    ppermute x20 -> x18, starting transfers between devices: 17.1 us -> 29.1 us  [per_device(): go_left = lambda x: lax.ppermute(x, 'ctx', left)]
    ppermute x21 -> x19, starting transfers between devices: 70.6 us -> 60.7 us  [per_device(): go_right = lambda x: lax.ppermute(x, 'ctx', right)]
    ppermute x0 -> x4, starting transfers between devices: none -> 5.6 us  [per_device(): lax.ppermute(x, 'ctx', pairs)]
    ppermute x0 -> x4, waiting for transfers between devices: none -> 4.86 us  [per_device(): lax.ppermute(x, 'ctx', pairs)]
    ppermute x21 -> x19, waiting for transfers between devices: 22.5 us -> 22.2 us  [per_device(): go_right = lambda x: lax.ppermute(x, 'ctx', right)]
  transfers between devices with their start and end apart: 50 -> 50, of which waited for: 32 -> 27; matrix products, arithmetic and copies ran while one was open for 0% -> 0% of each run, Pallas kernels for 10% -> 10%
where the time goes in v8:
time: 170 us; the launch traced here: 169 us
  starting transfers between devices  99.5 us (59%)
  waiting for transfers between devices  40.9 us (24%)
  Pallas kernels  27.7 us (16%)
    ppermute x19, starting transfers between devices, per_device(): go_right = lambda x: lax.ppermute(x, 'ctx', right)  60.7 us
    ppermute x18, starting transfers between devices, per_device(): go_left = lambda x: lax.ppermute(x, 'ctx', left)  29.1 us
    ppermute x19, waiting for transfers between devices, per_device(): go_right = lambda x: lax.ppermute(x, 'ctx', right)  22.2 us
    ppermute x18, waiting for transfers between devices, per_device(): go_left = lambda x: lax.ppermute(x, 'ctx', left)  12.6 us
    pallas_call x5, Pallas kernels, call(): pl.pallas_call(kernel, in_specs=[pl.BlockSpec(memory_space=pltpu.SMEM)] +...  8.57 us
    ppermute x4, starting transfers between devices, per_device(): lax.ppermute(x, 'ctx', pairs)  5.6 us
    ppermute x4, waiting for transfers between devices, per_device(): lax.ppermute(x, 'ctx', pairs)  4.86 us
    pallas_call x2, Pallas kernels, down_call(): pl.pallas_call(down_kernel, in_specs=[vmem] * 2 + more, out_specs=[vmem]...  4.69 us
  transfers between devices with their start and end apart: 50, of which 27 were waited for; matrix products, arithmetic and copies ran while one was open for 0% of the time, Pallas kernels for 10%

profile of v8, /device:TPU:0, one launch (start us, length us, event | category | flops | bytes accessed | tf_op | source)
XLA Modules:
  0.0 169.4 jit_solution(2076560642265332583)
XLA Ops:
  0.6 1.9 %halves.1 = (bf16[256,512]{1,0:T(8,128)(2,1)S(1)}, bf16[256,512]{1,0:T(8,128)(2,1)S(1)}, bf16[128,4096]{1,0:T(8,128)(2,1)S(1)}, bf16[128,4096]{1,0:T(8,128)(2,1)S(1)}) custom-call(s32[1]{0:T(128)} %bitcast.me_ref.refs_0_, bf16[128,1024]{1,0:T(8,128)(2,1)} %refs_0_.2, bf16[128,1024]{1,0:T(8,128)(2,1)} %refs_1_.2, bf16[128,8192]{1,0:T(8,128)(2,1)} %refs_2_.1), custom_call_target="tpu_custom_call" | custom-call | flops 1 | bytes 1 | tf_op jit(solution)/shard_map/halves/pallas_call | solution.py:426
  3.1 3.0 %collective-permute-start.1 = (bf16[256,512]{1,0:T(8,128)(2,1)S(1)}, bf16[256,512]{1,0:T(8,128)(2,1)S(1)}, u32[]{:S(2)}, u32[]{:S(2)}) collective-permute-start(bf16[256,512]{1,0:T(8,128)(2,1)S(1)} %get-tuple-element.92.own_ref.refs_9_), channel_id=1, source_target_pairs={{0,4},{1,5},{4,8},{5,9},{8,12},{9,13},{12,14},{13,15},{14,10},{15,... | collective-permute-start | bytes 786440 | tf_op jit(solution)/shard_map/ppermute | solution.py:692
  8.3 3.8 %attend_own.1 = (f32[4,2048,128]{2,1,0:T(8,128)S(1)}, f32[4,2048,128]{2,1,0:T(8,128)S(1)}, f32[4,2048,128]{2,1,0:T(8,128)S(1)}) custom-call(s32[1]{0:T(128)} %bitcast.me_ref.refs_0_, bf16[128,4096]{1,0:T(8,128)(2,1)S(1)} %get-tuple-element.90.q_ref, bf16[128,4096]{1,0:T(8,128)(2,1)S(1)} %collective-permute-done.sib_q_ref, ...), custom_call_target="tpu_custom_call" | custom-call | flops 1 | bytes 1 | tf_op jit(solution)/shard_map/attend_own/pallas_call | solution.py:332
  13.2 2.2 %collective-permute-done.2.refs_2_.refs_13_ = bf16[256,512]{1,0:T(8,128)(2,1)S(1)} collective-permute-done((bf16[256,512]{1,0:T(8,128)(2,1)S(1)}, bf16[256,512]{1,0:T(8,128)(2,1)S(1)}, u32[]{:S(2)}, u32[]{:S(2)}) %collective-permute-start.2) | collective-permute-done | bytes 262176 | tf_op jit(solution)/shard_map/ppermute | solution.py:693
  18.5 1.9 %collective-permute-start.10 = (bf16[256,512]{1,0:T(8,128)(2,1)S(1)}, bf16[256,512]{1,0:T(8,128)(2,1)S(1)}, u32[]{:S(2)}, u32[]{:S(2)}) collective-permute-start(bf16[256,512]{1,0:T(8,128)(2,1)S(1)} %collective-permute-done.6.refs_1_.refs_12_), channel_id=1, source_target_pairs={{0,4},{1,5},{4,8},{5,9},{8,12},{9,13},{12,14},{13,15},{14,10},{15,... | collective-permute-start | bytes 786440 | tf_op jit(solution)/shard_map/ppermute | solution.py:692
  20.6 3.4 %collective-permute-done.4.refs_0_.refs_15_ = bf16[256,512]{1,0:T(8,128)(2,1)S(1)} collective-permute-done((bf16[256,512]{1,0:T(8,128)(2,1)S(1)}, bf16[256,512]{1,0:T(8,128)(2,1)S(1)}, u32[]{:S(2)}, u32[]{:S(2)}) %collective-permute-start.4) | collective-permute-done | bytes 262176 | tf_op jit(solution)/shard_map/ppermute | solution.py:692
  24.0 1.7 %collective-permute-done.5.refs_2_.refs_17_ = bf16[256,512]{1,0:T(8,128)(2,1)S(1)} collective-permute-done((bf16[256,512]{1,0:T(8,128)(2,1)S(1)}, bf16[256,512]{1,0:T(8,128)(2,1)S(1)}, u32[]{:S(2)}, u32[]{:S(2)}) %collective-permute-start.5) | collective-permute-done | bytes 262176 | tf_op jit(solution)/shard_map/ppermute | solution.py:693
  25.7 2.4 %collective-permute-start.8 = (bf16[256,512]{1,0:T(8,128)(2,1)S(1)}, bf16[256,512]{1,0:T(8,128)(2,1)S(1)}, u32[]{:S(2)}, u32[]{:S(2)}) collective-permute-start(bf16[256,512]{1,0:T(8,128)(2,1)S(1)} %collective-permute-done.4.refs_0_.refs_15_), channel_id=1, source_target_pairs={{0,4},{1,5},{4,8},{5,9},{8,12},{9,13},{12,14},{13,15},{14,10},{15,... | collective-permute-start | bytes 786440 | tf_op jit(solution)/shard_map/ppermute | solution.py:692
  33.0 2.2 %collective-permute-done.8.refs_0_.refs_19_ = bf16[256,512]{1,0:T(8,128)(2,1)S(1)} collective-permute-done((bf16[256,512]{1,0:T(8,128)(2,1)S(1)}, bf16[256,512]{1,0:T(8,128)(2,1)S(1)}, u32[]{:S(2)}, u32[]{:S(2)}) %collective-permute-start.8) | collective-permute-done | bytes 262176 | tf_op jit(solution)/shard_map/ppermute | solution.py:692
  35.2 1.7 %collective-permute-done.9.refs_2_.refs_21_ = bf16[256,512]{1,0:T(8,128)(2,1)S(1)} collective-permute-done((bf16[256,512]{1,0:T(8,128)(2,1)S(1)}, bf16[256,512]{1,0:T(8,128)(2,1)S(1)}, u32[]{:S(2)}, u32[]{:S(2)}) %collective-permute-start.9) | collective-permute-done | bytes 262176 | tf_op jit(solution)/shard_map/ppermute | solution.py:693
  36.9 3.2 %collective-permute-start.12 = (bf16[256,512]{1,0:T(8,128)(2,1)S(1)}, bf16[256,512]{1,0:T(8,128)(2,1)S(1)}, u32[]{:S(2)}, u32[]{:S(2)}) collective-permute-start(bf16[256,512]{1,0:T(8,128)(2,1)S(1)} %collective-permute-done.8.refs_0_.refs_19_), channel_id=1, source_target_pairs={{0,4},{1,5},{4,8},{5,9},{8,12},{9,13},{12,14},{13,15},{14,10},{15,... | collective-permute-start | bytes 786440 | tf_op jit(solution)/shard_map/ppermute | solution.py:692
  40.8 1.7 %collective-permute-done.14.refs_3_.refs_22_ = bf16[256,512]{1,0:T(8,128)(2,1)S(1)} collective-permute-done((bf16[256,512]{1,0:T(8,128)(2,1)S(1)}, bf16[256,512]{1,0:T(8,128)(2,1)S(1)}, u32[]{:S(2)}, u32[]{:S(2)}) %collective-permute-start.14) | collective-permute-done | bytes 262176 | tf_op jit(solution)/shard_map/ppermute | solution.py:693
  42.5 1.6 collective-permute-start.15
  44.8 4.3 %collective-permute-done.15.refs_1_.refs_24_ = bf16[128,512]{1,0:T(8,128)(2,1)S(1)} collective-permute-done((bf16[128,512]{1,0:T(8,128)(2,1)S(1)}, bf16[128,512]{1,0:T(8,128)(2,1)S(1)}, u32[]{:S(2)}, u32[]{:S(2)}) %collective-permute-start.15) | collective-permute-done | bytes 131104 | tf_op jit(solution)/shard_map/ppermute | solution.py:692
  49.8 4.7 %attend_last.1 = (bf16[128,4096]{1,0:T(8,128)(2,1)S(1)}, bf16[128,4096]{1,0:T(8,128)(2,1)S(1)}, bf16[16,4224]{1,0:T(8,128)(2,1)S(1)}, bf16[16,4224]{1,0:T(8,128)...) custom-call(s32[1]{0:T(128)} %bitcast.me_ref.refs_0_, ...), custom_call_target="tpu_custom_call" | custom-call | flops 1 | bytes 1 | tf_op jit(solution)/shard_map/attend_last/pallas_call | solution.py:332
  56.6 1.8 %collective-permute-start.21 = (bf16[16,4224]{1,0:T(8,128)(2,1)S(1)}, bf16[16,4224]{1,0:T(8,128)(2,1)S(1)}, u32[]{:S(2)}, u32[]{:S(2)}) collective-permute-start(bf16[16,4224]{1,0:T(8,128)(2,1)S(1)} %get-tuple-element.132.refs_0_), channel_id=1, source_target_pairs={{0,4},{1,5},{4,8},{5,9},{8,12},{9,13},{12,14},{13,15},{14,10},{15,... | collective-permute-start | bytes 405512 | tf_op jit(solution)/shard_map/ppermute | solution.py:692
  63.7 37.9 %collective-permute-start.25 = (bf16[16,4224]{1,0:T(8,128)(2,1)S(1)}, bf16[16,4224]{1,0:T(8,128)(2,1)S(1)}, u32[]{:S(2)}, u32[]{:S(2)}) collective-permute-start(bf16[16,4224]{1,0:T(8,128)(2,1)S(1)} %collective-permute-done.21.refs_2_), channel_id=1, source_target_pairs={{0,4},{1,5},{4,8},{5,9},{8,12},{9,13},{12,14},{13,15},{14,10},{15,... | collective-permute-start | bytes 405512 | tf_op jit(solution)/shard_map/ppermute | solution.py:692
  101.7 7.1 %collective-permute-start.23 = (bf16[16,4224]{1,0:T(8,128)(2,1)S(1)}, bf16[16,4224]{1,0:T(8,128)(2,1)S(1)}, u32[]{:S(2)}, u32[]{:S(2)}) collective-permute-start(bf16[16,4224]{1,0:T(8,128)(2,1)S(1)} %collective-permute-done.19.refs_0_), channel_id=1, source_target_pairs={{4,0},{5,1},{8,4},{9,5},{12,8},{13,9},{14,12},{15,13},{10,14},{11,... | collective-permute-start | bytes 405512 | tf_op jit(solution)/shard_map/ppermute | solution.py:693
  108.8 3.3 %collective-permute-start.28 = (bf16[16,4224]{1,0:T(8,128)(2,1)S(1)}, bf16[16,4224]{1,0:T(8,128)(2,1)S(1)}, u32[]{:S(2)}, u32[]{:S(2)}) collective-permute-start(bf16[16,4224]{1,0:T(8,128)(2,1)S(1)} %collective-permute-done.19.refs_0_), channel_id=1, source_target_pairs={{8,0},{9,1},{12,4},{13,5},{14,8},{15,9},{10,12},{11,13},{6,14},{7,... | collective-permute-start | bytes 405512 | tf_op jit(solution)/shard_map/ppermute | solution.py:695
  113.6 2.2 %collective-permute-start.31 = (bf16[16,4224]{1,0:T(8,128)(2,1)S(1)}, bf16[16,4224]{1,0:T(8,128)(2,1)S(1)}, u32[]{:S(2)}, u32[]{:S(2)}) collective-permute-start(bf16[16,4224]{1,0:T(8,128)(2,1)S(1)} %collective-permute-done.26.refs_3_), channel_id=1, source_target_pairs={{4,0},{5,1},{8,4},{9,5},{12,8},{13,9},{14,12},{15,13},{10,14},{11,... | collective-permute-start | bytes 405512 | tf_op jit(solution)/shard_map/ppermute | solution.py:693
  115.9 4.8 %collective-permute-done.29.refs_5_ = bf16[16,4224]{1,0:T(8,128)(2,1)S(1)} collective-permute-done((bf16[16,4224]{1,0:T(8,128)(2,1)S(1)}, bf16[16,4224]{1,0:T(8,128)(2,1)S(1)}, u32[]{:S(2)}, u32[]{:S(2)}) %collective-permute-start.29) | collective-permute-done | bytes 135200 | tf_op jit(solution)/shard_map/ppermute | solution.py:695
  121.7 4.6 %hidden_first.1 = (f32[256,768]{1,0:T(8,128)S(1)}, f32[256,768]{1,0:T(8,128)S(1)}, bf16[4096,768]{1,0:T(8,128)(2,1)S(1)}, bf16[4096,768]{1,0:T(8,128)(2,1)S(1)}) custom-call(s32[1]{0:T(128)} %bitcast.me_ref.refs_0_, bf16[256,4224]{1,0:T(8,128)(2,1)S(1)} %place.7.rows_ref.own_ref, bf16[4096,768]{1,0:T(8,128)(2,1)S(1)} %get-tuple-element.161.gate_ref, ...), custom_call_target="tpu_custom_call" | custom-call | flops 3221225472 | bytes 12582912 | tf_op jit(solution)/shard_map/hidden_first/pallas_call | solution.py:529
  126.4 4.6 %hidden_second.1 = (bf16[256,768]{1,0:T(8,128)(2,1)S(1)}, bf16[768,4096]{1,0:T(8,128)(2,1)S(1)}, bf16[768,4096]{1,0:T(8,128)(2,1)S(1)}) custom-call(bf16[256,4224]{1,0:T(8,128)(2,1)S(1)} %collective-permute-done.32.rows_ref, bf16[4096,768]{1,0:T(8,128)(2,1)S(1)} %get-tuple-element.163.gate_ref, bf16[4096,768]{1,0:T(8,128)(2,1)S(1)} %get-tuple-element.164.up_ref, ...), custom_call_target="tpu_custom_call" | custom-call | flops 3221225472 | bytes 12582912 | tf_op jit(solution)/shard_map/hidden_second/pallas_call | solution.py:539
  131.0 2.4 %down.2 = (bf16[128,4096]{1,0:T(8,128)(2,1)S(1)}, bf16[128,4096]{1,0:T(8,128)(2,1)S(1)}, bf16[128,8192]{1,0:T(8,128)(2,1)}) custom-call(bf16[256,768]{1,0:T(8,128)(2,1)S(1)} %get-tuple-element.167.hidden_ref, bf16[768,4096]{1,0:T(8,128)(2,1)S(1)} %get-tuple-element.168.down_ref, s32[1]{0:T(128)} %bitcast.me_ref.refs_0_, ...), custom_call_target="tpu_custom_call" | custom-call | flops 1610612736 | bytes 8388608 | tf_op jit(solution)/shard_map/down/pallas_call | solution.py:591
  133.5 2.3 %down.3 = (bf16[128,4096]{1,0:T(8,128)(2,1)S(1)}, bf16[128,4096]{1,0:T(8,128)(2,1)S(1)}) custom-call(bf16[256,768]{1,0:T(8,128)(2,1)S(1)} %get-tuple-element.167.hidden_ref, bf16[768,4096]{1,0:T(8,128)(2,1)S(1)} %get-tuple-element.172.down_ref), custom_call_target="tpu_custom_call" | custom-call | flops 1610612736 | bytes 8388608 | tf_op jit(solution)/shard_map/down/pallas_call | solution.py:591
  136.4 3.7 %collective-permute-start.47 = (bf16[16,4096]{1,0:T(8,128)(2,1)S(1)}, bf16[16,4096]{1,0:T(8,128)(2,1)S(1)}, u32[]{:S(2)}, u32[]{:S(2)}) collective-permute-start(bf16[16,4096]{1,0:T(8,128)(2,1)S(1)} %add.25), channel_id=1, source_target_pairs={{4,0},{5,1},{8,4},{9,5},{12,8},{13,9},{14,12},{15,13},{10,14},{11,... | collective-permute-start | bytes 393224 | tf_op jit(solution)/shard_map/ppermute | solution.py:693
  141.4 1.9 %collective-permute-start.39 = (bf16[16,4096]{1,0:T(8,128)(2,1)S(1)}, bf16[16,4096]{1,0:T(8,128)(2,1)S(1)}, u32[]{:S(2)}, u32[]{:S(2)}) collective-permute-start(bf16[16,4096]{1,0:T(8,128)(2,1)S(1)} %add.18), channel_id=1, source_target_pairs={{8,0},{9,1},{12,4},{13,5},{14,8},{15,9},{10,12},{11,13},{6,14},{7,... | collective-permute-start | bytes 393224 | tf_op jit(solution)/shard_map/ppermute | solution.py:695
  143.4 2.1 %collective-permute-start.38 = (bf16[16,4096]{1,0:T(8,128)(2,1)S(1)}, bf16[16,4096]{1,0:T(8,128)(2,1)S(1)}, u32[]{:S(2)}, u32[]{:S(2)}) collective-permute-start(bf16[16,4096]{1,0:T(8,128)(2,1)S(1)} %add.17), channel_id=1, source_target_pairs={{4,0},{5,1},{8,4},{9,5},{12,8},{13,9},{14,12},{15,13},{10,14},{11,... | collective-permute-start | bytes 393224 | tf_op jit(solution)/shard_map/ppermute | solution.py:693
  145.6 2.3 %collective-permute-done.43.refs_0_ = bf16[16,4096]{1,0:T(8,128)(2,1)S(1)} collective-permute-done((bf16[16,4096]{1,0:T(8,128)(2,1)S(1)}, bf16[16,4096]{1,0:T(8,128)(2,1)S(1)}, u32[]{:S(2)}, u32[]{:S(2)}) %collective-permute-start.43) | collective-permute-done | bytes 131104 | tf_op jit(solution)/shard_map/ppermute | solution.py:692
  148.0 5.2 %collective-permute-start.48 = (bf16[16,4096]{1,0:T(8,128)(2,1)S(1)}, bf16[16,4096]{1,0:T(8,128)(2,1)S(1)}, u32[]{:S(2)}, u32[]{:S(2)}) collective-permute-start(bf16[16,4096]{1,0:T(8,128)(2,1)S(1)} %add.26), channel_id=1, source_target_pairs={{4,0},{5,1},{8,4},{9,5},{12,8},{13,9},{14,12},{15,13},{10,14},{11,... | collective-permute-start | bytes 393224 | tf_op jit(solution)/shard_map/ppermute | solution.py:693
  153.6 1.8 %collective-permute-start.40 = (bf16[16,4096]{1,0:T(8,128)(2,1)S(1)}, bf16[16,4096]{1,0:T(8,128)(2,1)S(1)}, u32[]{:S(2)}, u32[]{:S(2)}) collective-permute-start(bf16[16,4096]{1,0:T(8,128)(2,1)S(1)} %add.19), channel_id=1, source_target_pairs={{4,0},{5,1},{8,4},{9,5},{12,8},{13,9},{14,12},{15,13},{10,14},{11,... | collective-permute-start | bytes 393224 | tf_op jit(solution)/shard_map/ppermute | solution.py:693
  157.0 2.2 %collective-permute-done.45.refs_0_ = bf16[16,4096]{1,0:T(8,128)(2,1)S(1)} collective-permute-done((bf16[16,4096]{1,0:T(8,128)(2,1)S(1)}, bf16[16,4096]{1,0:T(8,128)(2,1)S(1)}, u32[]{:S(2)}, u32[]{:S(2)}) %collective-permute-start.45) | collective-permute-done | bytes 131104 | tf_op jit(solution)/shard_map/ppermute | solution.py:692
  (114 shorter events, 38.2 us)
Async XLA Ops:
  3.1 10.0 %collective-permute-start.1 = (bf16[256,512]{1,0:T(8,128)(2,1)S(1)}, bf16[256,512]{1,0:T(8,128)(2,1)S(1)}, u32[]{:S(2)}, u32[]{:S(2)}) collective-permute-start(bf16[256,512]{1,0:T(8,128)(2,1)S(1)} %get-tuple-element.92.own_ref.refs_9_), channel_id=1, source_target_pairs={{0,4},{1,5},{4,8},{5,9},{8,12},{9,13},{12,14},{13,15},{14,10},{15,... | collective-permute-start | bytes 786440 | tf_op jit(solution)/shard_map/ppermute | solution.py:692
  6.1 9.2 %collective-permute-start.2 = (bf16[256,512]{1,0:T(8,128)(2,1)S(1)}, bf16[256,512]{1,0:T(8,128)(2,1)S(1)}, u32[]{:S(2)}, u32[]{:S(2)}) collective-permute-start(bf16[256,512]{1,0:T(8,128)(2,1)S(1)} %get-tuple-element.92.own_ref.refs_9_), channel_id=1, source_target_pairs={{4,0},{5,1},{8,4},{9,5},{12,8},{13,9},{14,12},{15,13},{10,14},{11,... | collective-permute-start | bytes 786440 | tf_op jit(solution)/shard_map/ppermute | solution.py:693
  6.1 12.3 %collective-permute-start.6 = (bf16[256,512]{1,0:T(8,128)(2,1)S(1)}, bf16[256,512]{1,0:T(8,128)(2,1)S(1)}, u32[]{:S(2)}, u32[]{:S(2)}) collective-permute-start(bf16[256,512]{1,0:T(8,128)(2,1)S(1)} %get-tuple-element.93), channel_id=1, source_target_pairs={{0,5},{1,4},{4,9},{5,8},{8,13},{9,12},{12,15},{13,14},{14,11},{15,... | collective-permute-start | bytes 786440 | tf_op jit(solution)/shard_map/ppermute | solution.py:718
  7.3 11.3 %collective-permute-start.7 = (bf16[256,512]{1,0:T(8,128)(2,1)S(1)}, bf16[256,512]{1,0:T(8,128)(2,1)S(1)}, u32[]{:S(2)}, u32[]{:S(2)}) collective-permute-start(bf16[256,512]{1,0:T(8,128)(2,1)S(1)} %get-tuple-element.93), channel_id=1, source_target_pairs={{4,1},{5,0},{8,5},{9,4},{12,9},{13,8},{14,13},{15,12},{10,15},{11,... | collective-permute-start | bytes 786440 | tf_op jit(solution)/shard_map/ppermute | solution.py:718
  15.3 8.7 %collective-permute-start.4 = (bf16[256,512]{1,0:T(8,128)(2,1)S(1)}, bf16[256,512]{1,0:T(8,128)(2,1)S(1)}, u32[]{:S(2)}, u32[]{:S(2)}) collective-permute-start(bf16[256,512]{1,0:T(8,128)(2,1)S(1)} %collective-permute-done.1.refs_0_.refs_11_), channel_id=1, source_target_pairs={{0,4},{1,5},{4,8},{5,9},{8,12},{9,13},{12,14},{13,15},{14,10},{15,... | collective-permute-start | bytes 786440 | tf_op jit(solution)/shard_map/ppermute | solution.py:692
  16.9 8.8 %collective-permute-start.5 = (bf16[256,512]{1,0:T(8,128)(2,1)S(1)}, bf16[256,512]{1,0:T(8,128)(2,1)S(1)}, u32[]{:S(2)}, u32[]{:S(2)}) collective-permute-start(bf16[256,512]{1,0:T(8,128)(2,1)S(1)} %collective-permute-done.2.refs_2_.refs_13_), channel_id=1, source_target_pairs={{4,0},{5,1},{8,4},{9,5},{12,8},{13,9},{14,12},{15,13},{10,14},{11,... | collective-permute-start | bytes 786440 | tf_op jit(solution)/shard_map/ppermute | solution.py:693
  18.5 11.0 %collective-permute-start.10 = (bf16[256,512]{1,0:T(8,128)(2,1)S(1)}, bf16[256,512]{1,0:T(8,128)(2,1)S(1)}, u32[]{:S(2)}, u32[]{:S(2)}) collective-permute-start(bf16[256,512]{1,0:T(8,128)(2,1)S(1)} %collective-permute-done.6.refs_1_.refs_12_), channel_id=1, source_target_pairs={{0,4},{1,5},{4,8},{5,9},{8,12},{9,13},{12,14},{13,15},{14,10},{15,... | collective-permute-start | bytes 786440 | tf_op jit(solution)/shard_map/ppermute | solution.py:692
  20.5 10.5 %collective-permute-start.11 = (bf16[256,512]{1,0:T(8,128)(2,1)S(1)}, bf16[256,512]{1,0:T(8,128)(2,1)S(1)}, u32[]{:S(2)}, u32[]{:S(2)}) collective-permute-start(bf16[256,512]{1,0:T(8,128)(2,1)S(1)} %collective-permute-done.7.refs_3_.refs_14_), channel_id=1, source_target_pairs={{4,0},{5,1},{8,4},{9,5},{12,8},{13,9},{14,12},{15,13},{10,14},{11,... | collective-permute-start | bytes 786440 | tf_op jit(solution)/shard_map/ppermute | solution.py:693
  25.7 9.5 %collective-permute-start.8 = (bf16[256,512]{1,0:T(8,128)(2,1)S(1)}, bf16[256,512]{1,0:T(8,128)(2,1)S(1)}, u32[]{:S(2)}, u32[]{:S(2)}) collective-permute-start(bf16[256,512]{1,0:T(8,128)(2,1)S(1)} %collective-permute-done.4.refs_0_.refs_15_), channel_id=1, source_target_pairs={{0,4},{1,5},{4,8},{5,9},{8,12},{9,13},{12,14},{13,15},{14,10},{15,... | collective-permute-start | bytes 786440 | tf_op jit(solution)/shard_map/ppermute | solution.py:692
  28.1 8.8 %collective-permute-start.9 = (bf16[256,512]{1,0:T(8,128)(2,1)S(1)}, bf16[256,512]{1,0:T(8,128)(2,1)S(1)}, u32[]{:S(2)}, u32[]{:S(2)}) collective-permute-start(bf16[256,512]{1,0:T(8,128)(2,1)S(1)} %collective-permute-done.5.refs_2_.refs_17_), channel_id=1, source_target_pairs={{4,0},{5,1},{8,4},{9,5},{12,8},{13,9},{14,12},{15,13},{10,14},{11,... | collective-permute-start | bytes 786440 | tf_op jit(solution)/shard_map/ppermute | solution.py:693
  31.0 9.8 %collective-permute-start.13 = (bf16[256,512]{1,0:T(8,128)(2,1)S(1)}, bf16[256,512]{1,0:T(8,128)(2,1)S(1)}, u32[]{:S(2)}, u32[]{:S(2)}) collective-permute-start(bf16[256,512]{1,0:T(8,128)(2,1)S(1)} %collective-permute-done.10.refs_1_.refs_16_), channel_id=1, source_target_pairs={{0,4},{1,5},{4,8},{5,9},{8,12},{9,13},{12,14},{13,15},{14,10},{15,... | collective-permute-start | bytes 786440 | tf_op jit(solution)/shard_map/ppermute | solution.py:692
  32.6 10.0 %collective-permute-start.14 = (bf16[256,512]{1,0:T(8,128)(2,1)S(1)}, bf16[256,512]{1,0:T(8,128)(2,1)S(1)}, u32[]{:S(2)}, u32[]{:S(2)}) collective-permute-start(bf16[256,512]{1,0:T(8,128)(2,1)S(1)} %collective-permute-done.11.refs_3_.refs_18_), channel_id=1, source_target_pairs={{4,0},{5,1},{8,4},{9,5},{12,8},{13,9},{14,12},{15,13},{10,14},{11,... | collective-permute-start | bytes 786440 | tf_op jit(solution)/shard_map/ppermute | solution.py:693
  36.9 12.9 %collective-permute-start.12 = (bf16[256,512]{1,0:T(8,128)(2,1)S(1)}, bf16[256,512]{1,0:T(8,128)(2,1)S(1)}, u32[]{:S(2)}, u32[]{:S(2)}) collective-permute-start(bf16[256,512]{1,0:T(8,128)(2,1)S(1)} %collective-permute-done.8.refs_0_.refs_19_), channel_id=1, source_target_pairs={{0,4},{1,5},{4,8},{5,9},{8,12},{9,13},{12,14},{13,15},{14,10},{15,... | collective-permute-start | bytes 786440 | tf_op jit(solution)/shard_map/ppermute | solution.py:692
  58.4 43.3 %collective-permute-start.22 = (bf16[16,4224]{1,0:T(8,128)(2,1)S(1)}, bf16[16,4224]{1,0:T(8,128)(2,1)S(1)}, u32[]{:S(2)}, u32[]{:S(2)}) collective-permute-start(bf16[16,4224]{1,0:T(8,128)(2,1)S(1)} %get-tuple-element.133.refs_1_), channel_id=1, source_target_pairs={{4,0},{5,1},{8,4},{9,5},{12,8},{13,9},{14,12},{15,13},{10,14},{11,... | collective-permute-start | bytes 405512 | tf_op jit(solution)/shard_map/ppermute | solution.py:693
  59.6 42.1 %collective-permute-start.19 = (bf16[16,4224]{1,0:T(8,128)(2,1)S(1)}, bf16[16,4224]{1,0:T(8,128)(2,1)S(1)}, u32[]{:S(2)}, u32[]{:S(2)}) collective-permute-start(bf16[16,4224]{1,0:T(8,128)(2,1)S(1)} %collective-permute-done.18.refs_0_), channel_id=1, source_target_pairs={{4,0},{5,1},{8,4},{9,5},{12,8},{13,9},{14,12},{15,13},{10,14},{11,... | collective-permute-start | bytes 405512 | tf_op jit(solution)/shard_map/ppermute | solution.py:693
  62.1 50.0 %collective-permute-start.24 = (bf16[16,4224]{1,0:T(8,128)(2,1)S(1)}, bf16[16,4224]{1,0:T(8,128)(2,1)S(1)}, u32[]{:S(2)}, u32[]{:S(2)}) collective-permute-start(bf16[16,4224]{1,0:T(8,128)(2,1)S(1)} %collective-permute-done.20.refs_1_), channel_id=1, source_target_pairs={{0,4},{1,5},{4,8},{5,9},{8,12},{9,13},{12,14},{13,15},{14,10},{15,... | collective-permute-start | bytes 405512 | tf_op jit(solution)/shard_map/ppermute | solution.py:692
  63.7 48.4 %collective-permute-start.25 = (bf16[16,4224]{1,0:T(8,128)(2,1)S(1)}, bf16[16,4224]{1,0:T(8,128)(2,1)S(1)}, u32[]{:S(2)}, u32[]{:S(2)}) collective-permute-start(bf16[16,4224]{1,0:T(8,128)(2,1)S(1)} %collective-permute-done.21.refs_2_), channel_id=1, source_target_pairs={{0,4},{1,5},{4,8},{5,9},{8,12},{9,13},{12,14},{13,15},{14,10},{15,... | collective-permute-start | bytes 405512 | tf_op jit(solution)/shard_map/ppermute | solution.py:692
  101.6 10.7 %collective-permute-start.26 = (bf16[16,4224]{1,0:T(8,128)(2,1)S(1)}, bf16[16,4224]{1,0:T(8,128)(2,1)S(1)}, u32[]{:S(2)}, u32[]{:S(2)}) collective-permute-start(bf16[16,4224]{1,0:T(8,128)(2,1)S(1)} %collective-permute-done.22.refs_3_), channel_id=1, source_target_pairs={{4,0},{5,1},{8,4},{9,5},{12,8},{13,9},{14,12},{15,13},{10,14},{11,... | collective-permute-start | bytes 405512 | tf_op jit(solution)/shard_map/ppermute | solution.py:693
  101.7 11.9 %collective-permute-start.23 = (bf16[16,4224]{1,0:T(8,128)(2,1)S(1)}, bf16[16,4224]{1,0:T(8,128)(2,1)S(1)}, u32[]{:S(2)}, u32[]{:S(2)}) collective-permute-start(bf16[16,4224]{1,0:T(8,128)(2,1)S(1)} %collective-permute-done.19.refs_0_), channel_id=1, source_target_pairs={{4,0},{5,1},{8,4},{9,5},{12,8},{13,9},{14,12},{15,13},{10,14},{11,... | collective-permute-start | bytes 405512 | tf_op jit(solution)/shard_map/ppermute | solution.py:693
  108.8 11.9 %collective-permute-start.28 = (bf16[16,4224]{1,0:T(8,128)(2,1)S(1)}, bf16[16,4224]{1,0:T(8,128)(2,1)S(1)}, u32[]{:S(2)}, u32[]{:S(2)}) collective-permute-start(bf16[16,4224]{1,0:T(8,128)(2,1)S(1)} %collective-permute-done.19.refs_0_), channel_id=1, source_target_pairs={{8,0},{9,1},{12,4},{13,5},{14,8},{15,9},{10,12},{11,13},{6,14},{7,... | collective-permute-start | bytes 405512 | tf_op jit(solution)/shard_map/ppermute | solution.py:695
  112.1 8.6 %collective-permute-start.29 = (bf16[16,4224]{1,0:T(8,128)(2,1)S(1)}, bf16[16,4224]{1,0:T(8,128)(2,1)S(1)}, u32[]{:S(2)}, u32[]{:S(2)}) collective-permute-start(bf16[16,4224]{1,0:T(8,128)(2,1)S(1)} %collective-permute-done.24.refs_1_), channel_id=1, source_target_pairs={{0,8},{1,9},{4,12},{5,13},{8,14},{9,15},{12,10},{13,11},{14,6},{15... | collective-permute-start | bytes 405512 | tf_op jit(solution)/shard_map/ppermute | solution.py:695
  112.2 8.6 %collective-permute-start.27 = (bf16[16,4224]{1,0:T(8,128)(2,1)S(1)}, bf16[16,4224]{1,0:T(8,128)(2,1)S(1)}, u32[]{:S(2)}, u32[]{:S(2)}) collective-permute-start(bf16[16,4224]{1,0:T(8,128)(2,1)S(1)} %collective-permute-done.24.refs_1_), channel_id=1, source_target_pairs={{0,4},{1,5},{4,8},{5,9},{8,12},{9,13},{12,14},{13,15},{14,10},{15,... | collective-permute-start | bytes 405512 | tf_op jit(solution)/shard_map/ppermute | solution.py:692
  112.4 8.7 %collective-permute-start.30 = (bf16[16,4224]{1,0:T(8,128)(2,1)S(1)}, bf16[16,4224]{1,0:T(8,128)(2,1)S(1)}, u32[]{:S(2)}, u32[]{:S(2)}) collective-permute-start(bf16[16,4224]{1,0:T(8,128)(2,1)S(1)} %collective-permute-done.25.refs_2_), channel_id=1, source_target_pairs={{0,4},{1,5},{4,8},{5,9},{8,12},{9,13},{12,14},{13,15},{14,10},{15,... | collective-permute-start | bytes 405512 | tf_op jit(solution)/shard_map/ppermute | solution.py:692
  113.6 7.5 %collective-permute-start.31 = (bf16[16,4224]{1,0:T(8,128)(2,1)S(1)}, bf16[16,4224]{1,0:T(8,128)(2,1)S(1)}, u32[]{:S(2)}, u32[]{:S(2)}) collective-permute-start(bf16[16,4224]{1,0:T(8,128)(2,1)S(1)} %collective-permute-done.26.refs_3_), channel_id=1, source_target_pairs={{4,0},{5,1},{8,4},{9,5},{12,8},{13,9},{14,12},{15,13},{10,14},{11,... | collective-permute-start | bytes 405512 | tf_op jit(solution)/shard_map/ppermute | solution.py:693
  121.2 9.8 %collective-permute-start.33 = (bf16[128,4096]{1,0:T(8,128)(2,1)S(1)}, bf16[128,4096]{1,0:T(8,128)(2,1)S(1)}, u32[]{:S(2)}, u32[]{:S(2)}) collective-permute-start(bf16[128,4096]{1,0:T(8,128)(2,1)S(1)} %get-tuple-element.170), channel_id=1, source_target_pairs={{0,1},{1,0},{2,3},{3,2},{4,5},{5,4},{6,7},{7,6},{8,9},{9,8},{10,11... | collective-permute-start | bytes 3145736 | tf_op jit(solution)/shard_map/ppermute | solution.py:694
  136.4 9.0 %collective-permute-start.47 = (bf16[16,4096]{1,0:T(8,128)(2,1)S(1)}, bf16[16,4096]{1,0:T(8,128)(2,1)S(1)}, u32[]{:S(2)}, u32[]{:S(2)}) collective-permute-start(bf16[16,4096]{1,0:T(8,128)(2,1)S(1)} %add.25), channel_id=1, source_target_pairs={{4,0},{5,1},{8,4},{9,5},{12,8},{13,9},{14,12},{15,13},{10,14},{11,... | collective-permute-start | bytes 393224 | tf_op jit(solution)/shard_map/ppermute | solution.py:693
  140.2 13.0 %collective-permute-start.44 = (bf16[16,4096]{1,0:T(8,128)(2,1)S(1)}, bf16[16,4096]{1,0:T(8,128)(2,1)S(1)}, u32[]{:S(2)}, u32[]{:S(2)}) collective-permute-start(bf16[16,4096]{1,0:T(8,128)(2,1)S(1)} %add.22), channel_id=1, source_target_pairs={{0,8},{1,9},{4,12},{5,13},{8,14},{9,15},{12,10},{13,11},{14,6},{15... | collective-permute-start | bytes 393224 | tf_op jit(solution)/shard_map/ppermute | solution.py:695
  140.6 7.4 %collective-permute-start.43 = (bf16[16,4096]{1,0:T(8,128)(2,1)S(1)}, bf16[16,4096]{1,0:T(8,128)(2,1)S(1)}, u32[]{:S(2)}, u32[]{:S(2)}) collective-permute-start(bf16[16,4096]{1,0:T(8,128)(2,1)S(1)} %add.21), channel_id=1, source_target_pairs={{0,4},{1,5},{4,8},{5,9},{8,12},{9,13},{12,14},{13,15},{14,10},{15,... | collective-permute-start | bytes 393224 | tf_op jit(solution)/shard_map/ppermute | solution.py:692
  141.4 12.1 %collective-permute-start.39 = (bf16[16,4096]{1,0:T(8,128)(2,1)S(1)}, bf16[16,4096]{1,0:T(8,128)(2,1)S(1)}, u32[]{:S(2)}, u32[]{:S(2)}) collective-permute-start(bf16[16,4096]{1,0:T(8,128)(2,1)S(1)} %add.18), channel_id=1, source_target_pairs={{8,0},{9,1},{12,4},{13,5},{14,8},{15,9},{10,12},{11,13},{6,14},{7,... | collective-permute-start | bytes 393224 | tf_op jit(solution)/shard_map/ppermute | solution.py:695
  143.4 10.2 %collective-permute-start.38 = (bf16[16,4096]{1,0:T(8,128)(2,1)S(1)}, bf16[16,4096]{1,0:T(8,128)(2,1)S(1)}, u32[]{:S(2)}, u32[]{:S(2)}) collective-permute-start(bf16[16,4096]{1,0:T(8,128)(2,1)S(1)} %add.17), channel_id=1, source_target_pairs={{4,0},{5,1},{8,4},{9,5},{12,8},{13,9},{14,12},{15,13},{10,14},{11,... | collective-permute-start | bytes 393224 | tf_op jit(solution)/shard_map/ppermute | solution.py:693
  145.5 9.9 %collective-permute-start.35 = (bf16[16,4096]{1,0:T(8,128)(2,1)S(1)}, bf16[16,4096]{1,0:T(8,128)(2,1)S(1)}, u32[]{:S(2)}, u32[]{:S(2)}) collective-permute-start(bf16[16,4096]{1,0:T(8,128)(2,1)S(1)} %add.14), channel_id=1, source_target_pairs={{0,4},{1,5},{4,8},{5,9},{8,12},{9,13},{12,14},{13,15},{14,10},{15,... | collective-permute-start | bytes 393224 | tf_op jit(solution)/shard_map/ppermute | solution.py:692
  148.0 9.0 %collective-permute-start.48 = (bf16[16,4096]{1,0:T(8,128)(2,1)S(1)}, bf16[16,4096]{1,0:T(8,128)(2,1)S(1)}, u32[]{:S(2)}, u32[]{:S(2)}) collective-permute-start(bf16[16,4096]{1,0:T(8,128)(2,1)S(1)} %add.26), channel_id=1, source_target_pairs={{4,0},{5,1},{8,4},{9,5},{12,8},{13,9},{14,12},{15,13},{10,14},{11,... | collective-permute-start | bytes 393224 | tf_op jit(solution)/shard_map/ppermute | solution.py:693
  (21 other events, 119.8 us)

commit v9 on v7

--- a/solution.py
+++ b/solution.py
@@ -604,37 +604,45 @@
     )(hidden, w_down, *halves)
 
 
-def spread_kernel(a_ref, b_ref, c_ref, d_ref, table_ref, *rest):
-    out_ref = rest[-1]
-    total = a_ref[...].astype(jnp.float32) + b_ref[...].astype(jnp.float32)
-    total += c_ref[...].astype(jnp.float32) + d_ref[...].astype(jnp.float32)
-    total = total.astype(jnp.bfloat16)
-    out_ref[...] = lax.dot_general(
-        table_ref[...],
-        jnp.concatenate([total] * PARTS, axis=0),
-        (((0,), (0,)), ((), ())),
-        preferred_element_type=jnp.float32,
-    ).astype(jnp.bfloat16)
+def spread_kernel(start, *refs):
+    parts, table_ref, out_ref, kept_ref, sems = refs[:4], refs[4], *refs[-3:]
+    table = table_ref[...]
+    width = kept_ref.shape[1]
+    cols = min(1024, width)
+    copies = []
+    for i in range(width // cols):
+        columns = slice(i * cols, (i + 1) * cols)
+        total = sum(ref[:CAP, columns].astype(jnp.float32) for ref in parts).astype(jnp.bfloat16)
+        kept_ref[:, columns] = lax.dot_general(
+            table,
+            jnp.concatenate([total] * PARTS, axis=0),
+            (((0,), (0,)), ((), ())),
+            preferred_element_type=jnp.float32,
+        ).astype(jnp.bfloat16)
+        target = out_ref.at[:, pl.ds(start + i * cols, cols)]
+        copies.append(pltpu.make_async_copy(kept_ref.at[:, pl.ds(i * cols, cols)], target, sems.at[i]))
+        copies[-1].start()
+    for copy in copies:
+        copy.wait()
 
 
 def spread_call(parts, table, piece, pieces, previous):
     tokens = table.shape[1]
-    piece_width = parts[0].shape[1]
-    cols = min(2048, piece_width)
-    steps = piece_width // cols
+    width = parts[0].shape[1]
     earlier = [] if previous is None else [previous]
+    vmem, anywhere = pl.BlockSpec(memory_space=pltpu.VMEM), pl.BlockSpec(memory_space=pl.ANY)
     return pl.pallas_call(
-        spread_kernel,
-        grid=(steps,),
-        in_specs=[pl.BlockSpec((CAP, cols), lambda i: (0, i))] * 4
-        + [pl.BlockSpec((PARTS * CAP, tokens), lambda i: (0, 0))]
-        + [pl.BlockSpec(memory_space=pl.ANY)] * len(earlier),
-        out_specs=pl.BlockSpec((tokens, cols), lambda i: (0, piece * steps + i)),
-        out_shape=jax.ShapeDtypeStruct((tokens, piece_width * pieces), jnp.bfloat16),
+        functools.partial(spread_kernel, piece * width),
+        in_specs=[vmem] * 5 + [anywhere] * len(earlier),
+        out_specs=anywhere,
+        out_shape=jax.ShapeDtypeStruct((tokens, width * pieces), jnp.bfloat16),
         input_output_aliases={5: 0} if earlier else {},
-        compiler_params=pltpu.CompilerParams(
-            dimension_semantics=("arbitrary",), vmem_limit_bytes=16 * MIB
-        ),
+        scratch_shapes=[
+            pltpu.VMEM((tokens, width), jnp.bfloat16),
+            pltpu.SemaphoreType.DMA((max(1, width // 1024),)),
+        ],
+        compiler_params=pltpu.CompilerParams(vmem_limit_bytes=8 * MIB),
+        cost_estimate=SMALL,
         name="spread",
     )(*parts, table, *earlier)
 

time: 167 us -> 167 us (level)
  transfers between devices with their start and end apart: 52 -> 52, of which waited for: 31 -> 32; matrix products, arithmetic and copies ran while one was open for 0% -> 0% of each run, Pallas kernels for 11% -> 10%
where the time goes in v9:
time: 167 us
  starting transfers between devices  93.5 us (56%)
  waiting for transfers between devices  44.4 us (27%)
  Pallas kernels  27.7 us (17%)
    ppermute x22, starting transfers between devices, per_device(): go_right = lambda x: lax.ppermute(x, 'ctx', right)  60.1 us
    ppermute x21, starting transfers between devices, per_device(): go_left = lambda x: lax.ppermute(x, 'ctx', left)  29.4 us
    ppermute x22, waiting for transfers between devices, per_device(): go_right = lambda x: lax.ppermute(x, 'ctx', right)  27.3 us
    ppermute x21, waiting for transfers between devices, per_device(): go_left = lambda x: lax.ppermute(x, 'ctx', left)  15.8 us
    pallas_call x5, Pallas kernels, call(): pl.pallas_call(kernel, in_specs=[pl.BlockSpec(memory_space=pltpu.SMEM)] +...  8.57 us
    pallas_call x2, Pallas kernels, down_call(): pl.pallas_call(down_kernel, in_specs=[vmem] * 2 + more, out_specs=[vmem]...  4.69 us
    pallas_call x1, Pallas kernels, hidden_calls(): pl.pallas_call(first_kernel, in_specs=[pl.BlockSpec(memory_space=pltpu.SM...  4.63 us
    pallas_call x1, Pallas kernels, hidden_calls(): pl.pallas_call(second_kernel, in_specs=[vmem] * 6 + [anywhere], out_specs...  4.63 us
  transfers between devices with their start and end apart: 52, of which 32 were waited for; matrix products, arithmetic and copies ran while one was open for 0% of the time, Pallas kernels for 10%

profile of v9, /device:TPU:0, one launch (start us, length us, event | category | flops | bytes accessed | tf_op | source)
XLA Modules:
  0.0 166.9 jit_solution(503741003409206376)
XLA Ops:
  0.6 1.9 %halves.1 = (bf16[256,512]{1,0:T(8,128)(2,1)S(1)}, bf16[256,512]{1,0:T(8,128)(2,1)S(1)}, bf16[128,4096]{1,0:T(8,128)(2,1)S(1)}, bf16[128,4096]{1,0:T(8,128)(2,1)S(1)}) custom-call(s32[1]{0:T(128)} %bitcast.me_ref.refs_0_, bf16[128,1024]{1,0:T(8,128)(2,1)} %refs_0_.2, bf16[128,1024]{1,0:T(8,128)(2,1)} %refs_1_.2, bf16[128,8192]{1,0:T(8,128)(2,1)} %refs_2_.1), custom_call_target="tpu_custom_call" | custom-call | flops 1 | bytes 1 | tf_op jit(solution)/shard_map/halves/pallas_call | solution.py:426
  3.1 3.0 %collective-permute-start.1 = (bf16[256,512]{1,0:T(8,128)(2,1)S(1)}, bf16[256,512]{1,0:T(8,128)(2,1)S(1)}, u32[]{:S(2)}, u32[]{:S(2)}) collective-permute-start(bf16[256,512]{1,0:T(8,128)(2,1)S(1)} %get-tuple-element.85.own_ref.refs_9_), channel_id=1, source_target_pairs={{0,4},{1,5},{4,8},{5,9},{8,12},{9,13},{12,14},{13,15},{14,10},{15,... | collective-permute-start | bytes 786440 | tf_op jit(solution)/shard_map/ppermute | solution.py:702
  8.3 3.8 %attend_own.1 = (f32[4,2048,128]{2,1,0:T(8,128)S(1)}, f32[4,2048,128]{2,1,0:T(8,128)S(1)}, f32[4,2048,128]{2,1,0:T(8,128)S(1)}) custom-call(s32[1]{0:T(128)} %bitcast.me_ref.refs_0_, bf16[128,4096]{1,0:T(8,128)(2,1)S(1)} %get-tuple-element.83.q_ref, bf16[128,4096]{1,0:T(8,128)(2,1)S(1)} %collective-permute-done.sib_q_ref, ...), custom_call_target="tpu_custom_call" | custom-call | flops 1 | bytes 1 | tf_op jit(solution)/shard_map/attend_own/pallas_call | solution.py:332
  13.2 2.2 %collective-permute-done.2.refs_2_.refs_13_ = bf16[256,512]{1,0:T(8,128)(2,1)S(1)} collective-permute-done((bf16[256,512]{1,0:T(8,128)(2,1)S(1)}, bf16[256,512]{1,0:T(8,128)(2,1)S(1)}, u32[]{:S(2)}, u32[]{:S(2)}) %collective-permute-start.2) | collective-permute-done | bytes 262176 | tf_op jit(solution)/shard_map/ppermute | solution.py:703
  18.5 1.9 %collective-permute-start.10 = (bf16[256,512]{1,0:T(8,128)(2,1)S(1)}, bf16[256,512]{1,0:T(8,128)(2,1)S(1)}, u32[]{:S(2)}, u32[]{:S(2)}) collective-permute-start(bf16[256,512]{1,0:T(8,128)(2,1)S(1)} %collective-permute-done.6.refs_1_.refs_12_), channel_id=1, source_target_pairs={{0,4},{1,5},{4,8},{5,9},{8,12},{9,13},{12,14},{13,15},{14,10},{15,... | collective-permute-start | bytes 786440 | tf_op jit(solution)/shard_map/ppermute | solution.py:702
  20.6 3.4 %collective-permute-done.4.refs_0_.refs_15_ = bf16[256,512]{1,0:T(8,128)(2,1)S(1)} collective-permute-done((bf16[256,512]{1,0:T(8,128)(2,1)S(1)}, bf16[256,512]{1,0:T(8,128)(2,1)S(1)}, u32[]{:S(2)}, u32[]{:S(2)}) %collective-permute-start.4) | collective-permute-done | bytes 262176 | tf_op jit(solution)/shard_map/ppermute | solution.py:702
  24.0 1.7 %collective-permute-done.5.refs_2_.refs_17_ = bf16[256,512]{1,0:T(8,128)(2,1)S(1)} collective-permute-done((bf16[256,512]{1,0:T(8,128)(2,1)S(1)}, bf16[256,512]{1,0:T(8,128)(2,1)S(1)}, u32[]{:S(2)}, u32[]{:S(2)}) %collective-permute-start.5) | collective-permute-done | bytes 262176 | tf_op jit(solution)/shard_map/ppermute | solution.py:703
  25.7 2.4 %collective-permute-start.8 = (bf16[256,512]{1,0:T(8,128)(2,1)S(1)}, bf16[256,512]{1,0:T(8,128)(2,1)S(1)}, u32[]{:S(2)}, u32[]{:S(2)}) collective-permute-start(bf16[256,512]{1,0:T(8,128)(2,1)S(1)} %collective-permute-done.4.refs_0_.refs_15_), channel_id=1, source_target_pairs={{0,4},{1,5},{4,8},{5,9},{8,12},{9,13},{12,14},{13,15},{14,10},{15,... | collective-permute-start | bytes 786440 | tf_op jit(solution)/shard_map/ppermute | solution.py:702
  33.0 2.2 %collective-permute-done.8.refs_0_.refs_19_ = bf16[256,512]{1,0:T(8,128)(2,1)S(1)} collective-permute-done((bf16[256,512]{1,0:T(8,128)(2,1)S(1)}, bf16[256,512]{1,0:T(8,128)(2,1)S(1)}, u32[]{:S(2)}, u32[]{:S(2)}) %collective-permute-start.8) | collective-permute-done | bytes 262176 | tf_op jit(solution)/shard_map/ppermute | solution.py:702
  35.2 1.7 %collective-permute-done.9.refs_2_.refs_21_ = bf16[256,512]{1,0:T(8,128)(2,1)S(1)} collective-permute-done((bf16[256,512]{1,0:T(8,128)(2,1)S(1)}, bf16[256,512]{1,0:T(8,128)(2,1)S(1)}, u32[]{:S(2)}, u32[]{:S(2)}) %collective-permute-start.9) | collective-permute-done | bytes 262176 | tf_op jit(solution)/shard_map/ppermute | solution.py:703
  36.9 3.2 %collective-permute-start.12 = (bf16[256,512]{1,0:T(8,128)(2,1)S(1)}, bf16[256,512]{1,0:T(8,128)(2,1)S(1)}, u32[]{:S(2)}, u32[]{:S(2)}) collective-permute-start(bf16[256,512]{1,0:T(8,128)(2,1)S(1)} %collective-permute-done.8.refs_0_.refs_19_), channel_id=1, source_target_pairs={{0,4},{1,5},{4,8},{5,9},{8,12},{9,13},{12,14},{13,15},{14,10},{15,... | collective-permute-start | bytes 786440 | tf_op jit(solution)/shard_map/ppermute | solution.py:702
  40.8 1.7 %collective-permute-done.14.refs_3_.refs_22_ = bf16[256,512]{1,0:T(8,128)(2,1)S(1)} collective-permute-done((bf16[256,512]{1,0:T(8,128)(2,1)S(1)}, bf16[256,512]{1,0:T(8,128)(2,1)S(1)}, u32[]{:S(2)}, u32[]{:S(2)}) %collective-permute-start.14) | collective-permute-done | bytes 262176 | tf_op jit(solution)/shard_map/ppermute | solution.py:703
  44.8 4.3 %collective-permute-done.15.refs_1_.refs_24_ = bf16[128,512]{1,0:T(8,128)(2,1)S(1)} collective-permute-done((bf16[128,512]{1,0:T(8,128)(2,1)S(1)}, bf16[128,512]{1,0:T(8,128)(2,1)S(1)}, u32[]{:S(2)}, u32[]{:S(2)}) %collective-permute-start.15) | collective-permute-done | bytes 131104 | tf_op jit(solution)/shard_map/ppermute | solution.py:702
  49.8 4.7 %attend_last.1 = (bf16[128,4096]{1,0:T(8,128)(2,1)S(1)}, bf16[128,4096]{1,0:T(8,128)(2,1)S(1)}, bf16[16,4224]{1,0:T(8,128)(2,1)S(1)}, bf16[16,4224]{1,0:T(8,128)...) custom-call(s32[1]{0:T(128)} %bitcast.me_ref.refs_0_, ...), custom_call_target="tpu_custom_call" | custom-call | flops 1 | bytes 1 | tf_op jit(solution)/shard_map/attend_last/pallas_call | solution.py:332
  56.6 1.8 %collective-permute-start.21 = (bf16[16,4224]{1,0:T(8,128)(2,1)S(1)}, bf16[16,4224]{1,0:T(8,128)(2,1)S(1)}, u32[]{:S(2)}, u32[]{:S(2)}) collective-permute-start(bf16[16,4224]{1,0:T(8,128)(2,1)S(1)} %get-tuple-element.125.refs_0_), channel_id=1, source_target_pairs={{0,4},{1,5},{4,8},{5,9},{8,12},{9,13},{12,14},{13,15},{14,10},{15,... | collective-permute-start | bytes 405512 | tf_op jit(solution)/shard_map/ppermute | solution.py:702
  63.7 37.9 %collective-permute-start.25 = (bf16[16,4224]{1,0:T(8,128)(2,1)S(1)}, bf16[16,4224]{1,0:T(8,128)(2,1)S(1)}, u32[]{:S(2)}, u32[]{:S(2)}) collective-permute-start(bf16[16,4224]{1,0:T(8,128)(2,1)S(1)} %collective-permute-done.21.refs_2_), channel_id=1, source_target_pairs={{0,4},{1,5},{4,8},{5,9},{8,12},{9,13},{12,14},{13,15},{14,10},{15,... | collective-permute-start | bytes 405512 | tf_op jit(solution)/shard_map/ppermute | solution.py:702
  101.7 7.1 %collective-permute-start.23 = (bf16[16,4224]{1,0:T(8,128)(2,1)S(1)}, bf16[16,4224]{1,0:T(8,128)(2,1)S(1)}, u32[]{:S(2)}, u32[]{:S(2)}) collective-permute-start(bf16[16,4224]{1,0:T(8,128)(2,1)S(1)} %collective-permute-done.19.refs_0_), channel_id=1, source_target_pairs={{4,0},{5,1},{8,4},{9,5},{12,8},{13,9},{14,12},{15,13},{10,14},{11,... | collective-permute-start | bytes 405512 | tf_op jit(solution)/shard_map/ppermute | solution.py:703
  110.3 2.0 %collective-permute-start.29 = (bf16[16,4224]{1,0:T(8,128)(2,1)S(1)}, bf16[16,4224]{1,0:T(8,128)(2,1)S(1)}, u32[]{:S(2)}, u32[]{:S(2)}) collective-permute-start(bf16[16,4224]{1,0:T(8,128)(2,1)S(1)} %collective-permute-done.26.refs_3_), channel_id=1, source_target_pairs={{4,0},{5,1},{8,4},{9,5},{12,8},{13,9},{14,12},{15,13},{10,14},{11,... | collective-permute-start | bytes 405512 | tf_op jit(solution)/shard_map/ppermute | solution.py:703
  118.2 1.8 %collective-permute-done.31.refs_5_ = bf16[16,4224]{1,0:T(8,128)(2,1)S(1)} collective-permute-done((bf16[16,4224]{1,0:T(8,128)(2,1)S(1)}, bf16[16,4224]{1,0:T(8,128)(2,1)S(1)}, u32[]{:S(2)}, u32[]{:S(2)}) %collective-permute-start.31) | collective-permute-done | bytes 135200 | tf_op jit(solution)/shard_map/ppermute | solution.py:702
  121.0 4.6 %hidden_first.1 = (f32[256,768]{1,0:T(8,128)S(1)}, f32[256,768]{1,0:T(8,128)S(1)}, bf16[4096,768]{1,0:T(8,128)(2,1)S(1)}, bf16[4096,768]{1,0:T(8,128)(2,1)S(1)}) custom-call(s32[1]{0:T(128)} %bitcast.me_ref.refs_0_, bf16[256,4224]{1,0:T(8,128)(2,1)S(1)} %place.7.rows_ref.own_ref, bf16[4096,768]{1,0:T(8,128)(2,1)S(1)} %get-tuple-element.147.gate_ref, ...), custom_call_target="tpu_custom_call" | custom-call | flops 3221225472 | bytes 12582912 | tf_op jit(solution)/shard_map/hidden_first/pallas_call | solution.py:529
  125.7 4.6 %hidden_second.1 = (bf16[256,768]{1,0:T(8,128)(2,1)S(1)}, bf16[768,4096]{1,0:T(8,128)(2,1)S(1)}, bf16[768,4096]{1,0:T(8,128)(2,1)S(1)}) custom-call(bf16[256,4224]{1,0:T(8,128)(2,1)S(1)} %collective-permute-done.32.rows_ref, bf16[4096,768]{1,0:T(8,128)(2,1)S(1)} %get-tuple-element.149.gate_ref, bf16[4096,768]{1,0:T(8,128)(2,1)S(1)} %get-tuple-element.150.up_ref, ...), custom_call_target="tpu_custom_call" | custom-call | flops 3221225472 | bytes 12582912 | tf_op jit(solution)/shard_map/hidden_second/pallas_call | solution.py:539
  130.3 2.4 %down.2 = (bf16[128,4096]{1,0:T(8,128)(2,1)S(1)}, bf16[128,4096]{1,0:T(8,128)(2,1)S(1)}, bf16[128,8192]{1,0:T(8,128)(2,1)}) custom-call(bf16[256,768]{1,0:T(8,128)(2,1)S(1)} %get-tuple-element.153.hidden_ref, bf16[768,4096]{1,0:T(8,128)(2,1)S(1)} %get-tuple-element.154.down_ref, s32[1]{0:T(128)} %bitcast.me_ref.refs_0_, ...), custom_call_target="tpu_custom_call" | custom-call | flops 1610612736 | bytes 8388608 | tf_op jit(solution)/shard_map/down/pallas_call | solution.py:591
  132.8 2.3 %down.3 = (bf16[128,4096]{1,0:T(8,128)(2,1)S(1)}, bf16[128,4096]{1,0:T(8,128)(2,1)S(1)}) custom-call(bf16[256,768]{1,0:T(8,128)(2,1)S(1)} %get-tuple-element.153.hidden_ref, bf16[768,4096]{1,0:T(8,128)(2,1)S(1)} %get-tuple-element.158.down_ref), custom_call_target="tpu_custom_call" | custom-call | flops 1610612736 | bytes 8388608 | tf_op jit(solution)/shard_map/down/pallas_call | solution.py:591
  135.7 1.8 %collective-permute-start.48 = (bf16[16,2048]{1,0:T(8,128)(2,1)S(1)}, bf16[16,2048]{1,0:T(8,128)(2,1)S(1)}, u32[]{:S(2)}, u32[]{:S(2)}) collective-permute-start(bf16[16,2048]{1,0:T(8,128)(2,1)S(1)} %add.28), channel_id=1, source_target_pairs={{4,0},{5,1},{8,4},{9,5},{12,8},{13,9},{14,12},{15,13},{10,14},{11,... | collective-permute-start | bytes 196616 | tf_op jit(solution)/shard_map/ppermute | solution.py:703
  138.0 1.8 %collective-permute-start.39 = (bf16[16,2048]{1,0:T(8,128)(2,1)S(1)}, bf16[16,2048]{1,0:T(8,128)(2,1)S(1)}, u32[]{:S(2)}, u32[]{:S(2)}) collective-permute-start(bf16[16,2048]{1,0:T(8,128)(2,1)S(1)} %add.20), channel_id=1, source_target_pairs={{4,0},{5,1},{8,4},{9,5},{12,8},{13,9},{14,12},{15,13},{10,14},{11,... | collective-permute-start | bytes 196616 | tf_op jit(solution)/shard_map/ppermute | solution.py:703
  140.2 1.8 %collective-permute-start.49 = (bf16[16,4096]{1,0:T(8,128)(2,1)S(1)}, bf16[16,4096]{1,0:T(8,128)(2,1)S(1)}, u32[]{:S(2)}, u32[]{:S(2)}) collective-permute-start(bf16[16,4096]{1,0:T(8,128)(2,1)S(1)} %add.29), channel_id=1, source_target_pairs={{4,0},{5,1},{8,4},{9,5},{12,8},{13,9},{14,12},{15,13},{10,14},{11,... | collective-permute-start | bytes 393224 | tf_op jit(solution)/shard_map/ppermute | solution.py:703
  142.5 1.8 %collective-permute-start.40 = (bf16[16,4096]{1,0:T(8,128)(2,1)S(1)}, bf16[16,4096]{1,0:T(8,128)(2,1)S(1)}, u32[]{:S(2)}, u32[]{:S(2)}) collective-permute-start(bf16[16,4096]{1,0:T(8,128)(2,1)S(1)} %add.21), channel_id=1, source_target_pairs={{4,0},{5,1},{8,4},{9,5},{12,8},{13,9},{14,12},{15,13},{10,14},{11,... | collective-permute-start | bytes 393224 | tf_op jit(solution)/shard_map/ppermute | solution.py:703
  146.4 2.1 %collective-permute-done.45.refs_0_ = bf16[16,4096]{1,0:T(8,128)(2,1)S(1)} collective-permute-done((bf16[16,4096]{1,0:T(8,128)(2,1)S(1)}, bf16[16,4096]{1,0:T(8,128)(2,1)S(1)}, u32[]{:S(2)}, u32[]{:S(2)}) %collective-permute-start.45) | collective-permute-done | bytes 131104 | tf_op jit(solution)/shard_map/ppermute | solution.py:702
  148.5 1.7 %collective-permute-start.50 = (bf16[16,4096]{1,0:T(8,128)(2,1)S(1)}, bf16[16,4096]{1,0:T(8,128)(2,1)S(1)}, u32[]{:S(2)}, u32[]{:S(2)}) collective-permute-start(bf16[16,4096]{1,0:T(8,128)(2,1)S(1)} %add.30), channel_id=1, source_target_pairs={{4,0},{5,1},{8,4},{9,5},{12,8},{13,9},{14,12},{15,13},{10,14},{11,... | collective-permute-start | bytes 393224 | tf_op jit(solution)/shard_map/ppermute | solution.py:703
  150.6 1.8 %collective-permute-start.41 = (bf16[16,4096]{1,0:T(8,128)(2,1)S(1)}, bf16[16,4096]{1,0:T(8,128)(2,1)S(1)}, u32[]{:S(2)}, u32[]{:S(2)}) collective-permute-start(bf16[16,4096]{1,0:T(8,128)(2,1)S(1)} %add.22), channel_id=1, source_target_pairs={{4,0},{5,1},{8,4},{9,5},{12,8},{13,9},{14,12},{15,13},{10,14},{11,... | collective-permute-start | bytes 393224 | tf_op jit(solution)/shard_map/ppermute | solution.py:703
  155.3 1.8 %collective-permute-start.51 = (bf16[16,4096]{1,0:T(8,128)(2,1)S(1)}, bf16[16,4096]{1,0:T(8,128)(2,1)S(1)}, u32[]{:S(2)}, u32[]{:S(2)}) collective-permute-start(bf16[16,4096]{1,0:T(8,128)(2,1)S(1)} %add.31), channel_id=1, source_target_pairs={{4,0},{5,1},{8,4},{9,5},{12,8},{13,9},{14,12},{15,13},{10,14},{11,... | collective-permute-start | bytes 393224 | tf_op jit(solution)/shard_map/ppermute | solution.py:703
  163.7 1.8 %collective-permute-done.38.refs_2_ = bf16[16,4096]{1,0:T(8,128)(2,1)S(1)} collective-permute-done((bf16[16,4096]{1,0:T(8,128)(2,1)S(1)}, bf16[16,4096]{1,0:T(8,128)(2,1)S(1)}, u32[]{:S(2)}, u32[]{:S(2)}) %collective-permute-start.38) | collective-permute-done | bytes 131104 | tf_op jit(solution)/shard_map/ppermute | solution.py:702
  (120 shorter events, 46.7 us)
Async XLA Ops:
  3.1 10.0 %collective-permute-start.1 = (bf16[256,512]{1,0:T(8,128)(2,1)S(1)}, bf16[256,512]{1,0:T(8,128)(2,1)S(1)}, u32[]{:S(2)}, u32[]{:S(2)}) collective-permute-start(bf16[256,512]{1,0:T(8,128)(2,1)S(1)} %get-tuple-element.85.own_ref.refs_9_), channel_id=1, source_target_pairs={{0,4},{1,5},{4,8},{5,9},{8,12},{9,13},{12,14},{13,15},{14,10},{15,... | collective-permute-start | bytes 786440 | tf_op jit(solution)/shard_map/ppermute | solution.py:702
  6.1 9.2 %collective-permute-start.2 = (bf16[256,512]{1,0:T(8,128)(2,1)S(1)}, bf16[256,512]{1,0:T(8,128)(2,1)S(1)}, u32[]{:S(2)}, u32[]{:S(2)}) collective-permute-start(bf16[256,512]{1,0:T(8,128)(2,1)S(1)} %get-tuple-element.85.own_ref.refs_9_), channel_id=1, source_target_pairs={{4,0},{5,1},{8,4},{9,5},{12,8},{13,9},{14,12},{15,13},{10,14},{11,... | collective-permute-start | bytes 786440 | tf_op jit(solution)/shard_map/ppermute | solution.py:703
  6.1 12.3 %collective-permute-start.6 = (bf16[256,512]{1,0:T(8,128)(2,1)S(1)}, bf16[256,512]{1,0:T(8,128)(2,1)S(1)}, u32[]{:S(2)}, u32[]{:S(2)}) collective-permute-start(bf16[256,512]{1,0:T(8,128)(2,1)S(1)} %get-tuple-element.86), channel_id=1, source_target_pairs={{0,5},{1,4},{4,9},{5,8},{8,13},{9,12},{12,15},{13,14},{14,11},{15,... | collective-permute-start | bytes 786440 | tf_op jit(solution)/shard_map/ppermute | solution.py:727
  7.3 11.3 %collective-permute-start.7 = (bf16[256,512]{1,0:T(8,128)(2,1)S(1)}, bf16[256,512]{1,0:T(8,128)(2,1)S(1)}, u32[]{:S(2)}, u32[]{:S(2)}) collective-permute-start(bf16[256,512]{1,0:T(8,128)(2,1)S(1)} %get-tuple-element.86), channel_id=1, source_target_pairs={{4,1},{5,0},{8,5},{9,4},{12,9},{13,8},{14,13},{15,12},{10,15},{11,... | collective-permute-start | bytes 786440 | tf_op jit(solution)/shard_map/ppermute | solution.py:727
  15.3 8.7 %collective-permute-start.4 = (bf16[256,512]{1,0:T(8,128)(2,1)S(1)}, bf16[256,512]{1,0:T(8,128)(2,1)S(1)}, u32[]{:S(2)}, u32[]{:S(2)}) collective-permute-start(bf16[256,512]{1,0:T(8,128)(2,1)S(1)} %collective-permute-done.1.refs_0_.refs_11_), channel_id=1, source_target_pairs={{0,4},{1,5},{4,8},{5,9},{8,12},{9,13},{12,14},{13,15},{14,10},{15,... | collective-permute-start | bytes 786440 | tf_op jit(solution)/shard_map/ppermute | solution.py:702
  16.9 8.8 %collective-permute-start.5 = (bf16[256,512]{1,0:T(8,128)(2,1)S(1)}, bf16[256,512]{1,0:T(8,128)(2,1)S(1)}, u32[]{:S(2)}, u32[]{:S(2)}) collective-permute-start(bf16[256,512]{1,0:T(8,128)(2,1)S(1)} %collective-permute-done.2.refs_2_.refs_13_), channel_id=1, source_target_pairs={{4,0},{5,1},{8,4},{9,5},{12,8},{13,9},{14,12},{15,13},{10,14},{11,... | collective-permute-start | bytes 786440 | tf_op jit(solution)/shard_map/ppermute | solution.py:703
  18.5 11.0 %collective-permute-start.10 = (bf16[256,512]{1,0:T(8,128)(2,1)S(1)}, bf16[256,512]{1,0:T(8,128)(2,1)S(1)}, u32[]{:S(2)}, u32[]{:S(2)}) collective-permute-start(bf16[256,512]{1,0:T(8,128)(2,1)S(1)} %collective-permute-done.6.refs_1_.refs_12_), channel_id=1, source_target_pairs={{0,4},{1,5},{4,8},{5,9},{8,12},{9,13},{12,14},{13,15},{14,10},{15,... | collective-permute-start | bytes 786440 | tf_op jit(solution)/shard_map/ppermute | solution.py:702
  20.5 10.5 %collective-permute-start.11 = (bf16[256,512]{1,0:T(8,128)(2,1)S(1)}, bf16[256,512]{1,0:T(8,128)(2,1)S(1)}, u32[]{:S(2)}, u32[]{:S(2)}) collective-permute-start(bf16[256,512]{1,0:T(8,128)(2,1)S(1)} %collective-permute-done.7.refs_3_.refs_14_), channel_id=1, source_target_pairs={{4,0},{5,1},{8,4},{9,5},{12,8},{13,9},{14,12},{15,13},{10,14},{11,... | collective-permute-start | bytes 786440 | tf_op jit(solution)/shard_map/ppermute | solution.py:703
  25.7 9.5 %collective-permute-start.8 = (bf16[256,512]{1,0:T(8,128)(2,1)S(1)}, bf16[256,512]{1,0:T(8,128)(2,1)S(1)}, u32[]{:S(2)}, u32[]{:S(2)}) collective-permute-start(bf16[256,512]{1,0:T(8,128)(2,1)S(1)} %collective-permute-done.4.refs_0_.refs_15_), channel_id=1, source_target_pairs={{0,4},{1,5},{4,8},{5,9},{8,12},{9,13},{12,14},{13,15},{14,10},{15,... | collective-permute-start | bytes 786440 | tf_op jit(solution)/shard_map/ppermute | solution.py:702
  28.1 8.8 %collective-permute-start.9 = (bf16[256,512]{1,0:T(8,128)(2,1)S(1)}, bf16[256,512]{1,0:T(8,128)(2,1)S(1)}, u32[]{:S(2)}, u32[]{:S(2)}) collective-permute-start(bf16[256,512]{1,0:T(8,128)(2,1)S(1)} %collective-permute-done.5.refs_2_.refs_17_), channel_id=1, source_target_pairs={{4,0},{5,1},{8,4},{9,5},{12,8},{13,9},{14,12},{15,13},{10,14},{11,... | collective-permute-start | bytes 786440 | tf_op jit(solution)/shard_map/ppermute | solution.py:703
  31.0 9.8 %collective-permute-start.13 = (bf16[256,512]{1,0:T(8,128)(2,1)S(1)}, bf16[256,512]{1,0:T(8,128)(2,1)S(1)}, u32[]{:S(2)}, u32[]{:S(2)}) collective-permute-start(bf16[256,512]{1,0:T(8,128)(2,1)S(1)} %collective-permute-done.10.refs_1_.refs_16_), channel_id=1, source_target_pairs={{0,4},{1,5},{4,8},{5,9},{8,12},{9,13},{12,14},{13,15},{14,10},{15,... | collective-permute-start | bytes 786440 | tf_op jit(solution)/shard_map/ppermute | solution.py:702
  32.6 10.0 %collective-permute-start.14 = (bf16[256,512]{1,0:T(8,128)(2,1)S(1)}, bf16[256,512]{1,0:T(8,128)(2,1)S(1)}, u32[]{:S(2)}, u32[]{:S(2)}) collective-permute-start(bf16[256,512]{1,0:T(8,128)(2,1)S(1)} %collective-permute-done.11.refs_3_.refs_18_), channel_id=1, source_target_pairs={{4,0},{5,1},{8,4},{9,5},{12,8},{13,9},{14,12},{15,13},{10,14},{11,... | collective-permute-start | bytes 786440 | tf_op jit(solution)/shard_map/ppermute | solution.py:703
  36.9 12.9 %collective-permute-start.12 = (bf16[256,512]{1,0:T(8,128)(2,1)S(1)}, bf16[256,512]{1,0:T(8,128)(2,1)S(1)}, u32[]{:S(2)}, u32[]{:S(2)}) collective-permute-start(bf16[256,512]{1,0:T(8,128)(2,1)S(1)} %collective-permute-done.8.refs_0_.refs_19_), channel_id=1, source_target_pairs={{0,4},{1,5},{4,8},{5,9},{8,12},{9,13},{12,14},{13,15},{14,10},{15,... | collective-permute-start | bytes 786440 | tf_op jit(solution)/shard_map/ppermute | solution.py:702
  42.5 6.6 %collective-permute-start.15 = (bf16[128,512]{1,0:T(8,128)(2,1)S(1)}, bf16[128,512]{1,0:T(8,128)(2,1)S(1)}, u32[]{:S(2)}, u32[]{:S(2)}) collective-permute-start(bf16[128,512]{1,0:T(8,128)(2,1)S(1)} %slice.6), channel_id=1, source_target_pairs={{0,4},{1,5},{4,8},{5,9},{8,12},{9,13},{12,14},{13,15},{14,10},{15,... | collective-permute-start | bytes 393224 | tf_op jit(solution)/shard_map/ppermute | solution.py:702
  55.6 6.5 %collective-permute-start.20 = (bf16[16,4224]{1,0:T(8,128)(2,1)S(1)}, bf16[16,4224]{1,0:T(8,128)(2,1)S(1)}, u32[]{:S(2)}, u32[]{:S(2)}) collective-permute-start(bf16[16,4224]{1,0:T(8,128)(2,1)S(1)} %get-tuple-element.126.refs_1_), channel_id=1, source_target_pairs={{0,4},{1,5},{4,8},{5,9},{8,12},{9,13},{12,14},{13,15},{14,10},{15,... | collective-permute-start | bytes 405512 | tf_op jit(solution)/shard_map/ppermute | solution.py:702
  56.6 7.1 %collective-permute-start.21 = (bf16[16,4224]{1,0:T(8,128)(2,1)S(1)}, bf16[16,4224]{1,0:T(8,128)(2,1)S(1)}, u32[]{:S(2)}, u32[]{:S(2)}) collective-permute-start(bf16[16,4224]{1,0:T(8,128)(2,1)S(1)} %get-tuple-element.125.refs_0_), channel_id=1, source_target_pairs={{0,4},{1,5},{4,8},{5,9},{8,12},{9,13},{12,14},{13,15},{14,10},{15,... | collective-permute-start | bytes 405512 | tf_op jit(solution)/shard_map/ppermute | solution.py:702
  58.4 43.3 %collective-permute-start.22 = (bf16[16,4224]{1,0:T(8,128)(2,1)S(1)}, bf16[16,4224]{1,0:T(8,128)(2,1)S(1)}, u32[]{:S(2)}, u32[]{:S(2)}) collective-permute-start(bf16[16,4224]{1,0:T(8,128)(2,1)S(1)} %get-tuple-element.126.refs_1_), channel_id=1, source_target_pairs={{4,0},{5,1},{8,4},{9,5},{12,8},{13,9},{14,12},{15,13},{10,14},{11,... | collective-permute-start | bytes 405512 | tf_op jit(solution)/shard_map/ppermute | solution.py:703
  59.6 42.1 %collective-permute-start.19 = (bf16[16,4224]{1,0:T(8,128)(2,1)S(1)}, bf16[16,4224]{1,0:T(8,128)(2,1)S(1)}, u32[]{:S(2)}, u32[]{:S(2)}) collective-permute-start(bf16[16,4224]{1,0:T(8,128)(2,1)S(1)} %collective-permute-done.18.refs_0_), channel_id=1, source_target_pairs={{4,0},{5,1},{8,4},{9,5},{12,8},{13,9},{14,12},{15,13},{10,14},{11,... | collective-permute-start | bytes 405512 | tf_op jit(solution)/shard_map/ppermute | solution.py:703
  62.1 46.7 %collective-permute-start.24 = (bf16[16,4224]{1,0:T(8,128)(2,1)S(1)}, bf16[16,4224]{1,0:T(8,128)(2,1)S(1)}, u32[]{:S(2)}, u32[]{:S(2)}) collective-permute-start(bf16[16,4224]{1,0:T(8,128)(2,1)S(1)} %collective-permute-done.20.refs_1_), channel_id=1, source_target_pairs={{0,4},{1,5},{4,8},{5,9},{8,12},{9,13},{12,14},{13,15},{14,10},{15,... | collective-permute-start | bytes 405512 | tf_op jit(solution)/shard_map/ppermute | solution.py:702
  63.7 45.1 %collective-permute-start.25 = (bf16[16,4224]{1,0:T(8,128)(2,1)S(1)}, bf16[16,4224]{1,0:T(8,128)(2,1)S(1)}, u32[]{:S(2)}, u32[]{:S(2)}) collective-permute-start(bf16[16,4224]{1,0:T(8,128)(2,1)S(1)} %collective-permute-done.21.refs_2_), channel_id=1, source_target_pairs={{0,4},{1,5},{4,8},{5,9},{8,12},{9,13},{12,14},{13,15},{14,10},{15,... | collective-permute-start | bytes 405512 | tf_op jit(solution)/shard_map/ppermute | solution.py:702
  101.6 8.7 %collective-permute-start.26 = (bf16[16,4224]{1,0:T(8,128)(2,1)S(1)}, bf16[16,4224]{1,0:T(8,128)(2,1)S(1)}, u32[]{:S(2)}, u32[]{:S(2)}) collective-permute-start(bf16[16,4224]{1,0:T(8,128)(2,1)S(1)} %collective-permute-done.22.refs_3_), channel_id=1, source_target_pairs={{4,0},{5,1},{8,4},{9,5},{12,8},{13,9},{14,12},{15,13},{10,14},{11,... | collective-permute-start | bytes 405512 | tf_op jit(solution)/shard_map/ppermute | solution.py:703
  101.7 11.5 %collective-permute-start.23 = (bf16[16,4224]{1,0:T(8,128)(2,1)S(1)}, bf16[16,4224]{1,0:T(8,128)(2,1)S(1)}, u32[]{:S(2)}, u32[]{:S(2)}) collective-permute-start(bf16[16,4224]{1,0:T(8,128)(2,1)S(1)} %collective-permute-done.19.refs_0_), channel_id=1, source_target_pairs={{4,0},{5,1},{8,4},{9,5},{12,8},{13,9},{14,12},{15,13},{10,14},{11,... | collective-permute-start | bytes 405512 | tf_op jit(solution)/shard_map/ppermute | solution.py:703
  108.8 5.9 %collective-permute-start.27 = (bf16[16,4224]{1,0:T(8,128)(2,1)S(1)}, bf16[16,4224]{1,0:T(8,128)(2,1)S(1)}, u32[]{:S(2)}, u32[]{:S(2)}) collective-permute-start(bf16[16,4224]{1,0:T(8,128)(2,1)S(1)} %collective-permute-done.24.refs_1_), channel_id=1, source_target_pairs={{0,4},{1,5},{4,8},{5,9},{8,12},{9,13},{12,14},{13,15},{14,10},{15,... | collective-permute-start | bytes 405512 | tf_op jit(solution)/shard_map/ppermute | solution.py:702
  110.3 6.7 %collective-permute-start.29 = (bf16[16,4224]{1,0:T(8,128)(2,1)S(1)}, bf16[16,4224]{1,0:T(8,128)(2,1)S(1)}, u32[]{:S(2)}, u32[]{:S(2)}) collective-permute-start(bf16[16,4224]{1,0:T(8,128)(2,1)S(1)} %collective-permute-done.26.refs_3_), channel_id=1, source_target_pairs={{4,0},{5,1},{8,4},{9,5},{12,8},{13,9},{14,12},{15,13},{10,14},{11,... | collective-permute-start | bytes 405512 | tf_op jit(solution)/shard_map/ppermute | solution.py:703
  112.3 5.9 %collective-permute-start.28 = (bf16[16,4224]{1,0:T(8,128)(2,1)S(1)}, bf16[16,4224]{1,0:T(8,128)(2,1)S(1)}, u32[]{:S(2)}, u32[]{:S(2)}) collective-permute-start(bf16[16,4224]{1,0:T(8,128)(2,1)S(1)} %collective-permute-done.25.refs_2_), channel_id=1, source_target_pairs={{0,4},{1,5},{4,8},{5,9},{8,12},{9,13},{12,14},{13,15},{14,10},{15,... | collective-permute-start | bytes 405512 | tf_op jit(solution)/shard_map/ppermute | solution.py:702
  120.5 9.8 %collective-permute-start.33 = (bf16[128,4096]{1,0:T(8,128)(2,1)S(1)}, bf16[128,4096]{1,0:T(8,128)(2,1)S(1)}, u32[]{:S(2)}, u32[]{:S(2)}) collective-permute-start(bf16[128,4096]{1,0:T(8,128)(2,1)S(1)} %get-tuple-element.156), channel_id=1, source_target_pairs={{0,1},{1,0},{2,3},{3,2},{4,5},{5,4},{6,7},{7,6},{8,9},{9,8},{10,11... | collective-permute-start | bytes 3145736 | tf_op jit(solution)/shard_map/ppermute | solution.py:704
  140.2 6.1 %collective-permute-start.49 = (bf16[16,4096]{1,0:T(8,128)(2,1)S(1)}, bf16[16,4096]{1,0:T(8,128)(2,1)S(1)}, u32[]{:S(2)}, u32[]{:S(2)}) collective-permute-start(bf16[16,4096]{1,0:T(8,128)(2,1)S(1)} %add.29), channel_id=1, source_target_pairs={{4,0},{5,1},{8,4},{9,5},{12,8},{13,9},{14,12},{15,13},{10,14},{11,... | collective-permute-start | bytes 393224 | tf_op jit(solution)/shard_map/ppermute | solution.py:703
  142.1 6.4 %collective-permute-start.45 = (bf16[16,4096]{1,0:T(8,128)(2,1)S(1)}, bf16[16,4096]{1,0:T(8,128)(2,1)S(1)}, u32[]{:S(2)}, u32[]{:S(2)}) collective-permute-start(bf16[16,4096]{1,0:T(8,128)(2,1)S(1)} %add.25), channel_id=1, source_target_pairs={{0,4},{1,5},{4,8},{5,9},{8,12},{9,13},{12,14},{13,15},{14,10},{15,... | collective-permute-start | bytes 393224 | tf_op jit(solution)/shard_map/ppermute | solution.py:702
  142.5 8.1 %collective-permute-start.40 = (bf16[16,4096]{1,0:T(8,128)(2,1)S(1)}, bf16[16,4096]{1,0:T(8,128)(2,1)S(1)}, u32[]{:S(2)}, u32[]{:S(2)}) collective-permute-start(bf16[16,4096]{1,0:T(8,128)(2,1)S(1)} %add.21), channel_id=1, source_target_pairs={{4,0},{5,1},{8,4},{9,5},{12,8},{13,9},{14,12},{15,13},{10,14},{11,... | collective-permute-start | bytes 393224 | tf_op jit(solution)/shard_map/ppermute | solution.py:703
  144.3 8.1 %collective-permute-start.36 = (bf16[16,4096]{1,0:T(8,128)(2,1)S(1)}, bf16[16,4096]{1,0:T(8,128)(2,1)S(1)}, u32[]{:S(2)}, u32[]{:S(2)}) collective-permute-start(bf16[16,4096]{1,0:T(8,128)(2,1)S(1)} %add.17), channel_id=1, source_target_pairs={{0,4},{1,5},{4,8},{5,9},{8,12},{9,13},{12,14},{13,15},{14,10},{15,... | collective-permute-start | bytes 393224 | tf_op jit(solution)/shard_map/ppermute | solution.py:702
  150.6 6.5 %collective-permute-start.41 = (bf16[16,4096]{1,0:T(8,128)(2,1)S(1)}, bf16[16,4096]{1,0:T(8,128)(2,1)S(1)}, u32[]{:S(2)}, u32[]{:S(2)}) collective-permute-start(bf16[16,4096]{1,0:T(8,128)(2,1)S(1)} %add.22), channel_id=1, source_target_pairs={{4,0},{5,1},{8,4},{9,5},{12,8},{13,9},{14,12},{15,13},{10,14},{11,... | collective-permute-start | bytes 393224 | tf_op jit(solution)/shard_map/ppermute | solution.py:703
  152.5 6.2 %collective-permute-start.37 = (bf16[16,4096]{1,0:T(8,128)(2,1)S(1)}, bf16[16,4096]{1,0:T(8,128)(2,1)S(1)}, u32[]{:S(2)}, u32[]{:S(2)}) collective-permute-start(bf16[16,4096]{1,0:T(8,128)(2,1)S(1)} %add.18), channel_id=1, source_target_pairs={{0,4},{1,5},{4,8},{5,9},{8,12},{9,13},{12,14},{13,15},{14,10},{15,... | collective-permute-start | bytes 393224 | tf_op jit(solution)/shard_map/ppermute | solution.py:702
  (23 other events, 116.1 us)

commit v10 on v9

--- a/solution.py
+++ b/solution.py
@@ -93,12 +93,12 @@
     return [ref[:, columns] for ref in queries]
 
 
-def for_groups(body):
+def for_groups(body, first=0, stop=HK // 2):
     def step(group, carry):
         body(group, pl.ds(pl.multiple_of(group * DH, DH), DH))
         return carry
 
-    lax.fori_loop(0, HK // 2, step, 0)
+    lax.fori_loop(first, stop, step, 0)
 
 
 def fold(queries, first, keys, values, shift):
@@ -165,7 +165,7 @@
     return copies
 
 
-def step_kernel(chips, places, loads, me_ref, q_ref, sib_q_ref, *refs):
+def step_kernel(chips, places, groups, loads, me_ref, q_ref, sib_q_ref, *refs):
     count = len(places)
     blocks, shift_ref = refs[:count], refs[count]
     refs = refs[count + 3 :]
@@ -184,7 +184,7 @@
                 acc_ref[group, rows, :] += update[:, :DH]
                 total_ref[group, rows, :] += update[:, DH:]
 
-        for_groups(one_group)
+        for_groups(one_group, *groups)
 
     for copy in copies:
         copy.wait()
@@ -356,10 +356,10 @@
         )
         return list(results[:2]), results[2], results[3:]
 
-    def step(self, blocks, places, shift, state, weights=()):
+    def step(self, blocks, places, groups, shift, state, weights=()):
         count, loads = len(blocks), len(weights)
         results = self.call(
-            functools.partial(step_kernel, self.chips, places, loads),
+            functools.partial(step_kernel, self.chips, places, groups, loads),
             "attend_step",
             (*blocks, shift, *state),
             [in_hbm(x) for x in weights],
@@ -732,17 +732,21 @@
     attention = Attention(me, (q_own, q_sib), chips)
     state, shift, _ = attention.own(own, sib)
     sources = [own, sib]
+    middle, late = HK // 4, None
     for step in range(1, half):
         *chains[0], state = lax.optimization_barrier((*chains[0], state))
+        if late is not None:
+            state, _ = attention.step(*late, (middle, HK // 2), shift, state)
         chains[1], _, state = lax.optimization_barrier((chains[1], chains[0], state))
-        blocks = [chain[side] for side in range(2) for chain in chains]
-        sources += blocks
+        late = [chain[side] for side in range(2) for chain in chains], [step, step, -step, -step]
+        sources += late[0]
         if step < half - 1:
             chains = [(go_right(chain[0]), go_left(chain[1])) for chain in chains]
         else:
             far_sib = go_right(chains[1][0][:tokens]), go_left(chains[1][1][tokens:])
             opposite = [go_right(chains[0][0]), *far_sib]
-        state, _ = attention.step(blocks, [step, step, -step, -step], shift, state)
+        state, _ = attention.step(*late, (0, middle), shift, state)
+    state, _ = attention.step(*late, (middle, HK // 2), shift, state)
     opposite, state = lax.optimization_barrier((opposite, state))
     sources += opposite
     mine, theirs, *picked, gate, up = attention.last(

time: 167 us -> 167 us (level)
    ppermute x22, starting transfers between devices: 60.1 us -> 62.6 us  [per_device(): go_right = lambda x: lax.ppermute(x, 'ctx', right)]
    ppermute x21, starting transfers between devices: 29.4 us -> 27.2 us  [per_device(): go_left = lambda x: lax.ppermute(x, 'ctx', left)]
    pallas_call x5 -> x8, Pallas kernels: 8.57 us -> 8.86 us  [call(): pl.pallas_call(kernel, in_specs=[pl.BlockSpec(memory_space=pltpu.SMEM)] +...]
  transfers between devices with their start and end apart: 52 -> 52, of which waited for: 32 -> 32; matrix products, arithmetic and copies ran while one was open for 0% -> 0% of each run, Pallas kernels for 10% -> 11%
where the time goes in v10:
time: 167 us
  starting transfers between devices  93.8 us (56%)
  waiting for transfers between devices  43.5 us (26%)
  Pallas kernels  28 us (17%)
    ppermute x22, starting transfers between devices, per_device(): go_right = lambda x: lax.ppermute(x, 'ctx', right)  62.6 us
    ppermute x21, starting transfers between devices, per_device(): go_left = lambda x: lax.ppermute(x, 'ctx', left)  27.2 us
    ppermute x22, waiting for transfers between devices, per_device(): go_right = lambda x: lax.ppermute(x, 'ctx', right)  26.2 us
    ppermute x21, waiting for transfers between devices, per_device(): go_left = lambda x: lax.ppermute(x, 'ctx', left)  16.1 us
    pallas_call x8, Pallas kernels, call(): pl.pallas_call(kernel, in_specs=[pl.BlockSpec(memory_space=pltpu.SMEM)] +...  8.86 us
    pallas_call x2, Pallas kernels, down_call(): pl.pallas_call(down_kernel, in_specs=[vmem] * 2 + more, out_specs=[vmem]...  4.69 us
    pallas_call x1, Pallas kernels, hidden_calls(): pl.pallas_call(first_kernel, in_specs=[pl.BlockSpec(memory_space=pltpu.SM...  4.63 us
    pallas_call x1, Pallas kernels, hidden_calls(): pl.pallas_call(second_kernel, in_specs=[vmem] * 6 + [anywhere], out_specs...  4.63 us
  transfers between devices with their start and end apart: 52, of which 32 were waited for; matrix products, arithmetic and copies ran while one was open for 0% of the time, Pallas kernels for 11%

profile of v10, /device:TPU:0, one launch (start us, length us, event | category | flops | bytes accessed | tf_op | source)
XLA Modules:
  0.0 166.6 jit_solution(16321152254760555668)
XLA Ops:
  0.6 1.9 %halves.1 = (bf16[256,512]{1,0:T(8,128)(2,1)S(1)}, bf16[256,512]{1,0:T(8,128)(2,1)S(1)}, bf16[128,4096]{1,0:T(8,128)(2,1)S(1)}, bf16[128,4096]{1,0:T(8,128)(2,1)S(1)}) custom-call(s32[1]{0:T(128)} %bitcast.me_ref.refs_0_, bf16[128,1024]{1,0:T(8,128)(2,1)} %refs_0_.2, bf16[128,1024]{1,0:T(8,128)(2,1)} %refs_1_.2, bf16[128,8192]{1,0:T(8,128)(2,1)} %refs_2_.1), custom_call_target="tpu_custom_call" | custom-call | flops 1 | bytes 1 | tf_op jit(solution)/shard_map/halves/pallas_call | solution.py:426
  3.1 3.0 %collective-permute-start.1 = (bf16[256,512]{1,0:T(8,128)(2,1)S(1)}, bf16[256,512]{1,0:T(8,128)(2,1)S(1)}, u32[]{:S(2)}, u32[]{:S(2)}) collective-permute-start(bf16[256,512]{1,0:T(8,128)(2,1)S(1)} %get-tuple-element.91.own_ref.refs_9_), channel_id=1, source_target_pairs={{0,4},{1,5},{4,8},{5,9},{8,12},{9,13},{12,14},{13,15},{14,10},{15,... | collective-permute-start | bytes 786440 | tf_op jit(solution)/shard_map/ppermute | solution.py:702
  8.3 3.8 %attend_own.1 = (f32[4,2048,128]{2,1,0:T(8,128)S(1)}, f32[4,2048,128]{2,1,0:T(8,128)S(1)}, f32[4,2048,128]{2,1,0:T(8,128)S(1)}) custom-call(s32[1]{0:T(128)} %bitcast.me_ref.refs_0_, bf16[128,4096]{1,0:T(8,128)(2,1)S(1)} %get-tuple-element.89.q_ref, bf16[128,4096]{1,0:T(8,128)(2,1)S(1)} %collective-permute-done.sib_q_ref, ...), custom_call_target="tpu_custom_call" | custom-call | flops 1 | bytes 1 | tf_op jit(solution)/shard_map/attend_own/pallas_call | solution.py:332
  13.2 2.2 %collective-permute-done.2.refs_2_.refs_13_ = bf16[256,512]{1,0:T(8,128)(2,1)S(1)} collective-permute-done((bf16[256,512]{1,0:T(8,128)(2,1)S(1)}, bf16[256,512]{1,0:T(8,128)(2,1)S(1)}, u32[]{:S(2)}, u32[]{:S(2)}) %collective-permute-start.2) | collective-permute-done | bytes 262176 | tf_op jit(solution)/shard_map/ppermute | solution.py:703
  18.5 1.9 %collective-permute-start.10 = (bf16[256,512]{1,0:T(8,128)(2,1)S(1)}, bf16[256,512]{1,0:T(8,128)(2,1)S(1)}, u32[]{:S(2)}, u32[]{:S(2)}) collective-permute-start(bf16[256,512]{1,0:T(8,128)(2,1)S(1)} %collective-permute-done.6.refs_1_.refs_12_), channel_id=1, source_target_pairs={{0,4},{1,5},{4,8},{5,9},{8,12},{9,13},{12,14},{13,15},{14,10},{15,... | collective-permute-start | bytes 786440 | tf_op jit(solution)/shard_map/ppermute | solution.py:702
  20.6 3.4 %collective-permute-done.4.refs_0_.refs_15_ = bf16[256,512]{1,0:T(8,128)(2,1)S(1)} collective-permute-done((bf16[256,512]{1,0:T(8,128)(2,1)S(1)}, bf16[256,512]{1,0:T(8,128)(2,1)S(1)}, u32[]{:S(2)}, u32[]{:S(2)}) %collective-permute-start.4) | collective-permute-done | bytes 262176 | tf_op jit(solution)/shard_map/ppermute | solution.py:702
  24.0 1.7 %collective-permute-done.5.refs_2_.refs_17_ = bf16[256,512]{1,0:T(8,128)(2,1)S(1)} collective-permute-done((bf16[256,512]{1,0:T(8,128)(2,1)S(1)}, bf16[256,512]{1,0:T(8,128)(2,1)S(1)}, u32[]{:S(2)}, u32[]{:S(2)}) %collective-permute-start.5) | collective-permute-done | bytes 262176 | tf_op jit(solution)/shard_map/ppermute | solution.py:703
  27.8 1.8 %collective-permute-done.10.refs_1_.refs_16_ = bf16[256,512]{1,0:T(8,128)(2,1)S(1)} collective-permute-done((bf16[256,512]{1,0:T(8,128)(2,1)S(1)}, bf16[256,512]{1,0:T(8,128)(2,1)S(1)}, u32[]{:S(2)}, u32[]{:S(2)}) %collective-permute-start.10) | collective-permute-done | bytes 262176 | tf_op jit(solution)/shard_map/ppermute | solution.py:702
  29.6 1.7 %collective-permute-done.11.refs_3_.refs_18_ = bf16[256,512]{1,0:T(8,128)(2,1)S(1)} collective-permute-done((bf16[256,512]{1,0:T(8,128)(2,1)S(1)}, bf16[256,512]{1,0:T(8,128)(2,1)S(1)}, u32[]{:S(2)}, u32[]{:S(2)}) %collective-permute-start.11) | collective-permute-done | bytes 262176 | tf_op jit(solution)/shard_map/ppermute | solution.py:703
  33.4 1.8 %collective-permute-done.8.refs_0_.refs_19_ = bf16[256,512]{1,0:T(8,128)(2,1)S(1)} collective-permute-done((bf16[256,512]{1,0:T(8,128)(2,1)S(1)}, bf16[256,512]{1,0:T(8,128)(2,1)S(1)}, u32[]{:S(2)}, u32[]{:S(2)}) %collective-permute-start.8) | collective-permute-done | bytes 262176 | tf_op jit(solution)/shard_map/ppermute | solution.py:702
  35.2 1.7 %collective-permute-done.9.refs_2_.refs_21_ = bf16[256,512]{1,0:T(8,128)(2,1)S(1)} collective-permute-done((bf16[256,512]{1,0:T(8,128)(2,1)S(1)}, bf16[256,512]{1,0:T(8,128)(2,1)S(1)}, u32[]{:S(2)}, u32[]{:S(2)}) %collective-permute-start.9) | collective-permute-done | bytes 262176 | tf_op jit(solution)/shard_map/ppermute | solution.py:703
  38.7 2.1 %collective-permute-done.13.refs_1_.refs_20_ = bf16[256,512]{1,0:T(8,128)(2,1)S(1)} collective-permute-done((bf16[256,512]{1,0:T(8,128)(2,1)S(1)}, bf16[256,512]{1,0:T(8,128)(2,1)S(1)}, u32[]{:S(2)}, u32[]{:S(2)}) %collective-permute-start.13) | collective-permute-done | bytes 262176 | tf_op jit(solution)/shard_map/ppermute | solution.py:702
  44.7 4.4 %collective-permute-done.15.refs_1_.refs_24_ = bf16[128,512]{1,0:T(8,128)(2,1)S(1)} collective-permute-done((bf16[128,512]{1,0:T(8,128)(2,1)S(1)}, bf16[128,512]{1,0:T(8,128)(2,1)S(1)}, u32[]{:S(2)}, u32[]{:S(2)}) %collective-permute-start.15) | collective-permute-done | bytes 131104 | tf_op jit(solution)/shard_map/ppermute | solution.py:702
  49.1 4.7 %attend_last.1 = (bf16[128,4096]{1,0:T(8,128)(2,1)S(1)}, bf16[128,4096]{1,0:T(8,128)(2,1)S(1)}, bf16[16,4224]{1,0:T(8,128)(2,1)S(1)}, bf16[16,4224]{1,0:T(8,128)...) custom-call(s32[1]{0:T(128)} %bitcast.me_ref.refs_0_, ...), custom_call_target="tpu_custom_call" | custom-call | flops 1 | bytes 1 | tf_op jit(solution)/shard_map/attend_last/pallas_call | solution.py:332
  53.8 1.8 %collective-permute-start.18 = (bf16[16,4224]{1,0:T(8,128)(2,1)S(1)}, bf16[16,4224]{1,0:T(8,128)(2,1)S(1)}, u32[]{:S(2)}, u32[]{:S(2)}) collective-permute-start(bf16[16,4224]{1,0:T(8,128)(2,1)S(1)} %get-tuple-element.137.refs_0_), channel_id=1, source_target_pairs={{4,0},{5,1},{8,4},{9,5},{12,8},{13,9},{14,12},{15,13},{10,14},{11,... | collective-permute-start | bytes 405512 | tf_op jit(solution)/shard_map/ppermute | solution.py:703
  55.9 2.3 %collective-permute-start.21 = (bf16[16,4224]{1,0:T(8,128)(2,1)S(1)}, bf16[16,4224]{1,0:T(8,128)(2,1)S(1)}, u32[]{:S(2)}, u32[]{:S(2)}) collective-permute-start(bf16[16,4224]{1,0:T(8,128)(2,1)S(1)} %get-tuple-element.137.refs_0_), channel_id=1, source_target_pairs={{0,4},{1,5},{4,8},{5,9},{8,12},{9,13},{12,14},{13,15},{14,10},{15,... | collective-permute-start | bytes 405512 | tf_op jit(solution)/shard_map/ppermute | solution.py:702
  59.4 2.2 %collective-permute-start.19 = (bf16[16,4224]{1,0:T(8,128)(2,1)S(1)}, bf16[16,4224]{1,0:T(8,128)(2,1)S(1)}, u32[]{:S(2)}, u32[]{:S(2)}) collective-permute-start(bf16[16,4224]{1,0:T(8,128)(2,1)S(1)} %collective-permute-done.18.refs_0_), channel_id=1, source_target_pairs={{4,0},{5,1},{8,4},{9,5},{12,8},{13,9},{14,12},{15,13},{10,14},{11,... | collective-permute-start | bytes 405512 | tf_op jit(solution)/shard_map/ppermute | solution.py:703
  62.3 2.1 %collective-permute-done.21.refs_2_ = bf16[16,4224]{1,0:T(8,128)(2,1)S(1)} collective-permute-done((bf16[16,4224]{1,0:T(8,128)(2,1)S(1)}, bf16[16,4224]{1,0:T(8,128)(2,1)S(1)}, u32[]{:S(2)}, u32[]{:S(2)}) %collective-permute-start.21) | collective-permute-done | bytes 135200 | tf_op jit(solution)/shard_map/ppermute | solution.py:702
  64.5 37.6 %collective-permute-start.25 = (bf16[16,4224]{1,0:T(8,128)(2,1)S(1)}, bf16[16,4224]{1,0:T(8,128)(2,1)S(1)}, u32[]{:S(2)}, u32[]{:S(2)}) collective-permute-start(bf16[16,4224]{1,0:T(8,128)(2,1)S(1)} %collective-permute-done.21.refs_2_), channel_id=1, source_target_pairs={{0,4},{1,5},{4,8},{5,9},{8,12},{9,13},{12,14},{13,15},{14,10},{15,... | collective-permute-start | bytes 405512 | tf_op jit(solution)/shard_map/ppermute | solution.py:702
  102.1 7.1 %collective-permute-start.23 = (bf16[16,4224]{1,0:T(8,128)(2,1)S(1)}, bf16[16,4224]{1,0:T(8,128)(2,1)S(1)}, u32[]{:S(2)}, u32[]{:S(2)}) collective-permute-start(bf16[16,4224]{1,0:T(8,128)(2,1)S(1)} %collective-permute-done.19.refs_0_), channel_id=1, source_target_pairs={{4,0},{5,1},{8,4},{9,5},{12,8},{13,9},{14,12},{15,13},{10,14},{11,... | collective-permute-start | bytes 405512 | tf_op jit(solution)/shard_map/ppermute | solution.py:703
  109.9 3.0 %collective-permute-start.29 = (bf16[16,4224]{1,0:T(8,128)(2,1)S(1)}, bf16[16,4224]{1,0:T(8,128)(2,1)S(1)}, u32[]{:S(2)}, u32[]{:S(2)}) collective-permute-start(bf16[16,4224]{1,0:T(8,128)(2,1)S(1)} %collective-permute-done.26.refs_3_), channel_id=1, source_target_pairs={{4,0},{5,1},{8,4},{9,5},{12,8},{13,9},{14,12},{15,13},{10,14},{11,... | collective-permute-start | bytes 405512 | tf_op jit(solution)/shard_map/ppermute | solution.py:703
  116.8 1.8 %collective-permute-done.28.refs_2_ = bf16[16,4224]{1,0:T(8,128)(2,1)S(1)} collective-permute-done((bf16[16,4224]{1,0:T(8,128)(2,1)S(1)}, bf16[16,4224]{1,0:T(8,128)(2,1)S(1)}, u32[]{:S(2)}, u32[]{:S(2)}) %collective-permute-start.28) | collective-permute-done | bytes 135200 | tf_op jit(solution)/shard_map/ppermute | solution.py:702
  121.9 4.6 %hidden_first.1 = (f32[256,768]{1,0:T(8,128)S(1)}, f32[256,768]{1,0:T(8,128)S(1)}, bf16[4096,768]{1,0:T(8,128)(2,1)S(1)}, bf16[4096,768]{1,0:T(8,128)(2,1)S(1)}) custom-call(s32[1]{0:T(128)} %bitcast.me_ref.refs_0_, bf16[256,4224]{1,0:T(8,128)(2,1)S(1)} %place.7.rows_ref.own_ref, bf16[4096,768]{1,0:T(8,128)(2,1)S(1)} %get-tuple-element.159.gate_ref, ...), custom_call_target="tpu_custom_call" | custom-call | flops 3221225472 | bytes 12582912 | tf_op jit(solution)/shard_map/hidden_first/pallas_call | solution.py:529
  126.5 4.6 %hidden_second.1 = (bf16[256,768]{1,0:T(8,128)(2,1)S(1)}, bf16[768,4096]{1,0:T(8,128)(2,1)S(1)}, bf16[768,4096]{1,0:T(8,128)(2,1)S(1)}) custom-call(bf16[256,4224]{1,0:T(8,128)(2,1)S(1)} %collective-permute-done.32.rows_ref, bf16[4096,768]{1,0:T(8,128)(2,1)S(1)} %get-tuple-element.161.gate_ref, bf16[4096,768]{1,0:T(8,128)(2,1)S(1)} %get-tuple-element.162.up_ref, ...), custom_call_target="tpu_custom_call" | custom-call | flops 3221225472 | bytes 12582912 | tf_op jit(solution)/shard_map/hidden_second/pallas_call | solution.py:539
  131.2 2.4 %down.2 = (bf16[128,4096]{1,0:T(8,128)(2,1)S(1)}, bf16[128,4096]{1,0:T(8,128)(2,1)S(1)}, bf16[128,8192]{1,0:T(8,128)(2,1)}) custom-call(bf16[256,768]{1,0:T(8,128)(2,1)S(1)} %get-tuple-element.165.hidden_ref, bf16[768,4096]{1,0:T(8,128)(2,1)S(1)} %get-tuple-element.166.down_ref, s32[1]{0:T(128)} %bitcast.me_ref.refs_0_, ...), custom_call_target="tpu_custom_call" | custom-call | flops 1610612736 | bytes 8388608 | tf_op jit(solution)/shard_map/down/pallas_call | solution.py:591
  133.7 2.3 %down.3 = (bf16[128,4096]{1,0:T(8,128)(2,1)S(1)}, bf16[128,4096]{1,0:T(8,128)(2,1)S(1)}) custom-call(bf16[256,768]{1,0:T(8,128)(2,1)S(1)} %get-tuple-element.165.hidden_ref, bf16[768,4096]{1,0:T(8,128)(2,1)S(1)} %get-tuple-element.170.down_ref), custom_call_target="tpu_custom_call" | custom-call | flops 1610612736 | bytes 8388608 | tf_op jit(solution)/shard_map/down/pallas_call | solution.py:591
  148.2 1.7 %collective-permute-start.50 = (bf16[16,4096]{1,0:T(8,128)(2,1)S(1)}, bf16[16,4096]{1,0:T(8,128)(2,1)S(1)}, u32[]{:S(2)}, u32[]{:S(2)}) collective-permute-start(bf16[16,4096]{1,0:T(8,128)(2,1)S(1)} %add.30), channel_id=1, source_target_pairs={{4,0},{5,1},{8,4},{9,5},{12,8},{13,9},{14,12},{15,13},{10,14},{11,... | collective-permute-start | bytes 393224 | tf_op jit(solution)/shard_map/ppermute | solution.py:703
  150.4 1.8 %collective-permute-start.41 = (bf16[16,4096]{1,0:T(8,128)(2,1)S(1)}, bf16[16,4096]{1,0:T(8,128)(2,1)S(1)}, u32[]{:S(2)}, u32[]{:S(2)}) collective-permute-start(bf16[16,4096]{1,0:T(8,128)(2,1)S(1)} %add.22), channel_id=1, source_target_pairs={{4,0},{5,1},{8,4},{9,5},{12,8},{13,9},{14,12},{15,13},{10,14},{11,... | collective-permute-start | bytes 393224 | tf_op jit(solution)/shard_map/ppermute | solution.py:703
  152.6 1.8 %collective-permute-done.50.refs_0_ = bf16[16,4096]{1,0:T(8,128)(2,1)S(1)} collective-permute-done((bf16[16,4096]{1,0:T(8,128)(2,1)S(1)}, bf16[16,4096]{1,0:T(8,128)(2,1)S(1)}, u32[]{:S(2)}, u32[]{:S(2)}) %collective-permute-start.50) | collective-permute-done | bytes 131104 | tf_op jit(solution)/shard_map/ppermute | solution.py:703
  155.0 1.8 %collective-permute-start.51 = (bf16[16,4096]{1,0:T(8,128)(2,1)S(1)}, bf16[16,4096]{1,0:T(8,128)(2,1)S(1)}, u32[]{:S(2)}, u32[]{:S(2)}) collective-permute-start(bf16[16,4096]{1,0:T(8,128)(2,1)S(1)} %add.31), channel_id=1, source_target_pairs={{4,0},{5,1},{8,4},{9,5},{12,8},{13,9},{14,12},{15,13},{10,14},{11,... | collective-permute-start | bytes 393224 | tf_op jit(solution)/shard_map/ppermute | solution.py:703
  158.5 1.7 collective-permute-start.42
  163.5 1.7 %collective-permute-done.38.refs_2_ = bf16[16,4096]{1,0:T(8,128)(2,1)S(1)} collective-permute-done((bf16[16,4096]{1,0:T(8,128)(2,1)S(1)}, bf16[16,4096]{1,0:T(8,128)(2,1)S(1)}, u32[]{:S(2)}, u32[]{:S(2)}) %collective-permute-start.38) | collective-permute-done | bytes 131104 | tf_op jit(solution)/shard_map/ppermute | solution.py:702
  (123 shorter events, 47.1 us)
Async XLA Ops:
  3.1 10.0 %collective-permute-start.1 = (bf16[256,512]{1,0:T(8,128)(2,1)S(1)}, bf16[256,512]{1,0:T(8,128)(2,1)S(1)}, u32[]{:S(2)}, u32[]{:S(2)}) collective-permute-start(bf16[256,512]{1,0:T(8,128)(2,1)S(1)} %get-tuple-element.91.own_ref.refs_9_), channel_id=1, source_target_pairs={{0,4},{1,5},{4,8},{5,9},{8,12},{9,13},{12,14},{13,15},{14,10},{15,... | collective-permute-start | bytes 786440 | tf_op jit(solution)/shard_map/ppermute | solution.py:702
  6.1 9.2 %collective-permute-start.2 = (bf16[256,512]{1,0:T(8,128)(2,1)S(1)}, bf16[256,512]{1,0:T(8,128)(2,1)S(1)}, u32[]{:S(2)}, u32[]{:S(2)}) collective-permute-start(bf16[256,512]{1,0:T(8,128)(2,1)S(1)} %get-tuple-element.91.own_ref.refs_9_), channel_id=1, source_target_pairs={{4,0},{5,1},{8,4},{9,5},{12,8},{13,9},{14,12},{15,13},{10,14},{11,... | collective-permute-start | bytes 786440 | tf_op jit(solution)/shard_map/ppermute | solution.py:703
  6.1 12.3 %collective-permute-start.6 = (bf16[256,512]{1,0:T(8,128)(2,1)S(1)}, bf16[256,512]{1,0:T(8,128)(2,1)S(1)}, u32[]{:S(2)}, u32[]{:S(2)}) collective-permute-start(bf16[256,512]{1,0:T(8,128)(2,1)S(1)} %get-tuple-element.92), channel_id=1, source_target_pairs={{0,5},{1,4},{4,9},{5,8},{8,13},{9,12},{12,15},{13,14},{14,11},{15,... | collective-permute-start | bytes 786440 | tf_op jit(solution)/shard_map/ppermute | solution.py:727
  7.3 11.3 %collective-permute-start.7 = (bf16[256,512]{1,0:T(8,128)(2,1)S(1)}, bf16[256,512]{1,0:T(8,128)(2,1)S(1)}, u32[]{:S(2)}, u32[]{:S(2)}) collective-permute-start(bf16[256,512]{1,0:T(8,128)(2,1)S(1)} %get-tuple-element.92), channel_id=1, source_target_pairs={{4,1},{5,0},{8,5},{9,4},{12,9},{13,8},{14,13},{15,12},{10,15},{11,... | collective-permute-start | bytes 786440 | tf_op jit(solution)/shard_map/ppermute | solution.py:727
  15.3 8.7 %collective-permute-start.4 = (bf16[256,512]{1,0:T(8,128)(2,1)S(1)}, bf16[256,512]{1,0:T(8,128)(2,1)S(1)}, u32[]{:S(2)}, u32[]{:S(2)}) collective-permute-start(bf16[256,512]{1,0:T(8,128)(2,1)S(1)} %collective-permute-done.1.refs_0_.refs_11_), channel_id=1, source_target_pairs={{0,4},{1,5},{4,8},{5,9},{8,12},{9,13},{12,14},{13,15},{14,10},{15,... | collective-permute-start | bytes 786440 | tf_op jit(solution)/shard_map/ppermute | solution.py:702
  16.9 8.8 %collective-permute-start.5 = (bf16[256,512]{1,0:T(8,128)(2,1)S(1)}, bf16[256,512]{1,0:T(8,128)(2,1)S(1)}, u32[]{:S(2)}, u32[]{:S(2)}) collective-permute-start(bf16[256,512]{1,0:T(8,128)(2,1)S(1)} %collective-permute-done.2.refs_2_.refs_13_), channel_id=1, source_target_pairs={{4,0},{5,1},{8,4},{9,5},{12,8},{13,9},{14,12},{15,13},{10,14},{11,... | collective-permute-start | bytes 786440 | tf_op jit(solution)/shard_map/ppermute | solution.py:703
  18.5 11.0 %collective-permute-start.10 = (bf16[256,512]{1,0:T(8,128)(2,1)S(1)}, bf16[256,512]{1,0:T(8,128)(2,1)S(1)}, u32[]{:S(2)}, u32[]{:S(2)}) collective-permute-start(bf16[256,512]{1,0:T(8,128)(2,1)S(1)} %collective-permute-done.6.refs_1_.refs_12_), channel_id=1, source_target_pairs={{0,4},{1,5},{4,8},{5,9},{8,12},{9,13},{12,14},{13,15},{14,10},{15,... | collective-permute-start | bytes 786440 | tf_op jit(solution)/shard_map/ppermute | solution.py:702
  20.5 10.8 %collective-permute-start.11 = (bf16[256,512]{1,0:T(8,128)(2,1)S(1)}, bf16[256,512]{1,0:T(8,128)(2,1)S(1)}, u32[]{:S(2)}, u32[]{:S(2)}) collective-permute-start(bf16[256,512]{1,0:T(8,128)(2,1)S(1)} %collective-permute-done.7.refs_3_.refs_14_), channel_id=1, source_target_pairs={{4,0},{5,1},{8,4},{9,5},{12,8},{13,9},{14,12},{15,13},{10,14},{11,... | collective-permute-start | bytes 786440 | tf_op jit(solution)/shard_map/ppermute | solution.py:703
  25.7 9.5 %collective-permute-start.8 = (bf16[256,512]{1,0:T(8,128)(2,1)S(1)}, bf16[256,512]{1,0:T(8,128)(2,1)S(1)}, u32[]{:S(2)}, u32[]{:S(2)}) collective-permute-start(bf16[256,512]{1,0:T(8,128)(2,1)S(1)} %collective-permute-done.4.refs_0_.refs_15_), channel_id=1, source_target_pairs={{0,4},{1,5},{4,8},{5,9},{8,12},{9,13},{12,14},{13,15},{14,10},{15,... | collective-permute-start | bytes 786440 | tf_op jit(solution)/shard_map/ppermute | solution.py:702
  27.3 9.7 %collective-permute-start.9 = (bf16[256,512]{1,0:T(8,128)(2,1)S(1)}, bf16[256,512]{1,0:T(8,128)(2,1)S(1)}, u32[]{:S(2)}, u32[]{:S(2)}) collective-permute-start(bf16[256,512]{1,0:T(8,128)(2,1)S(1)} %collective-permute-done.5.refs_2_.refs_17_), channel_id=1, source_target_pairs={{4,0},{5,1},{8,4},{9,5},{12,8},{13,9},{14,12},{15,13},{10,14},{11,... | collective-permute-start | bytes 786440 | tf_op jit(solution)/shard_map/ppermute | solution.py:703
  31.3 9.5 %collective-permute-start.13 = (bf16[256,512]{1,0:T(8,128)(2,1)S(1)}, bf16[256,512]{1,0:T(8,128)(2,1)S(1)}, u32[]{:S(2)}, u32[]{:S(2)}) collective-permute-start(bf16[256,512]{1,0:T(8,128)(2,1)S(1)} %collective-permute-done.10.refs_1_.refs_16_), channel_id=1, source_target_pairs={{0,4},{1,5},{4,8},{5,9},{8,12},{9,13},{12,14},{13,15},{14,10},{15,... | collective-permute-start | bytes 786440 | tf_op jit(solution)/shard_map/ppermute | solution.py:702
  32.9 9.3 %collective-permute-start.14 = (bf16[256,512]{1,0:T(8,128)(2,1)S(1)}, bf16[256,512]{1,0:T(8,128)(2,1)S(1)}, u32[]{:S(2)}, u32[]{:S(2)}) collective-permute-start(bf16[256,512]{1,0:T(8,128)(2,1)S(1)} %collective-permute-done.11.refs_3_.refs_18_), channel_id=1, source_target_pairs={{4,0},{5,1},{8,4},{9,5},{12,8},{13,9},{14,12},{15,13},{10,14},{11,... | collective-permute-start | bytes 786440 | tf_op jit(solution)/shard_map/ppermute | solution.py:703
  36.9 12.2 %collective-permute-start.12 = (bf16[256,512]{1,0:T(8,128)(2,1)S(1)}, bf16[256,512]{1,0:T(8,128)(2,1)S(1)}, u32[]{:S(2)}, u32[]{:S(2)}) collective-permute-start(bf16[256,512]{1,0:T(8,128)(2,1)S(1)} %collective-permute-done.8.refs_0_.refs_19_), channel_id=1, source_target_pairs={{0,4},{1,5},{4,8},{5,9},{8,12},{9,13},{12,14},{13,15},{14,10},{15,... | collective-permute-start | bytes 786440 | tf_op jit(solution)/shard_map/ppermute | solution.py:702
  42.2 6.9 %collective-permute-start.15 = (bf16[128,512]{1,0:T(8,128)(2,1)S(1)}, bf16[128,512]{1,0:T(8,128)(2,1)S(1)}, u32[]{:S(2)}, u32[]{:S(2)}) collective-permute-start(bf16[128,512]{1,0:T(8,128)(2,1)S(1)} %slice.6), channel_id=1, source_target_pairs={{0,4},{1,5},{4,8},{5,9},{8,12},{9,13},{12,14},{13,15},{14,10},{15,... | collective-permute-start | bytes 393224 | tf_op jit(solution)/shard_map/ppermute | solution.py:702
  55.6 6.4 %collective-permute-start.20 = (bf16[16,4224]{1,0:T(8,128)(2,1)S(1)}, bf16[16,4224]{1,0:T(8,128)(2,1)S(1)}, u32[]{:S(2)}, u32[]{:S(2)}) collective-permute-start(bf16[16,4224]{1,0:T(8,128)(2,1)S(1)} %get-tuple-element.138.refs_1_), channel_id=1, source_target_pairs={{0,4},{1,5},{4,8},{5,9},{8,12},{9,13},{12,14},{13,15},{14,10},{15,... | collective-permute-start | bytes 405512 | tf_op jit(solution)/shard_map/ppermute | solution.py:702
  55.9 8.5 %collective-permute-start.21 = (bf16[16,4224]{1,0:T(8,128)(2,1)S(1)}, bf16[16,4224]{1,0:T(8,128)(2,1)S(1)}, u32[]{:S(2)}, u32[]{:S(2)}) collective-permute-start(bf16[16,4224]{1,0:T(8,128)(2,1)S(1)} %get-tuple-element.137.refs_0_), channel_id=1, source_target_pairs={{0,4},{1,5},{4,8},{5,9},{8,12},{9,13},{12,14},{13,15},{14,10},{15,... | collective-permute-start | bytes 405512 | tf_op jit(solution)/shard_map/ppermute | solution.py:702
  58.2 43.9 %collective-permute-start.22 = (bf16[16,4224]{1,0:T(8,128)(2,1)S(1)}, bf16[16,4224]{1,0:T(8,128)(2,1)S(1)}, u32[]{:S(2)}, u32[]{:S(2)}) collective-permute-start(bf16[16,4224]{1,0:T(8,128)(2,1)S(1)} %get-tuple-element.138.refs_1_), channel_id=1, source_target_pairs={{4,0},{5,1},{8,4},{9,5},{12,8},{13,9},{14,12},{15,13},{10,14},{11,... | collective-permute-start | bytes 405512 | tf_op jit(solution)/shard_map/ppermute | solution.py:703
  59.4 42.7 %collective-permute-start.19 = (bf16[16,4224]{1,0:T(8,128)(2,1)S(1)}, bf16[16,4224]{1,0:T(8,128)(2,1)S(1)}, u32[]{:S(2)}, u32[]{:S(2)}) collective-permute-start(bf16[16,4224]{1,0:T(8,128)(2,1)S(1)} %collective-permute-done.18.refs_0_), channel_id=1, source_target_pairs={{4,0},{5,1},{8,4},{9,5},{12,8},{13,9},{14,12},{15,13},{10,14},{11,... | collective-permute-start | bytes 405512 | tf_op jit(solution)/shard_map/ppermute | solution.py:703
  62.0 47.2 %collective-permute-start.24 = (bf16[16,4224]{1,0:T(8,128)(2,1)S(1)}, bf16[16,4224]{1,0:T(8,128)(2,1)S(1)}, u32[]{:S(2)}, u32[]{:S(2)}) collective-permute-start(bf16[16,4224]{1,0:T(8,128)(2,1)S(1)} %collective-permute-done.20.refs_1_), channel_id=1, source_target_pairs={{0,4},{1,5},{4,8},{5,9},{8,12},{9,13},{12,14},{13,15},{14,10},{15,... | collective-permute-start | bytes 405512 | tf_op jit(solution)/shard_map/ppermute | solution.py:702
  64.5 44.7 %collective-permute-start.25 = (bf16[16,4224]{1,0:T(8,128)(2,1)S(1)}, bf16[16,4224]{1,0:T(8,128)(2,1)S(1)}, u32[]{:S(2)}, u32[]{:S(2)}) collective-permute-start(bf16[16,4224]{1,0:T(8,128)(2,1)S(1)} %collective-permute-done.21.refs_2_), channel_id=1, source_target_pairs={{0,4},{1,5},{4,8},{5,9},{8,12},{9,13},{12,14},{13,15},{14,10},{15,... | collective-permute-start | bytes 405512 | tf_op jit(solution)/shard_map/ppermute | solution.py:702
  102.1 7.9 %collective-permute-start.26 = (bf16[16,4224]{1,0:T(8,128)(2,1)S(1)}, bf16[16,4224]{1,0:T(8,128)(2,1)S(1)}, u32[]{:S(2)}, u32[]{:S(2)}) collective-permute-start(bf16[16,4224]{1,0:T(8,128)(2,1)S(1)} %collective-permute-done.22.refs_3_), channel_id=1, source_target_pairs={{4,0},{5,1},{8,4},{9,5},{12,8},{13,9},{14,12},{15,13},{10,14},{11,... | collective-permute-start | bytes 405512 | tf_op jit(solution)/shard_map/ppermute | solution.py:703
  102.1 10.8 %collective-permute-start.23 = (bf16[16,4224]{1,0:T(8,128)(2,1)S(1)}, bf16[16,4224]{1,0:T(8,128)(2,1)S(1)}, u32[]{:S(2)}, u32[]{:S(2)}) collective-permute-start(bf16[16,4224]{1,0:T(8,128)(2,1)S(1)} %collective-permute-done.19.refs_0_), channel_id=1, source_target_pairs={{4,0},{5,1},{8,4},{9,5},{12,8},{13,9},{14,12},{15,13},{10,14},{11,... | collective-permute-start | bytes 405512 | tf_op jit(solution)/shard_map/ppermute | solution.py:703
  109.9 6.9 %collective-permute-start.29 = (bf16[16,4224]{1,0:T(8,128)(2,1)S(1)}, bf16[16,4224]{1,0:T(8,128)(2,1)S(1)}, u32[]{:S(2)}, u32[]{:S(2)}) collective-permute-start(bf16[16,4224]{1,0:T(8,128)(2,1)S(1)} %collective-permute-done.26.refs_3_), channel_id=1, source_target_pairs={{4,0},{5,1},{8,4},{9,5},{12,8},{13,9},{14,12},{15,13},{10,14},{11,... | collective-permute-start | bytes 405512 | tf_op jit(solution)/shard_map/ppermute | solution.py:703
  121.4 9.8 %collective-permute-start.33 = (bf16[128,4096]{1,0:T(8,128)(2,1)S(1)}, bf16[128,4096]{1,0:T(8,128)(2,1)S(1)}, u32[]{:S(2)}, u32[]{:S(2)}) collective-permute-start(bf16[128,4096]{1,0:T(8,128)(2,1)S(1)} %get-tuple-element.168), channel_id=1, source_target_pairs={{0,1},{1,0},{2,3},{3,2},{4,5},{5,4},{6,7},{7,6},{8,9},{9,8},{10,11... | collective-permute-start | bytes 3145736 | tf_op jit(solution)/shard_map/ppermute | solution.py:704
  141.0 6.0 %collective-permute-start.49 = (bf16[16,4096]{1,0:T(8,128)(2,1)S(1)}, bf16[16,4096]{1,0:T(8,128)(2,1)S(1)}, u32[]{:S(2)}, u32[]{:S(2)}) collective-permute-start(bf16[16,4096]{1,0:T(8,128)(2,1)S(1)} %add.29), channel_id=1, source_target_pairs={{4,0},{5,1},{8,4},{9,5},{12,8},{13,9},{14,12},{15,13},{10,14},{11,... | collective-permute-start | bytes 393224 | tf_op jit(solution)/shard_map/ppermute | solution.py:703
  141.9 6.3 %collective-permute-start.45 = (bf16[16,4096]{1,0:T(8,128)(2,1)S(1)}, bf16[16,4096]{1,0:T(8,128)(2,1)S(1)}, u32[]{:S(2)}, u32[]{:S(2)}) collective-permute-start(bf16[16,4096]{1,0:T(8,128)(2,1)S(1)} %add.25), channel_id=1, source_target_pairs={{0,4},{1,5},{4,8},{5,9},{8,12},{9,13},{12,14},{13,15},{14,10},{15,... | collective-permute-start | bytes 393224 | tf_op jit(solution)/shard_map/ppermute | solution.py:702
  143.6 6.8 %collective-permute-start.40 = (bf16[16,4096]{1,0:T(8,128)(2,1)S(1)}, bf16[16,4096]{1,0:T(8,128)(2,1)S(1)}, u32[]{:S(2)}, u32[]{:S(2)}) collective-permute-start(bf16[16,4096]{1,0:T(8,128)(2,1)S(1)} %add.21), channel_id=1, source_target_pairs={{4,0},{5,1},{8,4},{9,5},{12,8},{13,9},{14,12},{15,13},{10,14},{11,... | collective-permute-start | bytes 393224 | tf_op jit(solution)/shard_map/ppermute | solution.py:703
  144.2 8.0 %collective-permute-start.36 = (bf16[16,4096]{1,0:T(8,128)(2,1)S(1)}, bf16[16,4096]{1,0:T(8,128)(2,1)S(1)}, u32[]{:S(2)}, u32[]{:S(2)}) collective-permute-start(bf16[16,4096]{1,0:T(8,128)(2,1)S(1)} %add.17), channel_id=1, source_target_pairs={{0,4},{1,5},{4,8},{5,9},{8,12},{9,13},{12,14},{13,15},{14,10},{15,... | collective-permute-start | bytes 393224 | tf_op jit(solution)/shard_map/ppermute | solution.py:702
  148.2 6.2 %collective-permute-start.50 = (bf16[16,4096]{1,0:T(8,128)(2,1)S(1)}, bf16[16,4096]{1,0:T(8,128)(2,1)S(1)}, u32[]{:S(2)}, u32[]{:S(2)}) collective-permute-start(bf16[16,4096]{1,0:T(8,128)(2,1)S(1)} %add.30), channel_id=1, source_target_pairs={{4,0},{5,1},{8,4},{9,5},{12,8},{13,9},{14,12},{15,13},{10,14},{11,... | collective-permute-start | bytes 393224 | tf_op jit(solution)/shard_map/ppermute | solution.py:703
  150.4 6.5 %collective-permute-start.41 = (bf16[16,4096]{1,0:T(8,128)(2,1)S(1)}, bf16[16,4096]{1,0:T(8,128)(2,1)S(1)}, u32[]{:S(2)}, u32[]{:S(2)}) collective-permute-start(bf16[16,4096]{1,0:T(8,128)(2,1)S(1)} %add.22), channel_id=1, source_target_pairs={{4,0},{5,1},{8,4},{9,5},{12,8},{13,9},{14,12},{15,13},{10,14},{11,... | collective-permute-start | bytes 393224 | tf_op jit(solution)/shard_map/ppermute | solution.py:703
  152.3 6.2 %collective-permute-start.37 = (bf16[16,4096]{1,0:T(8,128)(2,1)S(1)}, bf16[16,4096]{1,0:T(8,128)(2,1)S(1)}, u32[]{:S(2)}, u32[]{:S(2)}) collective-permute-start(bf16[16,4096]{1,0:T(8,128)(2,1)S(1)} %add.18), channel_id=1, source_target_pairs={{0,4},{1,5},{4,8},{5,9},{8,12},{9,13},{12,14},{13,15},{14,10},{15,... | collective-permute-start | bytes 393224 | tf_op jit(solution)/shard_map/ppermute | solution.py:702
  155.0 6.0 %collective-permute-start.51 = (bf16[16,4096]{1,0:T(8,128)(2,1)S(1)}, bf16[16,4096]{1,0:T(8,128)(2,1)S(1)}, u32[]{:S(2)}, u32[]{:S(2)}) collective-permute-start(bf16[16,4096]{1,0:T(8,128)(2,1)S(1)} %add.31), channel_id=1, source_target_pairs={{4,0},{5,1},{8,4},{9,5},{12,8},{13,9},{14,12},{15,13},{10,14},{11,... | collective-permute-start | bytes 393224 | tf_op jit(solution)/shard_map/ppermute | solution.py:703
  (23 other events, 115.7 us)

commit v11 on v10

--- a/solution.py
+++ b/solution.py
@@ -294,12 +294,12 @@
         for first, rows in chunks(tokens):
             update = fold(queries, first, keys, values, shift_ref[group, rows, :])
             total = total_ref[group, rows, :] + update[:, DH:]
-            worst_ref[...] = jnp.maximum(worst_ref[...], total)
+            worst_ref[...] = jnp.maximum(worst_ref[...], jnp.where(total <= SUM_LIMIT, 0.0, 1.0))
             results.append(divide(acc_ref[group, rows, :] + update[:, :DH], total))
         put(group, jnp.concatenate(results, axis=0))
 
     for_groups(one_group)
-    fits = jnp.max(worst_ref[...]) <= SUM_LIMIT
+    fits = jnp.max(worst_ref[...]) < 0.5
 
     @pl.when(jnp.logical_not(fits))
     def _():

time: 167 us -> 167 us (level)
  transfers between devices with their start and end apart: 52 -> 52, of which waited for: 32 -> 31; matrix products, arithmetic and copies ran while one was open for 0% -> 0% of each run, Pallas kernels for 11% -> 11%
where the time goes in v11:
time: 167 us
  starting transfers between devices  94 us (56%)
  waiting for transfers between devices  43.5 us (26%)
  Pallas kernels  28 us (17%)
    ppermute x22, starting transfers between devices, per_device(): go_right = lambda x: lax.ppermute(x, 'ctx', right)  62.9 us
    ppermute x21, starting transfers between devices, per_device(): go_left = lambda x: lax.ppermute(x, 'ctx', left)  27.1 us
    ppermute x22, waiting for transfers between devices, per_device(): go_right = lambda x: lax.ppermute(x, 'ctx', right)  26.1 us
    ppermute x21, waiting for transfers between devices, per_device(): go_left = lambda x: lax.ppermute(x, 'ctx', left)  16.1 us
    pallas_call x8, Pallas kernels, call(): pl.pallas_call(kernel, in_specs=[pl.BlockSpec(memory_space=pltpu.SMEM)] +...  8.86 us
    pallas_call x2, Pallas kernels, down_call(): pl.pallas_call(down_kernel, in_specs=[vmem] * 2 + more, out_specs=[vmem]...  4.7 us
    pallas_call x1, Pallas kernels, hidden_calls(): pl.pallas_call(first_kernel, in_specs=[pl.BlockSpec(memory_space=pltpu.SM...  4.63 us
    pallas_call x1, Pallas kernels, hidden_calls(): pl.pallas_call(second_kernel, in_specs=[vmem] * 6 + [anywhere], out_specs...  4.63 us
  transfers between devices with their start and end apart: 52, of which 31 were waited for; matrix products, arithmetic and copies ran while one was open for 0% of the time, Pallas kernels for 11%

profile of v11, /device:TPU:0, one launch (start us, length us, event | category | flops | bytes accessed | tf_op | source)
XLA Modules:
  0.0 166.8 jit_solution(8537039755756577097)
XLA Ops:
  0.6 1.9 %halves.1 = (bf16[256,512]{1,0:T(8,128)(2,1)S(1)}, bf16[256,512]{1,0:T(8,128)(2,1)S(1)}, bf16[128,4096]{1,0:T(8,128)(2,1)S(1)}, bf16[128,4096]{1,0:T(8,128)(2,1)S(1)}) custom-call(s32[1]{0:T(128)} %bitcast.me_ref.refs_0_, bf16[128,1024]{1,0:T(8,128)(2,1)} %refs_0_.2, bf16[128,1024]{1,0:T(8,128)(2,1)} %refs_1_.2, bf16[128,8192]{1,0:T(8,128)(2,1)} %refs_2_.1), custom_call_target="tpu_custom_call" | custom-call | flops 1 | bytes 1 | tf_op jit(solution)/shard_map/halves/pallas_call | solution.py:426
  3.1 3.0 %collective-permute-start.1 = (bf16[256,512]{1,0:T(8,128)(2,1)S(1)}, bf16[256,512]{1,0:T(8,128)(2,1)S(1)}, u32[]{:S(2)}, u32[]{:S(2)}) collective-permute-start(bf16[256,512]{1,0:T(8,128)(2,1)S(1)} %get-tuple-element.91.own_ref.refs_9_), channel_id=1, source_target_pairs={{0,4},{1,5},{4,8},{5,9},{8,12},{9,13},{12,14},{13,15},{14,10},{15,... | collective-permute-start | bytes 786440 | tf_op jit(solution)/shard_map/ppermute | solution.py:702
  8.3 3.8 %attend_own.1 = (f32[4,2048,128]{2,1,0:T(8,128)S(1)}, f32[4,2048,128]{2,1,0:T(8,128)S(1)}, f32[4,2048,128]{2,1,0:T(8,128)S(1)}) custom-call(s32[1]{0:T(128)} %bitcast.me_ref.refs_0_, bf16[128,4096]{1,0:T(8,128)(2,1)S(1)} %get-tuple-element.89.q_ref, bf16[128,4096]{1,0:T(8,128)(2,1)S(1)} %collective-permute-done.sib_q_ref, ...), custom_call_target="tpu_custom_call" | custom-call | flops 1 | bytes 1 | tf_op jit(solution)/shard_map/attend_own/pallas_call | solution.py:332
  13.2 2.2 %collective-permute-done.2.refs_2_.refs_13_ = bf16[256,512]{1,0:T(8,128)(2,1)S(1)} collective-permute-done((bf16[256,512]{1,0:T(8,128)(2,1)S(1)}, bf16[256,512]{1,0:T(8,128)(2,1)S(1)}, u32[]{:S(2)}, u32[]{:S(2)}) %collective-permute-start.2) | collective-permute-done | bytes 262176 | tf_op jit(solution)/shard_map/ppermute | solution.py:703
  18.5 1.9 %collective-permute-start.10 = (bf16[256,512]{1,0:T(8,128)(2,1)S(1)}, bf16[256,512]{1,0:T(8,128)(2,1)S(1)}, u32[]{:S(2)}, u32[]{:S(2)}) collective-permute-start(bf16[256,512]{1,0:T(8,128)(2,1)S(1)} %collective-permute-done.6.refs_1_.refs_12_), channel_id=1, source_target_pairs={{0,4},{1,5},{4,8},{5,9},{8,12},{9,13},{12,14},{13,15},{14,10},{15,... | collective-permute-start | bytes 786440 | tf_op jit(solution)/shard_map/ppermute | solution.py:702
  20.6 3.4 %collective-permute-done.4.refs_0_.refs_15_ = bf16[256,512]{1,0:T(8,128)(2,1)S(1)} collective-permute-done((bf16[256,512]{1,0:T(8,128)(2,1)S(1)}, bf16[256,512]{1,0:T(8,128)(2,1)S(1)}, u32[]{:S(2)}, u32[]{:S(2)}) %collective-permute-start.4) | collective-permute-done | bytes 262176 | tf_op jit(solution)/shard_map/ppermute | solution.py:702
  24.0 1.7 %collective-permute-done.5.refs_2_.refs_17_ = bf16[256,512]{1,0:T(8,128)(2,1)S(1)} collective-permute-done((bf16[256,512]{1,0:T(8,128)(2,1)S(1)}, bf16[256,512]{1,0:T(8,128)(2,1)S(1)}, u32[]{:S(2)}, u32[]{:S(2)}) %collective-permute-start.5) | collective-permute-done | bytes 262176 | tf_op jit(solution)/shard_map/ppermute | solution.py:703
  27.8 1.8 %collective-permute-done.10.refs_1_.refs_16_ = bf16[256,512]{1,0:T(8,128)(2,1)S(1)} collective-permute-done((bf16[256,512]{1,0:T(8,128)(2,1)S(1)}, bf16[256,512]{1,0:T(8,128)(2,1)S(1)}, u32[]{:S(2)}, u32[]{:S(2)}) %collective-permute-start.10) | collective-permute-done | bytes 262176 | tf_op jit(solution)/shard_map/ppermute | solution.py:702
  29.6 1.7 %collective-permute-done.11.refs_3_.refs_18_ = bf16[256,512]{1,0:T(8,128)(2,1)S(1)} collective-permute-done((bf16[256,512]{1,0:T(8,128)(2,1)S(1)}, bf16[256,512]{1,0:T(8,128)(2,1)S(1)}, u32[]{:S(2)}, u32[]{:S(2)}) %collective-permute-start.11) | collective-permute-done | bytes 262176 | tf_op jit(solution)/shard_map/ppermute | solution.py:703
  33.4 1.8 %collective-permute-done.8.refs_0_.refs_19_ = bf16[256,512]{1,0:T(8,128)(2,1)S(1)} collective-permute-done((bf16[256,512]{1,0:T(8,128)(2,1)S(1)}, bf16[256,512]{1,0:T(8,128)(2,1)S(1)}, u32[]{:S(2)}, u32[]{:S(2)}) %collective-permute-start.8) | collective-permute-done | bytes 262176 | tf_op jit(solution)/shard_map/ppermute | solution.py:702
  35.2 1.7 %collective-permute-done.9.refs_2_.refs_21_ = bf16[256,512]{1,0:T(8,128)(2,1)S(1)} collective-permute-done((bf16[256,512]{1,0:T(8,128)(2,1)S(1)}, bf16[256,512]{1,0:T(8,128)(2,1)S(1)}, u32[]{:S(2)}, u32[]{:S(2)}) %collective-permute-start.9) | collective-permute-done | bytes 262176 | tf_op jit(solution)/shard_map/ppermute | solution.py:703
  38.7 2.1 %collective-permute-done.13.refs_1_.refs_20_ = bf16[256,512]{1,0:T(8,128)(2,1)S(1)} collective-permute-done((bf16[256,512]{1,0:T(8,128)(2,1)S(1)}, bf16[256,512]{1,0:T(8,128)(2,1)S(1)}, u32[]{:S(2)}, u32[]{:S(2)}) %collective-permute-start.13) | collective-permute-done | bytes 262176 | tf_op jit(solution)/shard_map/ppermute | solution.py:702
  44.7 4.4 %collective-permute-done.15.refs_1_.refs_24_ = bf16[128,512]{1,0:T(8,128)(2,1)S(1)} collective-permute-done((bf16[128,512]{1,0:T(8,128)(2,1)S(1)}, bf16[128,512]{1,0:T(8,128)(2,1)S(1)}, u32[]{:S(2)}, u32[]{:S(2)}) %collective-permute-start.15) | collective-permute-done | bytes 131104 | tf_op jit(solution)/shard_map/ppermute | solution.py:702
  49.1 4.7 %attend_last.1 = (bf16[128,4096]{1,0:T(8,128)(2,1)S(1)}, bf16[128,4096]{1,0:T(8,128)(2,1)S(1)}, bf16[16,4224]{1,0:T(8,128)(2,1)S(1)}, bf16[16,4224]{1,0:T(8,128)...) custom-call(s32[1]{0:T(128)} %bitcast.me_ref.refs_0_, ...), custom_call_target="tpu_custom_call" | custom-call | flops 1 | bytes 1 | tf_op jit(solution)/shard_map/attend_last/pallas_call | solution.py:332
  53.8 1.8 %collective-permute-start.18 = (bf16[16,4224]{1,0:T(8,128)(2,1)S(1)}, bf16[16,4224]{1,0:T(8,128)(2,1)S(1)}, u32[]{:S(2)}, u32[]{:S(2)}) collective-permute-start(bf16[16,4224]{1,0:T(8,128)(2,1)S(1)} %get-tuple-element.137.refs_0_), channel_id=1, source_target_pairs={{4,0},{5,1},{8,4},{9,5},{12,8},{13,9},{14,12},{15,13},{10,14},{11,... | collective-permute-start | bytes 405512 | tf_op jit(solution)/shard_map/ppermute | solution.py:703
  55.9 2.3 %collective-permute-start.21 = (bf16[16,4224]{1,0:T(8,128)(2,1)S(1)}, bf16[16,4224]{1,0:T(8,128)(2,1)S(1)}, u32[]{:S(2)}, u32[]{:S(2)}) collective-permute-start(bf16[16,4224]{1,0:T(8,128)(2,1)S(1)} %get-tuple-element.137.refs_0_), channel_id=1, source_target_pairs={{0,4},{1,5},{4,8},{5,9},{8,12},{9,13},{12,14},{13,15},{14,10},{15,... | collective-permute-start | bytes 405512 | tf_op jit(solution)/shard_map/ppermute | solution.py:702
  59.4 2.2 %collective-permute-start.19 = (bf16[16,4224]{1,0:T(8,128)(2,1)S(1)}, bf16[16,4224]{1,0:T(8,128)(2,1)S(1)}, u32[]{:S(2)}, u32[]{:S(2)}) collective-permute-start(bf16[16,4224]{1,0:T(8,128)(2,1)S(1)} %collective-permute-done.18.refs_0_), channel_id=1, source_target_pairs={{4,0},{5,1},{8,4},{9,5},{12,8},{13,9},{14,12},{15,13},{10,14},{11,... | collective-permute-start | bytes 405512 | tf_op jit(solution)/shard_map/ppermute | solution.py:703
  62.3 2.1 %collective-permute-done.21.refs_2_ = bf16[16,4224]{1,0:T(8,128)(2,1)S(1)} collective-permute-done((bf16[16,4224]{1,0:T(8,128)(2,1)S(1)}, bf16[16,4224]{1,0:T(8,128)(2,1)S(1)}, u32[]{:S(2)}, u32[]{:S(2)}) %collective-permute-start.21) | collective-permute-done | bytes 135200 | tf_op jit(solution)/shard_map/ppermute | solution.py:702
  64.5 37.8 %collective-permute-start.25 = (bf16[16,4224]{1,0:T(8,128)(2,1)S(1)}, bf16[16,4224]{1,0:T(8,128)(2,1)S(1)}, u32[]{:S(2)}, u32[]{:S(2)}) collective-permute-start(bf16[16,4224]{1,0:T(8,128)(2,1)S(1)} %collective-permute-done.21.refs_2_), channel_id=1, source_target_pairs={{0,4},{1,5},{4,8},{5,9},{8,12},{9,13},{12,14},{13,15},{14,10},{15,... | collective-permute-start | bytes 405512 | tf_op jit(solution)/shard_map/ppermute | solution.py:702
  102.3 7.1 %collective-permute-start.23 = (bf16[16,4224]{1,0:T(8,128)(2,1)S(1)}, bf16[16,4224]{1,0:T(8,128)(2,1)S(1)}, u32[]{:S(2)}, u32[]{:S(2)}) collective-permute-start(bf16[16,4224]{1,0:T(8,128)(2,1)S(1)} %collective-permute-done.19.refs_0_), channel_id=1, source_target_pairs={{4,0},{5,1},{8,4},{9,5},{12,8},{13,9},{14,12},{15,13},{10,14},{11,... | collective-permute-start | bytes 405512 | tf_op jit(solution)/shard_map/ppermute | solution.py:703
  110.1 2.9 %collective-permute-start.29 = (bf16[16,4224]{1,0:T(8,128)(2,1)S(1)}, bf16[16,4224]{1,0:T(8,128)(2,1)S(1)}, u32[]{:S(2)}, u32[]{:S(2)}) collective-permute-start(bf16[16,4224]{1,0:T(8,128)(2,1)S(1)} %collective-permute-done.26.refs_3_), channel_id=1, source_target_pairs={{4,0},{5,1},{8,4},{9,5},{12,8},{13,9},{14,12},{15,13},{10,14},{11,... | collective-permute-start | bytes 405512 | tf_op jit(solution)/shard_map/ppermute | solution.py:703
  117.0 1.8 %collective-permute-done.28.refs_2_ = bf16[16,4224]{1,0:T(8,128)(2,1)S(1)} collective-permute-done((bf16[16,4224]{1,0:T(8,128)(2,1)S(1)}, bf16[16,4224]{1,0:T(8,128)(2,1)S(1)}, u32[]{:S(2)}, u32[]{:S(2)}) %collective-permute-start.28) | collective-permute-done | bytes 135200 | tf_op jit(solution)/shard_map/ppermute | solution.py:702
  122.0 4.6 %hidden_first.1 = (f32[256,768]{1,0:T(8,128)S(1)}, f32[256,768]{1,0:T(8,128)S(1)}, bf16[4096,768]{1,0:T(8,128)(2,1)S(1)}, bf16[4096,768]{1,0:T(8,128)(2,1)S(1)}) custom-call(s32[1]{0:T(128)} %bitcast.me_ref.refs_0_, bf16[256,4224]{1,0:T(8,128)(2,1)S(1)} %place.7.rows_ref.own_ref, bf16[4096,768]{1,0:T(8,128)(2,1)S(1)} %get-tuple-element.159.gate_ref, ...), custom_call_target="tpu_custom_call" | custom-call | flops 3221225472 | bytes 12582912 | tf_op jit(solution)/shard_map/hidden_first/pallas_call | solution.py:529
  126.7 4.6 %hidden_second.1 = (bf16[256,768]{1,0:T(8,128)(2,1)S(1)}, bf16[768,4096]{1,0:T(8,128)(2,1)S(1)}, bf16[768,4096]{1,0:T(8,128)(2,1)S(1)}) custom-call(bf16[256,4224]{1,0:T(8,128)(2,1)S(1)} %collective-permute-done.32.rows_ref, bf16[4096,768]{1,0:T(8,128)(2,1)S(1)} %get-tuple-element.161.gate_ref, bf16[4096,768]{1,0:T(8,128)(2,1)S(1)} %get-tuple-element.162.up_ref, ...), custom_call_target="tpu_custom_call" | custom-call | flops 3221225472 | bytes 12582912 | tf_op jit(solution)/shard_map/hidden_second/pallas_call | solution.py:539
  131.3 2.4 %down.2 = (bf16[128,4096]{1,0:T(8,128)(2,1)S(1)}, bf16[128,4096]{1,0:T(8,128)(2,1)S(1)}, bf16[128,8192]{1,0:T(8,128)(2,1)}) custom-call(bf16[256,768]{1,0:T(8,128)(2,1)S(1)} %get-tuple-element.165.hidden_ref, bf16[768,4096]{1,0:T(8,128)(2,1)S(1)} %get-tuple-element.166.down_ref, s32[1]{0:T(128)} %bitcast.me_ref.refs_0_, ...), custom_call_target="tpu_custom_call" | custom-call | flops 1610612736 | bytes 8388608 | tf_op jit(solution)/shard_map/down/pallas_call | solution.py:591
  133.8 2.3 %down.3 = (bf16[128,4096]{1,0:T(8,128)(2,1)S(1)}, bf16[128,4096]{1,0:T(8,128)(2,1)S(1)}) custom-call(bf16[256,768]{1,0:T(8,128)(2,1)S(1)} %get-tuple-element.165.hidden_ref, bf16[768,4096]{1,0:T(8,128)(2,1)S(1)} %get-tuple-element.170.down_ref), custom_call_target="tpu_custom_call" | custom-call | flops 1610612736 | bytes 8388608 | tf_op jit(solution)/shard_map/down/pallas_call | solution.py:591
  148.4 1.7 %collective-permute-start.50 = (bf16[16,4096]{1,0:T(8,128)(2,1)S(1)}, bf16[16,4096]{1,0:T(8,128)(2,1)S(1)}, u32[]{:S(2)}, u32[]{:S(2)}) collective-permute-start(bf16[16,4096]{1,0:T(8,128)(2,1)S(1)} %add.30), channel_id=1, source_target_pairs={{4,0},{5,1},{8,4},{9,5},{12,8},{13,9},{14,12},{15,13},{10,14},{11,... | collective-permute-start | bytes 393224 | tf_op jit(solution)/shard_map/ppermute | solution.py:703
  150.6 1.8 %collective-permute-start.41 = (bf16[16,4096]{1,0:T(8,128)(2,1)S(1)}, bf16[16,4096]{1,0:T(8,128)(2,1)S(1)}, u32[]{:S(2)}, u32[]{:S(2)}) collective-permute-start(bf16[16,4096]{1,0:T(8,128)(2,1)S(1)} %add.22), channel_id=1, source_target_pairs={{4,0},{5,1},{8,4},{9,5},{12,8},{13,9},{14,12},{15,13},{10,14},{11,... | collective-permute-start | bytes 393224 | tf_op jit(solution)/shard_map/ppermute | solution.py:703
  152.8 1.8 %collective-permute-done.50.refs_0_ = bf16[16,4096]{1,0:T(8,128)(2,1)S(1)} collective-permute-done((bf16[16,4096]{1,0:T(8,128)(2,1)S(1)}, bf16[16,4096]{1,0:T(8,128)(2,1)S(1)}, u32[]{:S(2)}, u32[]{:S(2)}) %collective-permute-start.50) | collective-permute-done | bytes 131104 | tf_op jit(solution)/shard_map/ppermute | solution.py:703
  155.2 1.8 %collective-permute-start.51 = (bf16[16,4096]{1,0:T(8,128)(2,1)S(1)}, bf16[16,4096]{1,0:T(8,128)(2,1)S(1)}, u32[]{:S(2)}, u32[]{:S(2)}) collective-permute-start(bf16[16,4096]{1,0:T(8,128)(2,1)S(1)} %add.31), channel_id=1, source_target_pairs={{4,0},{5,1},{8,4},{9,5},{12,8},{13,9},{14,12},{15,13},{10,14},{11,... | collective-permute-start | bytes 393224 | tf_op jit(solution)/shard_map/ppermute | solution.py:703
  158.7 1.7 collective-permute-start.42
  163.7 1.7 %collective-permute-done.38.refs_2_ = bf16[16,4096]{1,0:T(8,128)(2,1)S(1)} collective-permute-done((bf16[16,4096]{1,0:T(8,128)(2,1)S(1)}, bf16[16,4096]{1,0:T(8,128)(2,1)S(1)}, u32[]{:S(2)}, u32[]{:S(2)}) %collective-permute-start.38) | collective-permute-done | bytes 131104 | tf_op jit(solution)/shard_map/ppermute | solution.py:702
  (123 shorter events, 47.1 us)
Async XLA Ops:
  3.1 10.0 %collective-permute-start.1 = (bf16[256,512]{1,0:T(8,128)(2,1)S(1)}, bf16[256,512]{1,0:T(8,128)(2,1)S(1)}, u32[]{:S(2)}, u32[]{:S(2)}) collective-permute-start(bf16[256,512]{1,0:T(8,128)(2,1)S(1)} %get-tuple-element.91.own_ref.refs_9_), channel_id=1, source_target_pairs={{0,4},{1,5},{4,8},{5,9},{8,12},{9,13},{12,14},{13,15},{14,10},{15,... | collective-permute-start | bytes 786440 | tf_op jit(solution)/shard_map/ppermute | solution.py:702
  6.1 9.2 %collective-permute-start.2 = (bf16[256,512]{1,0:T(8,128)(2,1)S(1)}, bf16[256,512]{1,0:T(8,128)(2,1)S(1)}, u32[]{:S(2)}, u32[]{:S(2)}) collective-permute-start(bf16[256,512]{1,0:T(8,128)(2,1)S(1)} %get-tuple-element.91.own_ref.refs_9_), channel_id=1, source_target_pairs={{4,0},{5,1},{8,4},{9,5},{12,8},{13,9},{14,12},{15,13},{10,14},{11,... | collective-permute-start | bytes 786440 | tf_op jit(solution)/shard_map/ppermute | solution.py:703
  6.1 12.3 %collective-permute-start.6 = (bf16[256,512]{1,0:T(8,128)(2,1)S(1)}, bf16[256,512]{1,0:T(8,128)(2,1)S(1)}, u32[]{:S(2)}, u32[]{:S(2)}) collective-permute-start(bf16[256,512]{1,0:T(8,128)(2,1)S(1)} %get-tuple-element.92), channel_id=1, source_target_pairs={{0,5},{1,4},{4,9},{5,8},{8,13},{9,12},{12,15},{13,14},{14,11},{15,... | collective-permute-start | bytes 786440 | tf_op jit(solution)/shard_map/ppermute | solution.py:727
  7.3 11.3 %collective-permute-start.7 = (bf16[256,512]{1,0:T(8,128)(2,1)S(1)}, bf16[256,512]{1,0:T(8,128)(2,1)S(1)}, u32[]{:S(2)}, u32[]{:S(2)}) collective-permute-start(bf16[256,512]{1,0:T(8,128)(2,1)S(1)} %get-tuple-element.92), channel_id=1, source_target_pairs={{4,1},{5,0},{8,5},{9,4},{12,9},{13,8},{14,13},{15,12},{10,15},{11,... | collective-permute-start | bytes 786440 | tf_op jit(solution)/shard_map/ppermute | solution.py:727
  15.3 8.7 %collective-permute-start.4 = (bf16[256,512]{1,0:T(8,128)(2,1)S(1)}, bf16[256,512]{1,0:T(8,128)(2,1)S(1)}, u32[]{:S(2)}, u32[]{:S(2)}) collective-permute-start(bf16[256,512]{1,0:T(8,128)(2,1)S(1)} %collective-permute-done.1.refs_0_.refs_11_), channel_id=1, source_target_pairs={{0,4},{1,5},{4,8},{5,9},{8,12},{9,13},{12,14},{13,15},{14,10},{15,... | collective-permute-start | bytes 786440 | tf_op jit(solution)/shard_map/ppermute | solution.py:702
  16.9 8.8 %collective-permute-start.5 = (bf16[256,512]{1,0:T(8,128)(2,1)S(1)}, bf16[256,512]{1,0:T(8,128)(2,1)S(1)}, u32[]{:S(2)}, u32[]{:S(2)}) collective-permute-start(bf16[256,512]{1,0:T(8,128)(2,1)S(1)} %collective-permute-done.2.refs_2_.refs_13_), channel_id=1, source_target_pairs={{4,0},{5,1},{8,4},{9,5},{12,8},{13,9},{14,12},{15,13},{10,14},{11,... | collective-permute-start | bytes 786440 | tf_op jit(solution)/shard_map/ppermute | solution.py:703
  18.5 11.0 %collective-permute-start.10 = (bf16[256,512]{1,0:T(8,128)(2,1)S(1)}, bf16[256,512]{1,0:T(8,128)(2,1)S(1)}, u32[]{:S(2)}, u32[]{:S(2)}) collective-permute-start(bf16[256,512]{1,0:T(8,128)(2,1)S(1)} %collective-permute-done.6.refs_1_.refs_12_), channel_id=1, source_target_pairs={{0,4},{1,5},{4,8},{5,9},{8,12},{9,13},{12,14},{13,15},{14,10},{15,... | collective-permute-start | bytes 786440 | tf_op jit(solution)/shard_map/ppermute | solution.py:702
  20.5 10.8 %collective-permute-start.11 = (bf16[256,512]{1,0:T(8,128)(2,1)S(1)}, bf16[256,512]{1,0:T(8,128)(2,1)S(1)}, u32[]{:S(2)}, u32[]{:S(2)}) collective-permute-start(bf16[256,512]{1,0:T(8,128)(2,1)S(1)} %collective-permute-done.7.refs_3_.refs_14_), channel_id=1, source_target_pairs={{4,0},{5,1},{8,4},{9,5},{12,8},{13,9},{14,12},{15,13},{10,14},{11,... | collective-permute-start | bytes 786440 | tf_op jit(solution)/shard_map/ppermute | solution.py:703
  25.7 9.5 %collective-permute-start.8 = (bf16[256,512]{1,0:T(8,128)(2,1)S(1)}, bf16[256,512]{1,0:T(8,128)(2,1)S(1)}, u32[]{:S(2)}, u32[]{:S(2)}) collective-permute-start(bf16[256,512]{1,0:T(8,128)(2,1)S(1)} %collective-permute-done.4.refs_0_.refs_15_), channel_id=1, source_target_pairs={{0,4},{1,5},{4,8},{5,9},{8,12},{9,13},{12,14},{13,15},{14,10},{15,... | collective-permute-start | bytes 786440 | tf_op jit(solution)/shard_map/ppermute | solution.py:702
  27.3 9.7 %collective-permute-start.9 = (bf16[256,512]{1,0:T(8,128)(2,1)S(1)}, bf16[256,512]{1,0:T(8,128)(2,1)S(1)}, u32[]{:S(2)}, u32[]{:S(2)}) collective-permute-start(bf16[256,512]{1,0:T(8,128)(2,1)S(1)} %collective-permute-done.5.refs_2_.refs_17_), channel_id=1, source_target_pairs={{4,0},{5,1},{8,4},{9,5},{12,8},{13,9},{14,12},{15,13},{10,14},{11,... | collective-permute-start | bytes 786440 | tf_op jit(solution)/shard_map/ppermute | solution.py:703
  31.3 9.5 %collective-permute-start.13 = (bf16[256,512]{1,0:T(8,128)(2,1)S(1)}, bf16[256,512]{1,0:T(8,128)(2,1)S(1)}, u32[]{:S(2)}, u32[]{:S(2)}) collective-permute-start(bf16[256,512]{1,0:T(8,128)(2,1)S(1)} %collective-permute-done.10.refs_1_.refs_16_), channel_id=1, source_target_pairs={{0,4},{1,5},{4,8},{5,9},{8,12},{9,13},{12,14},{13,15},{14,10},{15,... | collective-permute-start | bytes 786440 | tf_op jit(solution)/shard_map/ppermute | solution.py:702
  32.9 9.3 %collective-permute-start.14 = (bf16[256,512]{1,0:T(8,128)(2,1)S(1)}, bf16[256,512]{1,0:T(8,128)(2,1)S(1)}, u32[]{:S(2)}, u32[]{:S(2)}) collective-permute-start(bf16[256,512]{1,0:T(8,128)(2,1)S(1)} %collective-permute-done.11.refs_3_.refs_18_), channel_id=1, source_target_pairs={{4,0},{5,1},{8,4},{9,5},{12,8},{13,9},{14,12},{15,13},{10,14},{11,... | collective-permute-start | bytes 786440 | tf_op jit(solution)/shard_map/ppermute | solution.py:703
  36.9 12.2 %collective-permute-start.12 = (bf16[256,512]{1,0:T(8,128)(2,1)S(1)}, bf16[256,512]{1,0:T(8,128)(2,1)S(1)}, u32[]{:S(2)}, u32[]{:S(2)}) collective-permute-start(bf16[256,512]{1,0:T(8,128)(2,1)S(1)} %collective-permute-done.8.refs_0_.refs_19_), channel_id=1, source_target_pairs={{0,4},{1,5},{4,8},{5,9},{8,12},{9,13},{12,14},{13,15},{14,10},{15,... | collective-permute-start | bytes 786440 | tf_op jit(solution)/shard_map/ppermute | solution.py:702
  42.2 6.9 %collective-permute-start.15 = (bf16[128,512]{1,0:T(8,128)(2,1)S(1)}, bf16[128,512]{1,0:T(8,128)(2,1)S(1)}, u32[]{:S(2)}, u32[]{:S(2)}) collective-permute-start(bf16[128,512]{1,0:T(8,128)(2,1)S(1)} %slice.6), channel_id=1, source_target_pairs={{0,4},{1,5},{4,8},{5,9},{8,12},{9,13},{12,14},{13,15},{14,10},{15,... | collective-permute-start | bytes 393224 | tf_op jit(solution)/shard_map/ppermute | solution.py:702
  55.6 6.4 %collective-permute-start.20 = (bf16[16,4224]{1,0:T(8,128)(2,1)S(1)}, bf16[16,4224]{1,0:T(8,128)(2,1)S(1)}, u32[]{:S(2)}, u32[]{:S(2)}) collective-permute-start(bf16[16,4224]{1,0:T(8,128)(2,1)S(1)} %get-tuple-element.138.refs_1_), channel_id=1, source_target_pairs={{0,4},{1,5},{4,8},{5,9},{8,12},{9,13},{12,14},{13,15},{14,10},{15,... | collective-permute-start | bytes 405512 | tf_op jit(solution)/shard_map/ppermute | solution.py:702
  55.9 8.5 %collective-permute-start.21 = (bf16[16,4224]{1,0:T(8,128)(2,1)S(1)}, bf16[16,4224]{1,0:T(8,128)(2,1)S(1)}, u32[]{:S(2)}, u32[]{:S(2)}) collective-permute-start(bf16[16,4224]{1,0:T(8,128)(2,1)S(1)} %get-tuple-element.137.refs_0_), channel_id=1, source_target_pairs={{0,4},{1,5},{4,8},{5,9},{8,12},{9,13},{12,14},{13,15},{14,10},{15,... | collective-permute-start | bytes 405512 | tf_op jit(solution)/shard_map/ppermute | solution.py:702
  58.2 44.0 %collective-permute-start.22 = (bf16[16,4224]{1,0:T(8,128)(2,1)S(1)}, bf16[16,4224]{1,0:T(8,128)(2,1)S(1)}, u32[]{:S(2)}, u32[]{:S(2)}) collective-permute-start(bf16[16,4224]{1,0:T(8,128)(2,1)S(1)} %get-tuple-element.138.refs_1_), channel_id=1, source_target_pairs={{4,0},{5,1},{8,4},{9,5},{12,8},{13,9},{14,12},{15,13},{10,14},{11,... | collective-permute-start | bytes 405512 | tf_op jit(solution)/shard_map/ppermute | solution.py:703
  59.4 42.9 %collective-permute-start.19 = (bf16[16,4224]{1,0:T(8,128)(2,1)S(1)}, bf16[16,4224]{1,0:T(8,128)(2,1)S(1)}, u32[]{:S(2)}, u32[]{:S(2)}) collective-permute-start(bf16[16,4224]{1,0:T(8,128)(2,1)S(1)} %collective-permute-done.18.refs_0_), channel_id=1, source_target_pairs={{4,0},{5,1},{8,4},{9,5},{12,8},{13,9},{14,12},{15,13},{10,14},{11,... | collective-permute-start | bytes 405512 | tf_op jit(solution)/shard_map/ppermute | solution.py:703
  62.0 47.3 %collective-permute-start.24 = (bf16[16,4224]{1,0:T(8,128)(2,1)S(1)}, bf16[16,4224]{1,0:T(8,128)(2,1)S(1)}, u32[]{:S(2)}, u32[]{:S(2)}) collective-permute-start(bf16[16,4224]{1,0:T(8,128)(2,1)S(1)} %collective-permute-done.20.refs_1_), channel_id=1, source_target_pairs={{0,4},{1,5},{4,8},{5,9},{8,12},{9,13},{12,14},{13,15},{14,10},{15,... | collective-permute-start | bytes 405512 | tf_op jit(solution)/shard_map/ppermute | solution.py:702
  64.5 44.9 %collective-permute-start.25 = (bf16[16,4224]{1,0:T(8,128)(2,1)S(1)}, bf16[16,4224]{1,0:T(8,128)(2,1)S(1)}, u32[]{:S(2)}, u32[]{:S(2)}) collective-permute-start(bf16[16,4224]{1,0:T(8,128)(2,1)S(1)} %collective-permute-done.21.refs_2_), channel_id=1, source_target_pairs={{0,4},{1,5},{4,8},{5,9},{8,12},{9,13},{12,14},{13,15},{14,10},{15,... | collective-permute-start | bytes 405512 | tf_op jit(solution)/shard_map/ppermute | solution.py:702
  102.2 7.9 %collective-permute-start.26 = (bf16[16,4224]{1,0:T(8,128)(2,1)S(1)}, bf16[16,4224]{1,0:T(8,128)(2,1)S(1)}, u32[]{:S(2)}, u32[]{:S(2)}) collective-permute-start(bf16[16,4224]{1,0:T(8,128)(2,1)S(1)} %collective-permute-done.22.refs_3_), channel_id=1, source_target_pairs={{4,0},{5,1},{8,4},{9,5},{12,8},{13,9},{14,12},{15,13},{10,14},{11,... | collective-permute-start | bytes 405512 | tf_op jit(solution)/shard_map/ppermute | solution.py:703
  102.3 10.8 %collective-permute-start.23 = (bf16[16,4224]{1,0:T(8,128)(2,1)S(1)}, bf16[16,4224]{1,0:T(8,128)(2,1)S(1)}, u32[]{:S(2)}, u32[]{:S(2)}) collective-permute-start(bf16[16,4224]{1,0:T(8,128)(2,1)S(1)} %collective-permute-done.19.refs_0_), channel_id=1, source_target_pairs={{4,0},{5,1},{8,4},{9,5},{12,8},{13,9},{14,12},{15,13},{10,14},{11,... | collective-permute-start | bytes 405512 | tf_op jit(solution)/shard_map/ppermute | solution.py:703
  110.1 6.8 %collective-permute-start.29 = (bf16[16,4224]{1,0:T(8,128)(2,1)S(1)}, bf16[16,4224]{1,0:T(8,128)(2,1)S(1)}, u32[]{:S(2)}, u32[]{:S(2)}) collective-permute-start(bf16[16,4224]{1,0:T(8,128)(2,1)S(1)} %collective-permute-done.26.refs_3_), channel_id=1, source_target_pairs={{4,0},{5,1},{8,4},{9,5},{12,8},{13,9},{14,12},{15,13},{10,14},{11,... | collective-permute-start | bytes 405512 | tf_op jit(solution)/shard_map/ppermute | solution.py:703
  121.5 9.8 %collective-permute-start.33 = (bf16[128,4096]{1,0:T(8,128)(2,1)S(1)}, bf16[128,4096]{1,0:T(8,128)(2,1)S(1)}, u32[]{:S(2)}, u32[]{:S(2)}) collective-permute-start(bf16[128,4096]{1,0:T(8,128)(2,1)S(1)} %get-tuple-element.168), channel_id=1, source_target_pairs={{0,1},{1,0},{2,3},{3,2},{4,5},{5,4},{6,7},{7,6},{8,9},{9,8},{10,11... | collective-permute-start | bytes 3145736 | tf_op jit(solution)/shard_map/ppermute | solution.py:704
  141.2 6.1 %collective-permute-start.49 = (bf16[16,4096]{1,0:T(8,128)(2,1)S(1)}, bf16[16,4096]{1,0:T(8,128)(2,1)S(1)}, u32[]{:S(2)}, u32[]{:S(2)}) collective-permute-start(bf16[16,4096]{1,0:T(8,128)(2,1)S(1)} %add.29), channel_id=1, source_target_pairs={{4,0},{5,1},{8,4},{9,5},{12,8},{13,9},{14,12},{15,13},{10,14},{11,... | collective-permute-start | bytes 393224 | tf_op jit(solution)/shard_map/ppermute | solution.py:703
  142.1 6.3 %collective-permute-start.45 = (bf16[16,4096]{1,0:T(8,128)(2,1)S(1)}, bf16[16,4096]{1,0:T(8,128)(2,1)S(1)}, u32[]{:S(2)}, u32[]{:S(2)}) collective-permute-start(bf16[16,4096]{1,0:T(8,128)(2,1)S(1)} %add.25), channel_id=1, source_target_pairs={{0,4},{1,5},{4,8},{5,9},{8,12},{9,13},{12,14},{13,15},{14,10},{15,... | collective-permute-start | bytes 393224 | tf_op jit(solution)/shard_map/ppermute | solution.py:702
  143.7 6.8 %collective-permute-start.40 = (bf16[16,4096]{1,0:T(8,128)(2,1)S(1)}, bf16[16,4096]{1,0:T(8,128)(2,1)S(1)}, u32[]{:S(2)}, u32[]{:S(2)}) collective-permute-start(bf16[16,4096]{1,0:T(8,128)(2,1)S(1)} %add.21), channel_id=1, source_target_pairs={{4,0},{5,1},{8,4},{9,5},{12,8},{13,9},{14,12},{15,13},{10,14},{11,... | collective-permute-start | bytes 393224 | tf_op jit(solution)/shard_map/ppermute | solution.py:703
  144.4 8.0 %collective-permute-start.36 = (bf16[16,4096]{1,0:T(8,128)(2,1)S(1)}, bf16[16,4096]{1,0:T(8,128)(2,1)S(1)}, u32[]{:S(2)}, u32[]{:S(2)}) collective-permute-start(bf16[16,4096]{1,0:T(8,128)(2,1)S(1)} %add.17), channel_id=1, source_target_pairs={{0,4},{1,5},{4,8},{5,9},{8,12},{9,13},{12,14},{13,15},{14,10},{15,... | collective-permute-start | bytes 393224 | tf_op jit(solution)/shard_map/ppermute | solution.py:702
  148.4 6.1 %collective-permute-start.50 = (bf16[16,4096]{1,0:T(8,128)(2,1)S(1)}, bf16[16,4096]{1,0:T(8,128)(2,1)S(1)}, u32[]{:S(2)}, u32[]{:S(2)}) collective-permute-start(bf16[16,4096]{1,0:T(8,128)(2,1)S(1)} %add.30), channel_id=1, source_target_pairs={{4,0},{5,1},{8,4},{9,5},{12,8},{13,9},{14,12},{15,13},{10,14},{11,... | collective-permute-start | bytes 393224 | tf_op jit(solution)/shard_map/ppermute | solution.py:703
  150.6 6.5 %collective-permute-start.41 = (bf16[16,4096]{1,0:T(8,128)(2,1)S(1)}, bf16[16,4096]{1,0:T(8,128)(2,1)S(1)}, u32[]{:S(2)}, u32[]{:S(2)}) collective-permute-start(bf16[16,4096]{1,0:T(8,128)(2,1)S(1)} %add.22), channel_id=1, source_target_pairs={{4,0},{5,1},{8,4},{9,5},{12,8},{13,9},{14,12},{15,13},{10,14},{11,... | collective-permute-start | bytes 393224 | tf_op jit(solution)/shard_map/ppermute | solution.py:703
  152.5 6.2 %collective-permute-start.37 = (bf16[16,4096]{1,0:T(8,128)(2,1)S(1)}, bf16[16,4096]{1,0:T(8,128)(2,1)S(1)}, u32[]{:S(2)}, u32[]{:S(2)}) collective-permute-start(bf16[16,4096]{1,0:T(8,128)(2,1)S(1)} %add.18), channel_id=1, source_target_pairs={{0,4},{1,5},{4,8},{5,9},{8,12},{9,13},{12,14},{13,15},{14,10},{15,... | collective-permute-start | bytes 393224 | tf_op jit(solution)/shard_map/ppermute | solution.py:702
  155.2 6.1 %collective-permute-start.51 = (bf16[16,4096]{1,0:T(8,128)(2,1)S(1)}, bf16[16,4096]{1,0:T(8,128)(2,1)S(1)}, u32[]{:S(2)}, u32[]{:S(2)}) collective-permute-start(bf16[16,4096]{1,0:T(8,128)(2,1)S(1)} %add.31), channel_id=1, source_target_pairs={{4,0},{5,1},{8,4},{9,5},{12,8},{13,9},{14,12},{15,13},{10,14},{11,... | collective-permute-start | bytes 393224 | tf_op jit(solution)/shard_map/ppermute | solution.py:703
  (23 other events, 115.7 us)

commit v12 on v11

--- a/solution.py
+++ b/solution.py
@@ -21,7 +21,7 @@
 SMALL = pl.CostEstimate(flops=1, bytes_accessed=1, transcendentals=0)
 SUM_LIMIT = 2.0**100
 PARTS = 3
-STACK = 4
+STACK = 8
 MIB = 1 << 20
 
 

time: 167 us -> 170 us (1.018)
  starting transfers between devices: 94 us -> 96.8 us
    ppermute x22, starting transfers between devices: 62.9 us -> 65.6 us  [per_device(): go_right = lambda x: lax.ppermute(x, 'ctx', right)]
  transfers between devices with their start and end apart: 52 -> 52, of which waited for: 31 -> 32; matrix products, arithmetic and copies ran while one was open for 0% -> 0% of each run, Pallas kernels for 11% -> 11%
where the time goes in v12:
time: 170 us
  starting transfers between devices  96.8 us (57%)
  waiting for transfers between devices  43.1 us (25%)
  Pallas kernels  28.3 us (17%)
    ppermute x22, starting transfers between devices, per_device(): go_right = lambda x: lax.ppermute(x, 'ctx', right)  65.6 us
    ppermute x21, starting transfers between devices, per_device(): go_left = lambda x: lax.ppermute(x, 'ctx', left)  27.2 us
    ppermute x22, waiting for transfers between devices, per_device(): go_right = lambda x: lax.ppermute(x, 'ctx', right)  25.7 us
    ppermute x21, waiting for transfers between devices, per_device(): go_left = lambda x: lax.ppermute(x, 'ctx', left)  16.1 us
    pallas_call x8, Pallas kernels, call(): pl.pallas_call(kernel, in_specs=[pl.BlockSpec(memory_space=pltpu.SMEM)] +...  9.21 us
    pallas_call x2, Pallas kernels, down_call(): pl.pallas_call(down_kernel, in_specs=[vmem] * 2 + more, out_specs=[vmem]...  4.69 us
    pallas_call x1, Pallas kernels, hidden_calls(): pl.pallas_call(first_kernel, in_specs=[pl.BlockSpec(memory_space=pltpu.SM...  4.63 us
    pallas_call x1, Pallas kernels, hidden_calls(): pl.pallas_call(second_kernel, in_specs=[vmem] * 6 + [anywhere], out_specs...  4.63 us
  transfers between devices with their start and end apart: 52, of which 32 were waited for; matrix products, arithmetic and copies ran while one was open for 0% of the time, Pallas kernels for 11%

profile of v12, /device:TPU:0, one launch (start us, length us, event | category | flops | bytes accessed | tf_op | source)
XLA Modules:
  0.0 169.5 jit_solution(16000392140287209850)
XLA Ops:
  0.6 1.9 %halves.1 = (bf16[256,512]{1,0:T(8,128)(2,1)S(1)}, bf16[256,512]{1,0:T(8,128)(2,1)S(1)}, bf16[128,4096]{1,0:T(8,128)(2,1)S(1)}, bf16[128,4096]{1,0:T(8,128)(2,1)S(1)}) custom-call(s32[1]{0:T(128)} %bitcast.me_ref.refs_0_, bf16[128,1024]{1,0:T(8,128)(2,1)} %refs_0_.2, bf16[128,1024]{1,0:T(8,128)(2,1)} %refs_1_.2, bf16[128,8192]{1,0:T(8,128)(2,1)} %refs_2_.1), custom_call_target="tpu_custom_call" | custom-call | flops 1 | bytes 1 | tf_op jit(solution)/shard_map/halves/pallas_call | solution.py:426
  3.1 3.0 %collective-permute-start.1 = (bf16[256,512]{1,0:T(8,128)(2,1)S(1)}, bf16[256,512]{1,0:T(8,128)(2,1)S(1)}, u32[]{:S(2)}, u32[]{:S(2)}) collective-permute-start(bf16[256,512]{1,0:T(8,128)(2,1)S(1)} %get-tuple-element.91.own_ref.refs_9_), channel_id=1, source_target_pairs={{0,4},{1,5},{4,8},{5,9},{8,12},{9,13},{12,14},{13,15},{14,10},{15,... | collective-permute-start | bytes 786440 | tf_op jit(solution)/shard_map/ppermute | solution.py:702
  8.3 4.0 %attend_own.1 = (f32[4,2048,128]{2,1,0:T(8,128)S(1)}, f32[4,2048,128]{2,1,0:T(8,128)S(1)}, f32[4,2048,128]{2,1,0:T(8,128)S(1)}) custom-call(s32[1]{0:T(128)} %bitcast.me_ref.refs_0_, bf16[128,4096]{1,0:T(8,128)(2,1)S(1)} %get-tuple-element.89.q_ref, bf16[128,4096]{1,0:T(8,128)(2,1)S(1)} %collective-permute-done.sib_q_ref, ...), custom_call_target="tpu_custom_call" | custom-call | flops 1 | bytes 1 | tf_op jit(solution)/shard_map/attend_own/pallas_call | solution.py:332
  13.2 2.2 %collective-permute-done.2.refs_2_.refs_13_ = bf16[256,512]{1,0:T(8,128)(2,1)S(1)} collective-permute-done((bf16[256,512]{1,0:T(8,128)(2,1)S(1)}, bf16[256,512]{1,0:T(8,128)(2,1)S(1)}, u32[]{:S(2)}, u32[]{:S(2)}) %collective-permute-start.2) | collective-permute-done | bytes 262176 | tf_op jit(solution)/shard_map/ppermute | solution.py:703
  18.5 1.9 %collective-permute-start.10 = (bf16[256,512]{1,0:T(8,128)(2,1)S(1)}, bf16[256,512]{1,0:T(8,128)(2,1)S(1)}, u32[]{:S(2)}, u32[]{:S(2)}) collective-permute-start(bf16[256,512]{1,0:T(8,128)(2,1)S(1)} %collective-permute-done.6.refs_1_.refs_12_), channel_id=1, source_target_pairs={{0,4},{1,5},{4,8},{5,9},{8,12},{9,13},{12,14},{13,15},{14,10},{15,... | collective-permute-start | bytes 786440 | tf_op jit(solution)/shard_map/ppermute | solution.py:702
  20.6 3.4 %collective-permute-done.4.refs_0_.refs_15_ = bf16[256,512]{1,0:T(8,128)(2,1)S(1)} collective-permute-done((bf16[256,512]{1,0:T(8,128)(2,1)S(1)}, bf16[256,512]{1,0:T(8,128)(2,1)S(1)}, u32[]{:S(2)}, u32[]{:S(2)}) %collective-permute-start.4) | collective-permute-done | bytes 262176 | tf_op jit(solution)/shard_map/ppermute | solution.py:702
  24.0 1.7 %collective-permute-done.5.refs_2_.refs_17_ = bf16[256,512]{1,0:T(8,128)(2,1)S(1)} collective-permute-done((bf16[256,512]{1,0:T(8,128)(2,1)S(1)}, bf16[256,512]{1,0:T(8,128)(2,1)S(1)}, u32[]{:S(2)}, u32[]{:S(2)}) %collective-permute-start.5) | collective-permute-done | bytes 262176 | tf_op jit(solution)/shard_map/ppermute | solution.py:703
  27.8 1.8 %collective-permute-done.10.refs_1_.refs_16_ = bf16[256,512]{1,0:T(8,128)(2,1)S(1)} collective-permute-done((bf16[256,512]{1,0:T(8,128)(2,1)S(1)}, bf16[256,512]{1,0:T(8,128)(2,1)S(1)}, u32[]{:S(2)}, u32[]{:S(2)}) %collective-permute-start.10) | collective-permute-done | bytes 262176 | tf_op jit(solution)/shard_map/ppermute | solution.py:702
  29.6 1.7 %collective-permute-done.11.refs_3_.refs_18_ = bf16[256,512]{1,0:T(8,128)(2,1)S(1)} collective-permute-done((bf16[256,512]{1,0:T(8,128)(2,1)S(1)}, bf16[256,512]{1,0:T(8,128)(2,1)S(1)}, u32[]{:S(2)}, u32[]{:S(2)}) %collective-permute-start.11) | collective-permute-done | bytes 262176 | tf_op jit(solution)/shard_map/ppermute | solution.py:703
  33.4 1.8 %collective-permute-done.8.refs_0_.refs_19_ = bf16[256,512]{1,0:T(8,128)(2,1)S(1)} collective-permute-done((bf16[256,512]{1,0:T(8,128)(2,1)S(1)}, bf16[256,512]{1,0:T(8,128)(2,1)S(1)}, u32[]{:S(2)}, u32[]{:S(2)}) %collective-permute-start.8) | collective-permute-done | bytes 262176 | tf_op jit(solution)/shard_map/ppermute | solution.py:702
  35.2 1.7 %collective-permute-done.9.refs_2_.refs_21_ = bf16[256,512]{1,0:T(8,128)(2,1)S(1)} collective-permute-done((bf16[256,512]{1,0:T(8,128)(2,1)S(1)}, bf16[256,512]{1,0:T(8,128)(2,1)S(1)}, u32[]{:S(2)}, u32[]{:S(2)}) %collective-permute-start.9) | collective-permute-done | bytes 262176 | tf_op jit(solution)/shard_map/ppermute | solution.py:703
  38.7 2.1 %collective-permute-done.13.refs_1_.refs_20_ = bf16[256,512]{1,0:T(8,128)(2,1)S(1)} collective-permute-done((bf16[256,512]{1,0:T(8,128)(2,1)S(1)}, bf16[256,512]{1,0:T(8,128)(2,1)S(1)}, u32[]{:S(2)}, u32[]{:S(2)}) %collective-permute-start.13) | collective-permute-done | bytes 262176 | tf_op jit(solution)/shard_map/ppermute | solution.py:702
  42.2 1.6 collective-permute-start.15
  44.7 4.4 %collective-permute-done.15.refs_1_.refs_24_ = bf16[128,512]{1,0:T(8,128)(2,1)S(1)} collective-permute-done((bf16[128,512]{1,0:T(8,128)(2,1)S(1)}, bf16[128,512]{1,0:T(8,128)(2,1)S(1)}, u32[]{:S(2)}, u32[]{:S(2)}) %collective-permute-start.15) | collective-permute-done | bytes 131104 | tf_op jit(solution)/shard_map/ppermute | solution.py:702
  49.1 4.9 %attend_last.1 = (bf16[128,4096]{1,0:T(8,128)(2,1)S(1)}, bf16[128,4096]{1,0:T(8,128)(2,1)S(1)}, bf16[16,4224]{1,0:T(8,128)(2,1)S(1)}, bf16[16,4224]{1,0:T(8,128)...) custom-call(s32[1]{0:T(128)} %bitcast.me_ref.refs_0_, ...), custom_call_target="tpu_custom_call" | custom-call | flops 1 | bytes 1 | tf_op jit(solution)/shard_map/attend_last/pallas_call | solution.py:332
  54.0 1.8 %collective-permute-start.18 = (bf16[16,4224]{1,0:T(8,128)(2,1)S(1)}, bf16[16,4224]{1,0:T(8,128)(2,1)S(1)}, u32[]{:S(2)}, u32[]{:S(2)}) collective-permute-start(bf16[16,4224]{1,0:T(8,128)(2,1)S(1)} %get-tuple-element.137.refs_0_), channel_id=1, source_target_pairs={{4,0},{5,1},{8,4},{9,5},{12,8},{13,9},{14,12},{15,13},{10,14},{11,... | collective-permute-start | bytes 405512 | tf_op jit(solution)/shard_map/ppermute | solution.py:703
  56.1 2.4 %collective-permute-start.21 = (bf16[16,4224]{1,0:T(8,128)(2,1)S(1)}, bf16[16,4224]{1,0:T(8,128)(2,1)S(1)}, u32[]{:S(2)}, u32[]{:S(2)}) collective-permute-start(bf16[16,4224]{1,0:T(8,128)(2,1)S(1)} %get-tuple-element.137.refs_0_), channel_id=1, source_target_pairs={{0,4},{1,5},{4,8},{5,9},{8,12},{9,13},{12,14},{13,15},{14,10},{15,... | collective-permute-start | bytes 405512 | tf_op jit(solution)/shard_map/ppermute | solution.py:702
  59.5 2.3 %collective-permute-start.19 = (bf16[16,4224]{1,0:T(8,128)(2,1)S(1)}, bf16[16,4224]{1,0:T(8,128)(2,1)S(1)}, u32[]{:S(2)}, u32[]{:S(2)}) collective-permute-start(bf16[16,4224]{1,0:T(8,128)(2,1)S(1)} %collective-permute-done.18.refs_0_), channel_id=1, source_target_pairs={{4,0},{5,1},{8,4},{9,5},{12,8},{13,9},{14,12},{15,13},{10,14},{11,... | collective-permute-start | bytes 405512 | tf_op jit(solution)/shard_map/ppermute | solution.py:703
  62.7 2.0 %collective-permute-done.21.refs_2_ = bf16[16,4224]{1,0:T(8,128)(2,1)S(1)} collective-permute-done((bf16[16,4224]{1,0:T(8,128)(2,1)S(1)}, bf16[16,4224]{1,0:T(8,128)(2,1)S(1)}, u32[]{:S(2)}, u32[]{:S(2)}) %collective-permute-start.21) | collective-permute-done | bytes 135200 | tf_op jit(solution)/shard_map/ppermute | solution.py:702
  64.7 40.2 %collective-permute-start.25 = (bf16[16,4224]{1,0:T(8,128)(2,1)S(1)}, bf16[16,4224]{1,0:T(8,128)(2,1)S(1)}, u32[]{:S(2)}, u32[]{:S(2)}) collective-permute-start(bf16[16,4224]{1,0:T(8,128)(2,1)S(1)} %collective-permute-done.21.refs_2_), channel_id=1, source_target_pairs={{0,4},{1,5},{4,8},{5,9},{8,12},{9,13},{12,14},{13,15},{14,10},{15,... | collective-permute-start | bytes 405512 | tf_op jit(solution)/shard_map/ppermute | solution.py:702
  105.0 7.1 %collective-permute-start.23 = (bf16[16,4224]{1,0:T(8,128)(2,1)S(1)}, bf16[16,4224]{1,0:T(8,128)(2,1)S(1)}, u32[]{:S(2)}, u32[]{:S(2)}) collective-permute-start(bf16[16,4224]{1,0:T(8,128)(2,1)S(1)} %collective-permute-done.19.refs_0_), channel_id=1, source_target_pairs={{4,0},{5,1},{8,4},{9,5},{12,8},{13,9},{14,12},{15,13},{10,14},{11,... | collective-permute-start | bytes 405512 | tf_op jit(solution)/shard_map/ppermute | solution.py:703
  112.8 3.0 %collective-permute-start.29 = (bf16[16,4224]{1,0:T(8,128)(2,1)S(1)}, bf16[16,4224]{1,0:T(8,128)(2,1)S(1)}, u32[]{:S(2)}, u32[]{:S(2)}) collective-permute-start(bf16[16,4224]{1,0:T(8,128)(2,1)S(1)} %collective-permute-done.26.refs_3_), channel_id=1, source_target_pairs={{4,0},{5,1},{8,4},{9,5},{12,8},{13,9},{14,12},{15,13},{10,14},{11,... | collective-permute-start | bytes 405512 | tf_op jit(solution)/shard_map/ppermute | solution.py:703
  119.7 1.8 %collective-permute-done.28.refs_2_ = bf16[16,4224]{1,0:T(8,128)(2,1)S(1)} collective-permute-done((bf16[16,4224]{1,0:T(8,128)(2,1)S(1)}, bf16[16,4224]{1,0:T(8,128)(2,1)S(1)}, u32[]{:S(2)}, u32[]{:S(2)}) %collective-permute-start.28) | collective-permute-done | bytes 135200 | tf_op jit(solution)/shard_map/ppermute | solution.py:702
  124.8 4.6 %hidden_first.1 = (f32[256,768]{1,0:T(8,128)S(1)}, f32[256,768]{1,0:T(8,128)S(1)}, bf16[4096,768]{1,0:T(8,128)(2,1)S(1)}, bf16[4096,768]{1,0:T(8,128)(2,1)S(1)}) custom-call(s32[1]{0:T(128)} %bitcast.me_ref.refs_0_, bf16[256,4224]{1,0:T(8,128)(2,1)S(1)} %place.7.rows_ref.own_ref, bf16[4096,768]{1,0:T(8,128)(2,1)S(1)} %get-tuple-element.159.gate_ref, ...), custom_call_target="tpu_custom_call" | custom-call | flops 3221225472 | bytes 12582912 | tf_op jit(solution)/shard_map/hidden_first/pallas_call | solution.py:529
  129.4 4.6 %hidden_second.1 = (bf16[256,768]{1,0:T(8,128)(2,1)S(1)}, bf16[768,4096]{1,0:T(8,128)(2,1)S(1)}, bf16[768,4096]{1,0:T(8,128)(2,1)S(1)}) custom-call(bf16[256,4224]{1,0:T(8,128)(2,1)S(1)} %collective-permute-done.32.rows_ref, bf16[4096,768]{1,0:T(8,128)(2,1)S(1)} %get-tuple-element.161.gate_ref, bf16[4096,768]{1,0:T(8,128)(2,1)S(1)} %get-tuple-element.162.up_ref, ...), custom_call_target="tpu_custom_call" | custom-call | flops 3221225472 | bytes 12582912 | tf_op jit(solution)/shard_map/hidden_second/pallas_call | solution.py:539
  134.1 2.4 %down.2 = (bf16[128,4096]{1,0:T(8,128)(2,1)S(1)}, bf16[128,4096]{1,0:T(8,128)(2,1)S(1)}, bf16[128,8192]{1,0:T(8,128)(2,1)}) custom-call(bf16[256,768]{1,0:T(8,128)(2,1)S(1)} %get-tuple-element.165.hidden_ref, bf16[768,4096]{1,0:T(8,128)(2,1)S(1)} %get-tuple-element.166.down_ref, s32[1]{0:T(128)} %bitcast.me_ref.refs_0_, ...), custom_call_target="tpu_custom_call" | custom-call | flops 1610612736 | bytes 8388608 | tf_op jit(solution)/shard_map/down/pallas_call | solution.py:591
  136.6 2.3 %down.3 = (bf16[128,4096]{1,0:T(8,128)(2,1)S(1)}, bf16[128,4096]{1,0:T(8,128)(2,1)S(1)}) custom-call(bf16[256,768]{1,0:T(8,128)(2,1)S(1)} %get-tuple-element.165.hidden_ref, bf16[768,4096]{1,0:T(8,128)(2,1)S(1)} %get-tuple-element.170.down_ref), custom_call_target="tpu_custom_call" | custom-call | flops 1610612736 | bytes 8388608 | tf_op jit(solution)/shard_map/down/pallas_call | solution.py:591
  151.1 1.7 %collective-permute-start.50 = (bf16[16,4096]{1,0:T(8,128)(2,1)S(1)}, bf16[16,4096]{1,0:T(8,128)(2,1)S(1)}, u32[]{:S(2)}, u32[]{:S(2)}) collective-permute-start(bf16[16,4096]{1,0:T(8,128)(2,1)S(1)} %add.30), channel_id=1, source_target_pairs={{4,0},{5,1},{8,4},{9,5},{12,8},{13,9},{14,12},{15,13},{10,14},{11,... | collective-permute-start | bytes 393224 | tf_op jit(solution)/shard_map/ppermute | solution.py:703
  153.3 1.8 %collective-permute-start.41 = (bf16[16,4096]{1,0:T(8,128)(2,1)S(1)}, bf16[16,4096]{1,0:T(8,128)(2,1)S(1)}, u32[]{:S(2)}, u32[]{:S(2)}) collective-permute-start(bf16[16,4096]{1,0:T(8,128)(2,1)S(1)} %add.22), channel_id=1, source_target_pairs={{4,0},{5,1},{8,4},{9,5},{12,8},{13,9},{14,12},{15,13},{10,14},{11,... | collective-permute-start | bytes 393224 | tf_op jit(solution)/shard_map/ppermute | solution.py:703
  155.5 1.8 %collective-permute-done.50.refs_0_ = bf16[16,4096]{1,0:T(8,128)(2,1)S(1)} collective-permute-done((bf16[16,4096]{1,0:T(8,128)(2,1)S(1)}, bf16[16,4096]{1,0:T(8,128)(2,1)S(1)}, u32[]{:S(2)}, u32[]{:S(2)}) %collective-permute-start.50) | collective-permute-done | bytes 131104 | tf_op jit(solution)/shard_map/ppermute | solution.py:703
  157.9 1.8 %collective-permute-start.51 = (bf16[16,4096]{1,0:T(8,128)(2,1)S(1)}, bf16[16,4096]{1,0:T(8,128)(2,1)S(1)}, u32[]{:S(2)}, u32[]{:S(2)}) collective-permute-start(bf16[16,4096]{1,0:T(8,128)(2,1)S(1)} %add.31), channel_id=1, source_target_pairs={{4,0},{5,1},{8,4},{9,5},{12,8},{13,9},{14,12},{15,13},{10,14},{11,... | collective-permute-start | bytes 393224 | tf_op jit(solution)/shard_map/ppermute | solution.py:703
  166.4 1.7 collective-permute-done.38.refs_2_
  (123 shorter events, 46.8 us)
Async XLA Ops:
  3.1 10.0 %collective-permute-start.1 = (bf16[256,512]{1,0:T(8,128)(2,1)S(1)}, bf16[256,512]{1,0:T(8,128)(2,1)S(1)}, u32[]{:S(2)}, u32[]{:S(2)}) collective-permute-start(bf16[256,512]{1,0:T(8,128)(2,1)S(1)} %get-tuple-element.91.own_ref.refs_9_), channel_id=1, source_target_pairs={{0,4},{1,5},{4,8},{5,9},{8,12},{9,13},{12,14},{13,15},{14,10},{15,... | collective-permute-start | bytes 786440 | tf_op jit(solution)/shard_map/ppermute | solution.py:702
  6.1 9.2 %collective-permute-start.2 = (bf16[256,512]{1,0:T(8,128)(2,1)S(1)}, bf16[256,512]{1,0:T(8,128)(2,1)S(1)}, u32[]{:S(2)}, u32[]{:S(2)}) collective-permute-start(bf16[256,512]{1,0:T(8,128)(2,1)S(1)} %get-tuple-element.91.own_ref.refs_9_), channel_id=1, source_target_pairs={{4,0},{5,1},{8,4},{9,5},{12,8},{13,9},{14,12},{15,13},{10,14},{11,... | collective-permute-start | bytes 786440 | tf_op jit(solution)/shard_map/ppermute | solution.py:703
  6.1 12.3 %collective-permute-start.6 = (bf16[256,512]{1,0:T(8,128)(2,1)S(1)}, bf16[256,512]{1,0:T(8,128)(2,1)S(1)}, u32[]{:S(2)}, u32[]{:S(2)}) collective-permute-start(bf16[256,512]{1,0:T(8,128)(2,1)S(1)} %get-tuple-element.92), channel_id=1, source_target_pairs={{0,5},{1,4},{4,9},{5,8},{8,13},{9,12},{12,15},{13,14},{14,11},{15,... | collective-permute-start | bytes 786440 | tf_op jit(solution)/shard_map/ppermute | solution.py:727
  7.3 11.3 %collective-permute-start.7 = (bf16[256,512]{1,0:T(8,128)(2,1)S(1)}, bf16[256,512]{1,0:T(8,128)(2,1)S(1)}, u32[]{:S(2)}, u32[]{:S(2)}) collective-permute-start(bf16[256,512]{1,0:T(8,128)(2,1)S(1)} %get-tuple-element.92), channel_id=1, source_target_pairs={{4,1},{5,0},{8,5},{9,4},{12,9},{13,8},{14,13},{15,12},{10,15},{11,... | collective-permute-start | bytes 786440 | tf_op jit(solution)/shard_map/ppermute | solution.py:727
  15.3 8.7 %collective-permute-start.4 = (bf16[256,512]{1,0:T(8,128)(2,1)S(1)}, bf16[256,512]{1,0:T(8,128)(2,1)S(1)}, u32[]{:S(2)}, u32[]{:S(2)}) collective-permute-start(bf16[256,512]{1,0:T(8,128)(2,1)S(1)} %collective-permute-done.1.refs_0_.refs_11_), channel_id=1, source_target_pairs={{0,4},{1,5},{4,8},{5,9},{8,12},{9,13},{12,14},{13,15},{14,10},{15,... | collective-permute-start | bytes 786440 | tf_op jit(solution)/shard_map/ppermute | solution.py:702
  16.9 8.8 %collective-permute-start.5 = (bf16[256,512]{1,0:T(8,128)(2,1)S(1)}, bf16[256,512]{1,0:T(8,128)(2,1)S(1)}, u32[]{:S(2)}, u32[]{:S(2)}) collective-permute-start(bf16[256,512]{1,0:T(8,128)(2,1)S(1)} %collective-permute-done.2.refs_2_.refs_13_), channel_id=1, source_target_pairs={{4,0},{5,1},{8,4},{9,5},{12,8},{13,9},{14,12},{15,13},{10,14},{11,... | collective-permute-start | bytes 786440 | tf_op jit(solution)/shard_map/ppermute | solution.py:703
  18.5 11.0 %collective-permute-start.10 = (bf16[256,512]{1,0:T(8,128)(2,1)S(1)}, bf16[256,512]{1,0:T(8,128)(2,1)S(1)}, u32[]{:S(2)}, u32[]{:S(2)}) collective-permute-start(bf16[256,512]{1,0:T(8,128)(2,1)S(1)} %collective-permute-done.6.refs_1_.refs_12_), channel_id=1, source_target_pairs={{0,4},{1,5},{4,8},{5,9},{8,12},{9,13},{12,14},{13,15},{14,10},{15,... | collective-permute-start | bytes 786440 | tf_op jit(solution)/shard_map/ppermute | solution.py:702
  20.5 10.8 %collective-permute-start.11 = (bf16[256,512]{1,0:T(8,128)(2,1)S(1)}, bf16[256,512]{1,0:T(8,128)(2,1)S(1)}, u32[]{:S(2)}, u32[]{:S(2)}) collective-permute-start(bf16[256,512]{1,0:T(8,128)(2,1)S(1)} %collective-permute-done.7.refs_3_.refs_14_), channel_id=1, source_target_pairs={{4,0},{5,1},{8,4},{9,5},{12,8},{13,9},{14,12},{15,13},{10,14},{11,... | collective-permute-start | bytes 786440 | tf_op jit(solution)/shard_map/ppermute | solution.py:703
  25.7 9.5 %collective-permute-start.8 = (bf16[256,512]{1,0:T(8,128)(2,1)S(1)}, bf16[256,512]{1,0:T(8,128)(2,1)S(1)}, u32[]{:S(2)}, u32[]{:S(2)}) collective-permute-start(bf16[256,512]{1,0:T(8,128)(2,1)S(1)} %collective-permute-done.4.refs_0_.refs_15_), channel_id=1, source_target_pairs={{0,4},{1,5},{4,8},{5,9},{8,12},{9,13},{12,14},{13,15},{14,10},{15,... | collective-permute-start | bytes 786440 | tf_op jit(solution)/shard_map/ppermute | solution.py:702
  27.3 9.7 %collective-permute-start.9 = (bf16[256,512]{1,0:T(8,128)(2,1)S(1)}, bf16[256,512]{1,0:T(8,128)(2,1)S(1)}, u32[]{:S(2)}, u32[]{:S(2)}) collective-permute-start(bf16[256,512]{1,0:T(8,128)(2,1)S(1)} %collective-permute-done.5.refs_2_.refs_17_), channel_id=1, source_target_pairs={{4,0},{5,1},{8,4},{9,5},{12,8},{13,9},{14,12},{15,13},{10,14},{11,... | collective-permute-start | bytes 786440 | tf_op jit(solution)/shard_map/ppermute | solution.py:703
  31.3 9.5 %collective-permute-start.13 = (bf16[256,512]{1,0:T(8,128)(2,1)S(1)}, bf16[256,512]{1,0:T(8,128)(2,1)S(1)}, u32[]{:S(2)}, u32[]{:S(2)}) collective-permute-start(bf16[256,512]{1,0:T(8,128)(2,1)S(1)} %collective-permute-done.10.refs_1_.refs_16_), channel_id=1, source_target_pairs={{0,4},{1,5},{4,8},{5,9},{8,12},{9,13},{12,14},{13,15},{14,10},{15,... | collective-permute-start | bytes 786440 | tf_op jit(solution)/shard_map/ppermute | solution.py:702
  32.9 9.3 %collective-permute-start.14 = (bf16[256,512]{1,0:T(8,128)(2,1)S(1)}, bf16[256,512]{1,0:T(8,128)(2,1)S(1)}, u32[]{:S(2)}, u32[]{:S(2)}) collective-permute-start(bf16[256,512]{1,0:T(8,128)(2,1)S(1)} %collective-permute-done.11.refs_3_.refs_18_), channel_id=1, source_target_pairs={{4,0},{5,1},{8,4},{9,5},{12,8},{13,9},{14,12},{15,13},{10,14},{11,... | collective-permute-start | bytes 786440 | tf_op jit(solution)/shard_map/ppermute | solution.py:703
  36.9 12.2 %collective-permute-start.12 = (bf16[256,512]{1,0:T(8,128)(2,1)S(1)}, bf16[256,512]{1,0:T(8,128)(2,1)S(1)}, u32[]{:S(2)}, u32[]{:S(2)}) collective-permute-start(bf16[256,512]{1,0:T(8,128)(2,1)S(1)} %collective-permute-done.8.refs_0_.refs_19_), channel_id=1, source_target_pairs={{0,4},{1,5},{4,8},{5,9},{8,12},{9,13},{12,14},{13,15},{14,10},{15,... | collective-permute-start | bytes 786440 | tf_op jit(solution)/shard_map/ppermute | solution.py:702
  42.2 6.9 %collective-permute-start.15 = (bf16[128,512]{1,0:T(8,128)(2,1)S(1)}, bf16[128,512]{1,0:T(8,128)(2,1)S(1)}, u32[]{:S(2)}, u32[]{:S(2)}) collective-permute-start(bf16[128,512]{1,0:T(8,128)(2,1)S(1)} %slice.6), channel_id=1, source_target_pairs={{0,4},{1,5},{4,8},{5,9},{8,12},{9,13},{12,14},{13,15},{14,10},{15,... | collective-permute-start | bytes 393224 | tf_op jit(solution)/shard_map/ppermute | solution.py:702
  55.8 6.5 %collective-permute-start.20 = (bf16[16,4224]{1,0:T(8,128)(2,1)S(1)}, bf16[16,4224]{1,0:T(8,128)(2,1)S(1)}, u32[]{:S(2)}, u32[]{:S(2)}) collective-permute-start(bf16[16,4224]{1,0:T(8,128)(2,1)S(1)} %get-tuple-element.138.refs_1_), channel_id=1, source_target_pairs={{0,4},{1,5},{4,8},{5,9},{8,12},{9,13},{12,14},{13,15},{14,10},{15,... | collective-permute-start | bytes 405512 | tf_op jit(solution)/shard_map/ppermute | solution.py:702
  56.1 8.6 %collective-permute-start.21 = (bf16[16,4224]{1,0:T(8,128)(2,1)S(1)}, bf16[16,4224]{1,0:T(8,128)(2,1)S(1)}, u32[]{:S(2)}, u32[]{:S(2)}) collective-permute-start(bf16[16,4224]{1,0:T(8,128)(2,1)S(1)} %get-tuple-element.137.refs_0_), channel_id=1, source_target_pairs={{0,4},{1,5},{4,8},{5,9},{8,12},{9,13},{12,14},{13,15},{14,10},{15,... | collective-permute-start | bytes 405512 | tf_op jit(solution)/shard_map/ppermute | solution.py:702
  58.5 46.4 %collective-permute-start.22 = (bf16[16,4224]{1,0:T(8,128)(2,1)S(1)}, bf16[16,4224]{1,0:T(8,128)(2,1)S(1)}, u32[]{:S(2)}, u32[]{:S(2)}) collective-permute-start(bf16[16,4224]{1,0:T(8,128)(2,1)S(1)} %get-tuple-element.138.refs_1_), channel_id=1, source_target_pairs={{4,0},{5,1},{8,4},{9,5},{12,8},{13,9},{14,12},{15,13},{10,14},{11,... | collective-permute-start | bytes 405512 | tf_op jit(solution)/shard_map/ppermute | solution.py:703
  59.5 45.5 %collective-permute-start.19 = (bf16[16,4224]{1,0:T(8,128)(2,1)S(1)}, bf16[16,4224]{1,0:T(8,128)(2,1)S(1)}, u32[]{:S(2)}, u32[]{:S(2)}) collective-permute-start(bf16[16,4224]{1,0:T(8,128)(2,1)S(1)} %collective-permute-done.18.refs_0_), channel_id=1, source_target_pairs={{4,0},{5,1},{8,4},{9,5},{12,8},{13,9},{14,12},{15,13},{10,14},{11,... | collective-permute-start | bytes 405512 | tf_op jit(solution)/shard_map/ppermute | solution.py:703
  62.3 49.8 %collective-permute-start.24 = (bf16[16,4224]{1,0:T(8,128)(2,1)S(1)}, bf16[16,4224]{1,0:T(8,128)(2,1)S(1)}, u32[]{:S(2)}, u32[]{:S(2)}) collective-permute-start(bf16[16,4224]{1,0:T(8,128)(2,1)S(1)} %collective-permute-done.20.refs_1_), channel_id=1, source_target_pairs={{0,4},{1,5},{4,8},{5,9},{8,12},{9,13},{12,14},{13,15},{14,10},{15,... | collective-permute-start | bytes 405512 | tf_op jit(solution)/shard_map/ppermute | solution.py:702
  64.7 47.4 %collective-permute-start.25 = (bf16[16,4224]{1,0:T(8,128)(2,1)S(1)}, bf16[16,4224]{1,0:T(8,128)(2,1)S(1)}, u32[]{:S(2)}, u32[]{:S(2)}) collective-permute-start(bf16[16,4224]{1,0:T(8,128)(2,1)S(1)} %collective-permute-done.21.refs_2_), channel_id=1, source_target_pairs={{0,4},{1,5},{4,8},{5,9},{8,12},{9,13},{12,14},{13,15},{14,10},{15,... | collective-permute-start | bytes 405512 | tf_op jit(solution)/shard_map/ppermute | solution.py:702
  105.0 7.9 %collective-permute-start.26 = (bf16[16,4224]{1,0:T(8,128)(2,1)S(1)}, bf16[16,4224]{1,0:T(8,128)(2,1)S(1)}, u32[]{:S(2)}, u32[]{:S(2)}) collective-permute-start(bf16[16,4224]{1,0:T(8,128)(2,1)S(1)} %collective-permute-done.22.refs_3_), channel_id=1, source_target_pairs={{4,0},{5,1},{8,4},{9,5},{12,8},{13,9},{14,12},{15,13},{10,14},{11,... | collective-permute-start | bytes 405512 | tf_op jit(solution)/shard_map/ppermute | solution.py:703
  105.0 10.8 %collective-permute-start.23 = (bf16[16,4224]{1,0:T(8,128)(2,1)S(1)}, bf16[16,4224]{1,0:T(8,128)(2,1)S(1)}, u32[]{:S(2)}, u32[]{:S(2)}) collective-permute-start(bf16[16,4224]{1,0:T(8,128)(2,1)S(1)} %collective-permute-done.19.refs_0_), channel_id=1, source_target_pairs={{4,0},{5,1},{8,4},{9,5},{12,8},{13,9},{14,12},{15,13},{10,14},{11,... | collective-permute-start | bytes 405512 | tf_op jit(solution)/shard_map/ppermute | solution.py:703
  112.8 6.9 %collective-permute-start.29 = (bf16[16,4224]{1,0:T(8,128)(2,1)S(1)}, bf16[16,4224]{1,0:T(8,128)(2,1)S(1)}, u32[]{:S(2)}, u32[]{:S(2)}) collective-permute-start(bf16[16,4224]{1,0:T(8,128)(2,1)S(1)} %collective-permute-done.26.refs_3_), channel_id=1, source_target_pairs={{4,0},{5,1},{8,4},{9,5},{12,8},{13,9},{14,12},{15,13},{10,14},{11,... | collective-permute-start | bytes 405512 | tf_op jit(solution)/shard_map/ppermute | solution.py:703
  124.3 9.8 %collective-permute-start.33 = (bf16[128,4096]{1,0:T(8,128)(2,1)S(1)}, bf16[128,4096]{1,0:T(8,128)(2,1)S(1)}, u32[]{:S(2)}, u32[]{:S(2)}) collective-permute-start(bf16[128,4096]{1,0:T(8,128)(2,1)S(1)} %get-tuple-element.168), channel_id=1, source_target_pairs={{0,1},{1,0},{2,3},{3,2},{4,5},{5,4},{6,7},{7,6},{8,9},{9,8},{10,11... | collective-permute-start | bytes 3145736 | tf_op jit(solution)/shard_map/ppermute | solution.py:704
  143.9 6.1 %collective-permute-start.49 = (bf16[16,4096]{1,0:T(8,128)(2,1)S(1)}, bf16[16,4096]{1,0:T(8,128)(2,1)S(1)}, u32[]{:S(2)}, u32[]{:S(2)}) collective-permute-start(bf16[16,4096]{1,0:T(8,128)(2,1)S(1)} %add.29), channel_id=1, source_target_pairs={{4,0},{5,1},{8,4},{9,5},{12,8},{13,9},{14,12},{15,13},{10,14},{11,... | collective-permute-start | bytes 393224 | tf_op jit(solution)/shard_map/ppermute | solution.py:703
  144.8 6.3 %collective-permute-start.45 = (bf16[16,4096]{1,0:T(8,128)(2,1)S(1)}, bf16[16,4096]{1,0:T(8,128)(2,1)S(1)}, u32[]{:S(2)}, u32[]{:S(2)}) collective-permute-start(bf16[16,4096]{1,0:T(8,128)(2,1)S(1)} %add.25), channel_id=1, source_target_pairs={{0,4},{1,5},{4,8},{5,9},{8,12},{9,13},{12,14},{13,15},{14,10},{15,... | collective-permute-start | bytes 393224 | tf_op jit(solution)/shard_map/ppermute | solution.py:702
  146.5 6.8 %collective-permute-start.40 = (bf16[16,4096]{1,0:T(8,128)(2,1)S(1)}, bf16[16,4096]{1,0:T(8,128)(2,1)S(1)}, u32[]{:S(2)}, u32[]{:S(2)}) collective-permute-start(bf16[16,4096]{1,0:T(8,128)(2,1)S(1)} %add.21), channel_id=1, source_target_pairs={{4,0},{5,1},{8,4},{9,5},{12,8},{13,9},{14,12},{15,13},{10,14},{11,... | collective-permute-start | bytes 393224 | tf_op jit(solution)/shard_map/ppermute | solution.py:703
  147.1 8.0 %collective-permute-start.36 = (bf16[16,4096]{1,0:T(8,128)(2,1)S(1)}, bf16[16,4096]{1,0:T(8,128)(2,1)S(1)}, u32[]{:S(2)}, u32[]{:S(2)}) collective-permute-start(bf16[16,4096]{1,0:T(8,128)(2,1)S(1)} %add.17), channel_id=1, source_target_pairs={{0,4},{1,5},{4,8},{5,9},{8,12},{9,13},{12,14},{13,15},{14,10},{15,... | collective-permute-start | bytes 393224 | tf_op jit(solution)/shard_map/ppermute | solution.py:702
  151.1 6.2 %collective-permute-start.50 = (bf16[16,4096]{1,0:T(8,128)(2,1)S(1)}, bf16[16,4096]{1,0:T(8,128)(2,1)S(1)}, u32[]{:S(2)}, u32[]{:S(2)}) collective-permute-start(bf16[16,4096]{1,0:T(8,128)(2,1)S(1)} %add.30), channel_id=1, source_target_pairs={{4,0},{5,1},{8,4},{9,5},{12,8},{13,9},{14,12},{15,13},{10,14},{11,... | collective-permute-start | bytes 393224 | tf_op jit(solution)/shard_map/ppermute | solution.py:703
  153.3 6.6 %collective-permute-start.41 = (bf16[16,4096]{1,0:T(8,128)(2,1)S(1)}, bf16[16,4096]{1,0:T(8,128)(2,1)S(1)}, u32[]{:S(2)}, u32[]{:S(2)}) collective-permute-start(bf16[16,4096]{1,0:T(8,128)(2,1)S(1)} %add.22), channel_id=1, source_target_pairs={{4,0},{5,1},{8,4},{9,5},{12,8},{13,9},{14,12},{15,13},{10,14},{11,... | collective-permute-start | bytes 393224 | tf_op jit(solution)/shard_map/ppermute | solution.py:703
  155.2 6.3 %collective-permute-start.37 = (bf16[16,4096]{1,0:T(8,128)(2,1)S(1)}, bf16[16,4096]{1,0:T(8,128)(2,1)S(1)}, u32[]{:S(2)}, u32[]{:S(2)}) collective-permute-start(bf16[16,4096]{1,0:T(8,128)(2,1)S(1)} %add.18), channel_id=1, source_target_pairs={{0,4},{1,5},{4,8},{5,9},{8,12},{9,13},{12,14},{13,15},{14,10},{15,... | collective-permute-start | bytes 393224 | tf_op jit(solution)/shard_map/ppermute | solution.py:702
  157.9 6.0 %collective-permute-start.51 = (bf16[16,4096]{1,0:T(8,128)(2,1)S(1)}, bf16[16,4096]{1,0:T(8,128)(2,1)S(1)}, u32[]{:S(2)}, u32[]{:S(2)}) collective-permute-start(bf16[16,4096]{1,0:T(8,128)(2,1)S(1)} %add.31), channel_id=1, source_target_pairs={{4,0},{5,1},{8,4},{9,5},{12,8},{13,9},{14,12},{15,13},{10,14},{11,... | collective-permute-start | bytes 393224 | tf_op jit(solution)/shard_map/ppermute | solution.py:703
  (23 other events, 115.7 us)
